TPU v7x, 32 devices: a whole 2x2x4 slice. The times are simulated.
32 devices in a mesh: region: 8 (over z, x), mode: 4 (over y, core).
Axes of the slice: x: 2, y: 2, z: 4, core: 2. Of those that a mesh axis runs over, the one named last changes fastest.
Arguments:
- measured: float32 [8, 256, 256], P('region'), may hold values from 0.05 to 20
- probe_modes: float32 [2, 4, 256, 256], P(None, 'mode'), may hold values from -1.5 to 1.5
- object_bands: float32 [2, 1024, 512], P(None, 'region'), may hold values from -4.2 to 4.2
- scan_offsets: int32 [8, 2], replicated, may hold values from 0 to 767, as said below
- band_owner: int32 [8], replicated, may hold values from 0 to 7, each once
Outputs:
- probe_out: float32 [2, 4, 256, 256], P(None, 'mode')
- object_out: float32 [2, 1024, 512], P(None, 'region')
Inputs may be any that keep to these rules, and one draw needn't show every extreme that they name: `scan_offsets`: every frame covers rows r to r + 255 within the bands r // 128 to r // 128 + 2; no band is covered by two frames of one region (frames f * 1 to f + 1 - 1 form region f).
All inputs are finite; a program needn't handle non-finite values.
Results may differ from a plain program's by a relative error of at most 0.0001.
Values sent between devices are 32-bit elements; how exact they have to be, the bound alone decides.
No kernel may reach another device: no remote copies, remote signals or barrier semaphores. Data moves between devices by JAX's collectives and lax.ppermute only.
A program may use at most 64 MiB of HBM per device.

v0:
```python
import math

import jax
import jax.numpy as jnp
from jax import lax
from jax.sharding import PartitionSpec as P

intensity_offset = 0.1
probe_damping = 1.0
object_damping = 1.0
highest = lax.Precision.HIGHEST


def fourier_tables(length, orientation):
    positions = jnp.arange(length, dtype=jnp.int32)
    product = positions[:, None] * positions[None, :] % length
    angles = product.astype(jnp.float32) * (2.0 * math.pi / length)
    normalizer = 1.0 / math.sqrt(length)
    cosine_table = jnp.cos(angles) * normalizer
    sine_table = orientation * jnp.sin(angles) * normalizer
    return (cosine_table, cosine_table + sine_table, sine_table - cosine_table)


def left_product(matrix, planes):
    return jnp.einsum("jk,...kl->...jl", matrix, planes, precision=highest)


def right_product(planes, matrix):
    return jnp.einsum("...jk,kl->...jl", planes, matrix, precision=highest)


def transform(real_part, imag_part, tables):
    cosine_table, plus_table, minus_table = tables
    common = left_product(cosine_table, real_part + imag_part)
    left_real = common - left_product(plus_table, imag_part)
    left_imag = common + left_product(minus_table, real_part)
    common = right_product(left_real + left_imag, cosine_table)
    right_real = common - right_product(left_imag, plus_table)
    right_imag = common + right_product(left_real, minus_table)
    return (right_real, right_imag)


def wave_change(probe_modes, windows, root_measured, forward_tables, inverse_tables):
    probe_real = probe_modes[0][None]
    probe_imag = probe_modes[1][None]
    window_real = windows[:, 0][:, None]
    window_imag = windows[:, 1][:, None]
    exit_real = probe_real * window_real - probe_imag * window_imag
    exit_imag = probe_real * window_imag + probe_imag * window_real
    wave_real, wave_imag = transform(exit_real, exit_imag, forward_tables)
    local_sum = jnp.sum(wave_real * wave_real + wave_imag * wave_imag, axis=1)
    summed = lax.psum(local_sum, "mode")
    factor = (root_measured / jnp.sqrt(summed + intensity_offset) - 1.0)[:, None]
    return transform(wave_real * factor, wave_imag * factor, inverse_tables)


def body(measured, probe_modes, object_bands, scan_offsets, band_owner):
    frames_dev = measured.shape[0]
    length = measured.shape[1]
    band_rows = length // 2
    width_total = object_bands.shape[2]
    region_count = lax.axis_size("region")
    mode_count = lax.axis_size("mode")
    share_rows = band_rows // mode_count
    region_index = lax.axis_index("region")
    mode_index = lax.axis_index("mode")
    forward_tables = fourier_tables(length, -1.0)
    inverse_tables = fourier_tables(length, 1.0)
    region_range = jnp.arange(region_count, dtype=jnp.int32)
    own_band = jnp.sum(region_range * (band_owner == region_index).astype(jnp.int32))
    first_rows = scan_offsets[:, 0]
    anchors = first_rows // band_rows
    touched = (
        ((anchors <= own_band) & (own_band <= anchors + 2))
        .astype(jnp.int32)
        .reshape(region_count, frames_dev)
    )
    source_has = jnp.sum(touched, axis=1)
    source_column = jnp.sum(touched * scan_offsets[:, 1].reshape(region_count, frames_dev), axis=1)
    own_rows = lax.dynamic_slice_in_dim(object_bands, mode_index * share_rows, share_rows, 1)

    def cut_piece(column, present):
        return lax.dynamic_slice_in_dim(own_rows, column, length, 2) * present.astype(jnp.float32)

    outgoing = jax.vmap(cut_piece)(source_column, source_has)
    incoming = lax.all_to_all(outgoing, "region", split_axis=0, concat_axis=0, tiled=True)
    own_offsets = lax.dynamic_slice_in_dim(scan_offsets, region_index * frames_dev, frames_dev, 0)
    own_anchor = own_offsets[:, 0] // band_rows
    own_lead = own_offsets[:, 0] - own_anchor * band_rows
    needed = (own_anchor[:, None] + jnp.arange(3, dtype=jnp.int32)[None, :]).reshape(-1)
    holder = jnp.sum(
        band_owner[None, :] * (needed[:, None] == region_range[None, :]).astype(jnp.int32), axis=1
    )
    selector = (holder[None, :] == region_range[:, None]).astype(jnp.float32)
    chosen = jnp.einsum("sp,scrn->pcrn", selector, incoming, precision=highest)
    assembled = lax.all_gather(chosen, "mode", axis=2, tiled=True)
    stacked = assembled.reshape(frames_dev, 3, 2, band_rows, length)
    stacked_rows = jnp.concatenate([stacked[:, 0], stacked[:, 1], stacked[:, 2]], axis=2)
    windows = jax.vmap(
        lambda frame_rows, lead_rows: lax.dynamic_slice_in_dim(frame_rows, lead_rows, length, 1)
    )(stacked_rows, own_lead)
    root_measured = jnp.sqrt(measured)
    window_real = windows[:, 0][:, None]
    window_imag = windows[:, 1][:, None]
    object_power = jnp.sum(windows[:, 0] ** 2 + windows[:, 1] ** 2, axis=0)
    change_real, change_imag = wave_change(
        probe_modes, windows, root_measured, forward_tables, inverse_tables
    )
    grad_real = jnp.sum(window_real * change_real + window_imag * change_imag, axis=0)
    grad_imag = jnp.sum(window_real * change_imag - window_imag * change_real, axis=0)
    gradient = jnp.stack([grad_real, grad_imag])
    gradient, power_total = lax.psum((gradient, object_power), "region")
    probe_modes = probe_modes + gradient / (power_total + probe_damping)
    change_real, change_imag = wave_change(
        probe_modes, windows, root_measured, forward_tables, inverse_tables
    )
    probe_real = probe_modes[0][None]
    probe_imag = probe_modes[1][None]
    numer_real = jnp.sum(probe_real * change_real + probe_imag * change_imag, axis=1)
    numer_imag = jnp.sum(probe_real * change_imag - probe_imag * change_real, axis=1)
    mode_power = jnp.sum(probe_modes[0] ** 2 + probe_modes[1] ** 2, axis=0)
    power_modes = lax.psum(mode_power, "mode")

    def split_pieces(frame_rows, lead_rows):
        return jnp.stack(
            [
                lax.dynamic_slice_in_dim(
                    frame_rows, band_rows - lead_rows + piece_number * band_rows, band_rows, 1
                )
                for piece_number in range(3)
            ]
        )

    channels = jnp.stack([numer_real, numer_imag], axis=1)
    padded = jnp.pad(channels, ((0, 0), (0, 0), (band_rows, band_rows), (0, 0)))
    pieces = jax.vmap(split_pieces)(padded, own_lead)
    row_pieces = lax.psum_scatter(pieces, "mode", scatter_dimension=3, tiled=True)
    power_frames = jnp.broadcast_to(
        jnp.pad(power_modes, ((band_rows, band_rows), (0, 0)))[None, None],
        (frames_dev, 1, 2 * band_rows + length, length),
    )
    power_pieces = jax.vmap(split_pieces)(power_frames, own_lead)
    power_share = lax.dynamic_slice_in_dim(power_pieces, mode_index * share_rows, share_rows, 3)
    row_pieces = jnp.concatenate([row_pieces, power_share], axis=2)
    channel_count = row_pieces.shape[2]
    flat_pieces = row_pieces.reshape(frames_dev * 3, channel_count, share_rows, length)
    outgoing_update = jnp.einsum("sp,pcrn->scrn", selector, flat_pieces, precision=highest)
    arriving = lax.all_to_all(outgoing_update, "region", split_axis=0, concat_axis=0, tiled=True)

    def place_piece(piece_rows, column):
        blank = jnp.zeros((piece_rows.shape[0], share_rows, width_total), jnp.float32)
        return lax.dynamic_update_slice_in_dim(blank, piece_rows, column, 2)

    placed = jnp.sum(jax.vmap(place_piece)(arriving, source_column), axis=0)
    density_rows = placed[2]
    new_rows = own_rows + placed[0:2] / (density_rows + object_damping)
    object_out = lax.all_gather(new_rows, "mode", axis=1, tiled=True)
    return (probe_modes, object_out)


def solution(mesh):
    in_specs = (
        P("region", None, None),
        P(None, "mode", None, None),
        P(None, "region", None),
        P(),
        P(),
    )
    out_specs = (P(None, "mode", None, None), P(None, "region", None))
    return jax.shard_map(body, mesh=mesh, in_specs=in_specs, out_specs=out_specs, check_vma=False)
```

profile of v0, /device:TPU:0, one launch (start us, length us, event | category | flops | bytes accessed | tf_op | source)
XLA Modules:
  0.0 386.2 jit_solution(12646329658769032133)
XLA Ops:
  11.6 2.8 gather_fusion
  16.2 7.3 %all-to-all-start = ((f32[8,2,32,256]{3,2,1,0:T(8,128)}), f32[8,2,32,256]{3,2,1,0:T(8,128)S(1)}, u32[]{:S(2)}, u32[]{:S(2)}) async-start(f32[8,2,32,256]{3,2,1,0:T(8,128)} %broadcast_multiply_fusion), calls=%async_computation | async-start | bytes 1048576 | tf_op jit(solution)/shard_map/all_to_all | solution.py:86
  28.0 9.9 %all-to-all-done = f32[8,2,32,256]{3,2,1,0:T(8,128)S(1)} async-done(((f32[8,2,32,256]{3,2,1,0:T(8,128)}), f32[8,2,32,256]{3,2,1,0:T(8,128)S(1)}, u32[]{:S(2)}, u32[]{:S(2)}) %all-to-all-start) | async-done | bytes 524320 | tf_op jit(solution)/shard_map/all_to_all | solution.py:86
  38.7 10.6 %all_gather.6 = f32[3,2,128,256]{3,0,2,1:T(4,128)S(1)} all-gather(f32[3,2,32,256]{3,0,2,1:T(4,128)S(1)} %fusion.2), channel_id=1, replica_groups=mesh['region'=8,'mode'=4] {'mode'}, dimensions={2}, use_global_device_ids=true | all-gather | bytes 983040 | tf_op jit(solution)/shard_map/all_gather | solution.py:96
  62.8 30.9 %all-reduce.11.cloned.1.call-done = f32[1,256,256]{2,1,0:T(8,128)} async-done(((f32[1,256,256]{2,1,0:T(8,128)}), f32[1,256,256]{2,1,0:T(8,128)}) %all-reduce.11.cloned.1.call-update) | async-done | bytes 262160 | tf_op jit(solution)/shard_map/psum | solution.py:52
  93.8 2.6 fusion.50
  107.3 74.8 %all-reduce.15.cloned.1.call-done = (f32[2,1,256,256]{3,0,2,1:T(2,128)}, f32[256,256]{1,0:T(8,128)}) async-done(((f32[2,1,256,256]{3,0,2,1:T(2,128)}, f32[256,256]{1,0:T(8,128)}), (f32[2,1,256,256]{3,0,2,1:T(2,128)}, f32[256,256]{1,0:T(8,128)})) %all-reduce.15.cloned.1.call-update) | async-done | bytes 786448 | tf_op jit(solution)/shard_map/psum | solution.py:112
  196.0 30.6 %all-reduce.13.cloned.1.call-done = f32[1,256,256]{2,1,0:T(8,128)} async-done(((f32[1,256,256]{2,1,0:T(8,128)}), f32[1,256,256]{2,1,0:T(8,128)}) %all-reduce.13.cloned.1.call-update) | async-done | bytes 262160 | tf_op jit(solution)/shard_map/psum | solution.py:52
  226.6 2.6 fusion.48
  243.2 35.0 %all-reduce.17.cloned.1.call-done = (f32[256,256]{1,0:T(8,128)}, f32[1,3,2,128,256]{4,2,1,0,3:T(2,128)}) async-done(((f32[256,256]{1,0:T(8,128)}, f32[1,3,2,128,256]{4,2,1,0,3:T(2,128)}), (f32[256,256]{1,0:T(8,128)}, f32[1,3,2,128,256]{4,2,1,0,3:T(2,128)})) %all-reduce.17.cloned.1.call-update) | async-done | bytes 1048592 | tf_op jit(solution)/shard_map/psum | solution.py:122
  282.3 5.5 %all-to-all-start.1 = ((f32[8,3,32,256]{3,2,1,0:T(8,128)}), f32[8,3,32,256]{3,2,1,0:T(8,128)S(1)}, u32[]{:S(2)}, u32[]{:S(2)}) async-start(f32[8,3,32,256]{3,2,1,0:T(8,128)} %copy.82), calls=%async_computation.1 | async-start | bytes 1572864 | tf_op jit(solution)/shard_map/all_to_all | solution.py:148
  288.7 18.9 %all-to-all-done.1 = f32[8,3,32,256]{3,2,1,0:T(8,128)S(1)} async-done(((f32[8,3,32,256]{3,2,1,0:T(8,128)}), f32[8,3,32,256]{3,2,1,0:T(8,128)S(1)}, u32[]{:S(2)}, u32[]{:S(2)}) %all-to-all-start.1) | async-done | bytes 786464 | tf_op jit(solution)/shard_map/all_to_all | solution.py:148
  307.9 62.6 %while.8 = (s32[]{:T(128)}, f32[8,3,32,512]{3,2,1,0:T(8,128)S(1)}, s32[8,4]{0,1:T(4,128)S(1)}, f32[8,3,32,256]{3,2,1,0:T(8,128)S(1)}, s32[]{:T(128)}, /*index=5*/s32[4]{0:T(128)S(1)}, s32[]{:T(128)}) while((s32[]{:T(128)}, f32[8,3,32,512]{3,2,1,0:T(8,128)S(1)}, s32[8,4]{0,1:T(4,128)S(1)}, f32[8,3,32,256]{3,2,1,0:T(8,128)S(1)}, s32[]{:T(128)}, ...), condition=%wide.while_cond.7, body=%wide.while_body.7.sunk | while | flops 24605 | bytes 491723 | solution.py:152
  308.6 3.2 and_reduce_fusion.2
  316.5 3.2 and_reduce_fusion.2
  324.1 3.2 and_reduce_fusion.2
  331.7 3.2 and_reduce_fusion.2
  339.6 3.2 and_reduce_fusion.2
  347.6 3.2 and_reduce_fusion.2
  352.8 2.2 dynamic-update-slice.10
  355.6 3.2 and_reduce_fusion.2
  360.8 2.2 dynamic-update-slice.10
  363.6 3.2 and_reduce_fusion.2
  371.7 6.9 %all_gather.7 = f32[2,128,512]{2,0,1:T(2,128)S(1)} all-gather(f32[2,32,512]{2,0,1:T(2,128)S(1)} %copy.83), channel_id=1, replica_groups=mesh['region'=8,'mode'=4] {'mode'}, dimensions={1}, use_global_device_ids=true | all-gather | bytes 655360 | tf_op jit(solution)/shard_map/all_gather | solution.py:157
  (128 shorter events, 99.2 us)
Async XLA Ops:
  15.3 8.2 %copy-start.2 = (s32[8,2]{0,1:T(2,128)S(1)}, s32[8,2]{0,1:T(2,128)}, u32[]{:S(2)}) copy-start(s32[8,2]{0,1:T(2,128)} %param.8) | copy-start | bytes 196
  15.3 12.1 %copy-start = (f32[2,1,256,256]{3,2,1,0:T(8,128)S(1)}, f32[2,1,256,256]{3,2,1,0:T(8,128)}, u32[]{:S(2)}) copy-start(f32[2,1,256,256]{3,2,1,0:T(8,128)} %param.6) | copy-start | bytes 1572868
  15.3 12.5 %copy-start.7 = (s32[8]{0:T(128)S(1)}, s32[8]{0:T(128)}, u32[]{:S(2)}) copy-start(s32[8]{0:T(128)} %param.9) | copy-start | bytes 100
  16.2 21.7 %all-to-all-start = ((f32[8,2,32,256]{3,2,1,0:T(8,128)}), f32[8,2,32,256]{3,2,1,0:T(8,128)S(1)}, u32[]{:S(2)}, u32[]{:S(2)}) async-start(f32[8,2,32,256]{3,2,1,0:T(8,128)} %broadcast_multiply_fusion), calls=%async_computation | async-start | bytes 1048576 | tf_op jit(solution)/shard_map/all_to_all | solution.py:86
  23.5 70.3 %all-reduce.11.cloned.1.call-start = ((), (), s32[]{:S(2)}) async-start(), calls=%async_computation.2 | async-start | bytes 524288 | tf_op jit(solution)/shard_map/psum | solution.py:52
  60.2 33.5 %copy-start.4 = (f32[1,256,256]{2,1,0:T(8,128)S(1)}, f32[1,256,256]{2,1,0:T(8,128)}, u32[]{:S(2)}) copy-start(f32[1,256,256]{2,1,0:T(8,128)} %param.5) | copy-start | bytes 786436
  62.8 119.3 %all-reduce.15.cloned.1.call-start = ((), (), s32[]{:S(2)}) async-start(), calls=%async_computation.4 | async-start | bytes 1572864 | tf_op jit(solution)/shard_map/psum | solution.py:112
  93.8 2.6 copy-start.6
  107.1 119.5 %all-reduce.13.cloned.1.call-start = ((), (), s32[]{:S(2)}) async-start(), calls=%async_computation.3 | async-start | bytes 524288 | tf_op jit(solution)/shard_map/psum | solution.py:52
  195.5 82.7 %all-reduce.17.cloned.1.call-start = ((), (), s32[]{:S(2)}) async-start(), calls=%async_computation.5 | async-start | bytes 2097152 | tf_op jit(solution)/shard_map/psum | solution.py:122
  226.6 2.6 copy-start.5
  240.3 1.6 copy-start.8
  281.1 6.7 %copy-start.3 = (s32[3]{0:T(128)S(1)}, s32[3]{0:T(128)}, u32[]{:S(2)}) copy-start(s32[3]{0:T(128)} %constant.114.clone.1) | copy-start | bytes 40
  282.3 25.4 %all-to-all-start.1 = ((f32[8,3,32,256]{3,2,1,0:T(8,128)}), f32[8,3,32,256]{3,2,1,0:T(8,128)S(1)}, u32[]{:S(2)}, u32[]{:S(2)}) async-start(f32[8,3,32,256]{3,2,1,0:T(8,128)} %copy.82), calls=%async_computation.1 | async-start | bytes 1572864 | tf_op jit(solution)/shard_map/all_to_all | solution.py:148
  287.8 20.1 %copy-start.1 = (s32[4]{0:T(128)S(1)}, s32[4]{0:T(128)}, u32[]{:S(2)}) copy-start(s32[4]{0:T(128)} %constant.549) | copy-start | bytes 52
Sparse Core Ops, SparseCore 0:
  62.9 30.8 all-reduce.10
  107.2 74.8 all-reduce.14
  195.6 30.9 all-reduce.12
  242.0 36.1 all-reduce.16
where the time goes:
time: 390 us; the launch traced here: 386 us
  waiting for transfers between devices  200 us (51%)
  other arithmetic  58 us (15%)
  matrix products  41.1 us (11%)
  local copies, waits for them, and re-layouts  37.1 us (10%)
  between operations  18.4 us (5%)
  blocking collectives  17.5 us (4%)
  starting transfers between devices  13.5 us (3%)
    psum x1, waiting for transfers between devices, body(): gradient, power_total = lax.psum((gradient, object_power), 'region')  74.8 us
    psum x2, waiting for transfers between devices, wave_change(): summed = lax.psum(local_sum, 'mode')  61.6 us
    scatter x16, other arithmetic  41.2 us
    psum x1, waiting for transfers between devices, body(): power_modes = lax.psum(mode_power, 'mode')  35 us
    scatter x24, local copies, waits for them, and re-layouts  21.2 us
    dot_general x12, matrix products, left_product(): return jnp.einsum('jk,...kl->...jl', matrix, planes, precision=highest)  21.2 us
    all_to_all x1, waiting for transfers between devices, body(): lax.all_to_all(outgoing_update, 'region', split_axis=0, concat_axis=0, ti...  18.9 us
    dot_general x12, matrix products, right_product(): return jnp.einsum('...jk,kl->...jl', planes, matrix, precision=highest)  18.6 us
  transfers between devices with their start and end apart: 6, of which 6 were waited for; matrix products, arithmetic and copies ran while one was open for 1% of the time, Pallas kernels for 0%

commit v1 on v0

v1 whole, which is shorter than its diff:
```python
import functools
import math

import jax
import jax.numpy as jnp
import ml_dtypes
import numpy as np
from jax import lax
from jax.experimental import pallas as pl
from jax.experimental.pallas import tpu as pltpu
from jax.sharding import PartitionSpec as P

intensity_offset = 0.1
probe_damping = 1.0
object_damping = 1.0
half = jnp.bfloat16
single = jnp.float32
axes = ("region", "mode")
on_chip = pl.BlockSpec(memory_space=pltpu.VMEM)
scalars = pl.BlockSpec(memory_space=pltpu.SMEM)


class Layout:
    def __init__(self, regions, helpers, length, frames, modes, width):
        self.regions, self.helpers = regions, helpers
        self.length, self.frames, self.modes, self.width = length, frames, modes, width
        self.halves = 2 if regions % 2 == 0 and helpers % 2 == 0 else 1
        self.lowers, self.cores = regions // self.halves, helpers // self.halves
        self.local_modes = modes // helpers
        self.band = length // 2
        self.share = self.band // helpers
        self.piece = length // regions
        self.part = length // self.cores

    def place(self):
        region, helper = lax.axis_index("region"), lax.axis_index("mode")
        upper, lower = region // self.lowers, region % self.lowers
        twin, core = helper // self.cores, helper % self.cores
        return upper, lower, twin, core

    def device(self, upper, lower, twin, core):
        return (upper * self.lowers + lower) * self.helpers + twin * self.cores + core

    def everyone(self):
        for upper in range(self.halves):
            for lower in range(self.lowers):
                for twin in range(self.halves):
                    for core in range(self.cores):
                        yield upper, lower, twin, core

    def cubes(self):
        return [
            [
                self.device(upper, lower, twin, core)
                for twin in range(self.halves)
                for lower in range(self.lowers)
            ]
            for upper in range(self.halves)
            for core in range(self.cores)
        ]

    def from_upper(self, array, step):
        pairs = [
            (self.device((u + step) % self.halves, l, t, c), self.device(u, l, t, c))
            for u, l, t, c in self.everyone()
        ]
        return lax.ppermute(array, axes, pairs)

    def from_core(self, array, step):
        pairs = [
            (self.device(u, l, t, (c + step) % self.cores), self.device(u, l, t, c))
            for u, l, t, c in self.everyone()
        ]
        return lax.ppermute(array, axes, pairs)

    def within_cube(self, array):
        return lax.all_to_all(
            array, axes, split_axis=0, concat_axis=0, tiled=True, axis_index_groups=self.cubes()
        )


def fourier_tables(length, cores):
    positions = np.arange(length)
    angles = (positions[:, None] * positions[None, :] % length) * (2.0 * math.pi / length)
    cosine, sine = np.cos(angles) / math.sqrt(length), np.sin(angles) / math.sqrt(length)
    plus = np.block([[cosine, -sine], [sine, cosine]])
    minus = np.block([[cosine, sine], [-sine, cosine]])
    rows = [
        np.concatenate([block, length + block]) for block in np.split(positions, cores)
    ]
    minus_parts = np.stack([minus[taken] for taken in rows])
    plus_parts = np.stack([plus[:, taken] for taken in rows])

    def pair(table):
        lead = table.astype(ml_dtypes.bfloat16)
        return np.stack([lead, (table - lead.astype(np.float64)).astype(ml_dtypes.bfloat16)])

    return pair(plus), pair(minus), pair(plus_parts), pair(minus_parts)


def split(values):
    lead = values.astype(half)
    return lead, (values - lead.astype(single)).astype(half)


def dot(left, right):
    return jnp.dot(left, right, preferred_element_type=single)


def from_left(table, values):
    lead, trail = split(values)
    return dot(table[0], lead) + dot(table[1], lead) + dot(table[0], trail)


def from_right(values, table):
    lead, trail = split(values)
    return dot(lead, table[0]) + dot(lead, table[1]) + dot(trail, table[0])


def beside(stacked):
    rows = stacked.shape[0] // 2
    return jnp.concatenate([stacked[:rows], stacked[rows:]], axis=1)


def above(planes):
    columns = planes.shape[1] // 2
    return jnp.concatenate([planes[:, :columns], planes[:, columns:]], axis=0)


def band_of_block(owner, block, layout):
    band = jnp.int32(0)
    for candidate in range(layout.regions):
        band = jnp.where(owner[candidate] == block, candidate, band)
    return band


def frame_over(offsets, region, band, layout):
    row, column = offsets[region * layout.frames, 0], offsets[region * layout.frames, 1]
    for extra in range(1, layout.frames):
        index = region * layout.frames + extra
        anchor = offsets[index, 0] // layout.band
        over = (anchor <= band) & (band <= anchor + 2)
        row = jnp.where(over, offsets[index, 0], row)
        column = jnp.where(over, offsets[index, 1], column)
    return row, column


def cut_kernel(layout, offsets, owner, *refs):
    blocks, out = refs[:-1], refs[-1]
    upper, lower, _, _ = layout.place()
    rows = 2 * layout.share
    for entry, block in enumerate(blocks):
        number = (upper + entry) % layout.halves * layout.lowers + lower
        band = band_of_block(owner, number, layout)
        values = block[...].reshape(rows, layout.width)
        for region in range(layout.regions):
            _, column = frame_over(offsets, region, band, layout)
            shift = (layout.width - column) % layout.width
            moved = pltpu.roll(values, shift, 1)[:, : layout.length]
            out[region, entry] = moved.reshape(2, layout.share, layout.length)


def choose_kernel(layout, offsets, owner, arrived, out):
    upper, lower, twin, core = layout.place()
    rows = lax.broadcasted_iota(jnp.int32, (layout.share, layout.length), 0)
    for frame in range(layout.frames):
        row = offsets[(twin * layout.lowers + lower) * layout.frames + frame, 0]
        anchor = row // layout.band
        lead = row - anchor * layout.band
        found = []
        for step in range(3):
            block = owner[anchor + step]
            entry = (block // layout.lowers + layout.halves - upper) % layout.halves
            found.append((block % layout.lowers, entry))
        for source in range(layout.halves):
            first = (source * layout.cores + core) * layout.share
            for plane in range(2):
                top, middle, bottom = (
                    arrived[source * layout.lowers + low, entry, plane] for low, entry in found
                )
                out[frame, plane, 0, source] = jnp.where(rows + first >= lead, top, bottom)
                out[frame, plane, 1, source] = middle


def first_kernel(layout, offsets, *refs):
    cores, frames, length = layout.cores, layout.frames, layout.length
    shares = refs[:cores]
    own_measured, other_measured, probes, plus, minus = refs[cores : cores + 5]
    windows, pieces, old_piece, inner, intensity, far = refs[cores + 5 :]
    upper, lower, twin, core = layout.place()
    region = twin * layout.lowers + lower
    plus_table, minus_table = (plus[0], plus[1]), (minus[0], minus[1])
    local = layout.local_modes
    first_mode = (upper * cores + core) * local
    own_frames = upper == twin
    for frame in range(frames):
        row = offsets[region * frames + frame, 0]
        lead = row % layout.band
        for step, share in enumerate(shares):
            inner[:, :, :, (core + step) % cores] = share[frame]
        for plane in range(2):
            wrapped = inner[plane].reshape(length, length)
            windows[frame, plane] = pltpu.roll(wrapped, (length - lead) % length, 0)
        window_real, window_imag = windows[frame, 0], windows[frame, 1]
        intensity[...] = jnp.zeros_like(intensity)

        def forward(mode):
            probe_real, probe_imag = probes[0, mode], probes[1, mode]
            leaving = jnp.concatenate(
                [
                    probe_real * window_real - probe_imag * window_imag,
                    probe_real * window_imag + probe_imag * window_real,
                ],
                axis=0,
            )
            return from_right(beside(from_left(minus_table, leaving)), plus_table)

        def add_mode(step, unused):
            mode = (first_mode + local + step) % layout.modes
            wave = forward(mode)
            intensity[...] += wave[:, :length] ** 2 + wave[:, length:] ** 2
            kept = jnp.maximum(step - (layout.modes - local), 0)
            far[kept] = wave
            return unused

        lax.fori_loop(0, layout.modes, add_mode, 0)
        measured = jnp.where(own_frames, own_measured[frame], other_measured[frame])
        factor = jnp.sqrt(measured) / jnp.sqrt(intensity[...] + intensity_offset) - 1.0
        factors = jnp.concatenate([factor, factor], axis=1)
        power = window_real**2 + window_imag**2
        cut = (layout.regions, layout.piece, length)
        pieces_here = [power]
        for kept in range(local):
            wave = far[kept] * factors
            change = from_left(plus_table, above(from_right(wave, minus_table)))
            change_real, change_imag = change[:length], change[length:]
            pieces_here.append(window_real * change_real + window_imag * change_imag)
            pieces_here.append(window_real * change_imag - window_imag * change_real)
        for channel, values in enumerate(pieces_here):
            if frame == 0:
                pieces[:, channel] = values.reshape(cut)
            else:
                pieces[:, channel] += values.reshape(cut)
    for kept in range(local):
        rows = pl.ds(region * layout.piece, layout.piece)
        for plane in range(2):
            old_piece[kept, plane] = probes[plane, first_mode + kept, rows, :]


def step_kernel(layout, arrived, old_piece, new_piece):
    total = jnp.sum(arrived[...], axis=0)
    damped = total[0] + probe_damping
    for kept in range(layout.local_modes):
        for plane in range(2):
            gradient = total[1 + 2 * kept + plane]
            new_piece[kept, plane] = old_piece[kept, plane] + gradient / damped


def second_kernel(layout, offsets, *refs):
    cores, frames, length = layout.cores, layout.frames, layout.length
    probes = refs[:cores]
    windows, own_measured, other_measured, plus, minus, left_plus, left_minus = refs[
        cores : cores + 7
    ]
    probe_out, probe_power, *others = refs[cores + 7 :]
    shares, (far, inner) = others[:cores], others[cores:]
    upper, lower, twin, core = layout.place()
    region = twin * layout.lowers + lower
    plus_table, minus_table = (plus[0], plus[1]), (minus[0], minus[1])
    part_minus = (left_minus[0, core], left_minus[1, core])
    part_plus = (left_plus[0, core], left_plus[1, core])
    local = layout.local_modes
    part = layout.part
    rows = pl.ds(pl.multiple_of(core * part, part), part)
    listed = [
        (step, entry, kept)
        for step in range(cores)
        for entry in range(layout.halves)
        for kept in range(local)
    ]

    def probe(step, entry, kept, plane):
        return probes[step][:, entry, kept, plane].reshape(length, length)

    own_entry = (twin + layout.halves - upper) % layout.halves
    for kept in range(local):
        for plane in range(2):
            probe_out[plane, kept] = probes[0][:, own_entry, kept, plane].reshape(length, length)
    power = jnp.zeros((length, length), single)
    for place in listed:
        power += probe(*place, 0) ** 2 + probe(*place, 1) ** 2
    probe_power[...] = power
    for frame in range(frames):
        window_real, window_imag = windows[frame, 0], windows[frame, 1]
        intensity = jnp.zeros((part, length), single)
        for number, place in enumerate(listed):
            probe_real, probe_imag = probe(*place, 0), probe(*place, 1)
            leaving = jnp.concatenate(
                [
                    probe_real * window_real - probe_imag * window_imag,
                    probe_real * window_imag + probe_imag * window_real,
                ],
                axis=0,
            )
            wave = from_right(beside(from_left(part_minus, leaving)), plus_table)
            intensity += wave[:, :length] ** 2 + wave[:, length:] ** 2
            far[number] = wave
        measured = jnp.where(upper == twin, own_measured[frame, rows, :], other_measured[frame, rows, :])
        factor = jnp.sqrt(measured) / jnp.sqrt(intensity + intensity_offset) - 1.0
        factors = jnp.concatenate([factor, factor], axis=1)
        numer_real = jnp.zeros((length, length), single)
        numer_imag = jnp.zeros((length, length), single)
        for number, place in enumerate(listed):
            change = from_left(part_plus, above(from_right(far[number] * factors, minus_table)))
            change_real, change_imag = change[:length], change[length:]
            probe_real, probe_imag = probe(*place, 0), probe(*place, 1)
            numer_real += probe_real * change_real + probe_imag * change_imag
            numer_imag += probe_real * change_imag - probe_imag * change_real
        lead = offsets[region * frames + frame, 0] % layout.band
        for plane, values in enumerate((numer_real, numer_imag)):
            turned = pltpu.roll(values, lead, 0)
            inner[plane] = turned.reshape(2, layout.halves, cores, layout.share, length)
        for step, share in enumerate(shares):
            share[frame] = inner[:, :, :, (core + cores - step) % cores]


def post_kernel(layout, offsets, owner, *refs):
    shares, out = refs[:-1], refs[-1]
    upper, lower, twin, _ = layout.place()
    region = twin * layout.lowers + lower
    for low in range(layout.lowers):
        band = band_of_block(owner, upper * layout.lowers + low, layout)
        frame, row = jnp.int32(0), offsets[region * layout.frames, 0]
        for extra in range(1, layout.frames):
            candidate = offsets[region * layout.frames + extra, 0]
            anchor = candidate // layout.band
            over = (anchor <= band) & (band <= anchor + 2)
            frame, row = jnp.where(over, extra, frame), jnp.where(over, candidate, row)
        slot = (band - row // layout.band == 1).astype(jnp.int32)
        for target in range(layout.halves):
            for plane in range(2):
                total = shares[0][frame, plane, slot, target]
                for share in shares[1:]:
                    total += share[frame, plane, slot, target]
                out[target * layout.lowers + low, plane] = total


def update_kernel(layout, offsets, owner, arrived, probe_power, rows_in, rows_out, doubled):
    upper, lower, twin, core = layout.place()
    length, share = layout.length, layout.share
    band = band_of_block(owner, upper * layout.lowers + lower, layout)
    first = (twin * layout.cores + core) * share
    rows = lax.broadcasted_iota(jnp.int32, (share, length), 0) + first
    doubled[0] = probe_power[...]
    doubled[1] = probe_power[...]
    powers = doubled.reshape(2 * length, length)
    total = jnp.zeros((3 * share, layout.width), single)
    blank = jnp.zeros((3 * share, layout.width - length), single)
    for region in range(layout.regions):
        row, column = frame_over(offsets, region, band, layout)
        anchor = row // layout.band
        lead = row - anchor * layout.band
        step = band - anchor
        begin = jnp.where(step == 0, lead, jnp.where((step == 1) | (step == 2), 0, layout.band))
        end = jnp.where(step == 2, lead, layout.band)
        inside = (rows >= begin) & (rows < end)
        slot = (step == 1).astype(jnp.int32)
        start = (slot * layout.band + first + length - lead) % length
        near = powers[pl.ds(pl.multiple_of(start // 8 * 8, 8), share + 8), :]
        near = pltpu.roll(near, (share + 8 - start % 8) % (share + 8), 0)[:share]
        terms = jnp.concatenate([arrived[region, 0], arrived[region, 1], near], axis=0)
        kept = jnp.where(jnp.concatenate([inside] * 3, axis=0), terms, 0.0)
        total += pltpu.roll(jnp.concatenate([kept, blank], axis=1), column, 1)
    damped = total[2 * share :] + object_damping
    for plane in range(2):
        rows_out[plane] = rows_in[plane] + total[plane * share : (plane + 1) * share] / damped


def call(kernel, name, operands, outputs, scratch=(), scalar_count=0):
    shapes = [jax.ShapeDtypeStruct(shape, single) for shape in outputs]
    return pl.pallas_call(
        kernel,
        name=name,
        out_shape=shapes,
        in_specs=[scalars] * scalar_count + [on_chip] * (len(operands) - scalar_count),
        out_specs=[on_chip] * len(shapes),
        scratch_shapes=[pltpu.VMEM(shape, single) for shape in scratch],
        compiler_params=pltpu.CompilerParams(vmem_limit_bytes=50 * 2**20),
    )(*operands)


def body(measured, probe_modes, object_bands, scan_offsets, band_owner):
    layout = Layout(
        lax.axis_size("region"),
        lax.axis_size("mode"),
        measured.shape[1],
        measured.shape[0],
        probe_modes.shape[1] * lax.axis_size("mode"),
        object_bands.shape[2],
    )
    regions, halves, cores = layout.regions, layout.halves, layout.cores
    length, share, piece, frames = layout.length, layout.share, layout.piece, layout.frames
    local = layout.local_modes
    plus, minus, left_plus, left_minus = fourier_tables(length, cores)
    helper = lax.axis_index("mode")

    own_rows = lax.dynamic_slice_in_dim(object_bands, helper * share, share, 1)
    blocks = [own_rows] + [layout.from_upper(own_rows, step) for step in range(1, halves)]
    probes = lax.all_gather(probe_modes, "mode", axis=1, tiled=True)
    other_measured = measured
    if halves > 1:
        pairs = [
            (layout.device(t, l, t, c), layout.device(u, l, t, c))
            for u, l, t, c in layout.everyone()
            if u != t
        ]
        other_measured = lax.ppermute(measured, axes, pairs)

    (cuts,) = call(
        functools.partial(cut_kernel, layout),
        "cut",
        (scan_offsets, band_owner, *blocks),
        [(regions, halves, 2, share, length)],
        scalar_count=2,
    )
    cuts = layout.within_cube(cuts)
    strip = (frames, 2, 2, halves, share, length)
    (chosen,) = call(
        functools.partial(choose_kernel, layout),
        "choose",
        (scan_offsets, band_owner, cuts),
        [strip],
        scalar_count=2,
    )
    strips = [chosen] + [layout.from_core(chosen, step) for step in range(1, cores)]
    inner = (2, 2, halves, cores, share, length)
    windows, pieces, old_piece = call(
        functools.partial(first_kernel, layout),
        "first",
        (scan_offsets, *strips, measured, other_measured, probes, plus, minus),
        [
            (frames, 2, length, length),
            (regions, 1 + 2 * local, piece, length),
            (local, 2, piece, length),
        ],
        scratch=[
            inner,
            (length, length),
            (local, length, 2 * length),
        ],
        scalar_count=1,
    )
    pieces = layout.within_cube(pieces)
    (new_piece,) = call(
        functools.partial(step_kernel, layout),
        "step",
        (pieces, old_piece),
        [(local, 2, piece, length)],
    )
    entries = [new_piece] + [layout.from_upper(new_piece, step) for step in range(1, halves)]
    spread = jnp.broadcast_to(jnp.stack(entries)[None], (regions, halves, local, 2, piece, length))
    gathered = layout.within_cube(spread)
    new_probes = [gathered] + [layout.from_core(gathered, step) for step in range(1, cores)]
    probe_out, probe_power, *shares = call(
        functools.partial(second_kernel, layout),
        "second",
        (
            scan_offsets,
            *new_probes,
            windows,
            measured,
            other_measured,
            plus,
            minus,
            left_plus,
            left_minus,
        ),
        [(2, local, length, length), (length, length)] + [strip] * cores,
        scratch=[
            (layout.modes, layout.part, 2 * length),
            inner,
        ],
        scalar_count=1,
    )
    shares = shares[:1] + [
        layout.from_core(sent, step) for step, sent in enumerate(shares[1:], start=1)
    ]
    (posted,) = call(
        functools.partial(post_kernel, layout),
        "post",
        (scan_offsets, band_owner, *shares),
        [(regions, 2, share, length)],
        scalar_count=2,
    )
    posted = layout.within_cube(posted)
    (new_rows,) = call(
        functools.partial(update_kernel, layout),
        "update",
        (scan_offsets, band_owner, posted, probe_power, own_rows),
        [(2, share, layout.width)],
        scratch=[(2, length, length)],
        scalar_count=2,
    )
    object_out = lax.all_gather(new_rows, "mode", axis=1, tiled=True)
    return probe_out, object_out


def solution(mesh):
    in_specs = (
        P("region", None, None),
        P(None, "mode", None, None),
        P(None, "region", None),
        P(),
        P(),
    )
    out_specs = (P(None, "mode", None, None), P(None, "region", None))
    return jax.shard_map(body, mesh=mesh, in_specs=in_specs, out_specs=out_specs, check_vma=False)
```

time: 390 us -> 140 us (0.36)
  waiting for transfers between devices: 200 us -> 33 us
  other arithmetic: 58 us -> 0.01 us
  matrix products: 41.1 us -> 0 us
  local copies, waits for them, and re-layouts: 37.1 us -> 3.66 us
  blocking collectives: 17.5 us -> 50.8 us
  Pallas kernels: 0 us -> 22.7 us
  between operations: 18.4 us -> 14.1 us
    psum x4 -> x0, waiting for transfers between devices: 171 us -> none  [the longest x1 74.8 us: body(): gradient, power_total = lax.psum((gradient, object_power), 'region')]
    all_to_all x0 -> x3, blocking collectives: none -> 44.2 us  [within_cube(): lax.all_to_all(array, axes, split_axis=0, concat_axis=0, tiled=True, axis...]
    scatter x17 -> x0, other arithmetic: 41.2 us -> none
    dot_general x26 -> x0, matrix products: 41.1 us -> none  [the longest x12 21.2 us: left_product(): return jnp.einsum('jk,...kl->...jl', matrix, planes, precision=highest)]
    pallas_call x0 -> x7, Pallas kernels: none -> 22.7 us  [call(): pl.pallas_call(kernel, name=name, out_shape=shapes, in_specs=[scalars] *...]
    scatter x24 -> x0, local copies, waits for them, and re-layouts: 21.2 us -> none
    ppermute x0 -> x6, waiting for transfers between devices: none -> 15.3 us  [the longest x2 9.78 us: from_upper(): return lax.ppermute(array, axes, pairs)]
    all_to_all x2 -> x1, waiting for transfers between devices: 28.9 us -> 17 us  [within_cube(): lax.all_to_all(array, axes, split_axis=0, concat_axis=0, tiled=True, axis...]
  transfers between devices with their start and end apart: 6 -> 8, of which waited for: 6 -> 6; matrix products, arithmetic and copies ran while one was open for 1% -> 1% of each run, Pallas kernels for 0% -> 1%
where the time goes in v1:
time: 140 us; the launch traced here: 139 us
  blocking collectives  50.8 us (36%)
  waiting for transfers between devices  33 us (24%)
  Pallas kernels  22.7 us (16%)
  starting transfers between devices  14.9 us (11%)
  between operations  14.1 us (10%)
  local copies, waits for them, and re-layouts  3.66 us (3%)
    all_to_all x3, blocking collectives, within_cube(): lax.all_to_all(array, axes, split_axis=0, concat_axis=0, tiled=True, axis...  44.2 us
    pallas_call x7, Pallas kernels, call(): pl.pallas_call(kernel, name=name, out_shape=shapes, in_specs=[scalars] *...  22.7 us
    all_to_all x1, waiting for transfers between devices, within_cube(): lax.all_to_all(array, axes, split_axis=0, concat_axis=0, tiled=True, axis...  17 us
    ppermute x2, waiting for transfers between devices, from_upper(): return lax.ppermute(array, axes, pairs)  9.78 us
    all_gather x1, blocking collectives, body(): object_out = lax.all_gather(new_rows, 'mode', axis=1, tiled=True)  6.51 us
    ppermute x3, waiting for transfers between devices, from_core(): return lax.ppermute(array, axes, pairs)  5.57 us
    ppermute x2, starting transfers between devices, from_upper(): return lax.ppermute(array, axes, pairs)  5.45 us
    ppermute x1, starting transfers between devices, body(): other_measured = lax.ppermute(measured, axes, pairs)  5.3 us
  transfers between devices with their start and end apart: 8, of which 6 were waited for; matrix products, arithmetic and copies ran while one was open for 1% of the time, Pallas kernels for 1%

profile of v1, /device:TPU:0, one launch (start us, length us, event | category | flops | bytes accessed | tf_op | source)
XLA Modules:
  0.0 139.2 jit_solution(15146757789243228723)
XLA Ops:
  7.2 0.7 all-gather.2.cloned.1.call-update
  8.3 4.1 %collective-permute-start = (f32[2,32,512]{2,1,0:T(8,128)S(1)}, f32[2,32,512]{2,1,0:T(8,128)S(1)}, u32[]{:S(2)}, u32[]{:S(2)}) collective-permute-start(f32[2,32,512]{2,1,0:T(8,128)S(1)} %constant_dynamic-slice_fusion.refs_0_.rows_in), channel_id=1, source_target_pairs={{16,0},{17,1},{18,2},{19,3},{20,4},{21,5},{22,6},{23,7},{24,8},{25... | collective-permute-start | bytes 393224 | tf_op jit(solution)/shard_map/ppermute | solution.py:67
  12.4 0.8 copy.14.offsets
  13.2 5.5 %collective-permute-done.refs_1_ = f32[2,32,512]{2,1,0:T(8,128)S(1)} collective-permute-done((f32[2,32,512]{2,1,0:T(8,128)S(1)}, f32[2,32,512]{2,1,0:T(8,128)S(1)}, u32[]{:S(2)}, u32[]{:S(2)}) %collective-permute-start) | collective-permute-done | bytes 131104 | tf_op jit(solution)/shard_map/ppermute | solution.py:67
  19.4 1.2 cut.1
  20.6 1.0 copy-done.2
  21.6 3.9 %all-to-all-start = ((f32[8,2,2,32,256]{4,3,2,1,0:T(8,128)}), f32[8,2,2,32,256]{4,3,2,1,0:T(8,128)S(1)}, u32[]{:S(2)}, u32[]{:S(2)}) async-start(f32[8,2,2,32,256]{4,3,2,1,0:T(8,128)} %copy-done.2), calls=%async_computation | async-start | bytes 2097152 | tf_op jit(solution)/shard_map/all_to_all | solution.py:77
  25.5 5.3 %collective-permute-start.2 = (f32[1,256,256]{2,1,0:T(8,128)S(1)}, f32[1,256,256]{2,1,0:T(8,128)S(1)}, u32[]{:S(2)}, u32[]{:S(2)}) collective-permute-start(f32[1,256,256]{2,1,0:T(8,128)S(1)} %copy-done.3), channel_id=1, source_target_pairs={{18,2},{19,3},{22,6},{23,7},{26,10},{27,11},{30,14},{31,15},{0,16}... | collective-permute-start | bytes 786440 | tf_op jit(solution)/shard_map/ppermute | solution.py:417
  30.8 17.0 %all-to-all-done.arrived = f32[8,2,2,32,256]{4,3,2,1,0:T(8,128)S(1)} async-done(((f32[8,2,2,32,256]{4,3,2,1,0:T(8,128)}), f32[8,2,2,32,256]{4,3,2,1,0:T(8,128)S(1)}, u32[]{:S(2)}, u32[]{:S(2)}) %all-to-all-start) | async-done | bytes 1048608 | tf_op jit(solution)/shard_map/all_to_all | solution.py:77
  47.8 0.7 choose.1.refs_0_
  48.6 1.5 %collective-permute-done.1.refs_1_ = f32[1,2,2,2,32,256]{5,4,3,2,1,0:T(8,128)S(1)} collective-permute-done((f32[1,2,2,2,32,256]{5,4,3,2,1,0:T(8,128)S(1)}, f32[1,2,2,2,32,256]{5,4,3,2,1,0:T(8,128)S(1)}, u32[]{:S(2)}, u32[]{:S(2)}) %collective-permute-start.1) | collective-permute-done | bytes 262176 | tf_op jit(solution)/shard_map/ppermute | solution.py:74
  50.1 10.7 %first.1 = (f32[1,2,256,256]{3,2,1,0:T(8,128)S(1)}, f32[8,3,32,256]{3,2,1,0:T(8,128)S(1)}, f32[1,2,32,256]{3,2,1,0:T(8,128)S(1)}) custom-call(s32[8,2]{1,0:T(8,128)S(1)} %copy.14.offsets, f32[1,2,2,2,32,256]{5,4,3,2,1,0:T(8,128)S(1)} %choose.1.refs_0_, f32[1,2,2,2,32,256]{5,4,3,2,1,0:T(8,128)S(1)} %collective-permute-done.1.refs_1_, ...), custom_call_target="tpu_custom_call" | custom-call | tf_op jit(solution)/shard_map/first/pallas_call | solution.py:381
  60.7 15.6 %all_to_all.20.arrived = f32[8,3,32,256]{3,2,1,0:T(8,128)S(1)} all-to-all(f32[8,3,32,256]{3,2,1,0:T(8,128)S(1)} %get-tuple-element.9), channel_id=1, replica_groups={{0,4,8,12,2,6,10,14},{1,5,9,13,3,7,11,15},{16,20,24,28,18,22,26,30},{17..., dimensions={0} | all-to-all | bytes 1572864 | tf_op jit(solution)/shard_map/all_to_all | solution.py:77
  76.4 1.4 collective-permute-start.3
  77.7 4.2 %collective-permute-done.3 = f32[1,2,32,256]{3,2,1,0:T(8,128)S(1)} collective-permute-done((f32[1,2,32,256]{3,2,1,0:T(8,128)S(1)}, f32[1,2,32,256]{3,2,1,0:T(8,128)S(1)}, u32[]{:S(2)}, u32[]{:S(2)}) %collective-permute-start.3) | collective-permute-done | bytes 65568 | tf_op jit(solution)/shard_map/ppermute | solution.py:67
  82.1 15.9 %all_to_all.21.refs_0_ = f32[8,2,1,2,32,256]{5,4,3,2,1,0:T(8,128)S(1)} all-to-all(f32[8,2,1,2,32,256]{5,4,3,2,1,0:T(8,128)S(1)} %broadcast_in_dim.9), channel_id=1, replica_groups={{0,4,8,12,2,6,10,14},{1,5,9,13,3,7,11,15},{16,20,24,28,18,22,26,30},{17..., dimensions={0} | all-to-all | bytes 2097152 | tf_op jit(solution)/shard_map/all_to_all | solution.py:77
  98.0 2.7 %collective-permute-done.4.refs_1_ = f32[8,2,1,2,32,256]{5,4,3,2,1,0:T(8,128)S(1)} collective-permute-done((f32[8,2,1,2,32,256]{5,4,3,2,1,0:T(8,128)S(1)}, f32[8,2,1,2,32,256]{5,4,3,2,1,0:T(8,128)S(1)}, u32[]{:S(2)}, u32[]{:S(2)}) %collective-permute-start.4) | collective-permute-done | bytes 1048608 | tf_op jit(solution)/shard_map/ppermute | solution.py:74
  100.7 8.3 %second.1 = (f32[2,1,256,256]{3,2,1,0:T(8,128)}, f32[256,256]{1,0:T(8,128)S(1)}, f32[1,2,2,2,32,256]{5,4,3,2,1,0:T(8,128)S(1)}, f32[1,2,2,2,32,256]{5,4,3,2,1,0:T(8,128)S(1)}) custom-call(s32[8,2]{1,0:T(8,128)S(1)} %copy.14.offsets, f32[8,2,1,2,32,256]{5,4,3,2,1,0:T(8,128)S(1)} %all_to_all.21.refs_0_, ...), custom_call_target="tpu_custom_call" | custom-call | tf_op jit(solution)/shard_map/second/pallas_call | solution.py:381
  109.1 1.4 %collective-permute-done.5.refs_1_ = f32[1,2,2,2,32,256]{5,4,3,2,1,0:T(8,128)S(1)} collective-permute-done((f32[1,2,2,2,32,256]{5,4,3,2,1,0:T(8,128)S(1)}, f32[1,2,2,2,32,256]{5,4,3,2,1,0:T(8,128)S(1)}, u32[]{:S(2)}, u32[]{:S(2)}) %collective-permute-start.5) | collective-permute-done | bytes 262176 | tf_op jit(solution)/shard_map/ppermute | solution.py:74
  110.5 0.7 post.1
  111.2 12.8 %all_to_all.22.arrived = f32[8,2,32,256]{3,2,1,0:T(8,128)S(1)} all-to-all(f32[8,2,32,256]{3,2,1,0:T(8,128)S(1)} %post.1), channel_id=1, replica_groups={{0,4,8,12,2,6,10,14},{1,5,9,13,3,7,11,15},{16,20,24,28,18,22,26,30},{17..., dimensions={0} | all-to-all | bytes 1048576 | tf_op jit(solution)/shard_map/all_to_all | solution.py:77
  124.0 1.0 update.1
  125.0 6.5 %all_gather.7 = f32[2,128,512]{2,1,0:T(8,128)S(1)} all-gather(f32[2,32,512]{2,1,0:T(8,128)S(1)} %update.1), channel_id=1, replica_groups=mesh['region'=8,'mode'=4] {'mode'}, dimensions={1}, use_global_device_ids=true | all-gather | bytes 655360 | tf_op jit(solution)/shard_map/all_gather | solution.py:504
  131.5 0.8 copy.18
  (21 shorter events, 1.5 us)
Async XLA Ops:
  7.2 1.1 copy-start
  7.2 40.6 %copy-start.5 = (s32[8]{0:T(128)S(1)}, s32[8]{0:T(128)}, u32[]{:S(2)}) copy-start(s32[8]{0:T(128)} %owner.7) | copy-start | bytes 100
  7.2 18.3 %copy-start.3 = (f32[1,256,256]{2,1,0:T(8,128)S(1)}, f32[1,256,256]{2,1,0:T(8,128)}, u32[]{:S(2)}) copy-start(f32[1,256,256]{2,1,0:T(8,128)} %refs_3_.1) | copy-start | bytes 786436
  7.2 42.9 %all-gather.2.cloned.1.call-start = ((), (), s32[]{:S(2)}) async-start(), calls=%async_computation.4 | async-start | bytes 2621440 | tf_op jit(solution)/shard_map/all_gather | solution.py:409
  8.3 10.4 %collective-permute-start = (f32[2,32,512]{2,1,0:T(8,128)S(1)}, f32[2,32,512]{2,1,0:T(8,128)S(1)}, u32[]{:S(2)}, u32[]{:S(2)}) collective-permute-start(f32[2,32,512]{2,1,0:T(8,128)S(1)} %constant_dynamic-slice_fusion.refs_0_.rows_in), channel_id=1, source_target_pairs={{16,0},{17,1},{18,2},{19,3},{20,4},{21,5},{22,6},{23,7},{24,8},{25... | collective-permute-start | bytes 393224 | tf_op jit(solution)/shard_map/ppermute | solution.py:67
  13.2 36.9 %copy-start.1 = (bf16[2,512,512]{2,1,0:T(8,128)(2,1)S(1)}, bf16[2,512,512]{2,1,0:T(8,128)(2,1)}, u32[]{:S(2)}) copy-start(bf16[2,512,512]{2,1,0:T(8,128)(2,1)} %constant.18.clone.refs_5_) | copy-start | bytes 3145732
  18.7 0.7 copy-start.4
  20.6 1.0 copy-start.2
  21.6 26.2 %all-to-all-start = ((f32[8,2,2,32,256]{4,3,2,1,0:T(8,128)}), f32[8,2,2,32,256]{4,3,2,1,0:T(8,128)S(1)}, u32[]{:S(2)}, u32[]{:S(2)}) async-start(f32[8,2,2,32,256]{4,3,2,1,0:T(8,128)} %copy-done.2), calls=%async_computation | async-start | bytes 2097152 | tf_op jit(solution)/shard_map/all_to_all | solution.py:77
  25.5 23.1 %collective-permute-start.2 = (f32[1,256,256]{2,1,0:T(8,128)S(1)}, f32[1,256,256]{2,1,0:T(8,128)S(1)}, u32[]{:S(2)}, u32[]{:S(2)}) collective-permute-start(f32[1,256,256]{2,1,0:T(8,128)S(1)} %copy-done.3), channel_id=1, source_target_pairs={{18,2},{19,3},{22,6},{23,7},{26,10},{27,11},{30,14},{31,15},{0,16}... | collective-permute-start | bytes 786440 | tf_op jit(solution)/shard_map/ppermute | solution.py:417
  48.5 1.6 %collective-permute-start.1 = (f32[1,2,2,2,32,256]{5,4,3,2,1,0:T(8,128)S(1)}, f32[1,2,2,2,32,256]{5,4,3,2,1,0:T(8,128)S(1)}, u32[]{:S(2)}, u32[]{:S(2)}) collective-permute-start(f32[1,2,2,2,32,256]{5,4,3,2,1,0:T(8,128)S(1)} %choose.1.refs_0_), channel_id=1, source_target_pairs={{1,0},{0,1},{3,2},{2,3},{5,4},{4,5},{7,6},{6,7},{9,8},{8,9},{11,10... | collective-permute-start | bytes 786440 | tf_op jit(solution)/shard_map/ppermute | solution.py:74
  76.4 5.6 %collective-permute-start.3 = (f32[1,2,32,256]{3,2,1,0:T(8,128)S(1)}, f32[1,2,32,256]{3,2,1,0:T(8,128)S(1)}, u32[]{:S(2)}, u32[]{:S(2)}) collective-permute-start(f32[1,2,32,256]{3,2,1,0:T(8,128)S(1)} %step.1), channel_id=1, source_target_pairs={{16,0},{17,1},{18,2},{19,3},{20,4},{21,5},{22,6},{23,7},{24,8},{25... | collective-permute-start | bytes 196616 | tf_op jit(solution)/shard_map/ppermute | solution.py:67
  98.0 2.7 %collective-permute-start.4 = (f32[8,2,1,2,32,256]{5,4,3,2,1,0:T(8,128)S(1)}, f32[8,2,1,2,32,256]{5,4,3,2,1,0:T(8,128)S(1)}, u32[]{:S(2)}, u32[]{:S(2)}) collective-permute-start(f32[8,2,1,2,32,256]{5,4,3,2,1,0:T(8,128)S(1)} %all_to_all.21.refs_0_), channel_id=1, source_target_pairs={{1,0},{0,1},{3,2},{2,3},{5,4},{4,5},{7,6},{6,7},{9,8},{8,9},{11,10... | collective-permute-start | bytes 3145736 | tf_op jit(solution)/shard_map/ppermute | solution.py:74
  109.0 1.5 %collective-permute-start.5 = (f32[1,2,2,2,32,256]{5,4,3,2,1,0:T(8,128)S(1)}, f32[1,2,2,2,32,256]{5,4,3,2,1,0:T(8,128)S(1)}, u32[]{:S(2)}, u32[]{:S(2)}) collective-permute-start(f32[1,2,2,2,32,256]{5,4,3,2,1,0:T(8,128)S(1)} %get-tuple-element.14), channel_id=1, source_target_pairs={{1,0},{0,1},{3,2},{2,3},{5,4},{4,5},{7,6},{6,7},{9,8},{8,9},{11,10... | collective-permute-start | bytes 786440 | tf_op jit(solution)/shard_map/ppermute | solution.py:74
Sparse Core Ops, SparseCore 0:
  9.6 32.9 all-gather.1

commit v2 on v1

--- a/solution.py
+++ b/solution.py
@@ -29,6 +29,7 @@
         self.local_modes = modes // helpers
         self.band = length // 2
         self.share = self.band // helpers
+        self.strip = self.band // self.cores
         self.piece = length // regions
         self.part = length // self.cores
 
@@ -72,6 +73,24 @@
             for u, l, t, c in self.everyone()
         ]
         return lax.ppermute(array, axes, pairs)
+
+    def from_twin(self, array, step):
+        pairs = [
+            (self.device(u, l, (t + step) % self.halves, c), self.device(u, l, t, c))
+            for u, l, t, c in self.everyone()
+        ]
+        return lax.ppermute(array, axes, pairs)
+
+    def within_row(self, array):
+        rows = [
+            [self.device(upper, lower, twin, core) for lower in range(self.lowers)]
+            for upper in range(self.halves)
+            for twin in range(self.halves)
+            for core in range(self.cores)
+        ]
+        return lax.all_to_all(
+            array, axes, split_axis=0, concat_axis=0, tiled=True, axis_index_groups=rows
+        )
 
     def within_cube(self, array):
         return lax.all_to_all(
@@ -145,106 +164,108 @@
     return row, column
 
 
-def cut_kernel(layout, offsets, owner, *refs):
-    blocks, out = refs[:-1], refs[-1]
-    upper, lower, _, _ = layout.place()
-    rows = 2 * layout.share
-    for entry, block in enumerate(blocks):
-        number = (upper + entry) % layout.halves * layout.lowers + lower
-        band = band_of_block(owner, number, layout)
-        values = block[...].reshape(rows, layout.width)
-        for region in range(layout.regions):
-            _, column = frame_over(offsets, region, band, layout)
-            shift = (layout.width - column) % layout.width
-            moved = pltpu.roll(values, shift, 1)[:, : layout.length]
-            out[region, entry] = moved.reshape(2, layout.share, layout.length)
+def cut_kernel(layout, offsets, owner, block, measured, out, sent):
+    upper, lower, twin, core = layout.place()
+    sent[...] = measured[:, pl.ds(pl.multiple_of(core * layout.part, layout.part), layout.part), :]
+    band = band_of_block(owner, upper * layout.lowers + lower, layout)
+    values = block[...].reshape(2 * layout.strip, layout.width)
+    for target in range(layout.lowers):
+        _, column = frame_over(offsets, twin * layout.lowers + target, band, layout)
+        shift = (layout.width - column) % layout.width
+        moved = pltpu.roll(values, shift, 1)[:, : layout.length]
+        out[target] = moved.reshape(2, layout.strip, layout.length)
 
 
 def choose_kernel(layout, offsets, owner, arrived, out):
     upper, lower, twin, core = layout.place()
-    rows = lax.broadcasted_iota(jnp.int32, (layout.share, layout.length), 0)
+    rows = lax.broadcasted_iota(jnp.int32, (layout.strip, layout.length), 0) + core * layout.strip
     for frame in range(layout.frames):
         row = offsets[(twin * layout.lowers + lower) * layout.frames + frame, 0]
         anchor = row // layout.band
         lead = row - anchor * layout.band
-        found = []
-        for step in range(3):
-            block = owner[anchor + step]
-            entry = (block // layout.lowers + layout.halves - upper) % layout.halves
-            found.append((block % layout.lowers, entry))
-        for source in range(layout.halves):
-            first = (source * layout.cores + core) * layout.share
-            for plane in range(2):
-                top, middle, bottom = (
-                    arrived[source * layout.lowers + low, entry, plane] for low, entry in found
-                )
-                out[frame, plane, 0, source] = jnp.where(rows + first >= lead, top, bottom)
-                out[frame, plane, 1, source] = middle
-
-
-def first_kernel(layout, offsets, *refs):
-    cores, frames, length = layout.cores, layout.frames, layout.length
-    shares = refs[:cores]
-    own_measured, other_measured, probes, plus, minus = refs[cores : cores + 5]
-    windows, pieces, old_piece, inner, intensity, far = refs[cores + 5 :]
+        blocks = [owner[anchor + step] for step in range(3)]
+        lows = [block % layout.lowers for block in blocks]
+        here = [block // layout.lowers == upper for block in blocks]
+        for plane in range(2):
+            top, middle, bottom = (arrived[low, plane] for low in lows)
+            first = jnp.where((rows >= lead) & here[0], top, 0.0)
+            out[frame, plane, 0] = jnp.where((rows < lead) & here[2], bottom, first)
+            out[frame, plane, 1] = jnp.where(here[1], middle, 0.0)
+
+
+def far_kernel(layout, offsets, *refs):
+    cores, halves, frames, length = layout.cores, layout.halves, layout.frames, layout.length
+    shares, probes = refs[: cores * halves], refs[cores * halves : (cores + 1) * halves]
+    plus, minus, windows, intensity, kept, old_piece, inner = refs[(cores + 1) * halves :]
     upper, lower, twin, core = layout.place()
     region = twin * layout.lowers + lower
     plus_table, minus_table = (plus[0], plus[1]), (minus[0], minus[1])
-    local = layout.local_modes
-    first_mode = (upper * cores + core) * local
-    own_frames = upper == twin
+    rows = pl.ds(pl.multiple_of(region * layout.piece, layout.piece), layout.piece)
     for frame in range(frames):
-        row = offsets[region * frames + frame, 0]
-        lead = row % layout.band
-        for step, share in enumerate(shares):
-            inner[:, :, :, (core + step) % cores] = share[frame]
+        lead = offsets[region * frames + frame, 0] % layout.band
+        for step in range(cores):
+            strip = shares[step * halves][frame]
+            for entry in range(1, halves):
+                strip += shares[step * halves + entry][frame]
+            inner[:, :, (core + step) % cores] = strip
         for plane in range(2):
             wrapped = inner[plane].reshape(length, length)
             windows[frame, plane] = pltpu.roll(wrapped, (length - lead) % length, 0)
         window_real, window_imag = windows[frame, 0], windows[frame, 1]
-        intensity[...] = jnp.zeros_like(intensity)
-
-        def forward(mode):
-            probe_real, probe_imag = probes[0, mode], probes[1, mode]
-            leaving = jnp.concatenate(
-                [
-                    probe_real * window_real - probe_imag * window_imag,
-                    probe_real * window_imag + probe_imag * window_real,
-                ],
-                axis=0,
-            )
-            return from_right(beside(from_left(minus_table, leaving)), plus_table)
-
-        def add_mode(step, unused):
-            mode = (first_mode + local + step) % layout.modes
-            wave = forward(mode)
-            intensity[...] += wave[:, :length] ** 2 + wave[:, length:] ** 2
-            kept = jnp.maximum(step - (layout.modes - local), 0)
-            far[kept] = wave
-            return unused
-
-        lax.fori_loop(0, layout.modes, add_mode, 0)
-        measured = jnp.where(own_frames, own_measured[frame], other_measured[frame])
-        factor = jnp.sqrt(measured) / jnp.sqrt(intensity[...] + intensity_offset) - 1.0
+        total = jnp.zeros((length, length), single)
+        for entry, probe in enumerate(probes):
+            goes_back = (twin + entry) % halves == upper
+            for local in range(layout.local_modes):
+                probe_real, probe_imag = probe[0, local], probe[1, local]
+                leaving = jnp.concatenate(
+                    [
+                        probe_real * window_real - probe_imag * window_imag,
+                        probe_real * window_imag + probe_imag * window_real,
+                    ],
+                    axis=0,
+                )
+                wave = from_right(beside(from_left(minus_table, leaving)), plus_table)
+                total += wave[:, :length] ** 2 + wave[:, length:] ** 2
+
+                @pl.when(goes_back)
+                def _():
+                    kept[frame, local] = wave
+                    for plane in range(2):
+                        old_piece[local, plane] = probe[plane, local, rows, :]
+
+        intensity[frame] = total
+
+
+def gradient_kernel(layout, *refs):
+    cores, frames, length = layout.cores, layout.frames, layout.length
+    intensities, parts = refs[:cores], refs[cores : 2 * cores]
+    windows, own_measured, kept, plus, minus, pieces, other_measured = refs[2 * cores :]
+    upper, _, twin, core = layout.place()
+    plus_table, minus_table = (plus[0], plus[1]), (minus[0], minus[1])
+    cut = (layout.regions, layout.piece, length)
+    for frame in range(frames):
+        window_real, window_imag = windows[frame, 0], windows[frame, 1]
+        intensity = intensities[0][frame]
+        for more in intensities[1:]:
+            intensity += more[frame]
+        for step, part in enumerate(parts):
+            other_measured[(core + step) % cores] = part[frame]
+        measured = other_measured[...].reshape(length, length)
+        measured = jnp.where(upper == twin, own_measured[frame], measured)
+        factor = jnp.sqrt(measured) / jnp.sqrt(intensity + intensity_offset) - 1.0
         factors = jnp.concatenate([factor, factor], axis=1)
-        power = window_real**2 + window_imag**2
-        cut = (layout.regions, layout.piece, length)
-        pieces_here = [power]
-        for kept in range(local):
-            wave = far[kept] * factors
+        channels = [window_real**2 + window_imag**2]
+        for local in range(layout.local_modes):
+            wave = kept[frame, local] * factors
             change = from_left(plus_table, above(from_right(wave, minus_table)))
             change_real, change_imag = change[:length], change[length:]
-            pieces_here.append(window_real * change_real + window_imag * change_imag)
-            pieces_here.append(window_real * change_imag - window_imag * change_real)
-        for channel, values in enumerate(pieces_here):
+            channels.append(window_real * change_real + window_imag * change_imag)
+            channels.append(window_real * change_imag - window_imag * change_real)
+        for channel, values in enumerate(channels):
             if frame == 0:
                 pieces[:, channel] = values.reshape(cut)
             else:
                 pieces[:, channel] += values.reshape(cut)
-    for kept in range(local):
-        rows = pl.ds(region * layout.piece, layout.piece)
-        for plane in range(2):
-            old_piece[kept, plane] = probes[plane, first_mode + kept, rows, :]
 
 
 def step_kernel(layout, arrived, old_piece, new_piece):
@@ -259,7 +280,7 @@
 def second_kernel(layout, offsets, *refs):
     cores, frames, length = layout.cores, layout.frames, layout.length
     probes = refs[:cores]
-    windows, own_measured, other_measured, plus, minus, left_plus, left_minus = refs[
+    windows, own_measured, part_measured, plus, minus, left_plus, left_minus = refs[
         cores : cores + 7
     ]
     probe_out, probe_power, *others = refs[cores + 7 :]
@@ -305,7 +326,7 @@
             wave = from_right(beside(from_left(part_minus, leaving)), plus_table)
             intensity += wave[:, :length] ** 2 + wave[:, length:] ** 2
             far[number] = wave
-        measured = jnp.where(upper == twin, own_measured[frame, rows, :], other_measured[frame, rows, :])
+        measured = jnp.where(upper == twin, own_measured[frame, rows, :], part_measured[frame])
         factor = jnp.sqrt(measured) / jnp.sqrt(intensity + intensity_offset) - 1.0
         factors = jnp.concatenate([factor, factor], axis=1)
         numer_real = jnp.zeros((length, length), single)
@@ -376,17 +397,24 @@
         rows_out[plane] = rows_in[plane] + total[plane * share : (plane + 1) * share] / damped
 
 
-def call(kernel, name, operands, outputs, scratch=(), scalar_count=0):
+def call(kernel, name, operands, outputs, scratch=(), scalar_count=0, after=()):
     shapes = [jax.ShapeDtypeStruct(shape, single) for shape in outputs]
+    count = len(operands)
+
+    def inner(*refs):
+        kernel(*refs[:count], *refs[count + len(after) :])
+
     return pl.pallas_call(
-        kernel,
+        inner,
         name=name,
         out_shape=shapes,
-        in_specs=[scalars] * scalar_count + [on_chip] * (len(operands) - scalar_count),
+        in_specs=[scalars] * scalar_count
+        + [on_chip] * (count - scalar_count)
+        + [pl.BlockSpec(memory_space=pl.ANY)] * len(after),
         out_specs=[on_chip] * len(shapes),
         scratch_shapes=[pltpu.VMEM(shape, single) for shape in scratch],
         compiler_params=pltpu.CompilerParams(vmem_limit_bytes=50 * 2**20),
-    )(*operands)
+    )(*operands, *after)
 
 
 def body(measured, probe_modes, object_bands, scan_offsets, band_owner):
@@ -403,52 +431,60 @@
     local = layout.local_modes
     plus, minus, left_plus, left_minus = fourier_tables(length, cores)
     helper = lax.axis_index("mode")
-
-    own_rows = lax.dynamic_slice_in_dim(object_bands, helper * share, share, 1)
-    blocks = [own_rows] + [layout.from_upper(own_rows, step) for step in range(1, halves)]
-    probes = lax.all_gather(probe_modes, "mode", axis=1, tiled=True)
-    other_measured = measured
+    core = helper % cores
+
+    strip_rows = lax.dynamic_slice_in_dim(object_bands, core * layout.strip, layout.strip, 1)
+    probes = [probe_modes] + [layout.from_twin(probe_modes, step) for step in range(1, halves)]
+    cuts, part_measured = call(
+        functools.partial(cut_kernel, layout),
+        "cut",
+        (scan_offsets, band_owner, strip_rows, measured),
+        [(layout.lowers, 2, layout.strip, length), (frames, layout.part, length)],
+        scalar_count=2,
+    )
     if halves > 1:
         pairs = [
             (layout.device(t, l, t, c), layout.device(u, l, t, c))
             for u, l, t, c in layout.everyone()
             if u != t
         ]
-        other_measured = lax.ppermute(measured, axes, pairs)
-
-    (cuts,) = call(
-        functools.partial(cut_kernel, layout),
-        "cut",
-        (scan_offsets, band_owner, *blocks),
-        [(regions, halves, 2, share, length)],
-        scalar_count=2,
-    )
-    cuts = layout.within_cube(cuts)
-    strip = (frames, 2, 2, halves, share, length)
+        part_measured = lax.ppermute(part_measured, axes, pairs)
+    measured_parts = [part_measured]
+    for step in range(1, cores):
+        measured_parts.append(layout.from_core(part_measured, step))
+    cuts = layout.within_row(cuts)
     (chosen,) = call(
         functools.partial(choose_kernel, layout),
         "choose",
         (scan_offsets, band_owner, cuts),
-        [strip],
+        [(frames, 2, 2, layout.strip, length)],
         scalar_count=2,
-    )
-    strips = [chosen] + [layout.from_core(chosen, step) for step in range(1, cores)]
-    inner = (2, 2, halves, cores, share, length)
-    windows, pieces, old_piece = call(
-        functools.partial(first_kernel, layout),
-        "first",
-        (scan_offsets, *strips, measured, other_measured, probes, plus, minus),
+        after=(part_measured,),
+    )
+    parts = [chosen] + [layout.from_upper(chosen, step) for step in range(1, halves)]
+    strips = list(parts)
+    for step in range(1, cores):
+        strips += [layout.from_core(part, step) for part in parts]
+    windows, intensity, kept, old_piece = call(
+        functools.partial(far_kernel, layout),
+        "far",
+        (scan_offsets, *strips, *probes, plus, minus),
         [
             (frames, 2, length, length),
-            (regions, 1 + 2 * local, piece, length),
+            (frames, length, length),
+            (frames, local, length, 2 * length),
             (local, 2, piece, length),
         ],
-        scratch=[
-            inner,
-            (length, length),
-            (local, length, 2 * length),
-        ],
+        scratch=[(2, 2, cores, layout.strip, length)],
         scalar_count=1,
+    )
+    intensities = [intensity] + [layout.from_core(intensity, step) for step in range(1, cores)]
+    (pieces,) = call(
+        functools.partial(gradient_kernel, layout),
+        "gradient",
+        (*intensities, *measured_parts, windows, measured, kept, plus, minus),
+        [(regions, 1 + 2 * local, piece, length)],
+        scratch=[(cores, layout.part, length)],
     )
     pieces = layout.within_cube(pieces)
     (new_piece,) = call(
@@ -460,6 +496,9 @@
     entries = [new_piece] + [layout.from_upper(new_piece, step) for step in range(1, halves)]
     spread = jnp.broadcast_to(jnp.stack(entries)[None], (regions, halves, local, 2, piece, length))
     gathered = layout.within_cube(spread)
+    strip = (frames, 2, 2, halves, share, length)
+    inner = (2, 2, halves, cores, share, length)
+    own_rows = lax.dynamic_slice_in_dim(object_bands, helper * share, share, 1)
     new_probes = [gathered] + [layout.from_core(gathered, step) for step in range(1, cores)]
     probe_out, probe_power, *shares = call(
         functools.partial(second_kernel, layout),
@@ -469,7 +508,7 @@
             *new_probes,
             windows,
             measured,
-            other_measured,
+            part_measured,
             plus,
             minus,
             left_plus,

time: 140 us -> 121 us (0.86)
  between operations: 14.1 us -> 0.78 us
  blocking collectives: 50.8 us -> 39.8 us
  starting transfers between devices: 14.9 us -> 18.9 us
  waiting for transfers between devices: 33 us -> 36.6 us
    all_to_all x3 -> x2, blocking collectives: 44.2 us -> 33.3 us  [within_cube(): lax.all_to_all(array, axes, split_axis=0, concat_axis=0, tiled=True, axis...]
    all_to_all x1, waiting for transfers between devices: 17 us -> 10.5 us  [within_cube(): lax.all_to_all(array, axes, split_axis=0, concat_axis=0, tiled=True, axis...]
    ppermute x2, waiting for transfers between devices: 9.78 us -> 15.3 us  [from_upper(): return lax.ppermute(array, axes, pairs)]
    all_to_all x0 -> x1, starting transfers between devices: none -> 5.35 us  [within_row(): lax.all_to_all(array, axes, split_axis=0, concat_axis=0, tiled=True, axis...]
    ppermute x1 -> x2, waiting for transfers between devices: 0.01 us -> 4.05 us  [the longest x1 4.05 us: body(): part_measured = lax.ppermute(part_measured, axes, pairs)]
    pallas_call x7 -> x8, Pallas kernels: 22.7 us -> 21.4 us  [call(): pl.pallas_call(inner, name=name, out_shape=shapes, in_specs=[scalars] * s...]
    ppermute x3 -> x6, waiting for transfers between devices: 5.57 us -> 6.8 us  [from_core(): return lax.ppermute(array, axes, pairs)]
    ppermute x1 -> x2, starting transfers between devices: 5.3 us -> 4.56 us  [the longest x1 4.49 us: body(): part_measured = lax.ppermute(part_measured, axes, pairs)]
  transfers between devices with their start and end apart: 8 -> 12, of which waited for: 6 -> 8; matrix products, arithmetic and copies ran while one was open for 1% -> 0% of each run, Pallas kernels for 1% -> 1%
where the time goes in v2:
time: 121 us; the launch traced here: 120 us
  blocking collectives  39.8 us (33%)
  waiting for transfers between devices  36.6 us (30%)
  Pallas kernels  21.4 us (18%)
  starting transfers between devices  18.9 us (16%)
  local copies, waits for them, and re-layouts  2.91 us (2%)
    all_to_all x2, blocking collectives, within_cube(): lax.all_to_all(array, axes, split_axis=0, concat_axis=0, tiled=True, axis...  33.3 us
    pallas_call x8, Pallas kernels, call(): pl.pallas_call(inner, name=name, out_shape=shapes, in_specs=[scalars] * s...  21.4 us
    ppermute x2, waiting for transfers between devices, from_upper(): return lax.ppermute(array, axes, pairs)  15.3 us
    all_to_all x1, waiting for transfers between devices, within_cube(): lax.all_to_all(array, axes, split_axis=0, concat_axis=0, tiled=True, axis...  10.5 us
    ppermute x6, waiting for transfers between devices, from_core(): return lax.ppermute(array, axes, pairs)  6.8 us
    all_gather x1, blocking collectives, body(): object_out = lax.all_gather(new_rows, 'mode', axis=1, tiled=True)  6.51 us
    all_to_all x1, starting transfers between devices, within_row(): lax.all_to_all(array, axes, split_axis=0, concat_axis=0, tiled=True, axis...  5.35 us
    ppermute x2, starting transfers between devices, from_upper(): return lax.ppermute(array, axes, pairs)  4.75 us
  transfers between devices with their start and end apart: 12, of which 8 were waited for; matrix products, arithmetic and copies ran while one was open for 0% of the time, Pallas kernels for 1%

profile of v2, /device:TPU:0, one launch (start us, length us, event | category | flops | bytes accessed | tf_op | source)
XLA Modules:
  0.0 120.3 jit_solution(1084424685576169318)
XLA Ops:
  1.7 0.9 copy-done.2
  2.6 1.8 %cut.1 = (f32[4,2,64,256]{3,2,1,0:T(8,128)}, f32[1,128,256]{2,1,0:T(8,128)S(1)}) custom-call(s32[8,2]{1,0:T(8,128)S(1)} %copy.14.refs_0_, s32[8]{0:T(128)S(1)} %copy-done.4, f32[2,64,512]{2,1,0:T(8,128)S(1)} %constant_dynamic-slice_fusion.1.refs_2_, f32[1,256,256]{2,1,0:T(8,128)S(1)} %copy-done.2), custom_call_target="tpu_custom_call" | custom-call | tf_op jit(solution)/shard_map/cut/pallas_call | solution.py:407
  4.4 5.4 %all-to-all-start = ((f32[4,2,64,256]{3,2,1,0:T(8,128)}), f32[4,2,64,256]{3,2,1,0:T(8,128)S(1)}, u32[]{:S(2)}, u32[]{:S(2)}) async-start(f32[4,2,64,256]{3,2,1,0:T(8,128)} %get-tuple-element.12), calls=%async_computation | async-start | bytes 1048576 | tf_op jit(solution)/shard_map/all_to_all | solution.py:91
  9.8 4.5 %collective-permute-start = (f32[1,128,256]{2,1,0:T(8,128)S(1)}, f32[1,128,256]{2,1,0:T(8,128)S(1)}, u32[]{:S(2)}, u32[]{:S(2)}) collective-permute-start(f32[1,128,256]{2,1,0:T(8,128)S(1)} %get-tuple-element.13), channel_id=1, source_target_pairs={{18,2},{19,3},{22,6},{23,7},{26,10},{27,11},{30,14},{31,15},{0,16}... | collective-permute-start | bytes 393224 | tf_op jit(solution)/shard_map/ppermute | solution.py:451
  14.3 4.0 %collective-permute-done.refs_3_.refs_2_.refs_5_ = f32[1,128,256]{2,1,0:T(8,128)S(1)} collective-permute-done((f32[1,128,256]{2,1,0:T(8,128)S(1)}, f32[1,128,256]{2,1,0:T(8,128)S(1)}, u32[]{:S(2)}, u32[]{:S(2)}) %collective-permute-start) | collective-permute-done | bytes 131104 | tf_op jit(solution)/shard_map/ppermute | solution.py:451
  19.1 3.5 %collective-permute-start.1 = (f32[1,2,2,64,256]{4,3,2,1,0:T(8,128)S(1)}, f32[1,2,2,64,256]{4,3,2,1,0:T(8,128)S(1)}, u32[]{:S(2)}, u32[]{:S(2)}) collective-permute-start(f32[1,2,2,64,256]{4,3,2,1,0:T(8,128)S(1)} %choose.1.refs_1_), channel_id=1, source_target_pairs={{16,0},{17,1},{18,2},{19,3},{20,4},{21,5},{22,6},{23,7},{24,8},{25... | collective-permute-start | bytes 786440 | tf_op jit(solution)/shard_map/ppermute | solution.py:68
  22.6 10.9 %collective-permute-done.1.refs_2_ = f32[1,2,2,64,256]{4,3,2,1,0:T(8,128)S(1)} collective-permute-done((f32[1,2,2,64,256]{4,3,2,1,0:T(8,128)S(1)}, f32[1,2,2,64,256]{4,3,2,1,0:T(8,128)S(1)}, u32[]{:S(2)}, u32[]{:S(2)}) %collective-permute-start.1) | collective-permute-done | bytes 262176 | tf_op jit(solution)/shard_map/ppermute | solution.py:68
  33.6 1.5 %collective-permute-done.3.refs_4_ = f32[1,2,2,64,256]{4,3,2,1,0:T(8,128)S(1)} collective-permute-done((f32[1,2,2,64,256]{4,3,2,1,0:T(8,128)S(1)}, f32[1,2,2,64,256]{4,3,2,1,0:T(8,128)S(1)}, u32[]{:S(2)}, u32[]{:S(2)}) %collective-permute-start.3) | collective-permute-done | bytes 262176 | tf_op jit(solution)/shard_map/ppermute | solution.py:75
  35.1 5.4 %far.1 = (f32[1,2,256,256]{3,2,1,0:T(8,128)S(1)}, f32[1,256,256]{2,1,0:T(8,128)S(1)}, f32[1,1,256,512]{3,2,1,0:T(8,128)S(1)}, f32[1,2,32,256]{3,2,1,0:T(8,128)S(1)}) custom-call(s32[8,2]{1,0:T(8,128)S(1)} %copy.14.refs_0_, f32[1,2,2,64,256]{4,3,2,1,0:T(8,128)S(1)} %choose.1.refs_1_, f32[1,2,2,64,256]{4,3,2,1,0:T(8,128)S(1)} %collective-permute-done.1.refs_2_, ...), custom_call_target="tpu_custom_call" | custom-call | tf_op jit(solution)/shard_map/far/pallas_call | solution.py:407
  41.1 1.2 %collective-permute-done.6.refs_3_ = f32[1,128,256]{2,1,0:T(8,128)S(1)} collective-permute-done((f32[1,128,256]{2,1,0:T(8,128)S(1)}, f32[1,128,256]{2,1,0:T(8,128)S(1)}, u32[]{:S(2)}, u32[]{:S(2)}) %collective-permute-start.6) | collective-permute-done | bytes 131104 | tf_op jit(solution)/shard_map/ppermute | solution.py:75
  42.3 2.5 %gradient.1 = f32[8,3,32,256]{3,2,1,0:T(8,128)S(1)} custom-call(f32[1,256,256]{2,1,0:T(8,128)S(1)} %get-tuple-element.14.refs_0_, f32[1,256,256]{2,1,0:T(8,128)S(1)} %collective-permute-done.5.refs_1_, f32[1,128,256]{2,1,0:T(8,128)S(1)} %collective-permute-done.refs_3_.refs_2_.refs_5_, f32[1,128,256]{2,1,0:T(8,128)S(1)} %collective-permute-done.6.refs_3_, ...), custom_call_target="tpu_custom_call" | custom-call | tf_op jit(solution)/shard_map/gradient/pallas_call | solution.py:407
  44.8 17.6 %all_to_all.20.refs_0_ = f32[8,3,32,256]{3,2,1,0:T(8,128)S(1)} all-to-all(f32[8,3,32,256]{3,2,1,0:T(8,128)S(1)} %gradient.1), channel_id=1, replica_groups={{0,4,8,12,2,6,10,14},{1,5,9,13,3,7,11,15},{16,20,24,28,18,22,26,30},{17..., dimensions={0} | all-to-all | bytes 1572864 | tf_op jit(solution)/shard_map/all_to_all | solution.py:96
  62.5 1.2 %collective-permute-start.7 = (f32[1,2,32,256]{3,2,1,0:T(8,128)S(1)}, f32[1,2,32,256]{3,2,1,0:T(8,128)S(1)}, u32[]{:S(2)}, u32[]{:S(2)}) collective-permute-start(f32[1,2,32,256]{3,2,1,0:T(8,128)S(1)} %step.1), channel_id=1, source_target_pairs={{16,0},{17,1},{18,2},{19,3},{20,4},{21,5},{22,6},{23,7},{24,8},{25... | collective-permute-start | bytes 196616 | tf_op jit(solution)/shard_map/ppermute | solution.py:68
  63.7 4.3 %collective-permute-done.7 = f32[1,2,32,256]{3,2,1,0:T(8,128)S(1)} collective-permute-done((f32[1,2,32,256]{3,2,1,0:T(8,128)S(1)}, f32[1,2,32,256]{3,2,1,0:T(8,128)S(1)}, u32[]{:S(2)}, u32[]{:S(2)}) %collective-permute-start.7) | collective-permute-done | bytes 65568 | tf_op jit(solution)/shard_map/ppermute | solution.py:68
  68.2 15.7 %all_to_all.21.refs_1_ = f32[8,2,1,2,32,256]{5,4,3,2,1,0:T(8,128)S(1)} all-to-all(f32[8,2,1,2,32,256]{5,4,3,2,1,0:T(8,128)S(1)} %broadcast_in_dim.9), channel_id=1, replica_groups={{0,4,8,12,2,6,10,14},{1,5,9,13,3,7,11,15},{16,20,24,28,18,22,26,30},{17..., dimensions={0} | all-to-all | bytes 2097152 | tf_op jit(solution)/shard_map/all_to_all | solution.py:96
  83.9 2.7 %collective-permute-done.8.refs_2_ = f32[8,2,1,2,32,256]{5,4,3,2,1,0:T(8,128)S(1)} collective-permute-done((f32[8,2,1,2,32,256]{5,4,3,2,1,0:T(8,128)S(1)}, f32[8,2,1,2,32,256]{5,4,3,2,1,0:T(8,128)S(1)}, u32[]{:S(2)}, u32[]{:S(2)}) %collective-permute-start.8) | collective-permute-done | bytes 1048608 | tf_op jit(solution)/shard_map/ppermute | solution.py:75
  86.6 8.4 %second.1 = (f32[2,1,256,256]{3,2,1,0:T(8,128)}, f32[256,256]{1,0:T(8,128)S(1)}, f32[1,2,2,2,32,256]{5,4,3,2,1,0:T(8,128)S(1)}, f32[1,2,2,2,32,256]{5,4,3,2,1,0:T(8,128)S(1)}) custom-call(s32[8,2]{1,0:T(8,128)S(1)} %copy.14.refs_0_, f32[8,2,1,2,32,256]{5,4,3,2,1,0:T(8,128)S(1)} %all_to_all.21.refs_1_, ...), custom_call_target="tpu_custom_call" | custom-call | tf_op jit(solution)/shard_map/second/pallas_call | solution.py:407
  95.1 1.4 %collective-permute-done.9.refs_3_ = f32[1,2,2,2,32,256]{5,4,3,2,1,0:T(8,128)S(1)} collective-permute-done((f32[1,2,2,2,32,256]{5,4,3,2,1,0:T(8,128)S(1)}, f32[1,2,2,2,32,256]{5,4,3,2,1,0:T(8,128)S(1)}, u32[]{:S(2)}, u32[]{:S(2)}) %collective-permute-start.9) | collective-permute-done | bytes 262176 | tf_op jit(solution)/shard_map/ppermute | solution.py:75
  96.5 1.5 %post.1 = f32[8,2,32,256]{3,2,1,0:T(8,128)} custom-call(s32[8,2]{1,0:T(8,128)S(1)} %copy.14.refs_0_, s32[8]{0:T(128)S(1)} %copy-done.4, f32[1,2,2,2,32,256]{5,4,3,2,1,0:T(8,128)S(1)} %get-tuple-element.19.refs_2_, f32[1,2,2,2,32,256]{5,4,3,2,1,0:T(8,128)S(1)} %collective-permute-done.9.refs_3_), custom_call_target="tpu_custom_call" | custom-call | tf_op jit(solution)/shard_map/post/pallas_call | solution.py:407
  98.0 3.5 %all-to-all-start.3 = ((f32[8,2,32,256]{3,2,1,0:T(8,128)}), f32[8,2,32,256]{3,2,1,0:T(8,128)S(1)}, u32[]{:S(2)}, u32[]{:S(2)}) async-start(f32[8,2,32,256]{3,2,1,0:T(8,128)} %post.1), calls=%async_computation.3 | async-start | bytes 1048576 | tf_op jit(solution)/shard_map/all_to_all | solution.py:96
  101.5 10.5 %all-to-all-done.3.refs_2_ = f32[8,2,32,256]{3,2,1,0:T(8,128)S(1)} async-done(((f32[8,2,32,256]{3,2,1,0:T(8,128)}), f32[8,2,32,256]{3,2,1,0:T(8,128)S(1)}, u32[]{:S(2)}, u32[]{:S(2)}) %all-to-all-start.3) | async-done | bytes 524320 | tf_op jit(solution)/shard_map/all_to_all | solution.py:96
  112.0 1.0 update.1
  113.0 6.5 %all_gather.3 = f32[2,128,512]{2,1,0:T(8,128)S(1)} all-gather(f32[2,32,512]{2,1,0:T(8,128)S(1)} %update.1), channel_id=1, replica_groups=mesh['region'=8,'mode'=4] {'mode'}, dimensions={1}, use_global_device_ids=true | all-gather | bytes 655360 | tf_op jit(solution)/shard_map/all_gather | solution.py:543
  119.6 0.8 copy.18
  (29 shorter events, 2.7 us)
Async XLA Ops:
  0.6 1.1 copy-start
  0.7 0.7 copy-start.5
  1.7 0.9 copy-start.2
  1.7 1.0 copy-start.4
  4.4 9.9 %copy-start.3 = (f32[2,1,256,256]{3,2,1,0:T(8,128)S(1)}, f32[2,1,256,256]{3,2,1,0:T(8,128)}, u32[]{:S(2)}) copy-start(f32[2,1,256,256]{3,2,1,0:T(8,128)} %refs_5_.2) | copy-start | bytes 1572868
  4.4 14.0 %all-to-all-start = ((f32[4,2,64,256]{3,2,1,0:T(8,128)}), f32[4,2,64,256]{3,2,1,0:T(8,128)S(1)}, u32[]{:S(2)}, u32[]{:S(2)}) async-start(f32[4,2,64,256]{3,2,1,0:T(8,128)} %get-tuple-element.12), calls=%async_computation | async-start | bytes 1048576 | tf_op jit(solution)/shard_map/all_to_all | solution.py:91
  9.8 8.6 %collective-permute-start = (f32[1,128,256]{2,1,0:T(8,128)S(1)}, f32[1,128,256]{2,1,0:T(8,128)S(1)}, u32[]{:S(2)}, u32[]{:S(2)}) collective-permute-start(f32[1,128,256]{2,1,0:T(8,128)S(1)} %get-tuple-element.13), channel_id=1, source_target_pairs={{18,2},{19,3},{22,6},{23,7},{26,10},{27,11},{30,14},{31,15},{0,16}... | collective-permute-start | bytes 393224 | tf_op jit(solution)/shard_map/ppermute | solution.py:451
  14.3 19.3 %collective-permute-start.4 = (f32[2,1,256,256]{3,2,1,0:T(8,128)S(1)}, f32[2,1,256,256]{3,2,1,0:T(8,128)S(1)}, u32[]{:S(2)}, u32[]{:S(2)}) collective-permute-start(f32[2,1,256,256]{3,2,1,0:T(8,128)S(1)} %copy-done.3), channel_id=1, source_target_pairs={{2,0},{3,1},{0,2},{1,3},{6,4},{7,5},{4,6},{5,7},{10,8},{11,9},{8,1... | collective-permute-start | bytes 1572872 | tf_op jit(solution)/shard_map/ppermute | solution.py:82
  19.1 23.2 %copy-start.1 = (bf16[2,512,512]{2,1,0:T(8,128)(2,1)S(1)}, bf16[2,512,512]{2,1,0:T(8,128)(2,1)}, u32[]{:S(2)}) copy-start(bf16[2,512,512]{2,1,0:T(8,128)(2,1)} %constant.32.clone.refs_7_.refs_6_) | copy-start | bytes 3145732
  19.1 14.4 %collective-permute-start.1 = (f32[1,2,2,64,256]{4,3,2,1,0:T(8,128)S(1)}, f32[1,2,2,64,256]{4,3,2,1,0:T(8,128)S(1)}, u32[]{:S(2)}, u32[]{:S(2)}) collective-permute-start(f32[1,2,2,64,256]{4,3,2,1,0:T(8,128)S(1)} %choose.1.refs_1_), channel_id=1, source_target_pairs={{16,0},{17,1},{18,2},{19,3},{20,4},{21,5},{22,6},{23,7},{24,8},{25... | collective-permute-start | bytes 786440 | tf_op jit(solution)/shard_map/ppermute | solution.py:68
  22.6 11.0 %collective-permute-start.2 = (f32[1,2,2,64,256]{4,3,2,1,0:T(8,128)S(1)}, f32[1,2,2,64,256]{4,3,2,1,0:T(8,128)S(1)}, u32[]{:S(2)}, u32[]{:S(2)}) collective-permute-start(f32[1,2,2,64,256]{4,3,2,1,0:T(8,128)S(1)} %choose.1.refs_1_), channel_id=1, source_target_pairs={{1,0},{0,1},{3,2},{2,3},{5,4},{4,5},{7,6},{6,7},{9,8},{8,9},{11,10... | collective-permute-start | bytes 786440 | tf_op jit(solution)/shard_map/ppermute | solution.py:75
  33.5 1.5 %collective-permute-start.3 = (f32[1,2,2,64,256]{4,3,2,1,0:T(8,128)S(1)}, f32[1,2,2,64,256]{4,3,2,1,0:T(8,128)S(1)}, u32[]{:S(2)}, u32[]{:S(2)}) collective-permute-start(f32[1,2,2,64,256]{4,3,2,1,0:T(8,128)S(1)} %collective-permute-done.1.refs_2_), channel_id=1, source_target_pairs={{1,0},{0,1},{3,2},{2,3},{5,4},{4,5},{7,6},{6,7},{9,8},{8,9},{11,10... | collective-permute-start | bytes 786440 | tf_op jit(solution)/shard_map/ppermute | solution.py:75
  40.5 1.8 %collective-permute-start.5 = (f32[1,256,256]{2,1,0:T(8,128)S(1)}, f32[1,256,256]{2,1,0:T(8,128)S(1)}, u32[]{:S(2)}, u32[]{:S(2)}) collective-permute-start(f32[1,256,256]{2,1,0:T(8,128)S(1)} %get-tuple-element.14.refs_0_), channel_id=1, source_target_pairs={{1,0},{0,1},{3,2},{2,3},{5,4},{4,5},{7,6},{6,7},{9,8},{8,9},{11,10... | collective-permute-start | bytes 786440 | tf_op jit(solution)/shard_map/ppermute | solution.py:75
  40.7 1.6 %collective-permute-start.6 = (f32[1,128,256]{2,1,0:T(8,128)S(1)}, f32[1,128,256]{2,1,0:T(8,128)S(1)}, u32[]{:S(2)}, u32[]{:S(2)}) collective-permute-start(f32[1,128,256]{2,1,0:T(8,128)S(1)} %collective-permute-done.refs_3_.refs_2_.refs_5_), channel_id=1, source_target_pairs={{1,0},{0,1},{3,2},{2,3},{5,4},{4,5},{7,6},{6,7},{9,8},{8,9},{11,10... | collective-permute-start | bytes 393224 | tf_op jit(solution)/shard_map/ppermute | solution.py:75
  62.5 5.6 %collective-permute-start.7 = (f32[1,2,32,256]{3,2,1,0:T(8,128)S(1)}, f32[1,2,32,256]{3,2,1,0:T(8,128)S(1)}, u32[]{:S(2)}, u32[]{:S(2)}) collective-permute-start(f32[1,2,32,256]{3,2,1,0:T(8,128)S(1)} %step.1), channel_id=1, source_target_pairs={{16,0},{17,1},{18,2},{19,3},{20,4},{21,5},{22,6},{23,7},{24,8},{25... | collective-permute-start | bytes 196616 | tf_op jit(solution)/shard_map/ppermute | solution.py:68
  83.9 2.7 %collective-permute-start.8 = (f32[8,2,1,2,32,256]{5,4,3,2,1,0:T(8,128)S(1)}, f32[8,2,1,2,32,256]{5,4,3,2,1,0:T(8,128)S(1)}, u32[]{:S(2)}, u32[]{:S(2)}) collective-permute-start(f32[8,2,1,2,32,256]{5,4,3,2,1,0:T(8,128)S(1)} %all_to_all.21.refs_1_), channel_id=1, source_target_pairs={{1,0},{0,1},{3,2},{2,3},{5,4},{4,5},{7,6},{6,7},{9,8},{8,9},{11,10... | collective-permute-start | bytes 3145736 | tf_op jit(solution)/shard_map/ppermute | solution.py:75
  95.0 1.5 %collective-permute-start.9 = (f32[1,2,2,2,32,256]{5,4,3,2,1,0:T(8,128)S(1)}, f32[1,2,2,2,32,256]{5,4,3,2,1,0:T(8,128)S(1)}, u32[]{:S(2)}, u32[]{:S(2)}) collective-permute-start(f32[1,2,2,2,32,256]{5,4,3,2,1,0:T(8,128)S(1)} %get-tuple-element.20), channel_id=1, source_target_pairs={{1,0},{0,1},{3,2},{2,3},{5,4},{4,5},{7,6},{6,7},{9,8},{8,9},{11,10... | collective-permute-start | bytes 786440 | tf_op jit(solution)/shard_map/ppermute | solution.py:75
  98.0 14.0 %all-to-all-start.3 = ((f32[8,2,32,256]{3,2,1,0:T(8,128)}), f32[8,2,32,256]{3,2,1,0:T(8,128)S(1)}, u32[]{:S(2)}, u32[]{:S(2)}) async-start(f32[8,2,32,256]{3,2,1,0:T(8,128)} %post.1), calls=%async_computation.3 | async-start | bytes 1048576 | tf_op jit(solution)/shard_map/all_to_all | solution.py:96

commit v3 on v2

--- a/solution.py
+++ b/solution.py
@@ -99,22 +99,30 @@
 
 
 def fourier_tables(length, cores):
-    positions = np.arange(length)
-    angles = (positions[:, None] * positions[None, :] % length) * (2.0 * math.pi / length)
-    cosine, sine = np.cos(angles) / math.sqrt(length), np.sin(angles) / math.sqrt(length)
-    plus = np.block([[cosine, -sine], [sine, cosine]])
-    minus = np.block([[cosine, sine], [-sine, cosine]])
-    rows = [
-        np.concatenate([block, length + block]) for block in np.split(positions, cores)
-    ]
-    minus_parts = np.stack([minus[taken] for taken in rows])
-    plus_parts = np.stack([plus[:, taken] for taken in rows])
+    near = np.arange(length // 2)
+    forms = []
+    for odd in range(2):
+        angles = near[:, None] * (2 * near[None, :] + odd) % length * (2.0 * math.pi / length)
+        cosine, sine = np.cos(angles) / math.sqrt(length), np.sin(angles) / math.sqrt(length)
+        forms.append(np.block([[cosine, -sine], [sine, cosine]]))
+    forward = np.stack(forms)
+    parts = []
+    for core in range(cores):
+        wanted = np.split(np.arange(length), cores)[core] % (length // 2)
+        columns = np.concatenate([wanted, length // 2 + wanted])
+        parts.append(forms[2 * core // cores][:, columns])
+    back_parts = np.stack(parts)
 
     def pair(table):
         lead = table.astype(ml_dtypes.bfloat16)
         return np.stack([lead, (table - lead.astype(np.float64)).astype(ml_dtypes.bfloat16)])
 
-    return pair(plus), pair(minus), pair(plus_parts), pair(minus_parts)
+    return (
+        pair(forward),
+        pair(forward.swapaxes(1, 2)),
+        pair(back_parts.swapaxes(1, 2)),
+        pair(back_parts),
+    )
 
 
 def split(values):
@@ -136,14 +144,56 @@
     return dot(lead, table[0]) + dot(lead, table[1]) + dot(trail, table[0])
 
 
-def beside(stacked):
-    rows = stacked.shape[0] // 2
-    return jnp.concatenate([stacked[:rows], stacked[rows:]], axis=1)
-
-
-def above(planes):
-    columns = planes.shape[1] // 2
-    return jnp.concatenate([planes[:, :columns], planes[:, columns:]], axis=0)
+def beside(left, right):
+    return jnp.concatenate([left, right], axis=1)
+
+
+def above(top, bottom):
+    return jnp.concatenate([top, bottom], axis=0)
+
+
+def table_of(tables, number):
+    return tables[0, number], tables[1, number]
+
+
+def columns_forward(real, imag, forward):
+    middle = real.shape[1] // 2
+    real_left, real_right = real[:, :middle], real[:, middle:]
+    imag_left, imag_right = imag[:, :middle], imag[:, middle:]
+    even = from_right(beside(real_left + real_right, imag_left + imag_right), table_of(forward, 0))
+    odd = from_right(beside(real_left - real_right, imag_left - imag_right), table_of(forward, 1))
+    return (
+        beside(even[:, :middle], odd[:, :middle]),
+        beside(even[:, middle:], odd[:, middle:]),
+    )
+
+
+def columns_back(real, imag, back):
+    middle = real.shape[1] // 2
+    even = from_right(beside(real[:, :middle], imag[:, :middle]), table_of(back, 0))
+    odd = from_right(beside(real[:, middle:], imag[:, middle:]), table_of(back, 1))
+    plus, minus = even + odd, even - odd
+    return (
+        beside(plus[:, :middle], minus[:, :middle]),
+        beside(plus[:, middle:], minus[:, middle:]),
+    )
+
+
+def rows_forward(real, imag, back):
+    middle = real.shape[0] // 2
+    real_top, real_bottom = real[:middle], real[middle:]
+    imag_top, imag_bottom = imag[:middle], imag[middle:]
+    even = from_left(table_of(back, 0), above(real_top + real_bottom, imag_top + imag_bottom))
+    odd = from_left(table_of(back, 1), above(real_top - real_bottom, imag_top - imag_bottom))
+    return above(even[:middle], odd[:middle]), above(even[middle:], odd[middle:])
+
+
+def rows_back(real, imag, forward):
+    middle = real.shape[0] // 2
+    even = from_left(table_of(forward, 0), above(real[:middle], imag[:middle]))
+    odd = from_left(table_of(forward, 1), above(real[middle:], imag[middle:]))
+    plus, minus = even + odd, even - odd
+    return above(plus[:middle], minus[:middle]), above(plus[middle:], minus[middle:])
 
 
 def band_of_block(owner, block, layout):
@@ -196,10 +246,9 @@
 def far_kernel(layout, offsets, *refs):
     cores, halves, frames, length = layout.cores, layout.halves, layout.frames, layout.length
     shares, probes = refs[: cores * halves], refs[cores * halves : (cores + 1) * halves]
-    plus, minus, windows, intensity, kept, old_piece, inner = refs[(cores + 1) * halves :]
+    forward, back, windows, intensity, kept, old_piece, inner = refs[(cores + 1) * halves :]
     upper, lower, twin, core = layout.place()
     region = twin * layout.lowers + lower
-    plus_table, minus_table = (plus[0], plus[1]), (minus[0], minus[1])
     rows = pl.ds(pl.multiple_of(region * layout.piece, layout.piece), layout.piece)
     for frame in range(frames):
         lead = offsets[region * frames + frame, 0] % layout.band
@@ -217,48 +266,62 @@
             goes_back = (twin + entry) % halves == upper
             for local in range(layout.local_modes):
                 probe_real, probe_imag = probe[0, local], probe[1, local]
-                leaving = jnp.concatenate(
-                    [
-                        probe_real * window_real - probe_imag * window_imag,
-                        probe_real * window_imag + probe_imag * window_real,
-                    ],
-                    axis=0,
+                wave = rows_forward(
+                    probe_real * window_real - probe_imag * window_imag,
+                    probe_real * window_imag + probe_imag * window_real,
+                    back,
                 )
-                wave = from_right(beside(from_left(minus_table, leaving)), plus_table)
-                total += wave[:, :length] ** 2 + wave[:, length:] ** 2
+                wave_real, wave_imag = columns_forward(*wave, forward)
+                total += wave_real**2 + wave_imag**2
 
                 @pl.when(goes_back)
                 def _():
-                    kept[frame, local] = wave
+                    kept[frame, local, 0] = wave_real
+                    kept[frame, local, 1] = wave_imag
                     for plane in range(2):
                         old_piece[local, plane] = probe[plane, local, rows, :]
 
         intensity[frame] = total
 
 
+def order_kernel(layout, own_measured, *refs):
+    parts, (out, other_measured) = refs[: layout.cores], refs[layout.cores :]
+    upper, _, twin, core = layout.place()
+    length = layout.length
+    rows = lax.broadcasted_iota(jnp.int32, (length, length), 0)
+    columns = lax.broadcasted_iota(jnp.int32, (length, length), 1)
+    middle = length // 2
+    pick_rows = (columns == jnp.where(rows < middle, 2 * rows, 2 * (rows - middle) + 1)).astype(half)
+    pick_columns = (rows == jnp.where(columns < middle, 2 * columns, 2 * (columns - middle) + 1)).astype(half)
+
+    def exact(product, values):
+        lead, rest = split(values)
+        trail = (values - lead.astype(single) - rest.astype(single)).astype(half)
+        return (product(lead) + product(rest)) + product(trail)
+
+    for frame in range(layout.frames):
+        for step, part in enumerate(parts):
+            other_measured[(core + step) % layout.cores] = part[frame]
+        measured = other_measured[...].reshape(length, length)
+        measured = jnp.sqrt(jnp.where(upper == twin, own_measured[frame], measured))
+        measured = exact(lambda values: dot(pick_rows, values), measured)
+        out[frame] = exact(lambda values: dot(values, pick_columns), measured)
+
+
 def gradient_kernel(layout, *refs):
     cores, frames, length = layout.cores, layout.frames, layout.length
-    intensities, parts = refs[:cores], refs[cores : 2 * cores]
-    windows, own_measured, kept, plus, minus, pieces, other_measured = refs[2 * cores :]
-    upper, _, twin, core = layout.place()
-    plus_table, minus_table = (plus[0], plus[1]), (minus[0], minus[1])
+    intensities, (roots, windows, kept, forward, back, pieces) = refs[:cores], refs[cores:]
     cut = (layout.regions, layout.piece, length)
     for frame in range(frames):
         window_real, window_imag = windows[frame, 0], windows[frame, 1]
         intensity = intensities[0][frame]
         for more in intensities[1:]:
             intensity += more[frame]
-        for step, part in enumerate(parts):
-            other_measured[(core + step) % cores] = part[frame]
-        measured = other_measured[...].reshape(length, length)
-        measured = jnp.where(upper == twin, own_measured[frame], measured)
-        factor = jnp.sqrt(measured) / jnp.sqrt(intensity + intensity_offset) - 1.0
-        factors = jnp.concatenate([factor, factor], axis=1)
+        factor = roots[frame] / jnp.sqrt(intensity + intensity_offset) - 1.0
         channels = [window_real**2 + window_imag**2]
         for local in range(layout.local_modes):
-            wave = kept[frame, local] * factors
-            change = from_left(plus_table, above(from_right(wave, minus_table)))
-            change_real, change_imag = change[:length], change[length:]
+            wave = columns_back(kept[frame, local, 0] * factor, kept[frame, local, 1] * factor, back)
+            change_real, change_imag = rows_back(*wave, forward)
             channels.append(window_real * change_real + window_imag * change_imag)
             channels.append(window_real * change_imag - window_imag * change_real)
         for channel, values in enumerate(channels):
@@ -280,19 +343,14 @@
 def second_kernel(layout, offsets, *refs):
     cores, frames, length = layout.cores, layout.frames, layout.length
     probes = refs[:cores]
-    windows, own_measured, part_measured, plus, minus, left_plus, left_minus = refs[
-        cores : cores + 7
-    ]
-    probe_out, probe_power, *others = refs[cores + 7 :]
+    windows, roots, forward, back, left_forward, left_back = refs[cores : cores + 6]
+    probe_out, probe_power, *others = refs[cores + 6 :]
     shares, (far, inner) = others[:cores], others[cores:]
     upper, lower, twin, core = layout.place()
     region = twin * layout.lowers + lower
-    plus_table, minus_table = (plus[0], plus[1]), (minus[0], minus[1])
-    part_minus = (left_minus[0, core], left_minus[1, core])
-    part_plus = (left_plus[0, core], left_plus[1, core])
-    local = layout.local_modes
-    part = layout.part
+    local, part, middle = layout.local_modes, layout.part, length // 2
     rows = pl.ds(pl.multiple_of(core * part, part), part)
+    sign = jnp.where(2 * core < cores, 1.0, -1.0)
     listed = [
         (step, entry, kept)
         for step in range(cores)
@@ -302,6 +360,9 @@
 
     def probe(step, entry, kept, plane):
         return probes[step][:, entry, kept, plane].reshape(length, length)
+
+    def fold(values):
+        return values[:middle] + sign * values[middle:]
 
     own_entry = (twin + layout.halves - upper) % layout.halves
     for kept in range(local):
@@ -316,24 +377,23 @@
         intensity = jnp.zeros((part, length), single)
         for number, place in enumerate(listed):
             probe_real, probe_imag = probe(*place, 0), probe(*place, 1)
-            leaving = jnp.concatenate(
-                [
-                    probe_real * window_real - probe_imag * window_imag,
-                    probe_real * window_imag + probe_imag * window_real,
-                ],
-                axis=0,
+            leaving = above(
+                fold(probe_real * window_real - probe_imag * window_imag),
+                fold(probe_real * window_imag + probe_imag * window_real),
             )
-            wave = from_right(beside(from_left(part_minus, leaving)), plus_table)
-            intensity += wave[:, :length] ** 2 + wave[:, length:] ** 2
-            far[number] = wave
-        measured = jnp.where(upper == twin, own_measured[frame, rows, :], part_measured[frame])
-        factor = jnp.sqrt(measured) / jnp.sqrt(intensity + intensity_offset) - 1.0
-        factors = jnp.concatenate([factor, factor], axis=1)
+            wave = from_left(table_of(left_forward, core), leaving)
+            wave_real, wave_imag = columns_forward(wave[:part], wave[part:], forward)
+            intensity += wave_real**2 + wave_imag**2
+            far[number, 0] = wave_real
+            far[number, 1] = wave_imag
+        factor = roots[frame, rows, :] / jnp.sqrt(intensity + intensity_offset) - 1.0
         numer_real = jnp.zeros((length, length), single)
         numer_imag = jnp.zeros((length, length), single)
         for number, place in enumerate(listed):
-            change = from_left(part_plus, above(from_right(far[number] * factors, minus_table)))
-            change_real, change_imag = change[:length], change[length:]
+            wave_real, wave_imag = columns_back(far[number, 0] * factor, far[number, 1] * factor, back)
+            change = from_left(table_of(left_back, core), above(wave_real, wave_imag))
+            change_real = above(change[:middle], sign * change[:middle])
+            change_imag = above(change[middle:], sign * change[middle:])
             probe_real, probe_imag = probe(*place, 0), probe(*place, 1)
             numer_real += probe_real * change_real + probe_imag * change_imag
             numer_imag += probe_real * change_imag - probe_imag * change_real
@@ -366,7 +426,7 @@
                 out[target * layout.lowers + low, plane] = total
 
 
-def update_kernel(layout, offsets, owner, arrived, probe_power, rows_in, rows_out, doubled):
+def update_kernel(layout, offsets, owner, arrived, probe_power, block, rows_out, doubled):
     upper, lower, twin, core = layout.place()
     length, share = layout.length, layout.share
     band = band_of_block(owner, upper * layout.lowers + lower, layout)
@@ -394,7 +454,8 @@
         total += pltpu.roll(jnp.concatenate([kept, blank], axis=1), column, 1)
     damped = total[2 * share :] + object_damping
     for plane in range(2):
-        rows_out[plane] = rows_in[plane] + total[plane * share : (plane + 1) * share] / damped
+        old = block[plane, pl.ds(pl.multiple_of(first, share), share), :]
+        rows_out[plane] = old + total[plane * share : (plane + 1) * share] / damped
 
 
 def call(kernel, name, operands, outputs, scratch=(), scalar_count=0, after=()):
@@ -429,7 +490,7 @@
     regions, halves, cores = layout.regions, layout.halves, layout.cores
     length, share, piece, frames = layout.length, layout.share, layout.piece, layout.frames
     local = layout.local_modes
-    plus, minus, left_plus, left_minus = fourier_tables(length, cores)
+    forward, back, left_forward, left_back = fourier_tables(length, cores)
     helper = lax.axis_index("mode")
     core = helper % cores
 
@@ -468,23 +529,29 @@
     windows, intensity, kept, old_piece = call(
         functools.partial(far_kernel, layout),
         "far",
-        (scan_offsets, *strips, *probes, plus, minus),
+        (scan_offsets, *strips, *probes, forward, back),
         [
             (frames, 2, length, length),
             (frames, length, length),
-            (frames, local, length, 2 * length),
+            (frames, local, 2, length, length),
             (local, 2, piece, length),
         ],
         scratch=[(2, 2, cores, layout.strip, length)],
         scalar_count=1,
     )
+    (roots,) = call(
+        functools.partial(order_kernel, layout),
+        "order",
+        (measured, *measured_parts),
+        [measured.shape],
+        scratch=[(cores, layout.part, length)],
+    )
     intensities = [intensity] + [layout.from_core(intensity, step) for step in range(1, cores)]
     (pieces,) = call(
         functools.partial(gradient_kernel, layout),
         "gradient",
-        (*intensities, *measured_parts, windows, measured, kept, plus, minus),
+        (*intensities, roots, windows, kept, forward, back),
         [(regions, 1 + 2 * local, piece, length)],
-        scratch=[(cores, layout.part, length)],
     )
     pieces = layout.within_cube(pieces)
     (new_piece,) = call(
@@ -498,7 +565,6 @@
     gathered = layout.within_cube(spread)
     strip = (frames, 2, 2, halves, share, length)
     inner = (2, 2, halves, cores, share, length)
-    own_rows = lax.dynamic_slice_in_dim(object_bands, helper * share, share, 1)
     new_probes = [gathered] + [layout.from_core(gathered, step) for step in range(1, cores)]
     probe_out, probe_power, *shares = call(
         functools.partial(second_kernel, layout),
@@ -507,16 +573,15 @@
             scan_offsets,
             *new_probes,
             windows,
-            measured,
-            part_measured,
-            plus,
-            minus,
-            left_plus,
-            left_minus,
+            roots,
+            forward,
+            back,
+            left_forward,
+            left_back,
         ),
         [(2, local, length, length), (length, length)] + [strip] * cores,
         scratch=[
-            (layout.modes, layout.part, 2 * length),
+            (layout.modes, 2, layout.part, length),
             inner,
         ],
         scalar_count=1,
@@ -535,7 +600,7 @@
     (new_rows,) = call(
         functools.partial(update_kernel, layout),
         "update",
-        (scan_offsets, band_owner, posted, probe_power, own_rows),
+        (scan_offsets, band_owner, posted, probe_power, object_bands),
         [(2, share, layout.width)],
         scratch=[(2, length, length)],
         scalar_count=2,

time: 121 us -> 113 us (0.934)
  blocking collectives: 39.8 us -> 52.7 us
  waiting for transfers between devices: 36.6 us -> 26 us
  Pallas kernels: 21.4 us -> 14 us
  starting transfers between devices: 18.9 us -> 15.5 us
    all_to_all x2 -> x3, blocking collectives: 33.3 us -> 46.2 us  [within_cube(): lax.all_to_all(array, axes, split_axis=0, concat_axis=0, tiled=True, axis...]
    all_to_all x1 -> x0, waiting for transfers between devices: 10.5 us -> none  [within_cube(): lax.all_to_all(array, axes, split_axis=0, concat_axis=0, tiled=True, axis...]
    pallas_call x8 -> x9, Pallas kernels: 21.4 us -> 14 us  [call(): pl.pallas_call(inner, name=name, out_shape=shapes, in_specs=[scalars] * s...]
    all_to_all x1 -> x0, starting transfers between devices: 3.49 us -> none  [within_cube(): lax.all_to_all(array, axes, split_axis=0, concat_axis=0, tiled=True, axis...]
    unnamed x14 -> x18, local copies, waits for them, and re-layouts: 2.77 us -> 2.58 us
  transfers between devices with their start and end apart: 12 -> 11, of which waited for: 8 -> 7; matrix products, arithmetic and copies ran while one was open for 0% -> 0% of each run, Pallas kernels for 1% -> 1%
where the time goes in v3:
time: 113 us
  blocking collectives  52.7 us (47%)
  waiting for transfers between devices  26 us (23%)
  starting transfers between devices  15.5 us (14%)
  Pallas kernels  14 us (12%)
  local copies, waits for them, and re-layouts  3.7 us (3%)
    all_to_all x3, blocking collectives, within_cube(): lax.all_to_all(array, axes, split_axis=0, concat_axis=0, tiled=True, axis...  46.2 us
    ppermute x2, waiting for transfers between devices, from_upper(): return lax.ppermute(array, axes, pairs)  15.3 us
    pallas_call x9, Pallas kernels, call(): pl.pallas_call(inner, name=name, out_shape=shapes, in_specs=[scalars] * s...  14 us
    ppermute x6, waiting for transfers between devices, from_core(): return lax.ppermute(array, axes, pairs)  6.8 us
    all_gather x1, blocking collectives, body(): object_out = lax.all_gather(new_rows, 'mode', axis=1, tiled=True)  6.51 us
    all_to_all x1, starting transfers between devices, within_row(): lax.all_to_all(array, axes, split_axis=0, concat_axis=0, tiled=True, axis...  5.35 us
    ppermute x2, starting transfers between devices, from_upper(): return lax.ppermute(array, axes, pairs)  4.75 us
    ppermute x1, starting transfers between devices, body(): part_measured = lax.ppermute(part_measured, axes, pairs)  4.62 us
  transfers between devices with their start and end apart: 11, of which 7 were waited for; matrix products, arithmetic and copies ran while one was open for 0% of the time, Pallas kernels for 1%

profile of v3, /device:TPU:0, one launch (start us, length us, event | category | flops | bytes accessed | tf_op | source)
XLA Modules:
  0.0 112.7 jit_solution(18254897144222069488)
XLA Ops:
  1.4 1.0 constant_dynamic-slice_fusion.refs_2_
  2.4 1.8 %cut.1 = (f32[4,2,64,256]{3,2,1,0:T(8,128)}, f32[1,128,256]{2,1,0:T(8,128)S(1)}) custom-call(s32[8,2]{1,0:T(8,128)S(1)} %copy.14.refs_0_, s32[8]{0:T(128)S(1)} %copy-done.5, f32[2,64,512]{2,1,0:T(8,128)S(1)} %constant_dynamic-slice_fusion.refs_2_, f32[1,256,256]{2,1,0:T(8,128)S(1)} %copy-done.3), custom_call_target="tpu_custom_call" | custom-call | tf_op jit(solution)/shard_map/cut/pallas_call | solution.py:468
  4.2 5.4 %all-to-all-start = ((f32[4,2,64,256]{3,2,1,0:T(8,128)}), f32[4,2,64,256]{3,2,1,0:T(8,128)S(1)}, u32[]{:S(2)}, u32[]{:S(2)}) async-start(f32[4,2,64,256]{3,2,1,0:T(8,128)} %get-tuple-element.12), calls=%async_computation | async-start | bytes 1048576 | tf_op jit(solution)/shard_map/all_to_all | solution.py:91
  9.6 4.6 %collective-permute-start = (f32[1,128,256]{2,1,0:T(8,128)S(1)}, f32[1,128,256]{2,1,0:T(8,128)S(1)}, u32[]{:S(2)}, u32[]{:S(2)}) collective-permute-start(f32[1,128,256]{2,1,0:T(8,128)S(1)} %get-tuple-element.13), channel_id=1, source_target_pairs={{18,2},{19,3},{22,6},{23,7},{26,10},{27,11},{30,14},{31,15},{0,16}... | collective-permute-start | bytes 393224 | tf_op jit(solution)/shard_map/ppermute | solution.py:512
  14.3 3.9 %collective-permute-done.refs_3_.refs_1_ = f32[1,128,256]{2,1,0:T(8,128)S(1)} collective-permute-done((f32[1,128,256]{2,1,0:T(8,128)S(1)}, f32[1,128,256]{2,1,0:T(8,128)S(1)}, u32[]{:S(2)}, u32[]{:S(2)}) %collective-permute-start) | collective-permute-done | bytes 131104 | tf_op jit(solution)/shard_map/ppermute | solution.py:512
  18.9 3.5 %collective-permute-start.1 = (f32[1,2,2,64,256]{4,3,2,1,0:T(8,128)S(1)}, f32[1,2,2,64,256]{4,3,2,1,0:T(8,128)S(1)}, u32[]{:S(2)}, u32[]{:S(2)}) collective-permute-start(f32[1,2,2,64,256]{4,3,2,1,0:T(8,128)S(1)} %choose.1.refs_1_), channel_id=1, source_target_pairs={{16,0},{17,1},{18,2},{19,3},{20,4},{21,5},{22,6},{23,7},{24,8},{25... | collective-permute-start | bytes 786440 | tf_op jit(solution)/shard_map/ppermute | solution.py:68
  22.4 10.9 %collective-permute-done.1.refs_2_ = f32[1,2,2,64,256]{4,3,2,1,0:T(8,128)S(1)} collective-permute-done((f32[1,2,2,64,256]{4,3,2,1,0:T(8,128)S(1)}, f32[1,2,2,64,256]{4,3,2,1,0:T(8,128)S(1)}, u32[]{:S(2)}, u32[]{:S(2)}) %collective-permute-start.1) | collective-permute-done | bytes 262176 | tf_op jit(solution)/shard_map/ppermute | solution.py:68
  33.3 1.5 %collective-permute-done.3.refs_4_ = f32[1,2,2,64,256]{4,3,2,1,0:T(8,128)S(1)} collective-permute-done((f32[1,2,2,64,256]{4,3,2,1,0:T(8,128)S(1)}, f32[1,2,2,64,256]{4,3,2,1,0:T(8,128)S(1)}, u32[]{:S(2)}, u32[]{:S(2)}) %collective-permute-start.3) | collective-permute-done | bytes 262176 | tf_op jit(solution)/shard_map/ppermute | solution.py:75
  34.9 2.9 %far.1 = (f32[1,2,256,256]{3,2,1,0:T(8,128)S(1)}, f32[1,256,256]{2,1,0:T(8,128)S(1)}, f32[1,1,2,256,256]{4,3,2,1,0:T(8,128)S(1)}, f32[1,2,32,256]{3,2,1,0:T(8,128)S(1)}) custom-call(s32[8,2]{1,0:T(8,128)S(1)} %copy.14.refs_0_, f32[1,2,2,64,256]{4,3,2,1,0:T(8,128)S(1)} %choose.1.refs_1_, f32[1,2,2,64,256]{4,3,2,1,0:T(8,128)S(1)} %collective-permute-done.1.refs_2_, ...), custom_call_target="tpu_custom_call" | custom-call | tf_op jit(solution)/shard_map/far/pallas_call | solution.py:468
  38.3 1.2 %collective-permute-done.6.refs_2_ = f32[1,128,256]{2,1,0:T(8,128)S(1)} collective-permute-done((f32[1,128,256]{2,1,0:T(8,128)S(1)}, f32[1,128,256]{2,1,0:T(8,128)S(1)}, u32[]{:S(2)}, u32[]{:S(2)}) %collective-permute-start.6) | collective-permute-done | bytes 131104 | tf_op jit(solution)/shard_map/ppermute | solution.py:75
  39.5 0.7 order.1.refs_2_.refs_4_
  40.3 0.9 gradient.1
  41.2 17.6 %all_to_all.20.refs_0_ = f32[8,3,32,256]{3,2,1,0:T(8,128)S(1)} all-to-all(f32[8,3,32,256]{3,2,1,0:T(8,128)S(1)} %gradient.1), channel_id=1, replica_groups={{0,4,8,12,2,6,10,14},{1,5,9,13,3,7,11,15},{16,20,24,28,18,22,26,30},{17..., dimensions={0} | all-to-all | bytes 1572864 | tf_op jit(solution)/shard_map/all_to_all | solution.py:96
  58.8 1.2 %collective-permute-start.7 = (f32[1,2,32,256]{3,2,1,0:T(8,128)S(1)}, f32[1,2,32,256]{3,2,1,0:T(8,128)S(1)}, u32[]{:S(2)}, u32[]{:S(2)}) collective-permute-start(f32[1,2,32,256]{3,2,1,0:T(8,128)S(1)} %step.1), channel_id=1, source_target_pairs={{16,0},{17,1},{18,2},{19,3},{20,4},{21,5},{22,6},{23,7},{24,8},{25... | collective-permute-start | bytes 196616 | tf_op jit(solution)/shard_map/ppermute | solution.py:68
  60.0 4.3 %collective-permute-done.7 = f32[1,2,32,256]{3,2,1,0:T(8,128)S(1)} collective-permute-done((f32[1,2,32,256]{3,2,1,0:T(8,128)S(1)}, f32[1,2,32,256]{3,2,1,0:T(8,128)S(1)}, u32[]{:S(2)}, u32[]{:S(2)}) %collective-permute-start.7) | collective-permute-done | bytes 65568 | tf_op jit(solution)/shard_map/ppermute | solution.py:68
  64.5 15.7 %all_to_all.21.refs_1_ = f32[8,2,1,2,32,256]{5,4,3,2,1,0:T(8,128)S(1)} all-to-all(f32[8,2,1,2,32,256]{5,4,3,2,1,0:T(8,128)S(1)} %broadcast_in_dim.9), channel_id=1, replica_groups={{0,4,8,12,2,6,10,14},{1,5,9,13,3,7,11,15},{16,20,24,28,18,22,26,30},{17..., dimensions={0} | all-to-all | bytes 2097152 | tf_op jit(solution)/shard_map/all_to_all | solution.py:96
  80.2 2.7 %collective-permute-done.8.refs_2_ = f32[8,2,1,2,32,256]{5,4,3,2,1,0:T(8,128)S(1)} collective-permute-done((f32[8,2,1,2,32,256]{5,4,3,2,1,0:T(8,128)S(1)}, f32[8,2,1,2,32,256]{5,4,3,2,1,0:T(8,128)S(1)}, u32[]{:S(2)}, u32[]{:S(2)}) %collective-permute-start.8) | collective-permute-done | bytes 1048608 | tf_op jit(solution)/shard_map/ppermute | solution.py:75
  82.9 1.0 copy-done.6
  83.9 5.3 %second.1 = (f32[2,1,256,256]{3,2,1,0:T(8,128)}, f32[256,256]{1,0:T(8,128)S(1)}, f32[1,2,2,2,32,256]{5,4,3,2,1,0:T(8,128)S(1)}, f32[1,2,2,2,32,256]{5,4,3,2,1,0:T(8,128)S(1)}) custom-call(s32[8,2]{1,0:T(8,128)S(1)} %copy.14.refs_0_, f32[8,2,1,2,32,256]{5,4,3,2,1,0:T(8,128)S(1)} %all_to_all.21.refs_1_, f32[8,2,1,2,32,256]{5,4,3,2,1,0:T(8,128)} %copy-done.6, ...), custom_call_target="tpu_custom_call" | custom-call | tf_op jit(solution)/shard_map/second/pallas_call | solution.py:468
  89.4 1.4 %collective-permute-done.9.refs_3_ = f32[1,2,2,2,32,256]{5,4,3,2,1,0:T(8,128)S(1)} collective-permute-done((f32[1,2,2,2,32,256]{5,4,3,2,1,0:T(8,128)S(1)}, f32[1,2,2,2,32,256]{5,4,3,2,1,0:T(8,128)S(1)}, u32[]{:S(2)}, u32[]{:S(2)}) %collective-permute-start.9) | collective-permute-done | bytes 262176 | tf_op jit(solution)/shard_map/ppermute | solution.py:75
  91.5 12.9 %all_to_all.22.refs_2_ = f32[8,2,32,256]{3,2,1,0:T(8,128)S(1)} all-to-all(f32[8,2,32,256]{3,2,1,0:T(8,128)S(1)} %post.1), channel_id=1, replica_groups={{0,4,8,12,2,6,10,14},{1,5,9,13,3,7,11,15},{16,20,24,28,18,22,26,30},{17..., dimensions={0} | all-to-all | bytes 1048576 | tf_op jit(solution)/shard_map/all_to_all | solution.py:96
  104.4 1.0 update.1
  105.4 6.5 %all_gather.3 = f32[2,128,512]{2,1,0:T(8,128)S(1)} all-gather(f32[2,32,512]{2,1,0:T(8,128)S(1)} %update.1), channel_id=1, replica_groups=mesh['region'=8,'mode'=4] {'mode'}, dimensions={1}, use_global_device_ids=true | all-gather | bytes 655360 | tf_op jit(solution)/shard_map/all_gather | solution.py:608
  111.9 0.8 copy.18
  (32 shorter events, 3.1 us)
Async XLA Ops:
  0.6 0.7 copy-start.7
  1.4 1.0 copy-start.3
  1.4 1.0 copy-start.5
  4.2 10.0 %copy-start.4 = (f32[2,1,256,256]{3,2,1,0:T(8,128)S(1)}, f32[2,1,256,256]{3,2,1,0:T(8,128)}, u32[]{:S(2)}) copy-start(f32[2,1,256,256]{3,2,1,0:T(8,128)} %refs_5_.3) | copy-start | bytes 1572868
  4.2 14.0 %all-to-all-start = ((f32[4,2,64,256]{3,2,1,0:T(8,128)}), f32[4,2,64,256]{3,2,1,0:T(8,128)S(1)}, u32[]{:S(2)}, u32[]{:S(2)}) async-start(f32[4,2,64,256]{3,2,1,0:T(8,128)} %get-tuple-element.12), calls=%async_computation | async-start | bytes 1048576 | tf_op jit(solution)/shard_map/all_to_all | solution.py:91
  9.6 25.3 %copy-start.1 = (bf16[2,2,256,256]{3,2,1,0:T(8,128)(2,1)S(1)}, bf16[2,2,256,256]{3,2,1,0:T(8,128)(2,1)}, u32[]{:S(2)}) copy-start(bf16[2,2,256,256]{3,2,1,0:T(8,128)(2,1)} %constant.26.clone.refs_7_.refs_5_.refs_8_) | copy-start | bytes 1572868
  9.6 8.6 %collective-permute-start = (f32[1,128,256]{2,1,0:T(8,128)S(1)}, f32[1,128,256]{2,1,0:T(8,128)S(1)}, u32[]{:S(2)}, u32[]{:S(2)}) collective-permute-start(f32[1,128,256]{2,1,0:T(8,128)S(1)} %get-tuple-element.13), channel_id=1, source_target_pairs={{18,2},{19,3},{22,6},{23,7},{26,10},{27,11},{30,14},{31,15},{0,16}... | collective-permute-start | bytes 393224 | tf_op jit(solution)/shard_map/ppermute | solution.py:512
  14.2 19.1 %collective-permute-start.4 = (f32[2,1,256,256]{3,2,1,0:T(8,128)S(1)}, f32[2,1,256,256]{3,2,1,0:T(8,128)S(1)}, u32[]{:S(2)}, u32[]{:S(2)}) collective-permute-start(f32[2,1,256,256]{3,2,1,0:T(8,128)S(1)} %copy-done.4), channel_id=1, source_target_pairs={{2,0},{3,1},{0,2},{1,3},{6,4},{7,5},{4,6},{5,7},{10,8},{11,9},{8,1... | collective-permute-start | bytes 1572872 | tf_op jit(solution)/shard_map/ppermute | solution.py:82
  18.9 14.5 %collective-permute-start.1 = (f32[1,2,2,64,256]{4,3,2,1,0:T(8,128)S(1)}, f32[1,2,2,64,256]{4,3,2,1,0:T(8,128)S(1)}, u32[]{:S(2)}, u32[]{:S(2)}) collective-permute-start(f32[1,2,2,64,256]{4,3,2,1,0:T(8,128)S(1)} %choose.1.refs_1_), channel_id=1, source_target_pairs={{16,0},{17,1},{18,2},{19,3},{20,4},{21,5},{22,6},{23,7},{24,8},{25... | collective-permute-start | bytes 786440 | tf_op jit(solution)/shard_map/ppermute | solution.py:68
  22.4 11.0 %collective-permute-start.2 = (f32[1,2,2,64,256]{4,3,2,1,0:T(8,128)S(1)}, f32[1,2,2,64,256]{4,3,2,1,0:T(8,128)S(1)}, u32[]{:S(2)}, u32[]{:S(2)}) collective-permute-start(f32[1,2,2,64,256]{4,3,2,1,0:T(8,128)S(1)} %choose.1.refs_1_), channel_id=1, source_target_pairs={{1,0},{0,1},{3,2},{2,3},{5,4},{4,5},{7,6},{6,7},{9,8},{8,9},{11,10... | collective-permute-start | bytes 786440 | tf_op jit(solution)/shard_map/ppermute | solution.py:75
  33.3 1.5 %collective-permute-start.3 = (f32[1,2,2,64,256]{4,3,2,1,0:T(8,128)S(1)}, f32[1,2,2,64,256]{4,3,2,1,0:T(8,128)S(1)}, u32[]{:S(2)}, u32[]{:S(2)}) collective-permute-start(f32[1,2,2,64,256]{4,3,2,1,0:T(8,128)S(1)} %collective-permute-done.1.refs_2_), channel_id=1, source_target_pairs={{1,0},{0,1},{3,2},{2,3},{5,4},{4,5},{7,6},{6,7},{9,8},{8,9},{11,10... | collective-permute-start | bytes 786440 | tf_op jit(solution)/shard_map/ppermute | solution.py:75
  37.7 2.5 %copy-start = (bf16[2,2,256,256]{3,2,1,0:T(8,128)(2,1)S(1)}, bf16[2,2,256,256]{3,2,1,0:T(8,128)(2,1)}, u32[]{:S(2)}) copy-start(bf16[2,2,256,256]{3,2,1,0:T(8,128)(2,1)} %constant.27.clone.refs_8_.refs_6_.refs_7_) | copy-start | bytes 1572868
  37.8 2.5 %collective-permute-start.5 = (f32[1,256,256]{2,1,0:T(8,128)S(1)}, f32[1,256,256]{2,1,0:T(8,128)S(1)}, u32[]{:S(2)}, u32[]{:S(2)}) collective-permute-start(f32[1,256,256]{2,1,0:T(8,128)S(1)} %get-tuple-element.14.refs_0_), channel_id=1, source_target_pairs={{1,0},{0,1},{3,2},{2,3},{5,4},{4,5},{7,6},{6,7},{9,8},{8,9},{11,10... | collective-permute-start | bytes 786440 | tf_op jit(solution)/shard_map/ppermute | solution.py:75
  38.0 1.6 %collective-permute-start.6 = (f32[1,128,256]{2,1,0:T(8,128)S(1)}, f32[1,128,256]{2,1,0:T(8,128)S(1)}, u32[]{:S(2)}, u32[]{:S(2)}) collective-permute-start(f32[1,128,256]{2,1,0:T(8,128)S(1)} %collective-permute-done.refs_3_.refs_1_), channel_id=1, source_target_pairs={{1,0},{0,1},{3,2},{2,3},{5,4},{4,5},{7,6},{6,7},{9,8},{8,9},{11,10... | collective-permute-start | bytes 393224 | tf_op jit(solution)/shard_map/ppermute | solution.py:75
  58.8 5.6 %collective-permute-start.7 = (f32[1,2,32,256]{3,2,1,0:T(8,128)S(1)}, f32[1,2,32,256]{3,2,1,0:T(8,128)S(1)}, u32[]{:S(2)}, u32[]{:S(2)}) collective-permute-start(f32[1,2,32,256]{3,2,1,0:T(8,128)S(1)} %step.1), channel_id=1, source_target_pairs={{16,0},{17,1},{18,2},{19,3},{20,4},{21,5},{22,6},{23,7},{24,8},{25... | collective-permute-start | bytes 196616 | tf_op jit(solution)/shard_map/ppermute | solution.py:68
  80.2 2.7 %collective-permute-start.8 = (f32[8,2,1,2,32,256]{5,4,3,2,1,0:T(8,128)S(1)}, f32[8,2,1,2,32,256]{5,4,3,2,1,0:T(8,128)S(1)}, u32[]{:S(2)}, u32[]{:S(2)}) collective-permute-start(f32[8,2,1,2,32,256]{5,4,3,2,1,0:T(8,128)S(1)} %all_to_all.21.refs_1_), channel_id=1, source_target_pairs={{1,0},{0,1},{3,2},{2,3},{5,4},{4,5},{7,6},{6,7},{9,8},{8,9},{11,10... | collective-permute-start | bytes 3145736 | tf_op jit(solution)/shard_map/ppermute | solution.py:75
  82.9 1.0 copy-start.6
  89.2 1.5 %collective-permute-start.9 = (f32[1,2,2,2,32,256]{5,4,3,2,1,0:T(8,128)S(1)}, f32[1,2,2,2,32,256]{5,4,3,2,1,0:T(8,128)S(1)}, u32[]{:S(2)}, u32[]{:S(2)}) collective-permute-start(f32[1,2,2,2,32,256]{5,4,3,2,1,0:T(8,128)S(1)} %get-tuple-element.20), channel_id=1, source_target_pairs={{1,0},{0,1},{3,2},{2,3},{5,4},{4,5},{7,6},{6,7},{9,8},{8,9},{11,10... | collective-permute-start | bytes 786440 | tf_op jit(solution)/shard_map/ppermute | solution.py:75
  91.5 12.9 %copy-start.2 = (f32[2,128,512]{2,1,0:T(8,128)S(1)}, f32[2,128,512]{2,1,0:T(8,128)}, u32[]{:S(2)}) copy-start(f32[2,128,512]{2,1,0:T(8,128)} %refs_4_.1) | copy-start | bytes 1572868

commit v4 on v3

v4 whole, which is shorter than its diff:
```python
import functools
import math

import jax
import jax.numpy as jnp
import ml_dtypes
import numpy as np
from jax import lax
from jax.experimental import pallas as pl
from jax.experimental.pallas import tpu as pltpu
from jax.sharding import PartitionSpec as P

intensity_offset = 0.1
probe_damping = 1.0
object_damping = 1.0
half = jnp.bfloat16
single = jnp.float32
axes = ("region", "mode")
lanes = 128
on_chip = pl.BlockSpec(memory_space=pltpu.VMEM)
scalars = pl.BlockSpec(memory_space=pltpu.SMEM)


class Layout:
    def __init__(self, regions, helpers, length, frames, modes, width):
        self.regions, self.helpers = regions, helpers
        self.length, self.frames, self.modes, self.width = length, frames, modes, width
        self.halves = 2 if regions % 2 == 0 and helpers % 2 == 0 else 1
        self.lowers, self.cores = regions // self.halves, helpers // self.halves
        self.local_modes = modes // helpers
        self.band = length // 2
        self.strip = self.band // self.cores
        self.share = self.band // helpers
        self.piece = length // regions
        self.part = length // self.cores

    def place(self):
        region, helper = lax.axis_index("region"), lax.axis_index("mode")
        upper, lower = region // self.lowers, region % self.lowers
        twin, core = helper // self.cores, helper % self.cores
        return upper, lower, twin, core

    def device(self, upper, lower, twin, core):
        return (upper * self.lowers + lower) * self.helpers + twin * self.cores + core

    def everyone(self):
        for upper in range(self.halves):
            for lower in range(self.lowers):
                for twin in range(self.halves):
                    for core in range(self.cores):
                        yield upper, lower, twin, core

    def cubes(self):
        return [
            [
                self.device(upper, lower, twin, core)
                for twin in range(self.halves)
                for lower in range(self.lowers)
            ]
            for upper in range(self.halves)
            for core in range(self.cores)
        ]

    def from_upper(self, array, step):
        pairs = [
            (self.device((u + step) % self.halves, l, t, c), self.device(u, l, t, c))
            for u, l, t, c in self.everyone()
        ]
        return lax.ppermute(array, axes, pairs)

    def from_core(self, array, step):
        pairs = [
            (self.device(u, l, t, (c + step) % self.cores), self.device(u, l, t, c))
            for u, l, t, c in self.everyone()
        ]
        return lax.ppermute(array, axes, pairs)

    def from_twin(self, array, step):
        pairs = [
            (self.device(u, l, (t + step) % self.halves, c), self.device(u, l, t, c))
            for u, l, t, c in self.everyone()
        ]
        return lax.ppermute(array, axes, pairs)

    def across(self, lower, step):
        if self.lowers & (self.lowers - 1) == 0:
            return lower ^ step
        return (lower + step) % self.lowers

    def to_row(self, array, step):
        pairs = [
            (self.device(u, l, t, c), self.device(u, self.across(l, step), t, c))
            for u, l, t, c in self.everyone()
        ]
        return lax.ppermute(array, axes, pairs)

    def within_cube(self, array):
        return lax.all_to_all(
            array, axes, split_axis=0, concat_axis=0, tiled=True, axis_index_groups=self.cubes()
        )


def fourier_tables(length):
    near = np.arange(length // 2)
    forms = []
    for odd in range(2):
        angles = near[:, None] * (2 * near[None, :] + odd) % length * (2.0 * math.pi / length)
        cosine, sine = np.cos(angles) / math.sqrt(length), np.sin(angles) / math.sqrt(length)
        forms.append(np.block([[cosine, -sine], [sine, cosine]]))
    forward = np.stack(forms)

    def pair(table):
        lead = table.astype(ml_dtypes.bfloat16)
        return np.stack([lead, (table - lead.astype(np.float64)).astype(ml_dtypes.bfloat16)])

    return pair(forward), pair(forward.swapaxes(1, 2))


def split(values):
    lead = values.astype(half)
    return lead, (values - lead.astype(single)).astype(half)


def dot(left, right):
    return jnp.dot(left, right, preferred_element_type=single)


def from_left(table, values):
    lead, trail = split(values)
    return dot(table[0], lead) + dot(table[1], lead) + dot(table[0], trail)


def from_right(values, table):
    lead, trail = split(values)
    return dot(lead, table[0]) + dot(lead, table[1]) + dot(trail, table[0])


def beside(left, right):
    return jnp.concatenate([left, right], axis=1)


def above(top, bottom):
    return jnp.concatenate([top, bottom], axis=0)


def table_of(tables, number):
    return tables[0, number], tables[1, number]


def columns_forward(real, imag, forward):
    middle = real.shape[1] // 2
    real_left, real_right = real[:, :middle], real[:, middle:]
    imag_left, imag_right = imag[:, :middle], imag[:, middle:]
    even = from_right(beside(real_left + real_right, imag_left + imag_right), table_of(forward, 0))
    odd = from_right(beside(real_left - real_right, imag_left - imag_right), table_of(forward, 1))
    return (
        beside(even[:, :middle], odd[:, :middle]),
        beside(even[:, middle:], odd[:, middle:]),
    )


def columns_back(real, imag, back):
    middle = real.shape[1] // 2
    even = from_right(beside(real[:, :middle], imag[:, :middle]), table_of(back, 0))
    odd = from_right(beside(real[:, middle:], imag[:, middle:]), table_of(back, 1))
    plus, minus = even + odd, even - odd
    return (
        beside(plus[:, :middle], minus[:, :middle]),
        beside(plus[:, middle:], minus[:, middle:]),
    )


def rows_forward(real, imag, back):
    middle = real.shape[0] // 2
    real_top, real_bottom = real[:middle], real[middle:]
    imag_top, imag_bottom = imag[:middle], imag[middle:]
    even = from_left(table_of(back, 0), above(real_top + real_bottom, imag_top + imag_bottom))
    odd = from_left(table_of(back, 1), above(real_top - real_bottom, imag_top - imag_bottom))
    return above(even[:middle], odd[:middle]), above(even[middle:], odd[middle:])


def rows_back(real, imag, forward):
    middle = real.shape[0] // 2
    even = from_left(table_of(forward, 0), above(real[:middle], imag[:middle]))
    odd = from_left(table_of(forward, 1), above(real[middle:], imag[middle:]))
    plus, minus = even + odd, even - odd
    return above(plus[:middle], minus[:middle]), above(plus[middle:], minus[middle:])


def band_of_block(owner, block, layout):
    band = jnp.int32(0)
    for candidate in range(layout.regions):
        band = jnp.where(owner[candidate] == block, candidate, band)
    return band


def frame_over(offsets, region, band, layout):
    row, column = offsets[0, region * layout.frames], offsets[1, region * layout.frames]
    for extra in range(1, layout.frames):
        index = region * layout.frames + extra
        anchor = offsets[0, index] // layout.band
        over = (anchor <= band) & (band <= anchor + 2)
        row = jnp.where(over, offsets[0, index], row)
        column = jnp.where(over, offsets[1, index], column)
    return row, column


def cut_kernel(layout, corners, owners, block, measured, *refs):
    outs, (sent, taken, offsets, owner, done) = refs[: layout.lowers], refs[layout.lowers :]
    upper, lower, twin, core = layout.place()
    strip = pl.ds(pl.multiple_of(core * layout.strip, layout.strip), layout.strip)
    part = pl.ds(pl.multiple_of(core * layout.part, layout.part), layout.part)
    copies = [
        pltpu.make_async_copy(corners, offsets, done.at[0]),
        pltpu.make_async_copy(owners, owner, done.at[1]),
        pltpu.make_async_copy(block.at[:, strip, :], taken.at[:, :, : layout.width], done.at[2]),
        pltpu.make_async_copy(measured.at[:, part, :], sent, done.at[3]),
    ]
    for copy in copies:
        copy.start()
    for copy in copies[:3]:
        copy.wait()
    band = band_of_block(owner, upper * layout.lowers + lower, layout)
    tiles = layout.length // lanes
    column_in_tile = lax.broadcasted_iota(jnp.int32, (2 * layout.strip, lanes), 1)
    for step, out in enumerate(outs):
        region = twin * layout.lowers + layout.across(lower, step)
        _, column = frame_over(offsets, region, band, layout)
        shift = column % lanes
        begin = pl.multiple_of(column - shift, lanes)
        kept = column_in_tile < lanes - shift
        turned = []
        for tile in range(tiles + 1):
            values = taken[:, :, pl.ds(begin + tile * lanes, lanes)].reshape(2 * layout.strip, lanes)
            turned.append(pltpu.roll(values, (lanes - shift) % lanes, 1))
        for tile in range(tiles):
            values = jnp.where(kept, turned[tile], turned[tile + 1])
            out[:, :, tile * lanes : (tile + 1) * lanes] = values.reshape(2, layout.strip, lanes)
    copies[3].wait()


def choose_kernel(layout, steps, offsets, owner, *refs):
    arrived, (*before, out) = refs[: len(steps)], refs[len(steps) :]
    upper, lower, twin, core = layout.place()
    rows = lax.broadcasted_iota(jnp.int32, (layout.strip, layout.length), 0) + core * layout.strip
    for frame in range(layout.frames):
        row = offsets[0, (twin * layout.lowers + lower) * layout.frames + frame]
        anchor = row // layout.band
        lead = row - anchor * layout.band
        blocks = [owner[anchor + step] for step in range(3)]
        masks = [rows >= lead, rows >= 0, rows < lead]
        for plane in range(2):
            slots = [ref[frame, plane] for ref in before]
            top, bottom = (slots[0][0], slots[0][1]) if before else (0.0, 0.0)
            for block, mask, slot in zip(blocks, masks, (0, 1, 0)):
                here = block // layout.lowers == upper
                values = top if slot == 0 else bottom
                for step, ref in zip(steps, arrived):
                    came = here & (layout.across(block % layout.lowers, step) == lower)
                    values = jnp.where(mask & came, ref[plane], values)
                top, bottom = (values, bottom) if slot == 0 else (top, values)
            out[frame, plane, 0] = top
            out[frame, plane, 1] = bottom


def leave(probe_real, probe_imag, window_real, window_imag, forward, back):
    wave = rows_forward(
        probe_real * window_real - probe_imag * window_imag,
        probe_real * window_imag + probe_imag * window_real,
        back,
    )
    return columns_forward(*wave, forward)


def come_back(far, factor, forward, back):
    return rows_back(*columns_back(far[0] * factor, far[1] * factor, back), forward)


def far_kernel(layout, offsets, *refs):
    cores, halves, frames, length = layout.cores, layout.halves, layout.frames, layout.length
    shares, probes = refs[: cores * halves], refs[cores * halves : (cores + 1) * halves]
    forward, back, windows, intensity, kept, old_pieces, inner = refs[(cores + 1) * halves :]
    upper, lower, twin, core = layout.place()
    region = twin * layout.lowers + lower
    rows = pl.ds(pl.multiple_of(region * layout.piece, layout.piece), layout.piece)
    for entry, probe in enumerate(probes):
        place = (twin + entry + halves - upper) % halves
        for local in range(layout.local_modes):
            for plane in range(2):
                old_pieces[place, local, plane] = probe[plane, local, rows, :]
    for frame in range(frames):
        lead = offsets[0, region * frames + frame] % layout.band
        for step in range(cores):
            strip = shares[step * halves][frame]
            for entry in range(1, halves):
                strip += shares[step * halves + entry][frame]
            inner[:, :, (core + step) % cores] = strip
        for plane in range(2):
            wrapped = inner[plane].reshape(length, length)
            windows[frame, plane] = pltpu.roll(wrapped, (length - lead) % length, 0)
        window = windows[frame, 0], windows[frame, 1]
        total = jnp.zeros((length, length), single)
        for entry, probe in enumerate(probes):
            for local in range(layout.local_modes):
                wave_real, wave_imag = leave(probe[0, local], probe[1, local], *window, forward, back)
                total += wave_real**2 + wave_imag**2

                @pl.when((twin + entry) % halves == upper)
                def _():
                    kept[frame, local, 0] = wave_real
                    kept[frame, local, 1] = wave_imag

        intensity[frame] = total


def order_kernel(layout, own_measured, *refs):
    parts, (out, other_measured) = refs[: layout.cores], refs[layout.cores :]
    upper, _, twin, core = layout.place()
    length = layout.length
    rows = lax.broadcasted_iota(jnp.int32, (length, length), 0)
    columns = lax.broadcasted_iota(jnp.int32, (length, length), 1)
    middle = length // 2
    pick_rows = (columns == jnp.where(rows < middle, 2 * rows, 2 * (rows - middle) + 1)).astype(half)
    pick_columns = (rows == jnp.where(columns < middle, 2 * columns, 2 * (columns - middle) + 1)).astype(half)

    def exact(product, values):
        lead, rest = split(values)
        trail = (values - lead.astype(single) - rest.astype(single)).astype(half)
        return (product(lead) + product(rest)) + product(trail)

    for frame in range(layout.frames):
        for step, part in enumerate(parts):
            other_measured[(core + step) % layout.cores] = part[frame]
        measured = other_measured[...].reshape(length, length)
        measured = jnp.sqrt(jnp.where(upper == twin, own_measured[frame], measured))
        measured = exact(lambda values: dot(pick_rows, values), measured)
        out[frame] = exact(lambda values: dot(values, pick_columns), measured)


def factor_of(root, intensities, frame):
    total = intensities[0][frame]
    for more in intensities[1:]:
        total += more[frame]
    return root[frame] / jnp.sqrt(total + intensity_offset) - 1.0


def gradient_kernel(layout, *refs):
    cores, frames, length, piece = layout.cores, layout.frames, layout.length, layout.piece
    intensities, (roots, windows, kept, forward, back, pieces) = refs[:cores], refs[cores:]
    upper, _, _, _ = layout.place()
    cut = (layout.regions, piece, length)
    part = piece // layout.halves
    for frame in range(frames):
        window_real, window_imag = windows[frame, 0], windows[frame, 1]
        factor = factor_of(roots, intensities, frame)
        channels = []
        for local in range(layout.local_modes):
            change_real, change_imag = come_back(kept[frame, local], factor, forward, back)
            channels.append(window_real * change_real + window_imag * change_imag)
            channels.append(window_real * change_imag - window_imag * change_real)
        channels = [values.reshape(cut) for values in channels]
        power = (window_real**2 + window_imag**2).reshape(cut)
        sent = power[:, :part]
        for other in range(1, layout.halves):
            sent = jnp.where(upper == other, power[:, other * part : (other + 1) * part], sent)
        first = 0
        for values in (*channels, sent):
            rows = slice(first, first + values.shape[1])
            if frame == 0:
                pieces[:, rows] = values
            else:
                pieces[:, rows] += values
            first += values.shape[1]


def sum_kernel(arrived, total):
    total[...] = jnp.sum(arrived[...], axis=0)


def step_kernel(layout, old_pieces, *refs):
    totals, out = refs[:-1], refs[-1]
    upper, _, _, _ = layout.place()
    halves, piece = layout.halves, layout.piece
    planes = 2 * layout.local_modes
    parts = []
    for place in range(halves):
        power = totals[0][planes * piece :]
        for entry in range(1, halves):
            power = jnp.where((upper + entry) % halves == place, totals[entry][planes * piece :], power)
        parts.append(power)
    damped = jnp.concatenate(parts, axis=0) + probe_damping
    for entry, total in enumerate(totals):
        for local in range(layout.local_modes):
            for plane in range(2):
                first = (2 * local + plane) * piece
                stepped = old_pieces[entry, local, plane] + total[first : first + piece] / damped
                for region in range(layout.regions):
                    out[region, entry, local, plane] = stepped


def new_probe(probes, entry, local, plane):
    values = probes[:, entry, local, plane]
    return values.reshape(values.shape[0] * values.shape[1], values.shape[2])


def again_kernel(layout, probes, windows, forward, back, probe_out, probe_power, intensity, fars):
    upper, _, twin, _ = layout.place()
    own_entry = (twin + layout.halves - upper) % layout.halves
    power = jnp.zeros((layout.length, layout.length), single)
    totals = [jnp.zeros((layout.length, layout.length), single) for _ in range(layout.frames)]
    for entry in range(layout.halves):
        for local in range(layout.local_modes):
            probe = [new_probe(probes, entry, local, plane) for plane in range(2)]
            power += probe[0] ** 2 + probe[1] ** 2
            for frame in range(layout.frames):
                wave_real, wave_imag = leave(*probe, windows[frame, 0], windows[frame, 1], forward, back)
                totals[frame] += wave_real**2 + wave_imag**2
                fars[frame, entry, local, 0] = wave_real
                fars[frame, entry, local, 1] = wave_imag
    probe_power[...] = power
    for frame, total in enumerate(totals):
        intensity[frame] = total
    for local in range(layout.local_modes):
        for plane in range(2):
            probe_out[plane, local] = new_probe(probes, own_entry, local, plane)


def terms_kernel(layout, offsets, *refs):
    cores, halves, frames, length = layout.cores, layout.halves, layout.frames, layout.length
    intensities = refs[:cores]
    roots, probes, fars, forward, back, *shares, inner = refs[cores:]
    upper, lower, twin, core = layout.place()
    region = twin * layout.lowers + lower
    for frame in range(frames):
        factor = factor_of(roots, intensities, frame)
        numer_real = jnp.zeros((length, length), single)
        numer_imag = jnp.zeros((length, length), single)
        for entry in range(halves):
            for local in range(layout.local_modes):
                change_real, change_imag = come_back(fars[frame, entry, local], factor, forward, back)
                probe_real, probe_imag = (new_probe(probes, entry, local, plane) for plane in range(2))
                numer_real += probe_real * change_real + probe_imag * change_imag
                numer_imag += probe_real * change_imag - probe_imag * change_real
        lead = offsets[0, region * frames + frame] % layout.band
        for plane, values in enumerate((numer_real, numer_imag)):
            turned = pltpu.roll(values, lead, 0)
            inner[plane] = turned.reshape(2, halves, cores, layout.share, length)
        for step, share in enumerate(shares):
            share[frame] = inner[:, :, :, (core + cores - step) % cores]


def post_kernel(layout, offsets, owner, *refs):
    shares, out = refs[:-1], refs[-1]
    upper, lower, twin, _ = layout.place()
    region = twin * layout.lowers + lower
    for low in range(layout.lowers):
        band = band_of_block(owner, upper * layout.lowers + low, layout)
        frame, row = jnp.int32(0), offsets[0, region * layout.frames]
        for extra in range(1, layout.frames):
            candidate = offsets[0, region * layout.frames + extra]
            anchor = candidate // layout.band
            over = (anchor <= band) & (band <= anchor + 2)
            frame, row = jnp.where(over, extra, frame), jnp.where(over, candidate, row)
        slot = (band - row // layout.band == 1).astype(jnp.int32)
        for target in range(layout.halves):
            for plane in range(2):
                total = shares[0][frame, plane, slot, target]
                for share in shares[1:]:
                    total += share[frame, plane, slot, target]
                out[target * layout.lowers + low, plane] = total


def update_kernel(layout, offsets, owner, arrived, block, *refs):
    powers, (rows_out, doubled, total) = refs[: layout.cores], refs[layout.cores :]
    upper, lower, twin, core = layout.place()
    length, share = layout.length, layout.share
    band = band_of_block(owner, upper * layout.lowers + lower, layout)
    first = (twin * layout.cores + core) * share
    rows = lax.broadcasted_iota(jnp.int32, (share, length), 0) + first
    power = powers[0][...]
    for more in powers[1:]:
        power += more[...]
    doubled[0] = power
    doubled[1] = power
    wide = doubled.reshape(2 * length, length)
    tiles = length // lanes
    column_in_tile = lax.broadcasted_iota(jnp.int32, (3 * share, lanes), 1)
    total[...] = jnp.zeros_like(total)
    for region in range(layout.regions):
        row, column = frame_over(offsets, region, band, layout)
        anchor = row // layout.band
        lead = row - anchor * layout.band
        step = band - anchor
        begin = jnp.where(step == 0, lead, jnp.where((step == 1) | (step == 2), 0, layout.band))
        end = jnp.where(step == 2, lead, layout.band)
        inside = (rows >= begin) & (rows < end)
        slot = (step == 1).astype(jnp.int32)
        start = (slot * layout.band + first + length - lead) % length
        near = wide[pl.ds(pl.multiple_of(start // 8 * 8, 8), share + 8), :]
        near = pltpu.roll(near, (share + 8 - start % 8) % (share + 8), 0)[:share]
        terms = jnp.concatenate([arrived[region, 0], arrived[region, 1], near], axis=0)
        terms = jnp.where(jnp.concatenate([inside] * 3, axis=0), terms, 0.0)
        shift = column % lanes
        begin = pl.multiple_of(column - shift, lanes)
        spilled = column_in_tile < shift
        turned = [
            pltpu.roll(terms[:, tile * lanes : (tile + 1) * lanes], shift, 1) for tile in range(tiles)
        ]
        for tile in range(tiles + 1):
            first_part = turned[tile] if tile < tiles else 0.0
            second_part = turned[tile - 1] if tile else 0.0
            total[:, pl.ds(begin + tile * lanes, lanes)] += jnp.where(spilled, second_part, first_part)
    damped = total[2 * share :, : layout.width] + object_damping
    for plane in range(2):
        old = block[plane, pl.ds(pl.multiple_of(first, share), share), :]
        rows_out[plane] = old + total[plane * share : (plane + 1) * share, : layout.width] / damped


def call(kernel, name, operands, outputs, scratch=(), scalar_count=0, after=()):
    shapes = [jax.ShapeDtypeStruct(shape, single) for shape in outputs]
    count = len(operands)

    def inner(*refs):
        kernel(*refs[:count], *refs[count + len(after) :])

    return pl.pallas_call(
        inner,
        name=name,
        out_shape=shapes,
        in_specs=[scalars] * scalar_count
        + [on_chip] * (count - scalar_count)
        + [pl.BlockSpec(memory_space=pl.ANY)] * len(after),
        out_specs=[on_chip] * len(shapes),
        scratch_shapes=[pltpu.VMEM(shape, single) for shape in scratch],
        compiler_params=pltpu.CompilerParams(vmem_limit_bytes=28 * 2**20),
    )(*operands, *after)


def body(measured, probe_modes, object_bands, scan_offsets, band_owner):
    layout = Layout(
        lax.axis_size("region"),
        lax.axis_size("mode"),
        measured.shape[1],
        measured.shape[0],
        probe_modes.shape[1] * lax.axis_size("mode"),
        object_bands.shape[2],
    )
    regions, halves, cores = layout.regions, layout.halves, layout.cores
    length, piece, frames = layout.length, layout.piece, layout.frames
    local, strip, share = layout.local_modes, layout.strip, layout.share
    forward, back = fourier_tables(length)
    corners = scan_offsets.T

    def from_cores(array):
        return [array] + [layout.from_core(array, step) for step in range(1, cores)]

    def from_uppers(array):
        return [array] + [layout.from_upper(array, step) for step in range(1, halves)]

    *cuts, part_measured = pl.pallas_call(
        functools.partial(cut_kernel, layout),
        name="cut",
        out_shape=[jax.ShapeDtypeStruct((2, strip, length), single)] * layout.lowers
        + [jax.ShapeDtypeStruct((frames, layout.part, length), single)],
        in_specs=[pl.BlockSpec(memory_space=pltpu.HBM)] * 4,
        out_specs=[on_chip] * (layout.lowers + 1),
        scratch_shapes=[
            pltpu.VMEM((2, strip, layout.width + lanes), single),
            pltpu.SMEM(corners.shape, jnp.int32),
            pltpu.SMEM(band_owner.shape, jnp.int32),
            pltpu.SemaphoreType.DMA((4,)),
        ],
        compiler_params=pltpu.CompilerParams(vmem_limit_bytes=60 * 2**20),
    )(corners, band_owner, object_bands, measured)
    probes = [probe_modes] + [layout.from_twin(probe_modes, step) for step in range(1, halves)]
    if halves > 1:
        pairs = [
            (layout.device(t, l, t, c), layout.device(u, l, t, c))
            for u, l, t, c in layout.everyone()
            if u != t
        ]
        part_measured = lax.ppermute(part_measured, axes, pairs)
    cuts = [cuts[0]] + [layout.to_row(cut, step) for step, cut in enumerate(cuts[1:], start=1)]
    chosen = []
    for steps in ((0,), tuple(range(1, layout.lowers))):
        chosen = call(
            functools.partial(choose_kernel, layout, steps),
            "choose",
            (corners, band_owner, *(cuts[step] for step in steps), *chosen),
            [(frames, 2, 2, strip, length)],
            scalar_count=2,
        )
    (chosen,) = chosen
    measured_parts = from_cores(part_measured)
    (roots,) = call(
        functools.partial(order_kernel, layout),
        "order",
        (measured, *measured_parts),
        [measured.shape],
        scratch=[(cores, layout.part, length)],
    )
    parts = from_uppers(chosen)
    held, roots, *received = lax.optimization_barrier((chosen, roots, *probes[1:]))
    probes = [probe_modes, *received]
    strips = list(parts)
    for step in range(1, cores):
        strips += [layout.from_core(part, step) for part in [held] + parts[1:]]
    windows, intensity, kept, old_pieces = call(
        functools.partial(far_kernel, layout),
        "far",
        (corners, *strips, *probes, forward, back),
        [
            (frames, 2, length, length),
            (frames, length, length),
            (frames, local, 2, length, length),
            (halves, local, 2, piece, length),
        ],
        scratch=[(2, 2, cores, strip, length)],
        scalar_count=1,
    )
    (pieces,) = call(
        functools.partial(gradient_kernel, layout),
        "gradient",
        (*from_cores(intensity), roots, windows, kept, forward, back),
        [(regions, 2 * local * piece + piece // halves, length)],
    )
    pieces = layout.within_cube(pieces)
    (total,) = call(sum_kernel, "sum", (pieces,), [pieces.shape[1:]])
    (spread,) = call(
        functools.partial(step_kernel, layout),
        "step",
        (old_pieces, *from_uppers(total)),
        [(regions, halves, local, 2, piece, length)],
    )
    new_probes = layout.within_cube(spread)
    probe_out, probe_power, intensity, fars = call(
        functools.partial(again_kernel, layout),
        "again",
        (new_probes, windows, forward, back),
        [
            (2, local, length, length),
            (length, length),
            (frames, length, length),
            (frames, halves, local, 2, length, length),
        ],
    )
    shares = call(
        functools.partial(terms_kernel, layout),
        "terms",
        (corners, *from_cores(intensity), roots, new_probes, fars, forward, back),
        [(frames, 2, 2, halves, share, length)] * cores,
        scratch=[(2, 2, halves, cores, share, length)],
        scalar_count=1,
    )
    shares = [shares[0]] + [
        layout.from_core(sent, step) for step, sent in enumerate(shares[1:], start=1)
    ]
    powers = from_cores(probe_power)
    (posted,) = call(
        functools.partial(post_kernel, layout),
        "post",
        (corners, band_owner, *shares),
        [(regions, 2, share, length)],
        scalar_count=2,
        after=powers,
    )
    posted = layout.within_cube(posted)
    (new_rows,) = call(
        functools.partial(update_kernel, layout),
        "update",
        (corners, band_owner, posted, object_bands, *powers),
        [(2, share, layout.width)],
        scratch=[(2, length, length), (3 * share, layout.width + lanes)],
        scalar_count=2,
    )
    object_out = lax.all_gather(new_rows, "mode", axis=1, tiled=True)
    return probe_out, object_out


def solution(mesh):
    in_specs = (
        P("region", None, None),
        P(None, "mode", None, None),
        P(None, "region", None),
        P(),
        P(),
    )
    out_specs = (P(None, "mode", None, None), P(None, "region", None))
    return jax.shard_map(body, mesh=mesh, in_specs=in_specs, out_specs=out_specs, check_vma=False)
```

time: 113 us -> 104 us (0.920)
  waiting for transfers between devices: 26 us -> 18.7 us
  starting transfers between devices: 15.5 us -> 18.3 us
  local copies, waits for them, and re-layouts: 3.7 us -> 1.73 us
  blocking collectives: 52.7 us -> 51 us
    all_to_all x1 -> x0, starting transfers between devices: 5.35 us -> none  [within_row(): lax.all_to_all(array, axes, split_axis=0, concat_axis=0, tiled=True, axis...]
    ppermute x1, waiting for transfers between devices: 3.91 us -> 0.01 us  [body(): part_measured = lax.ppermute(part_measured, axes, pairs)]
    ppermute x0 -> x3, starting transfers between devices: none -> 3.55 us  [to_row(): return lax.ppermute(array, axes, pairs)]
    ppermute x2, waiting for transfers between devices: 15.3 us -> 12.1 us  [from_upper(): return lax.ppermute(array, axes, pairs)]
    ppermute x1, starting transfers between devices: 0.07 us -> 3.03 us  [from_twin(): return lax.ppermute(array, axes, pairs)]
    pallas_call x9 -> x11, Pallas kernels: 14 us -> 11.6 us  [call(): pl.pallas_call(inner, name=name, out_shape=shapes, in_specs=[scalars] * s...]
    pallas_call x0 -> x1, Pallas kernels: none -> 2.08 us  [body(): pl.pallas_call(functools.partial(cut_kernel, layout), name='cut', out_sha...]
    all_to_all x3, blocking collectives: 46.2 us -> 44.5 us  [within_cube(): lax.all_to_all(array, axes, split_axis=0, concat_axis=0, tiled=True, axis...]
  transfers between devices with their start and end apart: 11 -> 14, of which waited for: 7 -> 8; matrix products, arithmetic and copies ran while one was open for 0% -> 0% of each run, Pallas kernels for 1% -> 6%
where the time goes in v4:
time: 104 us
  blocking collectives  51 us (49%)
  waiting for transfers between devices  18.7 us (18%)
  starting transfers between devices  18.3 us (18%)
  Pallas kernels  13.6 us (13%)
  local copies, waits for them, and re-layouts  1.73 us (2%)
    all_to_all x3, blocking collectives, within_cube(): lax.all_to_all(array, axes, split_axis=0, concat_axis=0, tiled=True, axis...  44.5 us
    ppermute x2, waiting for transfers between devices, from_upper(): return lax.ppermute(array, axes, pairs)  12.1 us
    pallas_call x11, Pallas kernels, call(): pl.pallas_call(inner, name=name, out_shape=shapes, in_specs=[scalars] * s...  11.6 us
    ppermute x7, waiting for transfers between devices, from_core(): return lax.ppermute(array, axes, pairs)  6.56 us
    all_gather x1, blocking collectives, body(): object_out = lax.all_gather(new_rows, 'mode', axis=1, tiled=True)  6.51 us
    ppermute x2, starting transfers between devices, from_upper(): return lax.ppermute(array, axes, pairs)  5.65 us
    ppermute x1, starting transfers between devices, body(): part_measured = lax.ppermute(part_measured, axes, pairs)  4.62 us
    ppermute x3, starting transfers between devices, to_row(): return lax.ppermute(array, axes, pairs)  3.55 us
  transfers between devices with their start and end apart: 14, of which 8 were waited for; matrix products, arithmetic and copies ran while one was open for 0% of the time, Pallas kernels for 6%

profile of v4, /device:TPU:0, one launch (start us, length us, event | category | flops | bytes accessed | tf_op | source)
XLA Modules:
  0.0 104.1 jit_solution(2713192285631968023)
XLA Ops:
  0.6 3.0 %collective-permute-start.6 = (f32[2,1,256,256]{3,2,1,0:T(8,128)}, f32[2,1,256,256]{3,2,1,0:T(8,128)S(1)}, u32[]{:S(2)}, u32[]{:S(2)}) collective-permute-start(f32[2,1,256,256]{3,2,1,0:T(8,128)} %refs_5_.2), channel_id=1, source_target_pairs={{2,0},{3,1},{0,2},{1,3},{6,4},{7,5},{4,6},{5,7},{10,8},{11,9},{8,1... | collective-permute-start | bytes 1572872 | tf_op jit(solution)/shard_map/ppermute | solution.py:83
  3.7 2.1 %cut.1 = (f32[2,64,256]{2,1,0:T(8,128)}, f32[2,64,256]{2,1,0:T(8,128)}, f32[2,64,256]{2,1,0:T(8,128)}, f32[2,64,256]{2,1,0:T(8,128)}, f32[1,128,256]{2,1,0:T(8,128)}) custom-call(s32[2,8]{1,0:T(2,128)} %bitcast.1, s32[8]{0:T(128)} %refs_1_.7, f32[2,128,512]{2,1,0:T(8,128)} %refs_3_.2, f32[1,256,256]{2,1,0:T(8,128)} %refs_0_.1), custom_call_target="tpu_custom_call" | custom-call | tf_op jit(solution)/shard_map/cut/pallas_call | solution.py:560
  5.7 1.6 %collective-permute-start = (f32[2,64,256]{2,1,0:T(8,128)}, f32[2,64,256]{2,1,0:T(8,128)S(1)}, u32[]{:S(2)}, u32[]{:S(2)}) collective-permute-start(f32[2,64,256]{2,1,0:T(8,128)} %get-tuple-element.20), channel_id=1, source_target_pairs={{0,4},{1,5},{2,6},{3,7},{4,0},{5,1},{6,2},{7,3},{8,12},{9,13},{10,... | collective-permute-start | bytes 393224 | tf_op jit(solution)/shard_map/ppermute | solution.py:95
  7.3 1.6 %collective-permute-start.1 = (f32[2,64,256]{2,1,0:T(8,128)}, f32[2,64,256]{2,1,0:T(8,128)S(1)}, u32[]{:S(2)}, u32[]{:S(2)}) collective-permute-start(f32[2,64,256]{2,1,0:T(8,128)} %get-tuple-element.21), channel_id=1, source_target_pairs={{0,8},{1,9},{2,10},{3,11},{4,12},{5,13},{6,14},{7,15},{8,0},{9,1},... | collective-permute-start | bytes 393224 | tf_op jit(solution)/shard_map/ppermute | solution.py:95
  9.3 4.6 %collective-permute-start.4 = (f32[1,128,256]{2,1,0:T(8,128)}, f32[1,128,256]{2,1,0:T(8,128)S(1)}, u32[]{:S(2)}, u32[]{:S(2)}) collective-permute-start(f32[1,128,256]{2,1,0:T(8,128)} %get-tuple-element.24), channel_id=1, source_target_pairs={{18,2},{19,3},{22,6},{23,7},{26,10},{27,11},{30,14},{31,15},{0,16}... | collective-permute-start | bytes 393224 | tf_op jit(solution)/shard_map/ppermute | solution.py:582
  14.0 0.9 copy-done.5
  16.2 2.4 %collective-permute-start.3 = (f32[1,2,2,64,256]{4,3,2,1,0:T(8,128)S(1)}, f32[1,2,2,64,256]{4,3,2,1,0:T(8,128)S(1)}, u32[]{:S(2)}, u32[]{:S(2)}) collective-permute-start(f32[1,2,2,64,256]{4,3,2,1,0:T(8,128)S(1)} %choose.3.refs_1_), channel_id=1, source_target_pairs={{16,0},{17,1},{18,2},{19,3},{20,4},{21,5},{22,6},{23,7},{24,8},{25... | collective-permute-start | bytes 786440 | tf_op jit(solution)/shard_map/ppermute | solution.py:69
  18.7 1.3 %collective-permute-done.5.refs_2_ = f32[1,128,256]{2,1,0:T(8,128)S(1)} collective-permute-done((f32[1,128,256]{2,1,0:T(8,128)S(1)}, f32[1,128,256]{2,1,0:T(8,128)S(1)}, u32[]{:S(2)}, u32[]{:S(2)}) %collective-permute-start.5) | collective-permute-done | bytes 131104 | tf_op jit(solution)/shard_map/ppermute | solution.py:76
  20.7 9.0 %collective-permute-done.3.refs_2_ = f32[1,2,2,64,256]{4,3,2,1,0:T(8,128)S(1)} collective-permute-done((f32[1,2,2,64,256]{4,3,2,1,0:T(8,128)S(1)}, f32[1,2,2,64,256]{4,3,2,1,0:T(8,128)S(1)}, u32[]{:S(2)}, u32[]{:S(2)}) %collective-permute-start.3) | collective-permute-done | bytes 262176 | tf_op jit(solution)/shard_map/ppermute | solution.py:69
  30.2 1.0 collective-permute-done.8.refs_4_
  31.6 2.4 %far.1 = (f32[1,2,256,256]{3,2,1,0:T(8,128)S(1)}, f32[1,256,256]{2,1,0:T(8,128)S(1)}, f32[1,1,2,256,256]{4,3,2,1,0:T(8,128)S(1)}, f32[2,1,2,32,256]{4,3,2,1,0:T(8,128)S(1)}) custom-call(s32[2,8]{1,0:T(2,128)S(1)} %bitcast.4, f32[1,2,2,64,256]{4,3,2,1,0:T(8,128)S(1)} %choose.3.refs_1_, f32[1,2,2,64,256]{4,3,2,1,0:T(8,128)S(1)} %collective-permute-done.3.refs_2_, ...), custom_call_target="tpu_custom_call" | custom-call | tf_op jit(solution)/shard_map/far/pallas_call | solution.py:526
  34.3 1.4 %collective-permute-done.9.refs_1_ = f32[1,256,256]{2,1,0:T(8,128)S(1)} collective-permute-done((f32[1,256,256]{2,1,0:T(8,128)S(1)}, f32[1,256,256]{2,1,0:T(8,128)S(1)}, u32[]{:S(2)}, u32[]{:S(2)}) %collective-permute-start.9) | collective-permute-done | bytes 262176 | tf_op jit(solution)/shard_map/ppermute | solution.py:76
  35.6 0.9 gradient.1
  36.5 15.3 %all_to_all.15.refs_0_ = f32[8,80,256]{2,1,0:T(8,128)S(1)} all-to-all(f32[8,80,256]{2,1,0:T(8,128)S(1)} %gradient.1), channel_id=1, replica_groups={{0,4,8,12,2,6,10,14},{1,5,9,13,3,7,11,15},{16,20,24,28,18,22,26,30},{17..., dimensions={0} | all-to-all | bytes 1310720 | tf_op jit(solution)/shard_map/all_to_all | solution.py:98
  51.9 3.2 %collective-permute-start.10 = (f32[80,256]{1,0:T(8,128)S(1)}, f32[80,256]{1,0:T(8,128)S(1)}, u32[]{:S(2)}, u32[]{:S(2)}) collective-permute-start(f32[80,256]{1,0:T(8,128)S(1)} %sum.1.refs_1_), channel_id=1, source_target_pairs={{16,0},{17,1},{18,2},{19,3},{20,4},{21,5},{22,6},{23,7},{24,8},{25... | collective-permute-start | bytes 245768 | tf_op jit(solution)/shard_map/ppermute | solution.py:69
  55.1 3.2 %collective-permute-done.10.refs_2_ = f32[80,256]{1,0:T(8,128)S(1)} collective-permute-done((f32[80,256]{1,0:T(8,128)S(1)}, f32[80,256]{1,0:T(8,128)S(1)}, u32[]{:S(2)}, u32[]{:S(2)}) %collective-permute-start.10) | collective-permute-done | bytes 81952 | tf_op jit(solution)/shard_map/ppermute | solution.py:69
  58.4 16.2 %all_to_all.16.refs_0_.refs_4_ = f32[8,2,1,2,32,256]{5,4,3,2,1,0:T(8,128)S(1)} all-to-all(f32[8,2,1,2,32,256]{5,4,3,2,1,0:T(8,128)S(1)} %step.1), channel_id=1, replica_groups={{0,4,8,12,2,6,10,14},{1,5,9,13,3,7,11,15},{16,20,24,28,18,22,26,30},{17..., dimensions={0} | all-to-all | bytes 2097152 | tf_op jit(solution)/shard_map/all_to_all | solution.py:98
  74.6 2.2 %again.1 = (f32[2,1,256,256]{3,2,1,0:T(8,128)}, f32[256,256]{1,0:T(8,128)S(1)}, f32[1,256,256]{2,1,0:T(8,128)S(1)}, f32[1,2,1,2,256,256]{5,4,3,2,1,0:T(8,128)S(1)}) custom-call(f32[8,2,1,2,32,256]{5,4,3,2,1,0:T(8,128)S(1)} %all_to_all.16.refs_0_.refs_4_, f32[1,2,256,256]{3,2,1,0:T(8,128)S(1)} %get-tuple-element.30.refs_3_.refs_1_, ...), custom_call_target="tpu_custom_call" | custom-call | tf_op jit(solution)/shard_map/again/pallas_call | solution.py:526
  77.4 1.0 collective-permute-done.11.refs_2_
  78.4 2.3 %terms.1 = (f32[1,2,2,2,32,256]{5,4,3,2,1,0:T(8,128)S(1)}, f32[1,2,2,2,32,256]{5,4,3,2,1,0:T(8,128)S(1)}) custom-call(s32[2,8]{1,0:T(2,128)S(1)} %bitcast.5, f32[1,256,256]{2,1,0:T(8,128)S(1)} %get-tuple-element.33.refs_1_, f32[1,256,256]{2,1,0:T(8,128)S(1)} %collective-permute-done.11.refs_2_, f32[1,256,256]{2,1,0:T(8,128)S(1)} %order.1.refs_2_.refs_3_, ...), custom_call_target="tpu_custom_call" | custom-call | tf_op jit(solution)/shard_map/terms/pallas_call | solution.py:526
  80.9 1.4 %collective-permute-done.12.refs_3_ = f32[1,2,2,2,32,256]{5,4,3,2,1,0:T(8,128)S(1)} collective-permute-done((f32[1,2,2,2,32,256]{5,4,3,2,1,0:T(8,128)S(1)}, f32[1,2,2,2,32,256]{5,4,3,2,1,0:T(8,128)S(1)}, u32[]{:S(2)}, u32[]{:S(2)}) %collective-permute-start.12) | collective-permute-done | bytes 262176 | tf_op jit(solution)/shard_map/ppermute | solution.py:76
  82.9 12.9 %all_to_all.17.refs_2_ = f32[8,2,32,256]{3,2,1,0:T(8,128)S(1)} all-to-all(f32[8,2,32,256]{3,2,1,0:T(8,128)S(1)} %post.1), channel_id=1, replica_groups={{0,4,8,12,2,6,10,14},{1,5,9,13,3,7,11,15},{16,20,24,28,18,22,26,30},{17..., dimensions={0} | all-to-all | bytes 1048576 | tf_op jit(solution)/shard_map/all_to_all | solution.py:98
  95.8 1.0 update.1
  96.8 6.5 %all_gather.3 = f32[2,128,512]{2,1,0:T(8,128)S(1)} all-gather(f32[2,32,512]{2,1,0:T(8,128)S(1)} %update.1), channel_id=1, replica_groups=mesh['region'=8,'mode'=4] {'mode'}, dimensions={1}, use_global_device_ids=true | all-gather | bytes 655360 | tf_op jit(solution)/shard_map/all_gather | solution.py:676
  (37 shorter events, 5.9 us)
Async XLA Ops:
  0.6 29.1 %collective-permute-start.6 = (f32[2,1,256,256]{3,2,1,0:T(8,128)}, f32[2,1,256,256]{3,2,1,0:T(8,128)S(1)}, u32[]{:S(2)}, u32[]{:S(2)}) collective-permute-start(f32[2,1,256,256]{3,2,1,0:T(8,128)} %refs_5_.2), channel_id=1, source_target_pairs={{2,0},{3,1},{0,2},{1,3},{6,4},{7,5},{4,6},{5,7},{10,8},{11,9},{8,1... | collective-permute-start | bytes 1572872 | tf_op jit(solution)/shard_map/ppermute | solution.py:83
  5.7 9.8 %collective-permute-start = (f32[2,64,256]{2,1,0:T(8,128)}, f32[2,64,256]{2,1,0:T(8,128)S(1)}, u32[]{:S(2)}, u32[]{:S(2)}) collective-permute-start(f32[2,64,256]{2,1,0:T(8,128)} %get-tuple-element.20), channel_id=1, source_target_pairs={{0,4},{1,5},{2,6},{3,7},{4,0},{5,1},{6,2},{7,3},{8,12},{9,13},{10,... | collective-permute-start | bytes 393224 | tf_op jit(solution)/shard_map/ppermute | solution.py:95
  7.3 8.2 %collective-permute-start.1 = (f32[2,64,256]{2,1,0:T(8,128)}, f32[2,64,256]{2,1,0:T(8,128)S(1)}, u32[]{:S(2)}, u32[]{:S(2)}) collective-permute-start(f32[2,64,256]{2,1,0:T(8,128)} %get-tuple-element.21), channel_id=1, source_target_pairs={{0,8},{1,9},{2,10},{3,11},{4,12},{5,13},{6,14},{7,15},{8,0},{9,1},... | collective-permute-start | bytes 393224 | tf_op jit(solution)/shard_map/ppermute | solution.py:95
  8.9 6.6 %collective-permute-start.2 = (f32[2,64,256]{2,1,0:T(8,128)}, f32[2,64,256]{2,1,0:T(8,128)S(1)}, u32[]{:S(2)}, u32[]{:S(2)}) collective-permute-start(f32[2,64,256]{2,1,0:T(8,128)} %get-tuple-element.22), channel_id=1, source_target_pairs={{0,12},{1,13},{2,14},{3,15},{4,8},{5,9},{6,10},{7,11},{8,4},{9,5},... | collective-permute-start | bytes 393224 | tf_op jit(solution)/shard_map/ppermute | solution.py:95
  9.3 4.6 %copy-start.6 = (s32[8,2]{0,1:T(2,128)S(1)}, s32[8,2]{0,1:T(2,128)}, u32[]{:S(2)}) copy-start(s32[8,2]{0,1:T(2,128)} %param.10) | copy-start | bytes 196
  9.3 4.6 %copy-start.7 = (s32[8]{0:T(128)S(1)}, s32[8]{0:T(128)}, u32[]{:S(2)}) copy-start(s32[8]{0:T(128)} %refs_1_.7) | copy-start | bytes 100
  9.3 9.3 %collective-permute-start.4 = (f32[1,128,256]{2,1,0:T(8,128)}, f32[1,128,256]{2,1,0:T(8,128)S(1)}, u32[]{:S(2)}, u32[]{:S(2)}) collective-permute-start(f32[1,128,256]{2,1,0:T(8,128)} %get-tuple-element.24), channel_id=1, source_target_pairs={{18,2},{19,3},{22,6},{23,7},{26,10},{27,11},{30,14},{31,15},{0,16}... | collective-permute-start | bytes 393224 | tf_op jit(solution)/shard_map/ppermute | solution.py:582
  14.0 0.9 copy-start.5
  14.9 16.7 %copy-start.4 = (f32[2,1,256,256]{3,2,1,0:T(8,128)S(1)}, f32[2,1,256,256]{3,2,1,0:T(8,128)}, u32[]{:S(2)}) copy-start(f32[2,1,256,256]{3,2,1,0:T(8,128)} %refs_5_.2) | copy-start | bytes 1572868
  15.5 4.5 %copy-start.3 = (f32[1,256,256]{2,1,0:T(8,128)S(1)}, f32[1,256,256]{2,1,0:T(8,128)}, u32[]{:S(2)}) copy-start(f32[1,256,256]{2,1,0:T(8,128)} %refs_0_.1) | copy-start | bytes 786436
  15.5 16.1 %copy-start.1 = (bf16[2,2,256,256]{3,2,1,0:T(8,128)(2,1)S(1)}, bf16[2,2,256,256]{3,2,1,0:T(8,128)(2,1)}, u32[]{:S(2)}) copy-start(bf16[2,2,256,256]{3,2,1,0:T(8,128)(2,1)} %constant.4.clone.refs_7_.refs_5_.refs_2_.refs_6_) | copy-start | bytes 1572868
  16.2 15.4 %copy-start = (bf16[2,2,256,256]{3,2,1,0:T(8,128)(2,1)S(1)}, bf16[2,2,256,256]{3,2,1,0:T(8,128)(2,1)}, u32[]{:S(2)}) copy-start(bf16[2,2,256,256]{3,2,1,0:T(8,128)(2,1)} %constant.5.clone.refs_8_.refs_6_.refs_3_.refs_7_) | copy-start | bytes 1572868
  16.2 13.5 %collective-permute-start.3 = (f32[1,2,2,64,256]{4,3,2,1,0:T(8,128)S(1)}, f32[1,2,2,64,256]{4,3,2,1,0:T(8,128)S(1)}, u32[]{:S(2)}, u32[]{:S(2)}) collective-permute-start(f32[1,2,2,64,256]{4,3,2,1,0:T(8,128)S(1)} %choose.3.refs_1_), channel_id=1, source_target_pairs={{16,0},{17,1},{18,2},{19,3},{20,4},{21,5},{22,6},{23,7},{24,8},{25... | collective-permute-start | bytes 786440 | tf_op jit(solution)/shard_map/ppermute | solution.py:69
  18.6 1.3 %collective-permute-start.5 = (f32[1,128,256]{2,1,0:T(8,128)S(1)}, f32[1,128,256]{2,1,0:T(8,128)S(1)}, u32[]{:S(2)}, u32[]{:S(2)}) collective-permute-start(f32[1,128,256]{2,1,0:T(8,128)S(1)} %collective-permute-done.4.refs_1_), channel_id=1, source_target_pairs={{1,0},{0,1},{3,2},{2,3},{5,4},{4,5},{7,6},{6,7},{9,8},{8,9},{11,10... | collective-permute-start | bytes 393224 | tf_op jit(solution)/shard_map/ppermute | solution.py:76
  29.7 1.5 %collective-permute-start.8 = (f32[1,2,2,64,256]{4,3,2,1,0:T(8,128)S(1)}, f32[1,2,2,64,256]{4,3,2,1,0:T(8,128)S(1)}, u32[]{:S(2)}, u32[]{:S(2)}) collective-permute-start(f32[1,2,2,64,256]{4,3,2,1,0:T(8,128)S(1)} %collective-permute-done.3.refs_2_), channel_id=1, source_target_pairs={{1,0},{0,1},{3,2},{2,3},{5,4},{4,5},{7,6},{6,7},{9,8},{8,9},{11,10... | collective-permute-start | bytes 786440 | tf_op jit(solution)/shard_map/ppermute | solution.py:76
  29.7 1.9 %collective-permute-start.7 = (f32[1,2,2,64,256]{4,3,2,1,0:T(8,128)S(1)}, f32[1,2,2,64,256]{4,3,2,1,0:T(8,128)S(1)}, u32[]{:S(2)}, u32[]{:S(2)}) collective-permute-start(f32[1,2,2,64,256]{4,3,2,1,0:T(8,128)S(1)} %choose.3.refs_1_), channel_id=1, source_target_pairs={{1,0},{0,1},{3,2},{2,3},{5,4},{4,5},{7,6},{6,7},{9,8},{8,9},{11,10... | collective-permute-start | bytes 786440 | tf_op jit(solution)/shard_map/ppermute | solution.py:76
  34.0 1.6 %collective-permute-start.9 = (f32[1,256,256]{2,1,0:T(8,128)S(1)}, f32[1,256,256]{2,1,0:T(8,128)S(1)}, u32[]{:S(2)}, u32[]{:S(2)}) collective-permute-start(f32[1,256,256]{2,1,0:T(8,128)S(1)} %get-tuple-element.28.refs_0_), channel_id=1, source_target_pairs={{1,0},{0,1},{3,2},{2,3},{5,4},{4,5},{7,6},{6,7},{9,8},{8,9},{11,10... | collective-permute-start | bytes 786440 | tf_op jit(solution)/shard_map/ppermute | solution.py:76
  51.9 6.4 %collective-permute-start.10 = (f32[80,256]{1,0:T(8,128)S(1)}, f32[80,256]{1,0:T(8,128)S(1)}, u32[]{:S(2)}, u32[]{:S(2)}) collective-permute-start(f32[80,256]{1,0:T(8,128)S(1)} %sum.1.refs_1_), channel_id=1, source_target_pairs={{16,0},{17,1},{18,2},{19,3},{20,4},{21,5},{22,6},{23,7},{24,8},{25... | collective-permute-start | bytes 245768 | tf_op jit(solution)/shard_map/ppermute | solution.py:69
  76.8 1.5 %collective-permute-start.11 = (f32[1,256,256]{2,1,0:T(8,128)S(1)}, f32[1,256,256]{2,1,0:T(8,128)S(1)}, u32[]{:S(2)}, u32[]{:S(2)}) collective-permute-start(f32[1,256,256]{2,1,0:T(8,128)S(1)} %get-tuple-element.33.refs_1_), channel_id=1, source_target_pairs={{1,0},{0,1},{3,2},{2,3},{5,4},{4,5},{7,6},{6,7},{9,8},{8,9},{11,10... | collective-permute-start | bytes 786440 | tf_op jit(solution)/shard_map/ppermute | solution.py:76
  76.8 4.0 %collective-permute-start.13 = (f32[256,256]{1,0:T(8,128)S(1)}, f32[256,256]{1,0:T(8,128)S(1)}, u32[]{:S(2)}, u32[]{:S(2)}) collective-permute-start(f32[256,256]{1,0:T(8,128)S(1)} %get-tuple-element.37.refs_4_), channel_id=1, source_target_pairs={{1,0},{0,1},{3,2},{2,3},{5,4},{4,5},{7,6},{6,7},{9,8},{8,9},{11,10... | collective-permute-start | bytes 786440 | tf_op jit(solution)/shard_map/ppermute | solution.py:76
  80.7 1.6 %collective-permute-start.12 = (f32[1,2,2,2,32,256]{5,4,3,2,1,0:T(8,128)S(1)}, f32[1,2,2,2,32,256]{5,4,3,2,1,0:T(8,128)S(1)}, u32[]{:S(2)}, u32[]{:S(2)}) collective-permute-start(f32[1,2,2,2,32,256]{5,4,3,2,1,0:T(8,128)S(1)} %get-tuple-element.36), channel_id=1, source_target_pairs={{1,0},{0,1},{3,2},{2,3},{5,4},{4,5},{7,6},{6,7},{9,8},{8,9},{11,10... | collective-permute-start | bytes 786440 | tf_op jit(solution)/shard_map/ppermute | solution.py:76
  82.9 12.9 %copy-start.2 = (f32[2,128,512]{2,1,0:T(8,128)S(1)}, f32[2,128,512]{2,1,0:T(8,128)}, u32[]{:S(2)}) copy-start(f32[2,128,512]{2,1,0:T(8,128)} %refs_3_.2) | copy-start | bytes 1572868

commit v5 on v4

--- a/solution.py
+++ b/solution.py
@@ -30,7 +30,7 @@
         self.local_modes = modes // helpers
         self.band = length // 2
         self.strip = self.band // self.cores
-        self.share = self.band // helpers
+        self.paired = self.lowers & (self.lowers - 1) == 0
         self.piece = length // regions
         self.part = length // self.cores
 
@@ -83,7 +83,7 @@
         return lax.ppermute(array, axes, pairs)
 
     def across(self, lower, step):
-        if self.lowers & (self.lowers - 1) == 0:
+        if self.paired:
             return lower ^ step
         return (lower + step) % self.lowers
 
@@ -263,17 +263,34 @@
             out[frame, plane, 1] = bottom
 
 
-def leave(probe_real, probe_imag, window_real, window_imag, forward, back):
+def side_by_side(stack, rows):
+    return jnp.concatenate([stack[at : at + rows] for at in range(0, stack.shape[0], rows)], axis=1)
+
+
+def one_above_another(row, columns):
+    return jnp.concatenate([row[:, at : at + columns] for at in range(0, row.shape[1], columns)], axis=0)
+
+
+def leave(probes, window_real, window_imag, forward, back):
+    length = window_real.shape[0]
     wave = rows_forward(
-        probe_real * window_real - probe_imag * window_imag,
-        probe_real * window_imag + probe_imag * window_real,
+        jnp.concatenate([real * window_real - imag * window_imag for real, imag in probes], axis=1),
+        jnp.concatenate([real * window_imag + imag * window_real for real, imag in probes], axis=1),
         back,
     )
-    return columns_forward(*wave, forward)
+    return columns_forward(*(one_above_another(part, length) for part in wave), forward)
 
 
 def come_back(far, factor, forward, back):
-    return rows_back(*columns_back(far[0] * factor, far[1] * factor, back), forward)
+    length = factor.shape[0]
+    factors = jnp.concatenate([factor] * (far.shape[1] // length), axis=0)
+    wave = columns_back(far[0] * factors, far[1] * factors, back)
+    return rows_back(*(side_by_side(part, length) for part in wave), forward)
+
+
+def power_of(real, imag, length):
+    power = real**2 + imag**2
+    return sum(power[at : at + length] for at in range(length, power.shape[0], length)) + power[:length]
 
 
 def far_kernel(layout, offsets, *refs):
@@ -298,19 +315,16 @@
         for plane in range(2):
             wrapped = inner[plane].reshape(length, length)
             windows[frame, plane] = pltpu.roll(wrapped, (length - lead) % length, 0)
-        window = windows[frame, 0], windows[frame, 1]
-        total = jnp.zeros((length, length), single)
-        for entry, probe in enumerate(probes):
-            for local in range(layout.local_modes):
-                wave_real, wave_imag = leave(probe[0, local], probe[1, local], *window, forward, back)
-                total += wave_real**2 + wave_imag**2
-
-                @pl.when((twin + entry) % halves == upper)
-                def _():
-                    kept[frame, local, 0] = wave_real
-                    kept[frame, local, 1] = wave_imag
-
-        intensity[frame] = total
+        listed = [(probe[0, k], probe[1, k]) for probe in probes for k in range(layout.local_modes)]
+        waves = leave(listed, windows[frame, 0], windows[frame, 1], forward, back)
+        intensity[frame] = power_of(*waves, length)
+        rows_kept = layout.local_modes * length
+        for entry in range(halves):
+
+            @pl.when((twin + entry) % halves == upper)
+            def _():
+                for plane, wave in enumerate(waves):
+                    kept[frame, plane] = wave[entry * rows_kept : (entry + 1) * rows_kept]
 
 
 def order_kernel(layout, own_measured, *refs):
@@ -354,8 +368,10 @@
         window_real, window_imag = windows[frame, 0], windows[frame, 1]
         factor = factor_of(roots, intensities, frame)
         channels = []
+        changes_real, changes_imag = come_back(kept[frame], factor, forward, back)
         for local in range(layout.local_modes):
-            change_real, change_imag = come_back(kept[frame, local], factor, forward, back)
+            columns = slice(local * length, (local + 1) * length)
+            change_real, change_imag = changes_real[:, columns], changes_imag[:, columns]
             channels.append(window_real * change_real + window_imag * change_imag)
             channels.append(window_real * change_imag - window_imag * change_real)
         channels = [values.reshape(cut) for values in channels]
@@ -406,20 +422,17 @@
 def again_kernel(layout, probes, windows, forward, back, probe_out, probe_power, intensity, fars):
     upper, _, twin, _ = layout.place()
     own_entry = (twin + layout.halves - upper) % layout.halves
-    power = jnp.zeros((layout.length, layout.length), single)
-    totals = [jnp.zeros((layout.length, layout.length), single) for _ in range(layout.frames)]
-    for entry in range(layout.halves):
-        for local in range(layout.local_modes):
-            probe = [new_probe(probes, entry, local, plane) for plane in range(2)]
-            power += probe[0] ** 2 + probe[1] ** 2
-            for frame in range(layout.frames):
-                wave_real, wave_imag = leave(*probe, windows[frame, 0], windows[frame, 1], forward, back)
-                totals[frame] += wave_real**2 + wave_imag**2
-                fars[frame, entry, local, 0] = wave_real
-                fars[frame, entry, local, 1] = wave_imag
-    probe_power[...] = power
-    for frame, total in enumerate(totals):
-        intensity[frame] = total
+    listed = [
+        [new_probe(probes, entry, local, plane) for plane in range(2)]
+        for entry in range(layout.halves)
+        for local in range(layout.local_modes)
+    ]
+    for frame in range(layout.frames):
+        waves = leave(listed, windows[frame, 0], windows[frame, 1], forward, back)
+        intensity[frame] = power_of(*waves, layout.length)
+        for plane, wave in enumerate(waves):
+            fars[frame, plane] = wave
+    probe_power[...] = sum(real**2 + imag**2 for real, imag in listed)
     for local in range(layout.local_modes):
         for plane in range(2):
             probe_out[plane, local] = new_probe(probes, own_entry, local, plane)
@@ -428,33 +441,36 @@
 def terms_kernel(layout, offsets, *refs):
     cores, halves, frames, length = layout.cores, layout.halves, layout.frames, layout.length
     intensities = refs[:cores]
-    roots, probes, fars, forward, back, *shares, inner = refs[cores:]
+    roots, probes, fars, forward, back, *strips, inner = refs[cores:]
     upper, lower, twin, core = layout.place()
     region = twin * layout.lowers + lower
     for frame in range(frames):
         factor = factor_of(roots, intensities, frame)
+        changes_real, changes_imag = come_back(fars[frame], factor, forward, back)
         numer_real = jnp.zeros((length, length), single)
         numer_imag = jnp.zeros((length, length), single)
         for entry in range(halves):
             for local in range(layout.local_modes):
-                change_real, change_imag = come_back(fars[frame, entry, local], factor, forward, back)
+                first = (entry * layout.local_modes + local) * length
+                change_real = changes_real[:, first : first + length]
+                change_imag = changes_imag[:, first : first + length]
                 probe_real, probe_imag = (new_probe(probes, entry, local, plane) for plane in range(2))
                 numer_real += probe_real * change_real + probe_imag * change_imag
                 numer_imag += probe_real * change_imag - probe_imag * change_real
         lead = offsets[0, region * frames + frame] % layout.band
         for plane, values in enumerate((numer_real, numer_imag)):
-            turned = pltpu.roll(values, lead, 0)
-            inner[plane] = turned.reshape(2, halves, cores, layout.share, length)
-        for step, share in enumerate(shares):
-            share[frame] = inner[:, :, :, (core + cores - step) % cores]
+            inner[plane] = pltpu.roll(values, lead, 0).reshape(2, cores, layout.strip, length)
+        for step, strip in enumerate(strips):
+            strip[frame] = inner[:, :, (core + cores - step) % cores]
 
 
 def post_kernel(layout, offsets, owner, *refs):
-    shares, out = refs[:-1], refs[-1]
+    strips, outs = refs[: layout.cores], refs[layout.cores :]
     upper, lower, twin, _ = layout.place()
     region = twin * layout.lowers + lower
-    for low in range(layout.lowers):
-        band = band_of_block(owner, upper * layout.lowers + low, layout)
+    for step, out in enumerate(outs):
+        block = upper * layout.lowers + layout.across(lower, step)
+        band = band_of_block(owner, block, layout)
         frame, row = jnp.int32(0), offsets[0, region * layout.frames]
         for extra in range(1, layout.frames):
             candidate = offsets[0, region * layout.frames + extra]
@@ -462,58 +478,104 @@
             over = (anchor <= band) & (band <= anchor + 2)
             frame, row = jnp.where(over, extra, frame), jnp.where(over, candidate, row)
         slot = (band - row // layout.band == 1).astype(jnp.int32)
-        for target in range(layout.halves):
-            for plane in range(2):
-                total = shares[0][frame, plane, slot, target]
-                for share in shares[1:]:
-                    total += share[frame, plane, slot, target]
-                out[target * layout.lowers + low, plane] = total
-
-
-def update_kernel(layout, offsets, owner, arrived, block, *refs):
-    powers, (rows_out, doubled, total) = refs[: layout.cores], refs[layout.cores :]
-    upper, lower, twin, core = layout.place()
-    length, share = layout.length, layout.share
+        for plane in range(2):
+            total = strips[0][frame, plane, slot]
+            for strip in strips[1:]:
+                total += strip[frame, plane, slot]
+            out[plane] = total
+
+
+class Cover:
+    def __init__(self, layout, offsets, region, band, core):
+        row, self.column = frame_over(offsets, region, band, layout)
+        anchor = row // layout.band
+        self.lead = row - anchor * layout.band
+        self.step = band - anchor
+        self.first = core * layout.strip
+        self.layout = layout
+
+    def inside(self):
+        band = self.layout.band
+        middle = (self.step == 1) | (self.step == 2)
+        begin = jnp.where(self.step == 0, self.lead, jnp.where(middle, 0, band))
+        end = jnp.where(self.step == 2, self.lead, band)
+        shape = (self.layout.strip, self.layout.length)
+        rows = lax.broadcasted_iota(jnp.int32, shape, 0) + self.first
+        return (rows >= begin) & (rows < end)
+
+    def start(self):
+        slot = (self.step == 1).astype(jnp.int32)
+        length = self.layout.length
+        return (slot * self.layout.band + self.first + length - self.lead) % length
+
+    def add(self, total, terms):
+        tiles = self.layout.length // lanes
+        shift = self.column % lanes
+        begin = pl.multiple_of(self.column - shift, lanes)
+        spilled = lax.broadcasted_iota(jnp.int32, (terms.shape[0], lanes), 1) < shift
+        turned = [
+            pltpu.roll(terms[:, tile * lanes : (tile + 1) * lanes], shift, 1) for tile in range(tiles)
+        ]
+        for tile in range(tiles + 1):
+            near = turned[tile] if tile < tiles else 0.0
+            over = turned[tile - 1] if tile else 0.0
+            total[:, pl.ds(begin + tile * lanes, lanes)] += jnp.where(spilled, over, near)
+
+
+def density_kernel(layout, offsets, owner, *refs):
+    powers, (out, doubled, total) = refs[: layout.cores], refs[layout.cores :]
+    upper, lower, _, core = layout.place()
+    strip, length = layout.strip, layout.length
     band = band_of_block(owner, upper * layout.lowers + lower, layout)
-    first = (twin * layout.cores + core) * share
-    rows = lax.broadcasted_iota(jnp.int32, (share, length), 0) + first
     power = powers[0][...]
     for more in powers[1:]:
         power += more[...]
     doubled[0] = power
     doubled[1] = power
     wide = doubled.reshape(2 * length, length)
-    tiles = length // lanes
-    column_in_tile = lax.broadcasted_iota(jnp.int32, (3 * share, lanes), 1)
     total[...] = jnp.zeros_like(total)
     for region in range(layout.regions):
-        row, column = frame_over(offsets, region, band, layout)
-        anchor = row // layout.band
-        lead = row - anchor * layout.band
-        step = band - anchor
-        begin = jnp.where(step == 0, lead, jnp.where((step == 1) | (step == 2), 0, layout.band))
-        end = jnp.where(step == 2, lead, layout.band)
-        inside = (rows >= begin) & (rows < end)
-        slot = (step == 1).astype(jnp.int32)
-        start = (slot * layout.band + first + length - lead) % length
-        near = wide[pl.ds(pl.multiple_of(start // 8 * 8, 8), share + 8), :]
-        near = pltpu.roll(near, (share + 8 - start % 8) % (share + 8), 0)[:share]
-        terms = jnp.concatenate([arrived[region, 0], arrived[region, 1], near], axis=0)
-        terms = jnp.where(jnp.concatenate([inside] * 3, axis=0), terms, 0.0)
-        shift = column % lanes
-        begin = pl.multiple_of(column - shift, lanes)
-        spilled = column_in_tile < shift
-        turned = [
-            pltpu.roll(terms[:, tile * lanes : (tile + 1) * lanes], shift, 1) for tile in range(tiles)
-        ]
-        for tile in range(tiles + 1):
-            first_part = turned[tile] if tile < tiles else 0.0
-            second_part = turned[tile - 1] if tile else 0.0
-            total[:, pl.ds(begin + tile * lanes, lanes)] += jnp.where(spilled, second_part, first_part)
-    damped = total[2 * share :, : layout.width] + object_damping
+        cover = Cover(layout, offsets, region, band, core)
+        start = cover.start()
+        near = wide[pl.ds(pl.multiple_of(start // 8 * 8, 8), strip + 8), :]
+        near = pltpu.roll(near, (strip + 8 - start % 8) % (strip + 8), 0)[:strip]
+        cover.add(total, jnp.where(cover.inside(), near, 0.0))
+    out[...] = total[:, : layout.width] + object_damping
+
+
+def place_kernel(layout, offsets, owner, *refs):
+    arrived, (out, total) = refs[: layout.lowers], refs[layout.lowers :]
+    upper, lower, twin, core = layout.place()
+    strip = layout.strip
+    band = band_of_block(owner, upper * layout.lowers + lower, layout)
+    total[...] = jnp.zeros_like(total)
+    for step, terms in enumerate(arrived):
+        source = layout.across(lower, step if layout.paired else layout.lowers - step)
+        cover = Cover(layout, offsets, twin * layout.lowers + source, band, core)
+        inside = cover.inside()
+        kept = [jnp.where(inside, terms[plane], 0.0) for plane in range(2)]
+        cover.add(total, jnp.concatenate(kept, axis=0))
     for plane in range(2):
-        old = block[plane, pl.ds(pl.multiple_of(first, share), share), :]
-        rows_out[plane] = old + total[plane * share : (plane + 1) * share, : layout.width] / damped
+        out[plane] = total[plane * strip : (plane + 1) * strip, : layout.width]
+
+
+def update_kernel(layout, density, block, *refs):
+    placed, out = refs[:-1], refs[-1]
+    _, _, _, core = layout.place()
+    rows = pl.ds(pl.multiple_of(core * layout.strip, layout.strip), layout.strip)
+    for plane in range(2):
+        total = placed[0][plane]
+        for more in placed[1:]:
+            total += more[plane]
+        out[plane] = block[plane, rows, :] + total / density[...]
+
+
+def join_kernel(layout, *refs):
+    strips, out = refs[:-1], refs[-1]
+    _, _, _, core = layout.place()
+    for step, strip in enumerate(strips):
+        first = (core + step) % layout.cores * layout.strip
+        out[:, pl.ds(pl.multiple_of(first, layout.strip), layout.strip), :] = strip[...]
 
 
 def call(kernel, name, operands, outputs, scratch=(), scalar_count=0, after=()):
@@ -547,7 +609,7 @@
     )
     regions, halves, cores = layout.regions, layout.halves, layout.cores
     length, piece, frames = layout.length, layout.piece, layout.frames
-    local, strip, share = layout.local_modes, layout.strip, layout.share
+    local, strip = layout.local_modes, layout.strip
     forward, back = fourier_tables(length)
     corners = scan_offsets.T
 
@@ -570,8 +632,13 @@
             pltpu.SMEM(band_owner.shape, jnp.int32),
             pltpu.SemaphoreType.DMA((4,)),
         ],
-        compiler_params=pltpu.CompilerParams(vmem_limit_bytes=60 * 2**20),
-    )(corners, band_owner, object_bands, measured)
+        compiler_params=pltpu.CompilerParams(vmem_limit_bytes=28 * 2**20),
+    )(
+        *(
+            pltpu.with_memory_space_constraint(array, pltpu.HBM)
+            for array in (corners, band_owner, object_bands, measured)
+        )
+    )
     probes = [probe_modes] + [layout.from_twin(probe_modes, step) for step in range(1, halves)]
     if halves > 1:
         pairs = [
@@ -612,7 +679,7 @@
         [
             (frames, 2, length, length),
             (frames, length, length),
-            (frames, local, 2, length, length),
+            (frames, 2, local * length, length),
             (halves, local, 2, piece, length),
         ],
         scratch=[(2, 2, cores, strip, length)],
@@ -641,39 +708,56 @@
             (2, local, length, length),
             (length, length),
             (frames, length, length),
-            (frames, halves, local, 2, length, length),
+            (frames, 2, halves * local * length, length),
         ],
     )
-    shares = call(
+    strips = call(
         functools.partial(terms_kernel, layout),
         "terms",
         (corners, *from_cores(intensity), roots, new_probes, fars, forward, back),
-        [(frames, 2, 2, halves, share, length)] * cores,
-        scratch=[(2, 2, halves, cores, share, length)],
+        [(frames, 2, 2, strip, length)] * cores,
+        scratch=[(2, 2, cores, strip, length)],
         scalar_count=1,
     )
-    shares = [shares[0]] + [
-        layout.from_core(sent, step) for step, sent in enumerate(shares[1:], start=1)
+    strips = [strips[0]] + [
+        layout.from_core(sent, step) for step, sent in enumerate(strips[1:], start=1)
     ]
-    powers = from_cores(probe_power)
-    (posted,) = call(
+    posted = call(
         functools.partial(post_kernel, layout),
         "post",
-        (corners, band_owner, *shares),
-        [(regions, 2, share, length)],
+        (corners, band_owner, *strips),
+        [(2, strip, length)] * layout.lowers,
         scalar_count=2,
-        after=powers,
-    )
-    posted = layout.within_cube(posted)
+    )
+    posted = [posted[0]] + [
+        layout.to_row(sent, step) for step, sent in enumerate(posted[1:], start=1)
+    ]
+    (density,) = call(
+        functools.partial(density_kernel, layout),
+        "density",
+        (corners, band_owner, *from_cores(probe_power)),
+        [(strip, layout.width)],
+        scratch=[(2, length, length), (strip, layout.width + lanes)],
+        scalar_count=2,
+    )
+    (placed,) = call(
+        functools.partial(place_kernel, layout),
+        "place",
+        (corners, band_owner, *posted),
+        [(2, strip, layout.width)],
+        scratch=[(2 * strip, layout.width + lanes)],
+        scalar_count=2,
+    )
+    placed = [placed] + [layout.from_twin(placed, step) for step in range(1, halves)]
     (new_rows,) = call(
         functools.partial(update_kernel, layout),
         "update",
-        (corners, band_owner, posted, object_bands, *powers),
-        [(2, share, layout.width)],
-        scratch=[(2, length, length), (3 * share, layout.width + lanes)],
-        scalar_count=2,
-    )
-    object_out = lax.all_gather(new_rows, "mode", axis=1, tiled=True)
+        (density, object_bands, *placed),
+        [(2, strip, layout.width)],
+    )
+    (object_out,) = call(
+        functools.partial(join_kernel, layout), "join", from_cores(new_rows), [object_bands.shape]
+    )
     return probe_out, object_out
 
 

time: 104 us -> 102 us (0.981)
  blocking collectives: 51 us -> 31.5 us
  waiting for transfers between devices: 18.7 us -> 32.9 us
  starting transfers between devices: 18.3 us -> 22.3 us
  local copies, waits for them, and re-layouts: 1.73 us -> 0.04 us
    all_to_all x3 -> x2, blocking collectives: 44.5 us -> 31.5 us  [within_cube(): lax.all_to_all(array, axes, split_axis=0, concat_axis=0, tiled=True, axis...]
    all_gather x1 -> x0, blocking collectives: 6.51 us -> none  [body(): object_out = lax.all_gather(new_rows, 'mode', axis=1, tiled=True)]
    ppermute x3 -> x6, waiting for transfers between devices: 0.01 us -> 6.47 us  [to_row(): return lax.ppermute(array, axes, pairs)]
    ppermute x1 -> x2, waiting for transfers between devices: 0.01 us -> 5.7 us  [from_twin(): return lax.ppermute(array, axes, pairs)]
    ppermute x3 -> x6, starting transfers between devices: 3.55 us -> 7.11 us  [to_row(): return lax.ppermute(array, axes, pairs)]
    ppermute x7 -> x8, waiting for transfers between devices: 6.56 us -> 8.59 us  [from_core(): return lax.ppermute(array, axes, pairs)]
    unnamed x17 -> x14, local copies, waits for them, and re-layouts: 1.73 us -> 0.04 us
    pallas_call x11 -> x14, Pallas kernels: 11.6 us -> 12.6 us  [call(): pl.pallas_call(inner, name=name, out_shape=shapes, in_specs=[scalars] * s...]
  transfers between devices with their start and end apart: 14 -> 19, of which waited for: 8 -> 14; matrix products, arithmetic and copies ran while one was open for 0% -> 0% of each run, Pallas kernels for 6% -> 5%
where the time goes in v5:
time: 102 us; the launch traced here: 101 us
  waiting for transfers between devices  32.9 us (32%)
  blocking collectives  31.5 us (31%)
  starting transfers between devices  22.3 us (22%)
  Pallas kernels  13.8 us (14%)
    all_to_all x2, blocking collectives, within_cube(): lax.all_to_all(array, axes, split_axis=0, concat_axis=0, tiled=True, axis...  31.5 us
    pallas_call x14, Pallas kernels, call(): pl.pallas_call(inner, name=name, out_shape=shapes, in_specs=[scalars] * s...  12.6 us
    ppermute x2, waiting for transfers between devices, from_upper(): return lax.ppermute(array, axes, pairs)  12.2 us
    ppermute x8, waiting for transfers between devices, from_core(): return lax.ppermute(array, axes, pairs)  8.59 us
    ppermute x6, starting transfers between devices, to_row(): return lax.ppermute(array, axes, pairs)  7.11 us
    ppermute x6, waiting for transfers between devices, to_row(): return lax.ppermute(array, axes, pairs)  6.47 us
    ppermute x2, starting transfers between devices, from_upper(): return lax.ppermute(array, axes, pairs)  5.9 us
    ppermute x2, waiting for transfers between devices, from_twin(): return lax.ppermute(array, axes, pairs)  5.7 us
  transfers between devices with their start and end apart: 19, of which 14 were waited for; matrix products, arithmetic and copies ran while one was open for 0% of the time, Pallas kernels for 5%

profile of v5, /device:TPU:0, one launch (start us, length us, event | category | flops | bytes accessed | tf_op | source)
XLA Modules:
  0.0 101.4 jit_solution(218816464010895421)
XLA Ops:
  0.6 3.0 %collective-permute-start.6 = (f32[2,1,256,256]{3,2,1,0:T(8,128)}, f32[2,1,256,256]{3,2,1,0:T(8,128)S(1)}, u32[]{:S(2)}, u32[]{:S(2)}) collective-permute-start(f32[2,1,256,256]{3,2,1,0:T(8,128)} %refs_5_.2), channel_id=1, source_target_pairs={{2,0},{3,1},{0,2},{1,3},{6,4},{7,5},{4,6},{5,7},{10,8},{11,9},{8,1... | collective-permute-start | bytes 1572872 | tf_op jit(solution)/shard_map/ppermute | solution.py:83
  3.7 1.3 %cut.1 = (f32[2,64,256]{2,1,0:T(8,128)S(1)}, f32[2,64,256]{2,1,0:T(8,128)S(1)}, f32[2,64,256]{2,1,0:T(8,128)S(1)}, f32[2,64,256]{2,1,0:T(8,128)S(1)}, f32[1,128,256]{2,1,0:T(8,128)S(1)}) custom-call(s32[2,8]{1,0:T(2,128)} %bitcast.1, s32[8]{0:T(128)} %refs_1_.10, f32[2,128,512]{2,1,0:T(8,128)} %refs_1_.11, f32[1,256,256]{2,1,0:T(8,128)} %refs_0_.1), custom_call_target="tpu_custom_call" | custom-call | tf_op jit(solution)/shard_map/cut/pallas_call | solution.py:622
  4.9 1.6 %collective-permute-start = (f32[2,64,256]{2,1,0:T(8,128)S(1)}, f32[2,64,256]{2,1,0:T(8,128)S(1)}, u32[]{:S(2)}, u32[]{:S(2)}) collective-permute-start(f32[2,64,256]{2,1,0:T(8,128)S(1)} %get-tuple-element.24), channel_id=1, source_target_pairs={{0,4},{1,5},{2,6},{3,7},{4,0},{5,1},{6,2},{7,3},{8,12},{9,13},{10,... | collective-permute-start | bytes 393224 | tf_op jit(solution)/shard_map/ppermute | solution.py:95
  6.5 1.6 %collective-permute-start.1 = (f32[2,64,256]{2,1,0:T(8,128)S(1)}, f32[2,64,256]{2,1,0:T(8,128)S(1)}, u32[]{:S(2)}, u32[]{:S(2)}) collective-permute-start(f32[2,64,256]{2,1,0:T(8,128)S(1)} %get-tuple-element.25), channel_id=1, source_target_pairs={{0,8},{1,9},{2,10},{3,11},{4,12},{5,13},{6,14},{7,15},{8,0},{9,1},... | collective-permute-start | bytes 393224 | tf_op jit(solution)/shard_map/ppermute | solution.py:95
  8.5 4.6 %collective-permute-start.4 = (f32[1,128,256]{2,1,0:T(8,128)S(1)}, f32[1,128,256]{2,1,0:T(8,128)S(1)}, u32[]{:S(2)}, u32[]{:S(2)}) collective-permute-start(f32[1,128,256]{2,1,0:T(8,128)S(1)} %get-tuple-element.28), channel_id=1, source_target_pairs={{18,2},{19,3},{22,6},{23,7},{26,10},{27,11},{30,14},{31,15},{0,16}... | collective-permute-start | bytes 393224 | tf_op jit(solution)/shard_map/ppermute | solution.py:649
  14.9 2.7 %collective-permute-start.3 = (f32[1,2,2,64,256]{4,3,2,1,0:T(8,128)S(1)}, f32[1,2,2,64,256]{4,3,2,1,0:T(8,128)S(1)}, u32[]{:S(2)}, u32[]{:S(2)}) collective-permute-start(f32[1,2,2,64,256]{4,3,2,1,0:T(8,128)S(1)} %choose.3.refs_1_), channel_id=1, source_target_pairs={{16,0},{17,1},{18,2},{19,3},{20,4},{21,5},{22,6},{23,7},{24,8},{25... | collective-permute-start | bytes 786440 | tf_op jit(solution)/shard_map/ppermute | solution.py:69
  17.6 1.3 %collective-permute-done.5.refs_2_ = f32[1,128,256]{2,1,0:T(8,128)S(1)} collective-permute-done((f32[1,128,256]{2,1,0:T(8,128)S(1)}, f32[1,128,256]{2,1,0:T(8,128)S(1)}, u32[]{:S(2)}, u32[]{:S(2)}) %collective-permute-start.5) | collective-permute-done | bytes 131104 | tf_op jit(solution)/shard_map/ppermute | solution.py:76
  19.7 9.0 %collective-permute-done.3.refs_2_ = f32[1,2,2,64,256]{4,3,2,1,0:T(8,128)S(1)} collective-permute-done((f32[1,2,2,64,256]{4,3,2,1,0:T(8,128)S(1)}, f32[1,2,2,64,256]{4,3,2,1,0:T(8,128)S(1)}, u32[]{:S(2)}, u32[]{:S(2)}) %collective-permute-start.3) | collective-permute-done | bytes 262176 | tf_op jit(solution)/shard_map/ppermute | solution.py:69
  30.6 2.1 %far.1 = (f32[1,2,256,256]{3,2,1,0:T(8,128)S(1)}, f32[1,256,256]{2,1,0:T(8,128)S(1)}, f32[1,2,256,256]{3,2,1,0:T(8,128)S(1)}, f32[2,1,2,32,256]{4,3,2,1,0:T(8,128)S(1)}) custom-call(s32[2,8]{1,0:T(2,128)S(1)} %bitcast.4, f32[1,2,2,64,256]{4,3,2,1,0:T(8,128)S(1)} %choose.3.refs_1_, f32[1,2,2,64,256]{4,3,2,1,0:T(8,128)S(1)} %collective-permute-done.3.refs_2_, ...), custom_call_target="tpu_custom_call" | custom-call | tf_op jit(solution)/shard_map/far/pallas_call | solution.py:588
  32.9 1.4 %collective-permute-done.9.refs_1_ = f32[1,256,256]{2,1,0:T(8,128)S(1)} collective-permute-done((f32[1,256,256]{2,1,0:T(8,128)S(1)}, f32[1,256,256]{2,1,0:T(8,128)S(1)}, u32[]{:S(2)}, u32[]{:S(2)}) %collective-permute-start.9) | collective-permute-done | bytes 262176 | tf_op jit(solution)/shard_map/ppermute | solution.py:76
  35.2 15.3 %all_to_all.10.refs_0_ = f32[8,80,256]{2,1,0:T(8,128)S(1)} all-to-all(f32[8,80,256]{2,1,0:T(8,128)S(1)} %gradient.1), channel_id=1, replica_groups={{0,4,8,12,2,6,10,14},{1,5,9,13,3,7,11,15},{16,20,24,28,18,22,26,30},{17..., dimensions={0} | all-to-all | bytes 1310720 | tf_op jit(solution)/shard_map/all_to_all | solution.py:98
  50.5 3.2 %collective-permute-start.10 = (f32[80,256]{1,0:T(8,128)S(1)}, f32[80,256]{1,0:T(8,128)S(1)}, u32[]{:S(2)}, u32[]{:S(2)}) collective-permute-start(f32[80,256]{1,0:T(8,128)S(1)} %sum.1.refs_1_), channel_id=1, source_target_pairs={{16,0},{17,1},{18,2},{19,3},{20,4},{21,5},{22,6},{23,7},{24,8},{25... | collective-permute-start | bytes 245768 | tf_op jit(solution)/shard_map/ppermute | solution.py:69
  53.8 3.2 %collective-permute-done.10.refs_2_ = f32[80,256]{1,0:T(8,128)S(1)} collective-permute-done((f32[80,256]{1,0:T(8,128)S(1)}, f32[80,256]{1,0:T(8,128)S(1)}, u32[]{:S(2)}, u32[]{:S(2)}) %collective-permute-start.10) | collective-permute-done | bytes 81952 | tf_op jit(solution)/shard_map/ppermute | solution.py:69
  57.1 16.2 %all_to_all.11.refs_0_.refs_4_ = f32[8,2,1,2,32,256]{5,4,3,2,1,0:T(8,128)S(1)} all-to-all(f32[8,2,1,2,32,256]{5,4,3,2,1,0:T(8,128)S(1)} %step.1), channel_id=1, replica_groups={{0,4,8,12,2,6,10,14},{1,5,9,13,3,7,11,15},{16,20,24,28,18,22,26,30},{17..., dimensions={0} | all-to-all | bytes 2097152 | tf_op jit(solution)/shard_map/all_to_all | solution.py:98
  73.3 2.1 %again.1 = (f32[2,1,256,256]{3,2,1,0:T(8,128)}, f32[256,256]{1,0:T(8,128)S(1)}, f32[1,256,256]{2,1,0:T(8,128)S(1)}, f32[1,2,512,256]{3,2,1,0:T(8,128)S(1)}) custom-call(f32[8,2,1,2,32,256]{5,4,3,2,1,0:T(8,128)S(1)} %all_to_all.11.refs_0_.refs_4_, f32[1,2,256,256]{3,2,1,0:T(8,128)S(1)} %get-tuple-element.34.refs_3_.refs_1_, ...), custom_call_target="tpu_custom_call" | custom-call | tf_op jit(solution)/shard_map/again/pallas_call | solution.py:588
  75.4 1.5 %collective-permute-done.12.refs_2_ = f32[1,256,256]{2,1,0:T(8,128)S(1)} collective-permute-done((f32[1,256,256]{2,1,0:T(8,128)S(1)}, f32[1,256,256]{2,1,0:T(8,128)S(1)}, u32[]{:S(2)}, u32[]{:S(2)}) %collective-permute-start.12) | collective-permute-done | bytes 262176 | tf_op jit(solution)/shard_map/ppermute | solution.py:76
  76.9 2.0 %terms.1 = (f32[1,2,2,64,256]{4,3,2,1,0:T(8,128)S(1)}, f32[1,2,2,64,256]{4,3,2,1,0:T(8,128)S(1)}) custom-call(s32[2,8]{1,0:T(2,128)S(1)} %bitcast.5, f32[1,256,256]{2,1,0:T(8,128)S(1)} %get-tuple-element.38.refs_1_, f32[1,256,256]{2,1,0:T(8,128)S(1)} %collective-permute-done.12.refs_2_, f32[1,256,256]{2,1,0:T(8,128)S(1)} %order.1.refs_2_.refs_3_, ...), custom_call_target="tpu_custom_call" | custom-call | tf_op jit(solution)/shard_map/terms/pallas_call | solution.py:588
  79.1 1.4 %collective-permute-done.13.refs_3_ = f32[1,2,2,64,256]{4,3,2,1,0:T(8,128)S(1)} collective-permute-done((f32[1,2,2,64,256]{4,3,2,1,0:T(8,128)S(1)}, f32[1,2,2,64,256]{4,3,2,1,0:T(8,128)S(1)}, u32[]{:S(2)}, u32[]{:S(2)}) %collective-permute-start.13) | collective-permute-done | bytes 262176 | tf_op jit(solution)/shard_map/ppermute | solution.py:76
  82.3 2.4 %collective-permute-start.16 = (f32[2,64,256]{2,1,0:T(8,128)S(1)}, f32[2,64,256]{2,1,0:T(8,128)S(1)}, u32[]{:S(2)}, u32[]{:S(2)}) collective-permute-start(f32[2,64,256]{2,1,0:T(8,128)S(1)} %get-tuple-element.45), channel_id=1, source_target_pairs={{0,12},{1,13},{2,14},{3,15},{4,8},{5,9},{6,10},{7,11},{8,4},{9,5},... | collective-permute-start | bytes 393224 | tf_op jit(solution)/shard_map/ppermute | solution.py:95
  84.8 2.0 %collective-permute-done.14.refs_3_ = f32[2,64,256]{2,1,0:T(8,128)S(1)} collective-permute-done((f32[2,64,256]{2,1,0:T(8,128)S(1)}, f32[2,64,256]{2,1,0:T(8,128)S(1)}, u32[]{:S(2)}, u32[]{:S(2)}) %collective-permute-start.14) | collective-permute-done | bytes 131104 | tf_op jit(solution)/shard_map/ppermute | solution.py:95
  86.8 1.0 %collective-permute-done.15.refs_4_ = f32[2,64,256]{2,1,0:T(8,128)S(1)} collective-permute-done((f32[2,64,256]{2,1,0:T(8,128)S(1)}, f32[2,64,256]{2,1,0:T(8,128)S(1)}, u32[]{:S(2)}, u32[]{:S(2)}) %collective-permute-start.15) | collective-permute-done | bytes 131104 | tf_op jit(solution)/shard_map/ppermute | solution.py:95
  87.8 3.0 %collective-permute-done.16.refs_5_ = f32[2,64,256]{2,1,0:T(8,128)S(1)} collective-permute-done((f32[2,64,256]{2,1,0:T(8,128)S(1)}, f32[2,64,256]{2,1,0:T(8,128)S(1)}, u32[]{:S(2)}, u32[]{:S(2)}) %collective-permute-start.16) | collective-permute-done | bytes 131104 | tf_op jit(solution)/shard_map/ppermute | solution.py:95
  93.2 5.7 %collective-permute-done.17.refs_3_ = f32[2,64,512]{2,1,0:T(8,128)S(1)} collective-permute-done((f32[2,64,512]{2,1,0:T(8,128)S(1)}, f32[2,64,512]{2,1,0:T(8,128)S(1)}, u32[]{:S(2)}, u32[]{:S(2)}) %collective-permute-start.17) | collective-permute-done | bytes 262176 | tf_op jit(solution)/shard_map/ppermute | solution.py:83
  99.0 1.5 %collective-permute-done.18.refs_1_ = f32[2,64,512]{2,1,0:T(8,128)S(1)} collective-permute-done((f32[2,64,512]{2,1,0:T(8,128)S(1)}, f32[2,64,512]{2,1,0:T(8,128)S(1)}, u32[]{:S(2)}, u32[]{:S(2)}) %collective-permute-start.18) | collective-permute-done | bytes 262176 | tf_op jit(solution)/shard_map/ppermute | solution.py:76
  (45 shorter events, 11.4 us)
Async XLA Ops:
  0.6 28.0 %collective-permute-start.6 = (f32[2,1,256,256]{3,2,1,0:T(8,128)}, f32[2,1,256,256]{3,2,1,0:T(8,128)S(1)}, u32[]{:S(2)}, u32[]{:S(2)}) collective-permute-start(f32[2,1,256,256]{3,2,1,0:T(8,128)} %refs_5_.2), channel_id=1, source_target_pairs={{2,0},{3,1},{0,2},{1,3},{6,4},{7,5},{4,6},{5,7},{10,8},{11,9},{8,1... | collective-permute-start | bytes 1572872 | tf_op jit(solution)/shard_map/ppermute | solution.py:83
  4.9 8.9 %collective-permute-start = (f32[2,64,256]{2,1,0:T(8,128)S(1)}, f32[2,64,256]{2,1,0:T(8,128)S(1)}, u32[]{:S(2)}, u32[]{:S(2)}) collective-permute-start(f32[2,64,256]{2,1,0:T(8,128)S(1)} %get-tuple-element.24), channel_id=1, source_target_pairs={{0,4},{1,5},{2,6},{3,7},{4,0},{5,1},{6,2},{7,3},{8,12},{9,13},{10,... | collective-permute-start | bytes 393224 | tf_op jit(solution)/shard_map/ppermute | solution.py:95
  6.5 7.3 %collective-permute-start.1 = (f32[2,64,256]{2,1,0:T(8,128)S(1)}, f32[2,64,256]{2,1,0:T(8,128)S(1)}, u32[]{:S(2)}, u32[]{:S(2)}) collective-permute-start(f32[2,64,256]{2,1,0:T(8,128)S(1)} %get-tuple-element.25), channel_id=1, source_target_pairs={{0,8},{1,9},{2,10},{3,11},{4,12},{5,13},{6,14},{7,15},{8,0},{9,1},... | collective-permute-start | bytes 393224 | tf_op jit(solution)/shard_map/ppermute | solution.py:95
  8.1 6.2 %collective-permute-start.2 = (f32[2,64,256]{2,1,0:T(8,128)S(1)}, f32[2,64,256]{2,1,0:T(8,128)S(1)}, u32[]{:S(2)}, u32[]{:S(2)}) collective-permute-start(f32[2,64,256]{2,1,0:T(8,128)S(1)} %get-tuple-element.26), channel_id=1, source_target_pairs={{0,12},{1,13},{2,14},{3,15},{4,8},{5,9},{6,10},{7,11},{8,4},{9,5},... | collective-permute-start | bytes 393224 | tf_op jit(solution)/shard_map/ppermute | solution.py:95
  8.5 9.1 %collective-permute-start.4 = (f32[1,128,256]{2,1,0:T(8,128)S(1)}, f32[1,128,256]{2,1,0:T(8,128)S(1)}, u32[]{:S(2)}, u32[]{:S(2)}) collective-permute-start(f32[1,128,256]{2,1,0:T(8,128)S(1)} %get-tuple-element.28), channel_id=1, source_target_pairs={{18,2},{19,3},{22,6},{23,7},{26,10},{27,11},{30,14},{31,15},{0,16}... | collective-permute-start | bytes 393224 | tf_op jit(solution)/shard_map/ppermute | solution.py:649
  13.1 17.4 %copy-start.4 = (f32[2,1,256,256]{3,2,1,0:T(8,128)S(1)}, f32[2,1,256,256]{3,2,1,0:T(8,128)}, u32[]{:S(2)}) copy-start(f32[2,1,256,256]{3,2,1,0:T(8,128)} %refs_5_.2) | copy-start | bytes 1572868
  13.8 5.2 %copy-start.3 = (f32[1,256,256]{2,1,0:T(8,128)S(1)}, f32[1,256,256]{2,1,0:T(8,128)}, u32[]{:S(2)}) copy-start(f32[1,256,256]{2,1,0:T(8,128)} %refs_0_.1) | copy-start | bytes 786436
  14.2 16.3 %copy-start.1 = (bf16[2,2,256,256]{3,2,1,0:T(8,128)(2,1)S(1)}, bf16[2,2,256,256]{3,2,1,0:T(8,128)(2,1)}, u32[]{:S(2)}) copy-start(bf16[2,2,256,256]{3,2,1,0:T(8,128)(2,1)} %constant.4.clone.refs_7_.refs_5_.refs_2_.refs_6_) | copy-start | bytes 1572868
  14.9 15.7 %copy-start = (bf16[2,2,256,256]{3,2,1,0:T(8,128)(2,1)S(1)}, bf16[2,2,256,256]{3,2,1,0:T(8,128)(2,1)}, u32[]{:S(2)}) copy-start(bf16[2,2,256,256]{3,2,1,0:T(8,128)(2,1)} %constant.5.clone.refs_8_.refs_6_.refs_3_.refs_7_) | copy-start | bytes 1572868
  14.9 13.7 %collective-permute-start.3 = (f32[1,2,2,64,256]{4,3,2,1,0:T(8,128)S(1)}, f32[1,2,2,64,256]{4,3,2,1,0:T(8,128)S(1)}, u32[]{:S(2)}, u32[]{:S(2)}) collective-permute-start(f32[1,2,2,64,256]{4,3,2,1,0:T(8,128)S(1)} %choose.3.refs_1_), channel_id=1, source_target_pairs={{16,0},{17,1},{18,2},{19,3},{20,4},{21,5},{22,6},{23,7},{24,8},{25... | collective-permute-start | bytes 786440 | tf_op jit(solution)/shard_map/ppermute | solution.py:69
  17.6 1.3 %collective-permute-start.5 = (f32[1,128,256]{2,1,0:T(8,128)S(1)}, f32[1,128,256]{2,1,0:T(8,128)S(1)}, u32[]{:S(2)}, u32[]{:S(2)}) collective-permute-start(f32[1,128,256]{2,1,0:T(8,128)S(1)} %collective-permute-done.4.refs_1_), channel_id=1, source_target_pairs={{1,0},{0,1},{3,2},{2,3},{5,4},{4,5},{7,6},{6,7},{9,8},{8,9},{11,10... | collective-permute-start | bytes 393224 | tf_op jit(solution)/shard_map/ppermute | solution.py:76
  28.7 1.5 %collective-permute-start.8 = (f32[1,2,2,64,256]{4,3,2,1,0:T(8,128)S(1)}, f32[1,2,2,64,256]{4,3,2,1,0:T(8,128)S(1)}, u32[]{:S(2)}, u32[]{:S(2)}) collective-permute-start(f32[1,2,2,64,256]{4,3,2,1,0:T(8,128)S(1)} %collective-permute-done.3.refs_2_), channel_id=1, source_target_pairs={{1,0},{0,1},{3,2},{2,3},{5,4},{4,5},{7,6},{6,7},{9,8},{8,9},{11,10... | collective-permute-start | bytes 786440 | tf_op jit(solution)/shard_map/ppermute | solution.py:76
  28.7 1.9 %collective-permute-start.7 = (f32[1,2,2,64,256]{4,3,2,1,0:T(8,128)S(1)}, f32[1,2,2,64,256]{4,3,2,1,0:T(8,128)S(1)}, u32[]{:S(2)}, u32[]{:S(2)}) collective-permute-start(f32[1,2,2,64,256]{4,3,2,1,0:T(8,128)S(1)} %choose.3.refs_1_), channel_id=1, source_target_pairs={{1,0},{0,1},{3,2},{2,3},{5,4},{4,5},{7,6},{6,7},{9,8},{8,9},{11,10... | collective-permute-start | bytes 786440 | tf_op jit(solution)/shard_map/ppermute | solution.py:76
  32.7 1.6 %collective-permute-start.9 = (f32[1,256,256]{2,1,0:T(8,128)S(1)}, f32[1,256,256]{2,1,0:T(8,128)S(1)}, u32[]{:S(2)}, u32[]{:S(2)}) collective-permute-start(f32[1,256,256]{2,1,0:T(8,128)S(1)} %get-tuple-element.32.refs_0_), channel_id=1, source_target_pairs={{1,0},{0,1},{3,2},{2,3},{5,4},{4,5},{7,6},{6,7},{9,8},{8,9},{11,10... | collective-permute-start | bytes 786440 | tf_op jit(solution)/shard_map/ppermute | solution.py:76
  50.5 6.4 %collective-permute-start.10 = (f32[80,256]{1,0:T(8,128)S(1)}, f32[80,256]{1,0:T(8,128)S(1)}, u32[]{:S(2)}, u32[]{:S(2)}) collective-permute-start(f32[80,256]{1,0:T(8,128)S(1)} %sum.1.refs_1_), channel_id=1, source_target_pairs={{16,0},{17,1},{18,2},{19,3},{20,4},{21,5},{22,6},{23,7},{24,8},{25... | collective-permute-start | bytes 245768 | tf_op jit(solution)/shard_map/ppermute | solution.py:69
  75.4 1.5 %collective-permute-start.12 = (f32[1,256,256]{2,1,0:T(8,128)S(1)}, f32[1,256,256]{2,1,0:T(8,128)S(1)}, u32[]{:S(2)}, u32[]{:S(2)}) collective-permute-start(f32[1,256,256]{2,1,0:T(8,128)S(1)} %get-tuple-element.38.refs_1_), channel_id=1, source_target_pairs={{1,0},{0,1},{3,2},{2,3},{5,4},{4,5},{7,6},{6,7},{9,8},{8,9},{11,10... | collective-permute-start | bytes 786440 | tf_op jit(solution)/shard_map/ppermute | solution.py:76
  78.9 1.6 %collective-permute-start.13 = (f32[1,2,2,64,256]{4,3,2,1,0:T(8,128)S(1)}, f32[1,2,2,64,256]{4,3,2,1,0:T(8,128)S(1)}, u32[]{:S(2)}, u32[]{:S(2)}) collective-permute-start(f32[1,2,2,64,256]{4,3,2,1,0:T(8,128)S(1)} %get-tuple-element.41), channel_id=1, source_target_pairs={{1,0},{0,1},{3,2},{2,3},{5,4},{4,5},{7,6},{6,7},{9,8},{8,9},{11,10... | collective-permute-start | bytes 786440 | tf_op jit(solution)/shard_map/ppermute | solution.py:76
  81.2 5.6 %collective-permute-start.14 = (f32[2,64,256]{2,1,0:T(8,128)S(1)}, f32[2,64,256]{2,1,0:T(8,128)S(1)}, u32[]{:S(2)}, u32[]{:S(2)}) collective-permute-start(f32[2,64,256]{2,1,0:T(8,128)S(1)} %get-tuple-element.43), channel_id=1, source_target_pairs={{0,4},{1,5},{2,6},{3,7},{4,0},{5,1},{6,2},{7,3},{8,12},{9,13},{10,... | collective-permute-start | bytes 393224 | tf_op jit(solution)/shard_map/ppermute | solution.py:95
  81.5 6.4 %collective-permute-start.15 = (f32[2,64,256]{2,1,0:T(8,128)S(1)}, f32[2,64,256]{2,1,0:T(8,128)S(1)}, u32[]{:S(2)}, u32[]{:S(2)}) collective-permute-start(f32[2,64,256]{2,1,0:T(8,128)S(1)} %get-tuple-element.44), channel_id=1, source_target_pairs={{0,8},{1,9},{2,10},{3,11},{4,12},{5,13},{6,14},{7,15},{8,0},{9,1},... | collective-permute-start | bytes 393224 | tf_op jit(solution)/shard_map/ppermute | solution.py:95
  82.3 8.5 %collective-permute-start.16 = (f32[2,64,256]{2,1,0:T(8,128)S(1)}, f32[2,64,256]{2,1,0:T(8,128)S(1)}, u32[]{:S(2)}, u32[]{:S(2)}) collective-permute-start(f32[2,64,256]{2,1,0:T(8,128)S(1)} %get-tuple-element.45), channel_id=1, source_target_pairs={{0,12},{1,13},{2,14},{3,15},{4,8},{5,9},{6,10},{7,11},{8,4},{9,5},... | collective-permute-start | bytes 393224 | tf_op jit(solution)/shard_map/ppermute | solution.py:95
  84.8 7.5 %collective-permute-start.11 = (f32[256,256]{1,0:T(8,128)S(1)}, f32[256,256]{1,0:T(8,128)S(1)}, u32[]{:S(2)}, u32[]{:S(2)}) collective-permute-start(f32[256,256]{1,0:T(8,128)S(1)} %get-tuple-element.37.refs_2_), channel_id=1, source_target_pairs={{1,0},{0,1},{3,2},{2,3},{5,4},{4,5},{7,6},{6,7},{9,8},{8,9},{11,10... | collective-permute-start | bytes 786440 | tf_op jit(solution)/shard_map/ppermute | solution.py:76
  91.6 7.3 %copy-start.2 = (f32[2,128,512]{2,1,0:T(8,128)S(1)}, f32[2,128,512]{2,1,0:T(8,128)}, u32[]{:S(2)}) copy-start(f32[2,128,512]{2,1,0:T(8,128)} %refs_1_.11) | copy-start | bytes 1572868
  91.6 7.3 %collective-permute-start.17 = (f32[2,64,512]{2,1,0:T(8,128)S(1)}, f32[2,64,512]{2,1,0:T(8,128)S(1)}, u32[]{:S(2)}, u32[]{:S(2)}) collective-permute-start(f32[2,64,512]{2,1,0:T(8,128)S(1)} %place.1.refs_2_), channel_id=1, source_target_pairs={{2,0},{3,1},{0,2},{1,3},{6,4},{7,5},{4,6},{5,7},{10,8},{11,9},{8,1... | collective-permute-start | bytes 786440 | tf_op jit(solution)/shard_map/ppermute | solution.py:83
  99.0 1.6 %collective-permute-start.18 = (f32[2,64,512]{2,1,0:T(8,128)S(1)}, f32[2,64,512]{2,1,0:T(8,128)S(1)}, u32[]{:S(2)}, u32[]{:S(2)}) collective-permute-start(f32[2,64,512]{2,1,0:T(8,128)S(1)} %update.1.refs_0_), channel_id=1, source_target_pairs={{1,0},{0,1},{3,2},{2,3},{5,4},{4,5},{7,6},{6,7},{9,8},{8,9},{11,10... | collective-permute-start | bytes 786440 | tf_op jit(solution)/shard_map/ppermute | solution.py:76
  (2 other events, 9.3 us)

commit v6 on v5

--- a/solution.py
+++ b/solution.py
@@ -667,8 +667,7 @@
         scratch=[(cores, layout.part, length)],
     )
     parts = from_uppers(chosen)
-    held, roots, *received = lax.optimization_barrier((chosen, roots, *probes[1:]))
-    probes = [probe_modes, *received]
+    held, roots = lax.optimization_barrier((chosen, roots))
     strips = list(parts)
     for step in range(1, cores):
         strips += [layout.from_core(part, step) for part in [held] + parts[1:]]

time: 102 us -> 101 us (level)
  starting transfers between devices: 22.3 us -> 20.9 us
    ppermute x2, starting transfers between devices: 3.65 us -> 2.55 us  [from_twin(): return lax.ppermute(array, axes, pairs)]
    ppermute x6, starting transfers between devices: 7.11 us -> 8.14 us  [to_row(): return lax.ppermute(array, axes, pairs)]
  transfers between devices with their start and end apart: 19 -> 19, of which waited for: 14 -> 12; matrix products, arithmetic and copies ran while one was open for 0% -> 0% of each run, Pallas kernels for 5% -> 4%
where the time goes in v6:
time: 101 us
  waiting for transfers between devices  33 us (33%)
  blocking collectives  32.2 us (32%)
  starting transfers between devices  20.9 us (21%)
  Pallas kernels  13.9 us (14%)
    all_to_all x2, blocking collectives, within_cube(): lax.all_to_all(array, axes, split_axis=0, concat_axis=0, tiled=True, axis...  32.2 us
    pallas_call x14, Pallas kernels, call(): pl.pallas_call(inner, name=name, out_shape=shapes, in_specs=[scalars] * s...  12.6 us
    ppermute x2, waiting for transfers between devices, from_upper(): return lax.ppermute(array, axes, pairs)  12.5 us
    ppermute x8, waiting for transfers between devices, from_core(): return lax.ppermute(array, axes, pairs)  8.72 us
    ppermute x6, starting transfers between devices, to_row(): return lax.ppermute(array, axes, pairs)  8.14 us
    ppermute x6, waiting for transfers between devices, to_row(): return lax.ppermute(array, axes, pairs)  6.05 us
    ppermute x2, waiting for transfers between devices, from_twin(): return lax.ppermute(array, axes, pairs)  5.7 us
    ppermute x2, starting transfers between devices, from_upper(): return lax.ppermute(array, axes, pairs)  4.92 us
  transfers between devices with their start and end apart: 19, of which 12 were waited for; matrix products, arithmetic and copies ran while one was open for 0% of the time, Pallas kernels for 4%

profile of v6, /device:TPU:0, one launch (start us, length us, event | category | flops | bytes accessed | tf_op | source)
XLA Modules:
  0.0 101.0 jit_solution(4417542820145917131)
XLA Ops:
  0.6 1.3 %cut.1 = (f32[2,64,256]{2,1,0:T(8,128)S(1)}, f32[2,64,256]{2,1,0:T(8,128)S(1)}, f32[2,64,256]{2,1,0:T(8,128)S(1)}, f32[2,64,256]{2,1,0:T(8,128)S(1)}, f32[1,128,256]{2,1,0:T(8,128)S(1)}) custom-call(s32[2,8]{1,0:T(2,128)} %bitcast.1, s32[8]{0:T(128)} %refs_1_.10, f32[2,128,512]{2,1,0:T(8,128)} %refs_1_.11, f32[1,256,256]{2,1,0:T(8,128)} %refs_0_.1), custom_call_target="tpu_custom_call" | custom-call | tf_op jit(solution)/shard_map/cut/pallas_call | solution.py:622
  2.0 3.0 %collective-permute-start = (f32[2,64,256]{2,1,0:T(8,128)S(1)}, f32[2,64,256]{2,1,0:T(8,128)S(1)}, u32[]{:S(2)}, u32[]{:S(2)}) collective-permute-start(f32[2,64,256]{2,1,0:T(8,128)S(1)} %get-tuple-element.23), channel_id=1, source_target_pairs={{0,4},{1,5},{2,6},{3,7},{4,0},{5,1},{6,2},{7,3},{8,12},{9,13},{10,... | collective-permute-start | bytes 393224 | tf_op jit(solution)/shard_map/ppermute | solution.py:95
  5.0 1.6 %collective-permute-start.1 = (f32[2,64,256]{2,1,0:T(8,128)S(1)}, f32[2,64,256]{2,1,0:T(8,128)S(1)}, u32[]{:S(2)}, u32[]{:S(2)}) collective-permute-start(f32[2,64,256]{2,1,0:T(8,128)S(1)} %get-tuple-element.24), channel_id=1, source_target_pairs={{0,8},{1,9},{2,10},{3,11},{4,12},{5,13},{6,14},{7,15},{8,0},{9,1},... | collective-permute-start | bytes 393224 | tf_op jit(solution)/shard_map/ppermute | solution.py:95
  6.6 1.9 %collective-permute-start.8 = (f32[2,1,256,256]{3,2,1,0:T(8,128)S(1)}, f32[2,1,256,256]{3,2,1,0:T(8,128)S(1)}, u32[]{:S(2)}, u32[]{:S(2)}) collective-permute-start(f32[2,1,256,256]{3,2,1,0:T(8,128)S(1)} %copy-done.4), channel_id=1, source_target_pairs={{2,0},{3,1},{0,2},{1,3},{6,4},{7,5},{4,6},{5,7},{10,8},{11,9},{8,1... | collective-permute-start | bytes 1572872 | tf_op jit(solution)/shard_map/ppermute | solution.py:83
  8.5 4.6 %collective-permute-start.4 = (f32[1,128,256]{2,1,0:T(8,128)S(1)}, f32[1,128,256]{2,1,0:T(8,128)S(1)}, u32[]{:S(2)}, u32[]{:S(2)}) collective-permute-start(f32[1,128,256]{2,1,0:T(8,128)S(1)} %get-tuple-element.27), channel_id=1, source_target_pairs={{18,2},{19,3},{22,6},{23,7},{26,10},{27,11},{30,14},{31,15},{0,16}... | collective-permute-start | bytes 393224 | tf_op jit(solution)/shard_map/ppermute | solution.py:649
  14.5 1.5 %collective-permute-start.3 = (f32[1,2,2,64,256]{4,3,2,1,0:T(8,128)S(1)}, f32[1,2,2,64,256]{4,3,2,1,0:T(8,128)S(1)}, u32[]{:S(2)}, u32[]{:S(2)}) collective-permute-start(f32[1,2,2,64,256]{4,3,2,1,0:T(8,128)S(1)} %choose.3.refs_1_), channel_id=1, source_target_pairs={{16,0},{17,1},{18,2},{19,3},{20,4},{21,5},{22,6},{23,7},{24,8},{25... | collective-permute-start | bytes 786440 | tf_op jit(solution)/shard_map/ppermute | solution.py:69
  16.1 1.3 %collective-permute-done.5.refs_2_ = f32[1,128,256]{2,1,0:T(8,128)S(1)} collective-permute-done((f32[1,128,256]{2,1,0:T(8,128)S(1)}, f32[1,128,256]{2,1,0:T(8,128)S(1)}, u32[]{:S(2)}, u32[]{:S(2)}) %collective-permute-start.5) | collective-permute-done | bytes 131104 | tf_op jit(solution)/shard_map/ppermute | solution.py:76
  18.4 9.3 %collective-permute-done.3.refs_2_ = f32[1,2,2,64,256]{4,3,2,1,0:T(8,128)S(1)} collective-permute-done((f32[1,2,2,64,256]{4,3,2,1,0:T(8,128)S(1)}, f32[1,2,2,64,256]{4,3,2,1,0:T(8,128)S(1)}, u32[]{:S(2)}, u32[]{:S(2)}) %collective-permute-start.3) | collective-permute-done | bytes 262176 | tf_op jit(solution)/shard_map/ppermute | solution.py:69
  27.8 1.5 %collective-permute-done.7.refs_4_ = f32[1,2,2,64,256]{4,3,2,1,0:T(8,128)S(1)} collective-permute-done((f32[1,2,2,64,256]{4,3,2,1,0:T(8,128)S(1)}, f32[1,2,2,64,256]{4,3,2,1,0:T(8,128)S(1)}, u32[]{:S(2)}, u32[]{:S(2)}) %collective-permute-start.7) | collective-permute-done | bytes 262176 | tf_op jit(solution)/shard_map/ppermute | solution.py:76
  29.3 2.1 %far.1 = (f32[1,2,256,256]{3,2,1,0:T(8,128)S(1)}, f32[1,256,256]{2,1,0:T(8,128)S(1)}, f32[1,2,256,256]{3,2,1,0:T(8,128)S(1)}, f32[2,1,2,32,256]{4,3,2,1,0:T(8,128)S(1)}) custom-call(s32[2,8]{1,0:T(2,128)S(1)} %bitcast.4, f32[1,2,2,64,256]{4,3,2,1,0:T(8,128)S(1)} %choose.3.refs_1_, f32[1,2,2,64,256]{4,3,2,1,0:T(8,128)S(1)} %collective-permute-done.3.refs_2_, ...), custom_call_target="tpu_custom_call" | custom-call | tf_op jit(solution)/shard_map/far/pallas_call | solution.py:588
  31.6 1.4 %collective-permute-done.9.refs_1_ = f32[1,256,256]{2,1,0:T(8,128)S(1)} collective-permute-done((f32[1,256,256]{2,1,0:T(8,128)S(1)}, f32[1,256,256]{2,1,0:T(8,128)S(1)}, u32[]{:S(2)}, u32[]{:S(2)}) %collective-permute-start.9) | collective-permute-done | bytes 262176 | tf_op jit(solution)/shard_map/ppermute | solution.py:76
  33.9 16.0 %all_to_all.10.refs_0_ = f32[8,80,256]{2,1,0:T(8,128)S(1)} all-to-all(f32[8,80,256]{2,1,0:T(8,128)S(1)} %gradient.1), channel_id=1, replica_groups={{0,4,8,12,2,6,10,14},{1,5,9,13,3,7,11,15},{16,20,24,28,18,22,26,30},{17..., dimensions={0} | all-to-all | bytes 1310720 | tf_op jit(solution)/shard_map/all_to_all | solution.py:98
  50.0 3.4 %collective-permute-start.10 = (f32[80,256]{1,0:T(8,128)S(1)}, f32[80,256]{1,0:T(8,128)S(1)}, u32[]{:S(2)}, u32[]{:S(2)}) collective-permute-start(f32[80,256]{1,0:T(8,128)S(1)} %sum.1.refs_1_), channel_id=1, source_target_pairs={{16,0},{17,1},{18,2},{19,3},{20,4},{21,5},{22,6},{23,7},{24,8},{25... | collective-permute-start | bytes 245768 | tf_op jit(solution)/shard_map/ppermute | solution.py:69
  53.3 3.2 %collective-permute-done.10.refs_2_ = f32[80,256]{1,0:T(8,128)S(1)} collective-permute-done((f32[80,256]{1,0:T(8,128)S(1)}, f32[80,256]{1,0:T(8,128)S(1)}, u32[]{:S(2)}, u32[]{:S(2)}) %collective-permute-start.10) | collective-permute-done | bytes 81952 | tf_op jit(solution)/shard_map/ppermute | solution.py:69
  56.6 16.2 %all_to_all.11.refs_0_.refs_4_ = f32[8,2,1,2,32,256]{5,4,3,2,1,0:T(8,128)S(1)} all-to-all(f32[8,2,1,2,32,256]{5,4,3,2,1,0:T(8,128)S(1)} %step.1), channel_id=1, replica_groups={{0,4,8,12,2,6,10,14},{1,5,9,13,3,7,11,15},{16,20,24,28,18,22,26,30},{17..., dimensions={0} | all-to-all | bytes 2097152 | tf_op jit(solution)/shard_map/all_to_all | solution.py:98
  72.8 2.1 %again.1 = (f32[2,1,256,256]{3,2,1,0:T(8,128)}, f32[256,256]{1,0:T(8,128)S(1)}, f32[1,256,256]{2,1,0:T(8,128)S(1)}, f32[1,2,512,256]{3,2,1,0:T(8,128)S(1)}) custom-call(f32[8,2,1,2,32,256]{5,4,3,2,1,0:T(8,128)S(1)} %all_to_all.11.refs_0_.refs_4_, f32[1,2,256,256]{3,2,1,0:T(8,128)S(1)} %get-tuple-element.32.refs_3_.refs_1_, ...), custom_call_target="tpu_custom_call" | custom-call | tf_op jit(solution)/shard_map/again/pallas_call | solution.py:588
  74.9 1.5 %collective-permute-done.12.refs_2_ = f32[1,256,256]{2,1,0:T(8,128)S(1)} collective-permute-done((f32[1,256,256]{2,1,0:T(8,128)S(1)}, f32[1,256,256]{2,1,0:T(8,128)S(1)}, u32[]{:S(2)}, u32[]{:S(2)}) %collective-permute-start.12) | collective-permute-done | bytes 262176 | tf_op jit(solution)/shard_map/ppermute | solution.py:76
  76.4 2.0 %terms.1 = (f32[1,2,2,64,256]{4,3,2,1,0:T(8,128)S(1)}, f32[1,2,2,64,256]{4,3,2,1,0:T(8,128)S(1)}) custom-call(s32[2,8]{1,0:T(2,128)S(1)} %bitcast.5, f32[1,256,256]{2,1,0:T(8,128)S(1)} %get-tuple-element.36.refs_1_, f32[1,256,256]{2,1,0:T(8,128)S(1)} %collective-permute-done.12.refs_2_, f32[1,256,256]{2,1,0:T(8,128)S(1)} %order.1.refs_2_.refs_3_, ...), custom_call_target="tpu_custom_call" | custom-call | tf_op jit(solution)/shard_map/terms/pallas_call | solution.py:588
  78.7 1.4 %collective-permute-done.13.refs_3_ = f32[1,2,2,64,256]{4,3,2,1,0:T(8,128)S(1)} collective-permute-done((f32[1,2,2,64,256]{4,3,2,1,0:T(8,128)S(1)}, f32[1,2,2,64,256]{4,3,2,1,0:T(8,128)S(1)}, u32[]{:S(2)}, u32[]{:S(2)}) %collective-permute-start.13) | collective-permute-done | bytes 262176 | tf_op jit(solution)/shard_map/ppermute | solution.py:76
  81.9 2.4 %collective-permute-start.16 = (f32[2,64,256]{2,1,0:T(8,128)S(1)}, f32[2,64,256]{2,1,0:T(8,128)S(1)}, u32[]{:S(2)}, u32[]{:S(2)}) collective-permute-start(f32[2,64,256]{2,1,0:T(8,128)S(1)} %get-tuple-element.43), channel_id=1, source_target_pairs={{0,12},{1,13},{2,14},{3,15},{4,8},{5,9},{6,10},{7,11},{8,4},{9,5},... | collective-permute-start | bytes 393224 | tf_op jit(solution)/shard_map/ppermute | solution.py:95
  84.3 2.0 %collective-permute-done.14.refs_3_ = f32[2,64,256]{2,1,0:T(8,128)S(1)} collective-permute-done((f32[2,64,256]{2,1,0:T(8,128)S(1)}, f32[2,64,256]{2,1,0:T(8,128)S(1)}, u32[]{:S(2)}, u32[]{:S(2)}) %collective-permute-start.14) | collective-permute-done | bytes 131104 | tf_op jit(solution)/shard_map/ppermute | solution.py:95
  87.4 3.0 %collective-permute-done.16.refs_5_ = f32[2,64,256]{2,1,0:T(8,128)S(1)} collective-permute-done((f32[2,64,256]{2,1,0:T(8,128)S(1)}, f32[2,64,256]{2,1,0:T(8,128)S(1)}, u32[]{:S(2)}, u32[]{:S(2)}) %collective-permute-start.16) | collective-permute-done | bytes 131104 | tf_op jit(solution)/shard_map/ppermute | solution.py:95
  92.7 5.7 %collective-permute-done.17.refs_3_ = f32[2,64,512]{2,1,0:T(8,128)S(1)} collective-permute-done((f32[2,64,512]{2,1,0:T(8,128)S(1)}, f32[2,64,512]{2,1,0:T(8,128)S(1)}, u32[]{:S(2)}, u32[]{:S(2)}) %collective-permute-start.17) | collective-permute-done | bytes 262176 | tf_op jit(solution)/shard_map/ppermute | solution.py:83
  98.6 1.5 %collective-permute-done.18.refs_1_ = f32[2,64,512]{2,1,0:T(8,128)S(1)} collective-permute-done((f32[2,64,512]{2,1,0:T(8,128)S(1)}, f32[2,64,512]{2,1,0:T(8,128)S(1)}, u32[]{:S(2)}, u32[]{:S(2)}) %collective-permute-start.18) | collective-permute-done | bytes 262176 | tf_op jit(solution)/shard_map/ppermute | solution.py:76
  (45 shorter events, 9.9 us)
Async XLA Ops:
  0.6 5.9 %copy-start.4 = (f32[2,1,256,256]{3,2,1,0:T(8,128)S(1)}, f32[2,1,256,256]{3,2,1,0:T(8,128)}, u32[]{:S(2)}) copy-start(f32[2,1,256,256]{3,2,1,0:T(8,128)} %refs_5_.2) | copy-start | bytes 1572868
  2.0 11.8 %collective-permute-start = (f32[2,64,256]{2,1,0:T(8,128)S(1)}, f32[2,64,256]{2,1,0:T(8,128)S(1)}, u32[]{:S(2)}, u32[]{:S(2)}) collective-permute-start(f32[2,64,256]{2,1,0:T(8,128)S(1)} %get-tuple-element.23), channel_id=1, source_target_pairs={{0,4},{1,5},{2,6},{3,7},{4,0},{5,1},{6,2},{7,3},{8,12},{9,13},{10,... | collective-permute-start | bytes 393224 | tf_op jit(solution)/shard_map/ppermute | solution.py:95
  5.0 8.8 %collective-permute-start.1 = (f32[2,64,256]{2,1,0:T(8,128)S(1)}, f32[2,64,256]{2,1,0:T(8,128)S(1)}, u32[]{:S(2)}, u32[]{:S(2)}) collective-permute-start(f32[2,64,256]{2,1,0:T(8,128)S(1)} %get-tuple-element.24), channel_id=1, source_target_pairs={{0,8},{1,9},{2,10},{3,11},{4,12},{5,13},{6,14},{7,15},{8,0},{9,1},... | collective-permute-start | bytes 393224 | tf_op jit(solution)/shard_map/ppermute | solution.py:95
  6.6 7.3 %collective-permute-start.2 = (f32[2,64,256]{2,1,0:T(8,128)S(1)}, f32[2,64,256]{2,1,0:T(8,128)S(1)}, u32[]{:S(2)}, u32[]{:S(2)}) collective-permute-start(f32[2,64,256]{2,1,0:T(8,128)S(1)} %get-tuple-element.25), channel_id=1, source_target_pairs={{0,12},{1,13},{2,14},{3,15},{4,8},{5,9},{6,10},{7,11},{8,4},{9,5},... | collective-permute-start | bytes 393224 | tf_op jit(solution)/shard_map/ppermute | solution.py:95
  6.6 21.2 %collective-permute-start.8 = (f32[2,1,256,256]{3,2,1,0:T(8,128)S(1)}, f32[2,1,256,256]{3,2,1,0:T(8,128)S(1)}, u32[]{:S(2)}, u32[]{:S(2)}) collective-permute-start(f32[2,1,256,256]{3,2,1,0:T(8,128)S(1)} %copy-done.4), channel_id=1, source_target_pairs={{2,0},{3,1},{0,2},{1,3},{6,4},{7,5},{4,6},{5,7},{10,8},{11,9},{8,1... | collective-permute-start | bytes 1572872 | tf_op jit(solution)/shard_map/ppermute | solution.py:83
  8.5 4.6 %copy-start.6 = (s32[8]{0:T(128)S(1)}, s32[8]{0:T(128)}, u32[]{:S(2)}) copy-start(s32[8]{0:T(128)} %refs_1_.10) | copy-start | bytes 100
  8.5 7.6 %collective-permute-start.4 = (f32[1,128,256]{2,1,0:T(8,128)S(1)}, f32[1,128,256]{2,1,0:T(8,128)S(1)}, u32[]{:S(2)}, u32[]{:S(2)}) collective-permute-start(f32[1,128,256]{2,1,0:T(8,128)S(1)} %get-tuple-element.27), channel_id=1, source_target_pairs={{18,2},{19,3},{22,6},{23,7},{26,10},{27,11},{30,14},{31,15},{0,16}... | collective-permute-start | bytes 393224 | tf_op jit(solution)/shard_map/ppermute | solution.py:649
  13.8 15.5 %copy-start.1 = (bf16[2,2,256,256]{3,2,1,0:T(8,128)(2,1)S(1)}, bf16[2,2,256,256]{3,2,1,0:T(8,128)(2,1)}, u32[]{:S(2)}) copy-start(bf16[2,2,256,256]{3,2,1,0:T(8,128)(2,1)} %constant.4.clone.refs_7_.refs_5_.refs_2_.refs_6_) | copy-start | bytes 1572868
  14.5 14.8 %copy-start = (bf16[2,2,256,256]{3,2,1,0:T(8,128)(2,1)S(1)}, bf16[2,2,256,256]{3,2,1,0:T(8,128)(2,1)}, u32[]{:S(2)}) copy-start(bf16[2,2,256,256]{3,2,1,0:T(8,128)(2,1)} %constant.5.clone.refs_8_.refs_6_.refs_3_.refs_7_) | copy-start | bytes 1572868
  14.5 13.2 %collective-permute-start.3 = (f32[1,2,2,64,256]{4,3,2,1,0:T(8,128)S(1)}, f32[1,2,2,64,256]{4,3,2,1,0:T(8,128)S(1)}, u32[]{:S(2)}, u32[]{:S(2)}) collective-permute-start(f32[1,2,2,64,256]{4,3,2,1,0:T(8,128)S(1)} %choose.3.refs_1_), channel_id=1, source_target_pairs={{16,0},{17,1},{18,2},{19,3},{20,4},{21,5},{22,6},{23,7},{24,8},{25... | collective-permute-start | bytes 786440 | tf_op jit(solution)/shard_map/ppermute | solution.py:69
  16.1 1.3 %collective-permute-start.5 = (f32[1,128,256]{2,1,0:T(8,128)S(1)}, f32[1,128,256]{2,1,0:T(8,128)S(1)}, u32[]{:S(2)}, u32[]{:S(2)}) collective-permute-start(f32[1,128,256]{2,1,0:T(8,128)S(1)} %collective-permute-done.4.refs_1_), channel_id=1, source_target_pairs={{1,0},{0,1},{3,2},{2,3},{5,4},{4,5},{7,6},{6,7},{9,8},{8,9},{11,10... | collective-permute-start | bytes 393224 | tf_op jit(solution)/shard_map/ppermute | solution.py:76
  18.2 9.6 %collective-permute-start.6 = (f32[1,2,2,64,256]{4,3,2,1,0:T(8,128)S(1)}, f32[1,2,2,64,256]{4,3,2,1,0:T(8,128)S(1)}, u32[]{:S(2)}, u32[]{:S(2)}) collective-permute-start(f32[1,2,2,64,256]{4,3,2,1,0:T(8,128)S(1)} %choose.3.refs_1_), channel_id=1, source_target_pairs={{1,0},{0,1},{3,2},{2,3},{5,4},{4,5},{7,6},{6,7},{9,8},{8,9},{11,10... | collective-permute-start | bytes 786440 | tf_op jit(solution)/shard_map/ppermute | solution.py:76
  27.8 1.5 %collective-permute-start.7 = (f32[1,2,2,64,256]{4,3,2,1,0:T(8,128)S(1)}, f32[1,2,2,64,256]{4,3,2,1,0:T(8,128)S(1)}, u32[]{:S(2)}, u32[]{:S(2)}) collective-permute-start(f32[1,2,2,64,256]{4,3,2,1,0:T(8,128)S(1)} %collective-permute-done.3.refs_2_), channel_id=1, source_target_pairs={{1,0},{0,1},{3,2},{2,3},{5,4},{4,5},{7,6},{6,7},{9,8},{8,9},{11,10... | collective-permute-start | bytes 786440 | tf_op jit(solution)/shard_map/ppermute | solution.py:76
  31.4 1.6 %collective-permute-start.9 = (f32[1,256,256]{2,1,0:T(8,128)S(1)}, f32[1,256,256]{2,1,0:T(8,128)S(1)}, u32[]{:S(2)}, u32[]{:S(2)}) collective-permute-start(f32[1,256,256]{2,1,0:T(8,128)S(1)} %get-tuple-element.30.refs_0_), channel_id=1, source_target_pairs={{1,0},{0,1},{3,2},{2,3},{5,4},{4,5},{7,6},{6,7},{9,8},{8,9},{11,10... | collective-permute-start | bytes 786440 | tf_op jit(solution)/shard_map/ppermute | solution.py:76
  50.0 6.5 %collective-permute-start.10 = (f32[80,256]{1,0:T(8,128)S(1)}, f32[80,256]{1,0:T(8,128)S(1)}, u32[]{:S(2)}, u32[]{:S(2)}) collective-permute-start(f32[80,256]{1,0:T(8,128)S(1)} %sum.1.refs_1_), channel_id=1, source_target_pairs={{16,0},{17,1},{18,2},{19,3},{20,4},{21,5},{22,6},{23,7},{24,8},{25... | collective-permute-start | bytes 245768 | tf_op jit(solution)/shard_map/ppermute | solution.py:69
  74.9 1.5 %collective-permute-start.12 = (f32[1,256,256]{2,1,0:T(8,128)S(1)}, f32[1,256,256]{2,1,0:T(8,128)S(1)}, u32[]{:S(2)}, u32[]{:S(2)}) collective-permute-start(f32[1,256,256]{2,1,0:T(8,128)S(1)} %get-tuple-element.36.refs_1_), channel_id=1, source_target_pairs={{1,0},{0,1},{3,2},{2,3},{5,4},{4,5},{7,6},{6,7},{9,8},{8,9},{11,10... | collective-permute-start | bytes 786440 | tf_op jit(solution)/shard_map/ppermute | solution.py:76
  78.5 1.6 %collective-permute-start.13 = (f32[1,2,2,64,256]{4,3,2,1,0:T(8,128)S(1)}, f32[1,2,2,64,256]{4,3,2,1,0:T(8,128)S(1)}, u32[]{:S(2)}, u32[]{:S(2)}) collective-permute-start(f32[1,2,2,64,256]{4,3,2,1,0:T(8,128)S(1)} %get-tuple-element.39), channel_id=1, source_target_pairs={{1,0},{0,1},{3,2},{2,3},{5,4},{4,5},{7,6},{6,7},{9,8},{8,9},{11,10... | collective-permute-start | bytes 786440 | tf_op jit(solution)/shard_map/ppermute | solution.py:76
  80.7 5.6 %collective-permute-start.14 = (f32[2,64,256]{2,1,0:T(8,128)S(1)}, f32[2,64,256]{2,1,0:T(8,128)S(1)}, u32[]{:S(2)}, u32[]{:S(2)}) collective-permute-start(f32[2,64,256]{2,1,0:T(8,128)S(1)} %get-tuple-element.41), channel_id=1, source_target_pairs={{0,4},{1,5},{2,6},{3,7},{4,0},{5,1},{6,2},{7,3},{8,12},{9,13},{10,... | collective-permute-start | bytes 393224 | tf_op jit(solution)/shard_map/ppermute | solution.py:95
  81.0 6.4 %collective-permute-start.15 = (f32[2,64,256]{2,1,0:T(8,128)S(1)}, f32[2,64,256]{2,1,0:T(8,128)S(1)}, u32[]{:S(2)}, u32[]{:S(2)}) collective-permute-start(f32[2,64,256]{2,1,0:T(8,128)S(1)} %get-tuple-element.42), channel_id=1, source_target_pairs={{0,8},{1,9},{2,10},{3,11},{4,12},{5,13},{6,14},{7,15},{8,0},{9,1},... | collective-permute-start | bytes 393224 | tf_op jit(solution)/shard_map/ppermute | solution.py:95
  81.9 8.5 %collective-permute-start.16 = (f32[2,64,256]{2,1,0:T(8,128)S(1)}, f32[2,64,256]{2,1,0:T(8,128)S(1)}, u32[]{:S(2)}, u32[]{:S(2)}) collective-permute-start(f32[2,64,256]{2,1,0:T(8,128)S(1)} %get-tuple-element.43), channel_id=1, source_target_pairs={{0,12},{1,13},{2,14},{3,15},{4,8},{5,9},{6,10},{7,11},{8,4},{9,5},... | collective-permute-start | bytes 393224 | tf_op jit(solution)/shard_map/ppermute | solution.py:95
  84.3 7.5 %collective-permute-start.11 = (f32[256,256]{1,0:T(8,128)S(1)}, f32[256,256]{1,0:T(8,128)S(1)}, u32[]{:S(2)}, u32[]{:S(2)}) collective-permute-start(f32[256,256]{1,0:T(8,128)S(1)} %get-tuple-element.35.refs_2_), channel_id=1, source_target_pairs={{1,0},{0,1},{3,2},{2,3},{5,4},{4,5},{7,6},{6,7},{9,8},{8,9},{11,10... | collective-permute-start | bytes 786440 | tf_op jit(solution)/shard_map/ppermute | solution.py:76
  91.2 7.3 %copy-start.2 = (f32[2,128,512]{2,1,0:T(8,128)S(1)}, f32[2,128,512]{2,1,0:T(8,128)}, u32[]{:S(2)}) copy-start(f32[2,128,512]{2,1,0:T(8,128)} %refs_1_.11) | copy-start | bytes 1572868
  91.2 7.3 %collective-permute-start.17 = (f32[2,64,512]{2,1,0:T(8,128)S(1)}, f32[2,64,512]{2,1,0:T(8,128)S(1)}, u32[]{:S(2)}, u32[]{:S(2)}) collective-permute-start(f32[2,64,512]{2,1,0:T(8,128)S(1)} %place.1.refs_2_), channel_id=1, source_target_pairs={{2,0},{3,1},{0,2},{1,3},{6,4},{7,5},{4,6},{5,7},{10,8},{11,9},{8,1... | collective-permute-start | bytes 786440 | tf_op jit(solution)/shard_map/ppermute | solution.py:83
  98.5 1.6 %collective-permute-start.18 = (f32[2,64,512]{2,1,0:T(8,128)S(1)}, f32[2,64,512]{2,1,0:T(8,128)S(1)}, u32[]{:S(2)}, u32[]{:S(2)}) collective-permute-start(f32[2,64,512]{2,1,0:T(8,128)S(1)} %update.1.refs_0_), channel_id=1, source_target_pairs={{1,0},{0,1},{3,2},{2,3},{5,4},{4,5},{7,6},{6,7},{9,8},{8,9},{11,10... | collective-permute-start | bytes 786440 | tf_op jit(solution)/shard_map/ppermute | solution.py:76
  (2 other events, 8.3 us)

commit v7 on v6

--- a/solution.py
+++ b/solution.py
@@ -293,18 +293,52 @@
     return sum(power[at : at + length] for at in range(length, power.shape[0], length)) + power[:length]
 
 
-def far_kernel(layout, offsets, *refs):
+def order_kernel(layout, own_measured, *refs):
+    parts, (out, other_measured) = refs[: layout.cores], refs[layout.cores :]
+    upper, _, twin, core = layout.place()
+    length = layout.length
+    rows = lax.broadcasted_iota(jnp.int32, (length, length), 0)
+    columns = lax.broadcasted_iota(jnp.int32, (length, length), 1)
+    middle = length // 2
+    pick_rows = (columns == jnp.where(rows < middle, 2 * rows, 2 * (rows - middle) + 1)).astype(half)
+    pick_columns = (rows == jnp.where(columns < middle, 2 * columns, 2 * (columns - middle) + 1)).astype(half)
+
+    def exact(product, values):
+        lead, rest = split(values)
+        trail = (values - lead.astype(single) - rest.astype(single)).astype(half)
+        return (product(lead) + product(rest)) + product(trail)
+
+    for frame in range(layout.frames):
+        for step, part in enumerate(parts):
+            other_measured[(core + step) % layout.cores] = part[frame]
+        measured = other_measured[...].reshape(length, length)
+        measured = jnp.sqrt(jnp.where(upper == twin, own_measured[frame], measured))
+        measured = exact(lambda values: dot(pick_rows, values), measured)
+        out[frame] = exact(lambda values: dot(values, pick_columns), measured)
+
+
+def factor_of(root, intensity):
+    return root / jnp.sqrt(intensity + intensity_offset) - 1.0
+
+
+def first_kernel(layout, offsets, *refs):
     cores, halves, frames, length = layout.cores, layout.halves, layout.frames, layout.length
-    shares, probes = refs[: cores * halves], refs[cores * halves : (cores + 1) * halves]
-    forward, back, windows, intensity, kept, old_pieces, inner = refs[(cores + 1) * halves :]
+    count = cores * halves
+    shares, probes, refs = refs[:count], refs[count : 2 * count], refs[2 * count :]
+    roots, forward, back, windows, pieces, old_pieces, inner, far = refs
     upper, lower, twin, core = layout.place()
     region = twin * layout.lowers + lower
-    rows = pl.ds(pl.multiple_of(region * layout.piece, layout.piece), layout.piece)
-    for entry, probe in enumerate(probes):
+    local, piece = layout.local_modes, layout.piece
+    rows = pl.ds(pl.multiple_of(region * piece, piece), piece)
+    for entry, probe in enumerate(probes[:halves]):
         place = (twin + entry + halves - upper) % halves
-        for local in range(layout.local_modes):
+        for k in range(local):
             for plane in range(2):
-                old_pieces[place, local, plane] = probe[plane, local, rows, :]
+                old_pieces[place, k, plane] = probe[plane, k, rows, :]
+    goes_back = (upper + halves - twin) % halves * local * length
+    kept = pl.ds(pl.multiple_of(goes_back, length), local * length)
+    cut = (layout.regions, piece, length)
+    part = piece // halves
     for frame in range(frames):
         lead = offsets[0, region * frames + frame] % layout.band
         for step in range(cores):
@@ -315,77 +349,31 @@
         for plane in range(2):
             wrapped = inner[plane].reshape(length, length)
             windows[frame, plane] = pltpu.roll(wrapped, (length - lead) % length, 0)
-        listed = [(probe[0, k], probe[1, k]) for probe in probes for k in range(layout.local_modes)]
-        waves = leave(listed, windows[frame, 0], windows[frame, 1], forward, back)
-        intensity[frame] = power_of(*waves, length)
-        rows_kept = layout.local_modes * length
-        for entry in range(halves):
-
-            @pl.when((twin + entry) % halves == upper)
-            def _():
-                for plane, wave in enumerate(waves):
-                    kept[frame, plane] = wave[entry * rows_kept : (entry + 1) * rows_kept]
-
-
-def order_kernel(layout, own_measured, *refs):
-    parts, (out, other_measured) = refs[: layout.cores], refs[layout.cores :]
-    upper, _, twin, core = layout.place()
-    length = layout.length
-    rows = lax.broadcasted_iota(jnp.int32, (length, length), 0)
-    columns = lax.broadcasted_iota(jnp.int32, (length, length), 1)
-    middle = length // 2
-    pick_rows = (columns == jnp.where(rows < middle, 2 * rows, 2 * (rows - middle) + 1)).astype(half)
-    pick_columns = (rows == jnp.where(columns < middle, 2 * columns, 2 * (columns - middle) + 1)).astype(half)
-
-    def exact(product, values):
-        lead, rest = split(values)
-        trail = (values - lead.astype(single) - rest.astype(single)).astype(half)
-        return (product(lead) + product(rest)) + product(trail)
-
-    for frame in range(layout.frames):
-        for step, part in enumerate(parts):
-            other_measured[(core + step) % layout.cores] = part[frame]
-        measured = other_measured[...].reshape(length, length)
-        measured = jnp.sqrt(jnp.where(upper == twin, own_measured[frame], measured))
-        measured = exact(lambda values: dot(pick_rows, values), measured)
-        out[frame] = exact(lambda values: dot(values, pick_columns), measured)
-
-
-def factor_of(root, intensities, frame):
-    total = intensities[0][frame]
-    for more in intensities[1:]:
-        total += more[frame]
-    return root[frame] / jnp.sqrt(total + intensity_offset) - 1.0
-
-
-def gradient_kernel(layout, *refs):
-    cores, frames, length, piece = layout.cores, layout.frames, layout.length, layout.piece
-    intensities, (roots, windows, kept, forward, back, pieces) = refs[:cores], refs[cores:]
-    upper, _, _, _ = layout.place()
-    cut = (layout.regions, piece, length)
-    part = piece // layout.halves
-    for frame in range(frames):
         window_real, window_imag = windows[frame, 0], windows[frame, 1]
-        factor = factor_of(roots, intensities, frame)
+        listed = [(probe[0, k], probe[1, k]) for probe in probes for k in range(local)]
+        waves = leave(listed, window_real, window_imag, forward, back)
+        for plane, wave in enumerate(waves):
+            far[plane] = wave[: halves * local * length]
+        factor = factor_of(roots[frame], power_of(*waves, length))
+        changes_real, changes_imag = come_back(far[:, kept, :], factor, forward, back)
         channels = []
-        changes_real, changes_imag = come_back(kept[frame], factor, forward, back)
-        for local in range(layout.local_modes):
-            columns = slice(local * length, (local + 1) * length)
+        for k in range(local):
+            columns = slice(k * length, (k + 1) * length)
             change_real, change_imag = changes_real[:, columns], changes_imag[:, columns]
             channels.append(window_real * change_real + window_imag * change_imag)
             channels.append(window_real * change_imag - window_imag * change_real)
         channels = [values.reshape(cut) for values in channels]
         power = (window_real**2 + window_imag**2).reshape(cut)
         sent = power[:, :part]
-        for other in range(1, layout.halves):
+        for other in range(1, halves):
             sent = jnp.where(upper == other, power[:, other * part : (other + 1) * part], sent)
         first = 0
         for values in (*channels, sent):
-            rows = slice(first, first + values.shape[1])
+            taken = slice(first, first + values.shape[1])
             if frame == 0:
-                pieces[:, rows] = values
+                pieces[:, taken] = values
             else:
-                pieces[:, rows] += values
+                pieces[:, taken] += values
             first += values.shape[1]
 
 
@@ -445,7 +433,10 @@
     upper, lower, twin, core = layout.place()
     region = twin * layout.lowers + lower
     for frame in range(frames):
-        factor = factor_of(roots, intensities, frame)
+        intensity = intensities[0][frame]
+        for more in intensities[1:]:
+            intensity += more[frame]
+        factor = factor_of(roots[frame], intensity)
         changes_real, changes_imag = come_back(fars[frame], factor, forward, back)
         numer_real = jnp.zeros((length, length), single)
         numer_imag = jnp.zeros((length, length), single)
@@ -671,24 +662,23 @@
     strips = list(parts)
     for step in range(1, cores):
         strips += [layout.from_core(part, step) for part in [held] + parts[1:]]
-    windows, intensity, kept, old_pieces = call(
-        functools.partial(far_kernel, layout),
-        "far",
-        (corners, *strips, *probes, forward, back),
+    every_probe = list(probes)
+    for step in range(1, cores):
+        every_probe += [layout.from_core(probe, step) for probe in probes]
+    windows, pieces, old_pieces = call(
+        functools.partial(first_kernel, layout),
+        "first",
+        (corners, *strips, *every_probe, roots, forward, back),
         [
             (frames, 2, length, length),
-            (frames, length, length),
-            (frames, 2, local * length, length),
+            (regions, 2 * local * piece + piece // halves, length),
             (halves, local, 2, piece, length),
         ],
-        scratch=[(2, 2, cores, strip, length)],
+        scratch=[
+            (2, 2, cores, strip, length),
+            (2, halves * local * length, length),
+        ],
         scalar_count=1,
-    )
-    (pieces,) = call(
-        functools.partial(gradient_kernel, layout),
-        "gradient",
-        (*from_cores(intensity), roots, windows, kept, forward, back),
-        [(regions, 2 * local * piece + piece // halves, length)],
     )
     pieces = layout.within_cube(pieces)
     (total,) = call(sum_kernel, "sum", (pieces,), [pieces.shape[1:]])

time: 101 us -> 101 us (level)
  blocking collectives: 32.2 us -> 30.1 us
  starting transfers between devices: 20.9 us -> 22.3 us
    all_to_all x2, blocking collectives: 32.2 us -> 30.1 us  [within_cube(): lax.all_to_all(array, axes, split_axis=0, concat_axis=0, tiled=True, axis...]
    ppermute x8 -> x9, waiting for transfers between devices: 8.72 us -> 7.57 us  [from_core(): return lax.ppermute(array, axes, pairs)]
    ppermute x2, starting transfers between devices: 2.55 us -> 3.65 us  [from_twin(): return lax.ppermute(array, axes, pairs)]
    ppermute x6, starting transfers between devices: 8.14 us -> 7.11 us  [to_row(): return lax.ppermute(array, axes, pairs)]
    pallas_call x14 -> x13, Pallas kernels: 12.6 us -> 13.4 us  [call(): pl.pallas_call(inner, name=name, out_shape=shapes, in_specs=[scalars] * s...]
  transfers between devices with their start and end apart: 19 -> 20, of which waited for: 12 -> 12; matrix products, arithmetic and copies ran while one was open for 0% -> 0% of each run, Pallas kernels for 4% -> 5%
where the time goes in v7:
time: 101 us; the launch traced here: 100 us
  waiting for transfers between devices  32.2 us (32%)
  blocking collectives  30.1 us (30%)
  starting transfers between devices  22.3 us (22%)
  Pallas kernels  14.8 us (15%)
    all_to_all x2, blocking collectives, within_cube(): lax.all_to_all(array, axes, split_axis=0, concat_axis=0, tiled=True, axis...  30.1 us
    pallas_call x13, Pallas kernels, call(): pl.pallas_call(inner, name=name, out_shape=shapes, in_specs=[scalars] * s...  13.4 us
    ppermute x2, waiting for transfers between devices, from_upper(): return lax.ppermute(array, axes, pairs)  12.5 us
    ppermute x9, waiting for transfers between devices, from_core(): return lax.ppermute(array, axes, pairs)  7.57 us
    ppermute x6, starting transfers between devices, to_row(): return lax.ppermute(array, axes, pairs)  7.11 us
    ppermute x6, waiting for transfers between devices, to_row(): return lax.ppermute(array, axes, pairs)  6.39 us
    ppermute x2, starting transfers between devices, from_upper(): return lax.ppermute(array, axes, pairs)  5.86 us
    ppermute x2, waiting for transfers between devices, from_twin(): return lax.ppermute(array, axes, pairs)  5.69 us
  transfers between devices with their start and end apart: 20, of which 12 were waited for; matrix products, arithmetic and copies ran while one was open for 0% of the time, Pallas kernels for 5%

profile of v7, /device:TPU:0, one launch (start us, length us, event | category | flops | bytes accessed | tf_op | source)
XLA Modules:
  0.0 100.3 jit_solution(10744696425493543452)
XLA Ops:
  0.6 3.0 %collective-permute-start.8 = (f32[2,1,256,256]{3,2,1,0:T(8,128)}, f32[2,1,256,256]{3,2,1,0:T(8,128)S(1)}, u32[]{:S(2)}, u32[]{:S(2)}) collective-permute-start(f32[2,1,256,256]{3,2,1,0:T(8,128)} %refs_5_.1), channel_id=1, source_target_pairs={{2,0},{3,1},{0,2},{1,3},{6,4},{7,5},{4,6},{5,7},{10,8},{11,9},{8,1... | collective-permute-start | bytes 1572872 | tf_op jit(solution)/shard_map/ppermute | solution.py:83
  3.7 1.3 %cut.1 = (f32[2,64,256]{2,1,0:T(8,128)S(1)}, f32[2,64,256]{2,1,0:T(8,128)S(1)}, f32[2,64,256]{2,1,0:T(8,128)S(1)}, f32[2,64,256]{2,1,0:T(8,128)S(1)}, f32[1,128,256]{2,1,0:T(8,128)S(1)}) custom-call(s32[2,8]{1,0:T(2,128)} %bitcast.1, s32[8]{0:T(128)} %refs_1_.10, f32[2,128,512]{2,1,0:T(8,128)} %refs_1_.11, f32[1,256,256]{2,1,0:T(8,128)} %refs_0_.1), custom_call_target="tpu_custom_call" | custom-call | tf_op jit(solution)/shard_map/cut/pallas_call | solution.py:613
  5.0 1.6 %collective-permute-start = (f32[2,64,256]{2,1,0:T(8,128)S(1)}, f32[2,64,256]{2,1,0:T(8,128)S(1)}, u32[]{:S(2)}, u32[]{:S(2)}) collective-permute-start(f32[2,64,256]{2,1,0:T(8,128)S(1)} %get-tuple-element.22), channel_id=1, source_target_pairs={{0,4},{1,5},{2,6},{3,7},{4,0},{5,1},{6,2},{7,3},{8,12},{9,13},{10,... | collective-permute-start | bytes 393224 | tf_op jit(solution)/shard_map/ppermute | solution.py:95
  6.5 1.6 %collective-permute-start.1 = (f32[2,64,256]{2,1,0:T(8,128)S(1)}, f32[2,64,256]{2,1,0:T(8,128)S(1)}, u32[]{:S(2)}, u32[]{:S(2)}) collective-permute-start(f32[2,64,256]{2,1,0:T(8,128)S(1)} %get-tuple-element.23), channel_id=1, source_target_pairs={{0,8},{1,9},{2,10},{3,11},{4,12},{5,13},{6,14},{7,15},{8,0},{9,1},... | collective-permute-start | bytes 393224 | tf_op jit(solution)/shard_map/ppermute | solution.py:95
  8.5 4.6 %collective-permute-start.4 = (f32[1,128,256]{2,1,0:T(8,128)S(1)}, f32[1,128,256]{2,1,0:T(8,128)S(1)}, u32[]{:S(2)}, u32[]{:S(2)}) collective-permute-start(f32[1,128,256]{2,1,0:T(8,128)S(1)} %get-tuple-element.26), channel_id=1, source_target_pairs={{18,2},{19,3},{22,6},{23,7},{26,10},{27,11},{30,14},{31,15},{0,16}... | collective-permute-start | bytes 393224 | tf_op jit(solution)/shard_map/ppermute | solution.py:640
  15.0 2.7 %collective-permute-start.3 = (f32[1,2,2,64,256]{4,3,2,1,0:T(8,128)S(1)}, f32[1,2,2,64,256]{4,3,2,1,0:T(8,128)S(1)}, u32[]{:S(2)}, u32[]{:S(2)}) collective-permute-start(f32[1,2,2,64,256]{4,3,2,1,0:T(8,128)S(1)} %choose.3.refs_1_), channel_id=1, source_target_pairs={{16,0},{17,1},{18,2},{19,3},{20,4},{21,5},{22,6},{23,7},{24,8},{25... | collective-permute-start | bytes 786440 | tf_op jit(solution)/shard_map/ppermute | solution.py:69
  18.2 1.6 %collective-permute-done.5.refs_2_ = f32[1,128,256]{2,1,0:T(8,128)S(1)} collective-permute-done((f32[1,128,256]{2,1,0:T(8,128)S(1)}, f32[1,128,256]{2,1,0:T(8,128)S(1)}, u32[]{:S(2)}, u32[]{:S(2)}) %collective-permute-start.5) | collective-permute-done | bytes 131104 | tf_op jit(solution)/shard_map/ppermute | solution.py:76
  20.7 9.2 %collective-permute-done.3.refs_2_ = f32[1,2,2,64,256]{4,3,2,1,0:T(8,128)S(1)} collective-permute-done((f32[1,2,2,64,256]{4,3,2,1,0:T(8,128)S(1)}, f32[1,2,2,64,256]{4,3,2,1,0:T(8,128)S(1)}, u32[]{:S(2)}, u32[]{:S(2)}) %collective-permute-start.3) | collective-permute-done | bytes 262176 | tf_op jit(solution)/shard_map/ppermute | solution.py:69
  29.9 1.5 %collective-permute-done.7.refs_4_ = f32[1,2,2,64,256]{4,3,2,1,0:T(8,128)S(1)} collective-permute-done((f32[1,2,2,64,256]{4,3,2,1,0:T(8,128)S(1)}, f32[1,2,2,64,256]{4,3,2,1,0:T(8,128)S(1)}, u32[]{:S(2)}, u32[]{:S(2)}) %collective-permute-start.7) | collective-permute-done | bytes 262176 | tf_op jit(solution)/shard_map/ppermute | solution.py:76
  31.5 3.9 %first.1 = (f32[1,2,256,256]{3,2,1,0:T(8,128)S(1)}, f32[8,80,256]{2,1,0:T(8,128)S(1)}, f32[2,1,2,32,256]{4,3,2,1,0:T(8,128)S(1)}) custom-call(s32[2,8]{1,0:T(2,128)S(1)} %bitcast.4, f32[1,2,2,64,256]{4,3,2,1,0:T(8,128)S(1)} %choose.3.refs_1_, f32[1,2,2,64,256]{4,3,2,1,0:T(8,128)S(1)} %collective-permute-done.3.refs_2_, ...), custom_call_target="tpu_custom_call" | custom-call | tf_op jit(solution)/shard_map/first/pallas_call | solution.py:579
  35.3 14.2 %all_to_all.10.refs_0_ = f32[8,80,256]{2,1,0:T(8,128)S(1)} all-to-all(f32[8,80,256]{2,1,0:T(8,128)S(1)} %get-tuple-element.30), channel_id=1, replica_groups={{0,4,8,12,2,6,10,14},{1,5,9,13,3,7,11,15},{16,20,24,28,18,22,26,30},{17..., dimensions={0} | all-to-all | bytes 1310720 | tf_op jit(solution)/shard_map/all_to_all | solution.py:98
  49.5 3.2 %collective-permute-start.11 = (f32[80,256]{1,0:T(8,128)S(1)}, f32[80,256]{1,0:T(8,128)S(1)}, u32[]{:S(2)}, u32[]{:S(2)}) collective-permute-start(f32[80,256]{1,0:T(8,128)S(1)} %sum.1.refs_1_), channel_id=1, source_target_pairs={{16,0},{17,1},{18,2},{19,3},{20,4},{21,5},{22,6},{23,7},{24,8},{25... | collective-permute-start | bytes 245768 | tf_op jit(solution)/shard_map/ppermute | solution.py:69
  52.7 3.3 %collective-permute-done.11.refs_2_ = f32[80,256]{1,0:T(8,128)S(1)} collective-permute-done((f32[80,256]{1,0:T(8,128)S(1)}, f32[80,256]{1,0:T(8,128)S(1)}, u32[]{:S(2)}, u32[]{:S(2)}) %collective-permute-start.11) | collective-permute-done | bytes 81952 | tf_op jit(solution)/shard_map/ppermute | solution.py:69
  56.2 16.0 %all_to_all.11.refs_0_.refs_4_ = f32[8,2,1,2,32,256]{5,4,3,2,1,0:T(8,128)S(1)} all-to-all(f32[8,2,1,2,32,256]{5,4,3,2,1,0:T(8,128)S(1)} %step.1), channel_id=1, replica_groups={{0,4,8,12,2,6,10,14},{1,5,9,13,3,7,11,15},{16,20,24,28,18,22,26,30},{17..., dimensions={0} | all-to-all | bytes 2097152 | tf_op jit(solution)/shard_map/all_to_all | solution.py:98
  72.1 2.1 %again.1 = (f32[2,1,256,256]{3,2,1,0:T(8,128)}, f32[256,256]{1,0:T(8,128)S(1)}, f32[1,256,256]{2,1,0:T(8,128)S(1)}, f32[1,2,512,256]{3,2,1,0:T(8,128)S(1)}) custom-call(f32[8,2,1,2,32,256]{5,4,3,2,1,0:T(8,128)S(1)} %all_to_all.11.refs_0_.refs_4_, f32[1,2,256,256]{3,2,1,0:T(8,128)S(1)} %get-tuple-element.31.refs_1_, bf16[2,2,256,256]{3,2,1,0:T(8,128)(2,1)S(1)} %copy-done.1, ...), custom_call_target="tpu_custom_call" | custom-call | tf_op jit(solution)/shard_map/again/pallas_call | solution.py:579
  74.2 1.5 %collective-permute-done.13.refs_2_ = f32[1,256,256]{2,1,0:T(8,128)S(1)} collective-permute-done((f32[1,256,256]{2,1,0:T(8,128)S(1)}, f32[1,256,256]{2,1,0:T(8,128)S(1)}, u32[]{:S(2)}, u32[]{:S(2)}) %collective-permute-start.13) | collective-permute-done | bytes 262176 | tf_op jit(solution)/shard_map/ppermute | solution.py:76
  75.8 2.0 %terms.1 = (f32[1,2,2,64,256]{4,3,2,1,0:T(8,128)S(1)}, f32[1,2,2,64,256]{4,3,2,1,0:T(8,128)S(1)}) custom-call(s32[2,8]{1,0:T(2,128)S(1)} %bitcast.5, f32[1,256,256]{2,1,0:T(8,128)S(1)} %get-tuple-element.34.refs_1_, f32[1,256,256]{2,1,0:T(8,128)S(1)} %collective-permute-done.13.refs_2_, f32[1,256,256]{2,1,0:T(8,128)S(1)} %order.1.refs_9_.refs_3_, ...), custom_call_target="tpu_custom_call" | custom-call | tf_op jit(solution)/shard_map/terms/pallas_call | solution.py:579
  78.0 1.4 %collective-permute-done.14.refs_3_ = f32[1,2,2,64,256]{4,3,2,1,0:T(8,128)S(1)} collective-permute-done((f32[1,2,2,64,256]{4,3,2,1,0:T(8,128)S(1)}, f32[1,2,2,64,256]{4,3,2,1,0:T(8,128)S(1)}, u32[]{:S(2)}, u32[]{:S(2)}) %collective-permute-start.14) | collective-permute-done | bytes 262176 | tf_op jit(solution)/shard_map/ppermute | solution.py:76
  81.2 2.4 %collective-permute-start.17 = (f32[2,64,256]{2,1,0:T(8,128)S(1)}, f32[2,64,256]{2,1,0:T(8,128)S(1)}, u32[]{:S(2)}, u32[]{:S(2)}) collective-permute-start(f32[2,64,256]{2,1,0:T(8,128)S(1)} %get-tuple-element.41), channel_id=1, source_target_pairs={{0,12},{1,13},{2,14},{3,15},{4,8},{5,9},{6,10},{7,11},{8,4},{9,5},... | collective-permute-start | bytes 393224 | tf_op jit(solution)/shard_map/ppermute | solution.py:95
  83.6 2.0 %collective-permute-done.15.refs_3_ = f32[2,64,256]{2,1,0:T(8,128)S(1)} collective-permute-done((f32[2,64,256]{2,1,0:T(8,128)S(1)}, f32[2,64,256]{2,1,0:T(8,128)S(1)}, u32[]{:S(2)}, u32[]{:S(2)}) %collective-permute-start.15) | collective-permute-done | bytes 131104 | tf_op jit(solution)/shard_map/ppermute | solution.py:95
  85.7 1.0 %collective-permute-done.16.refs_4_ = f32[2,64,256]{2,1,0:T(8,128)S(1)} collective-permute-done((f32[2,64,256]{2,1,0:T(8,128)S(1)}, f32[2,64,256]{2,1,0:T(8,128)S(1)}, u32[]{:S(2)}, u32[]{:S(2)}) %collective-permute-start.16) | collective-permute-done | bytes 131104 | tf_op jit(solution)/shard_map/ppermute | solution.py:95
  86.7 3.0 %collective-permute-done.17.refs_5_ = f32[2,64,256]{2,1,0:T(8,128)S(1)} collective-permute-done((f32[2,64,256]{2,1,0:T(8,128)S(1)}, f32[2,64,256]{2,1,0:T(8,128)S(1)}, u32[]{:S(2)}, u32[]{:S(2)}) %collective-permute-start.17) | collective-permute-done | bytes 131104 | tf_op jit(solution)/shard_map/ppermute | solution.py:95
  92.1 5.7 %collective-permute-done.18.refs_3_ = f32[2,64,512]{2,1,0:T(8,128)S(1)} collective-permute-done((f32[2,64,512]{2,1,0:T(8,128)S(1)}, f32[2,64,512]{2,1,0:T(8,128)S(1)}, u32[]{:S(2)}, u32[]{:S(2)}) %collective-permute-start.18) | collective-permute-done | bytes 262176 | tf_op jit(solution)/shard_map/ppermute | solution.py:83
  97.9 1.5 %collective-permute-done.19.refs_1_ = f32[2,64,512]{2,1,0:T(8,128)S(1)} collective-permute-done((f32[2,64,512]{2,1,0:T(8,128)S(1)}, f32[2,64,512]{2,1,0:T(8,128)S(1)}, u32[]{:S(2)}, u32[]{:S(2)}) %collective-permute-start.19) | collective-permute-done | bytes 262176 | tf_op jit(solution)/shard_map/ppermute | solution.py:76
  (46 shorter events, 9.2 us)
Async XLA Ops:
  0.6 17.0 %collective-permute-start.8 = (f32[2,1,256,256]{3,2,1,0:T(8,128)}, f32[2,1,256,256]{3,2,1,0:T(8,128)S(1)}, u32[]{:S(2)}, u32[]{:S(2)}) collective-permute-start(f32[2,1,256,256]{3,2,1,0:T(8,128)} %refs_5_.1), channel_id=1, source_target_pairs={{2,0},{3,1},{0,2},{1,3},{6,4},{7,5},{4,6},{5,7},{10,8},{11,9},{8,1... | collective-permute-start | bytes 1572872 | tf_op jit(solution)/shard_map/ppermute | solution.py:83
  3.7 10.2 %copy-start.4 = (f32[2,1,256,256]{3,2,1,0:T(8,128)S(1)}, f32[2,1,256,256]{3,2,1,0:T(8,128)}, u32[]{:S(2)}) copy-start(f32[2,1,256,256]{3,2,1,0:T(8,128)} %refs_5_.1) | copy-start | bytes 1572868
  5.0 8.9 %collective-permute-start = (f32[2,64,256]{2,1,0:T(8,128)S(1)}, f32[2,64,256]{2,1,0:T(8,128)S(1)}, u32[]{:S(2)}, u32[]{:S(2)}) collective-permute-start(f32[2,64,256]{2,1,0:T(8,128)S(1)} %get-tuple-element.22), channel_id=1, source_target_pairs={{0,4},{1,5},{2,6},{3,7},{4,0},{5,1},{6,2},{7,3},{8,12},{9,13},{10,... | collective-permute-start | bytes 393224 | tf_op jit(solution)/shard_map/ppermute | solution.py:95
  6.5 7.4 %collective-permute-start.1 = (f32[2,64,256]{2,1,0:T(8,128)S(1)}, f32[2,64,256]{2,1,0:T(8,128)S(1)}, u32[]{:S(2)}, u32[]{:S(2)}) collective-permute-start(f32[2,64,256]{2,1,0:T(8,128)S(1)} %get-tuple-element.23), channel_id=1, source_target_pairs={{0,8},{1,9},{2,10},{3,11},{4,12},{5,13},{6,14},{7,15},{8,0},{9,1},... | collective-permute-start | bytes 393224 | tf_op jit(solution)/shard_map/ppermute | solution.py:95
  8.1 6.2 %collective-permute-start.2 = (f32[2,64,256]{2,1,0:T(8,128)S(1)}, f32[2,64,256]{2,1,0:T(8,128)S(1)}, u32[]{:S(2)}, u32[]{:S(2)}) collective-permute-start(f32[2,64,256]{2,1,0:T(8,128)S(1)} %get-tuple-element.24), channel_id=1, source_target_pairs={{0,12},{1,13},{2,14},{3,15},{4,8},{5,9},{6,10},{7,11},{8,4},{9,5},... | collective-permute-start | bytes 393224 | tf_op jit(solution)/shard_map/ppermute | solution.py:95
  8.5 9.1 %collective-permute-start.4 = (f32[1,128,256]{2,1,0:T(8,128)S(1)}, f32[1,128,256]{2,1,0:T(8,128)S(1)}, u32[]{:S(2)}, u32[]{:S(2)}) collective-permute-start(f32[1,128,256]{2,1,0:T(8,128)S(1)} %get-tuple-element.26), channel_id=1, source_target_pairs={{18,2},{19,3},{22,6},{23,7},{26,10},{27,11},{30,14},{31,15},{0,16}... | collective-permute-start | bytes 393224 | tf_op jit(solution)/shard_map/ppermute | solution.py:640
  13.9 16.1 %collective-permute-start.9 = (f32[2,1,256,256]{3,2,1,0:T(8,128)S(1)}, f32[2,1,256,256]{3,2,1,0:T(8,128)S(1)}, u32[]{:S(2)}, u32[]{:S(2)}) collective-permute-start(f32[2,1,256,256]{3,2,1,0:T(8,128)S(1)} %copy-done.4), channel_id=1, source_target_pairs={{1,0},{0,1},{3,2},{2,3},{5,4},{4,5},{7,6},{6,7},{9,8},{8,9},{11,10... | collective-permute-start | bytes 1572872 | tf_op jit(solution)/shard_map/ppermute | solution.py:76
  14.3 17.2 %copy-start.1 = (bf16[2,2,256,256]{3,2,1,0:T(8,128)(2,1)S(1)}, bf16[2,2,256,256]{3,2,1,0:T(8,128)(2,1)}, u32[]{:S(2)}) copy-start(bf16[2,2,256,256]{3,2,1,0:T(8,128)(2,1)} %constant.4.clone.refs_10_.refs_2_.refs_6_) | copy-start | bytes 1572868
  15.0 16.5 %copy-start = (bf16[2,2,256,256]{3,2,1,0:T(8,128)(2,1)S(1)}, bf16[2,2,256,256]{3,2,1,0:T(8,128)(2,1)}, u32[]{:S(2)}) copy-start(bf16[2,2,256,256]{3,2,1,0:T(8,128)(2,1)} %constant.5.clone.refs_11_.refs_3_.refs_7_) | copy-start | bytes 1572868
  15.0 14.9 %collective-permute-start.3 = (f32[1,2,2,64,256]{4,3,2,1,0:T(8,128)S(1)}, f32[1,2,2,64,256]{4,3,2,1,0:T(8,128)S(1)}, u32[]{:S(2)}, u32[]{:S(2)}) collective-permute-start(f32[1,2,2,64,256]{4,3,2,1,0:T(8,128)S(1)} %choose.3.refs_1_), channel_id=1, source_target_pairs={{16,0},{17,1},{18,2},{19,3},{20,4},{21,5},{22,6},{23,7},{24,8},{25... | collective-permute-start | bytes 786440 | tf_op jit(solution)/shard_map/ppermute | solution.py:69
  17.6 13.8 %collective-permute-start.10 = (f32[2,1,256,256]{3,2,1,0:T(8,128)S(1)}, f32[2,1,256,256]{3,2,1,0:T(8,128)S(1)}, u32[]{:S(2)}, u32[]{:S(2)}) collective-permute-start(f32[2,1,256,256]{3,2,1,0:T(8,128)S(1)} %collective-permute-done.8.refs_6_), channel_id=1, source_target_pairs={{1,0},{0,1},{3,2},{2,3},{5,4},{4,5},{7,6},{6,7},{9,8},{8,9},{11,10... | collective-permute-start | bytes 1572872 | tf_op jit(solution)/shard_map/ppermute | solution.py:76
  17.7 2.1 %collective-permute-start.5 = (f32[1,128,256]{2,1,0:T(8,128)S(1)}, f32[1,128,256]{2,1,0:T(8,128)S(1)}, u32[]{:S(2)}, u32[]{:S(2)}) collective-permute-start(f32[1,128,256]{2,1,0:T(8,128)S(1)} %collective-permute-done.4.refs_1_), channel_id=1, source_target_pairs={{1,0},{0,1},{3,2},{2,3},{5,4},{4,5},{7,6},{6,7},{9,8},{8,9},{11,10... | collective-permute-start | bytes 393224 | tf_op jit(solution)/shard_map/ppermute | solution.py:76
  20.5 9.5 %collective-permute-start.6 = (f32[1,2,2,64,256]{4,3,2,1,0:T(8,128)S(1)}, f32[1,2,2,64,256]{4,3,2,1,0:T(8,128)S(1)}, u32[]{:S(2)}, u32[]{:S(2)}) collective-permute-start(f32[1,2,2,64,256]{4,3,2,1,0:T(8,128)S(1)} %choose.3.refs_1_), channel_id=1, source_target_pairs={{1,0},{0,1},{3,2},{2,3},{5,4},{4,5},{7,6},{6,7},{9,8},{8,9},{11,10... | collective-permute-start | bytes 786440 | tf_op jit(solution)/shard_map/ppermute | solution.py:76
  29.9 1.5 %collective-permute-start.7 = (f32[1,2,2,64,256]{4,3,2,1,0:T(8,128)S(1)}, f32[1,2,2,64,256]{4,3,2,1,0:T(8,128)S(1)}, u32[]{:S(2)}, u32[]{:S(2)}) collective-permute-start(f32[1,2,2,64,256]{4,3,2,1,0:T(8,128)S(1)} %collective-permute-done.3.refs_2_), channel_id=1, source_target_pairs={{1,0},{0,1},{3,2},{2,3},{5,4},{4,5},{7,6},{6,7},{9,8},{8,9},{11,10... | collective-permute-start | bytes 786440 | tf_op jit(solution)/shard_map/ppermute | solution.py:76
  49.5 6.5 %collective-permute-start.11 = (f32[80,256]{1,0:T(8,128)S(1)}, f32[80,256]{1,0:T(8,128)S(1)}, u32[]{:S(2)}, u32[]{:S(2)}) collective-permute-start(f32[80,256]{1,0:T(8,128)S(1)} %sum.1.refs_1_), channel_id=1, source_target_pairs={{16,0},{17,1},{18,2},{19,3},{20,4},{21,5},{22,6},{23,7},{24,8},{25... | collective-permute-start | bytes 245768 | tf_op jit(solution)/shard_map/ppermute | solution.py:69
  74.2 1.5 %collective-permute-start.13 = (f32[1,256,256]{2,1,0:T(8,128)S(1)}, f32[1,256,256]{2,1,0:T(8,128)S(1)}, u32[]{:S(2)}, u32[]{:S(2)}) collective-permute-start(f32[1,256,256]{2,1,0:T(8,128)S(1)} %get-tuple-element.34.refs_1_), channel_id=1, source_target_pairs={{1,0},{0,1},{3,2},{2,3},{5,4},{4,5},{7,6},{6,7},{9,8},{8,9},{11,10... | collective-permute-start | bytes 786440 | tf_op jit(solution)/shard_map/ppermute | solution.py:76
  77.8 1.6 %collective-permute-start.14 = (f32[1,2,2,64,256]{4,3,2,1,0:T(8,128)S(1)}, f32[1,2,2,64,256]{4,3,2,1,0:T(8,128)S(1)}, u32[]{:S(2)}, u32[]{:S(2)}) collective-permute-start(f32[1,2,2,64,256]{4,3,2,1,0:T(8,128)S(1)} %get-tuple-element.37), channel_id=1, source_target_pairs={{1,0},{0,1},{3,2},{2,3},{5,4},{4,5},{7,6},{6,7},{9,8},{8,9},{11,10... | collective-permute-start | bytes 786440 | tf_op jit(solution)/shard_map/ppermute | solution.py:76
  80.1 5.6 %collective-permute-start.15 = (f32[2,64,256]{2,1,0:T(8,128)S(1)}, f32[2,64,256]{2,1,0:T(8,128)S(1)}, u32[]{:S(2)}, u32[]{:S(2)}) collective-permute-start(f32[2,64,256]{2,1,0:T(8,128)S(1)} %get-tuple-element.39), channel_id=1, source_target_pairs={{0,4},{1,5},{2,6},{3,7},{4,0},{5,1},{6,2},{7,3},{8,12},{9,13},{10,... | collective-permute-start | bytes 393224 | tf_op jit(solution)/shard_map/ppermute | solution.py:95
  80.3 6.4 %collective-permute-start.16 = (f32[2,64,256]{2,1,0:T(8,128)S(1)}, f32[2,64,256]{2,1,0:T(8,128)S(1)}, u32[]{:S(2)}, u32[]{:S(2)}) collective-permute-start(f32[2,64,256]{2,1,0:T(8,128)S(1)} %get-tuple-element.40), channel_id=1, source_target_pairs={{0,8},{1,9},{2,10},{3,11},{4,12},{5,13},{6,14},{7,15},{8,0},{9,1},... | collective-permute-start | bytes 393224 | tf_op jit(solution)/shard_map/ppermute | solution.py:95
  81.2 8.4 %collective-permute-start.17 = (f32[2,64,256]{2,1,0:T(8,128)S(1)}, f32[2,64,256]{2,1,0:T(8,128)S(1)}, u32[]{:S(2)}, u32[]{:S(2)}) collective-permute-start(f32[2,64,256]{2,1,0:T(8,128)S(1)} %get-tuple-element.41), channel_id=1, source_target_pairs={{0,12},{1,13},{2,14},{3,15},{4,8},{5,9},{6,10},{7,11},{8,4},{9,5},... | collective-permute-start | bytes 393224 | tf_op jit(solution)/shard_map/ppermute | solution.py:95
  83.6 7.5 %collective-permute-start.12 = (f32[256,256]{1,0:T(8,128)S(1)}, f32[256,256]{1,0:T(8,128)S(1)}, u32[]{:S(2)}, u32[]{:S(2)}) collective-permute-start(f32[256,256]{1,0:T(8,128)S(1)} %get-tuple-element.33.refs_2_), channel_id=1, source_target_pairs={{1,0},{0,1},{3,2},{2,3},{5,4},{4,5},{7,6},{6,7},{9,8},{8,9},{11,10... | collective-permute-start | bytes 786440 | tf_op jit(solution)/shard_map/ppermute | solution.py:76
  90.5 7.3 %copy-start.2 = (f32[2,128,512]{2,1,0:T(8,128)S(1)}, f32[2,128,512]{2,1,0:T(8,128)}, u32[]{:S(2)}) copy-start(f32[2,128,512]{2,1,0:T(8,128)} %refs_1_.11) | copy-start | bytes 1572868
  90.5 7.3 %collective-permute-start.18 = (f32[2,64,512]{2,1,0:T(8,128)S(1)}, f32[2,64,512]{2,1,0:T(8,128)S(1)}, u32[]{:S(2)}, u32[]{:S(2)}) collective-permute-start(f32[2,64,512]{2,1,0:T(8,128)S(1)} %place.1.refs_2_), channel_id=1, source_target_pairs={{2,0},{3,1},{0,2},{1,3},{6,4},{7,5},{4,6},{5,7},{10,8},{11,9},{8,1... | collective-permute-start | bytes 786440 | tf_op jit(solution)/shard_map/ppermute | solution.py:83
  97.8 1.6 %collective-permute-start.19 = (f32[2,64,512]{2,1,0:T(8,128)S(1)}, f32[2,64,512]{2,1,0:T(8,128)S(1)}, u32[]{:S(2)}, u32[]{:S(2)}) collective-permute-start(f32[2,64,512]{2,1,0:T(8,128)S(1)} %update.1.refs_0_), channel_id=1, source_target_pairs={{1,0},{0,1},{3,2},{2,3},{5,4},{4,5},{7,6},{6,7},{9,8},{8,9},{11,10... | collective-permute-start | bytes 786440 | tf_op jit(solution)/shard_map/ppermute | solution.py:76
  (3 other events, 15.2 us)

commit v8 on v7

--- a/solution.py
+++ b/solution.py
@@ -18,7 +18,6 @@
 axes = ("region", "mode")
 lanes = 128
 on_chip = pl.BlockSpec(memory_space=pltpu.VMEM)
-scalars = pl.BlockSpec(memory_space=pltpu.SMEM)
 
 
 class Layout:
@@ -185,6 +184,18 @@
     odd = from_left(table_of(forward, 1), above(real[middle:], imag[middle:]))
     plus, minus = even + odd, even - odd
     return above(plus[:middle], minus[:middle]), above(plus[middle:], minus[middle:])
+
+
+class Table:
+    def __init__(self, ref):
+        self.values = ref[...].astype(single)
+        self.rows = lax.broadcasted_iota(jnp.int32, self.values.shape, 0)
+        self.columns = lax.broadcasted_iota(jnp.int32, self.values.shape, 1)
+
+    def __getitem__(self, place):
+        row, column = place if isinstance(place, tuple) else (0, place)
+        wanted = (self.rows == row) & (self.columns == column)
+        return jnp.sum(jnp.where(wanted, self.values, 0.0)).astype(jnp.int32)
 
 
 def band_of_block(owner, block, layout):
@@ -407,9 +418,15 @@
     return values.reshape(values.shape[0] * values.shape[1], values.shape[2])
 
 
-def again_kernel(layout, probes, windows, forward, back, probe_out, probe_power, intensity, fars):
+def probe_kernel(layout, probes, out):
     upper, _, twin, _ = layout.place()
-    own_entry = (twin + layout.halves - upper) % layout.halves
+    entry = (twin + layout.halves - upper) % layout.halves
+    for local in range(layout.local_modes):
+        for plane in range(2):
+            out[plane, local] = new_probe(probes, entry, local, plane)
+
+
+def again_kernel(layout, probes, windows, forward, back, probe_power, intensity, fars):
     listed = [
         [new_probe(probes, entry, local, plane) for plane in range(2)]
         for entry in range(layout.halves)
@@ -421,9 +438,6 @@
         for plane, wave in enumerate(waves):
             fars[frame, plane] = wave
     probe_power[...] = sum(real**2 + imag**2 for real, imag in listed)
-    for local in range(layout.local_modes):
-        for plane in range(2):
-            probe_out[plane, local] = new_probe(probes, own_entry, local, plane)
 
 
 def terms_kernel(layout, offsets, *refs):
@@ -574,14 +588,14 @@
     count = len(operands)
 
     def inner(*refs):
-        kernel(*refs[:count], *refs[count + len(after) :])
+        tables = [Table(ref) for ref in refs[:scalar_count]]
+        kernel(*tables, *refs[scalar_count:count], *refs[count + len(after) :])
 
     return pl.pallas_call(
         inner,
         name=name,
         out_shape=shapes,
-        in_specs=[scalars] * scalar_count
-        + [on_chip] * (count - scalar_count)
+        in_specs=[on_chip] * count
         + [pl.BlockSpec(memory_space=pl.ANY)] * len(after),
         out_specs=[on_chip] * len(shapes),
         scratch_shapes=[pltpu.VMEM(shape, single) for shape in scratch],
@@ -602,7 +616,7 @@
     length, piece, frames = layout.length, layout.piece, layout.frames
     local, strip = layout.local_modes, layout.strip
     forward, back = fourier_tables(length)
-    corners = scan_offsets.T
+    corners, owners = scan_offsets.T, band_owner[None]
 
     def from_cores(array):
         return [array] + [layout.from_core(array, step) for step in range(1, cores)]
@@ -644,7 +658,7 @@
         chosen = call(
             functools.partial(choose_kernel, layout, steps),
             "choose",
-            (corners, band_owner, *(cuts[step] for step in steps), *chosen),
+            (corners, owners, *(cuts[step] for step in steps), *chosen),
             [(frames, 2, 2, strip, length)],
             scalar_count=2,
         )
@@ -689,12 +703,17 @@
         [(regions, halves, local, 2, piece, length)],
     )
     new_probes = layout.within_cube(spread)
-    probe_out, probe_power, intensity, fars = call(
+    (probe_out,) = call(
+        functools.partial(probe_kernel, layout),
+        "probe",
+        (new_probes,),
+        [(2, local, length, length)],
+    )
+    probe_power, intensity, fars = call(
         functools.partial(again_kernel, layout),
         "again",
         (new_probes, windows, forward, back),
         [
-            (2, local, length, length),
             (length, length),
             (frames, length, length),
             (frames, 2, halves * local * length, length),
@@ -714,7 +733,7 @@
     posted = call(
         functools.partial(post_kernel, layout),
         "post",
-        (corners, band_owner, *strips),
+        (corners, owners, *strips),
         [(2, strip, length)] * layout.lowers,
         scalar_count=2,
     )
@@ -724,7 +743,7 @@
     (density,) = call(
         functools.partial(density_kernel, layout),
         "density",
-        (corners, band_owner, *from_cores(probe_power)),
+        (corners, owners, *from_cores(probe_power)),
         [(strip, layout.width)],
         scratch=[(2, length, length), (strip, layout.width + lanes)],
         scalar_count=2,
@@ -732,7 +751,7 @@
     (placed,) = call(
         functools.partial(place_kernel, layout),
         "place",
-        (corners, band_owner, *posted),
+        (corners, owners, *posted),
         [(2, strip, layout.width)],
         scratch=[(2 * strip, layout.width + lanes)],
         scalar_count=2,

time: 101 us -> 97.9 us (0.969)
  Pallas kernels: 14.8 us -> 11.9 us
    pallas_call x13 -> x14, Pallas kernels: 13.4 us -> 10.6 us  [call(): pl.pallas_call(inner, name=name, out_shape=shapes, in_specs=[on_chip] * c...]
where the time goes in v8:
time: 97.9 us; the launch traced here: 97.6 us
  waiting for transfers between devices  31.6 us (32%)
  blocking collectives  30.4 us (31%)
  starting transfers between devices  22.2 us (23%)
  Pallas kernels  11.9 us (12%)
    all_to_all x2, blocking collectives, within_cube(): lax.all_to_all(array, axes, split_axis=0, concat_axis=0, tiled=True, axis...  30.4 us
    ppermute x2, waiting for transfers between devices, from_upper(): return lax.ppermute(array, axes, pairs)  12.6 us
    pallas_call x14, Pallas kernels, call(): pl.pallas_call(inner, name=name, out_shape=shapes, in_specs=[on_chip] * c...  10.6 us
    ppermute x6, starting transfers between devices, to_row(): return lax.ppermute(array, axes, pairs)  7.11 us
    ppermute x9, waiting for transfers between devices, from_core(): return lax.ppermute(array, axes, pairs)  6.71 us
    ppermute x6, waiting for transfers between devices, to_row(): return lax.ppermute(array, axes, pairs)  6.24 us
    ppermute x2, waiting for transfers between devices, from_twin(): return lax.ppermute(array, axes, pairs)  6.08 us
    ppermute x2, starting transfers between devices, from_upper(): return lax.ppermute(array, axes, pairs)  5.86 us
  transfers between devices with their start and end apart: 20, of which 12 were waited for; matrix products, arithmetic and copies ran while one was open for 0% of the time, Pallas kernels for 5%

profile of v8, /device:TPU:0, one launch (start us, length us, event | category | flops | bytes accessed | tf_op | source)
XLA Modules:
  0.0 97.6 jit_solution(3217361839989054621)
XLA Ops:
  0.6 3.0 %collective-permute-start.8 = (f32[2,1,256,256]{3,2,1,0:T(8,128)}, f32[2,1,256,256]{3,2,1,0:T(8,128)S(1)}, u32[]{:S(2)}, u32[]{:S(2)}) collective-permute-start(f32[2,1,256,256]{3,2,1,0:T(8,128)} %refs_5_.1), channel_id=1, source_target_pairs={{2,0},{3,1},{0,2},{1,3},{6,4},{7,5},{4,6},{5,7},{10,8},{11,9},{8,1... | collective-permute-start | bytes 1572872 | tf_op jit(solution)/shard_map/ppermute | solution.py:82
  3.7 1.3 %cut.1 = (f32[2,64,256]{2,1,0:T(8,128)S(1)}, f32[2,64,256]{2,1,0:T(8,128)S(1)}, f32[2,64,256]{2,1,0:T(8,128)S(1)}, f32[2,64,256]{2,1,0:T(8,128)S(1)}, f32[1,128,256]{2,1,0:T(8,128)S(1)}) custom-call(s32[2,8]{1,0:T(2,128)} %bitcast.2, s32[8]{0:T(128)} %owners.1, f32[2,128,512]{2,1,0:T(8,128)} %refs_1_.1, f32[1,256,256]{2,1,0:T(8,128)} %refs_0_.1), custom_call_target="tpu_custom_call" | custom-call | tf_op jit(solution)/shard_map/cut/pallas_call | solution.py:627
  5.0 1.6 %collective-permute-start = (f32[2,64,256]{2,1,0:T(8,128)S(1)}, f32[2,64,256]{2,1,0:T(8,128)S(1)}, u32[]{:S(2)}, u32[]{:S(2)}) collective-permute-start(f32[2,64,256]{2,1,0:T(8,128)S(1)} %get-tuple-element.21), channel_id=1, source_target_pairs={{0,4},{1,5},{2,6},{3,7},{4,0},{5,1},{6,2},{7,3},{8,12},{9,13},{10,... | collective-permute-start | bytes 393224 | tf_op jit(solution)/shard_map/ppermute | solution.py:94
  6.5 1.6 %collective-permute-start.1 = (f32[2,64,256]{2,1,0:T(8,128)S(1)}, f32[2,64,256]{2,1,0:T(8,128)S(1)}, u32[]{:S(2)}, u32[]{:S(2)}) collective-permute-start(f32[2,64,256]{2,1,0:T(8,128)S(1)} %get-tuple-element.22), channel_id=1, source_target_pairs={{0,8},{1,9},{2,10},{3,11},{4,12},{5,13},{6,14},{7,15},{8,0},{9,1},... | collective-permute-start | bytes 393224 | tf_op jit(solution)/shard_map/ppermute | solution.py:94
  8.5 4.5 %collective-permute-start.4 = (f32[1,128,256]{2,1,0:T(8,128)S(1)}, f32[1,128,256]{2,1,0:T(8,128)S(1)}, u32[]{:S(2)}, u32[]{:S(2)}) collective-permute-start(f32[1,128,256]{2,1,0:T(8,128)S(1)} %get-tuple-element.25), channel_id=1, source_target_pairs={{18,2},{19,3},{22,6},{23,7},{26,10},{27,11},{30,14},{31,15},{0,16}... | collective-permute-start | bytes 393224 | tf_op jit(solution)/shard_map/ppermute | solution.py:654
  14.7 2.7 %collective-permute-start.3 = (f32[1,2,2,64,256]{4,3,2,1,0:T(8,128)S(1)}, f32[1,2,2,64,256]{4,3,2,1,0:T(8,128)S(1)}, u32[]{:S(2)}, u32[]{:S(2)}) collective-permute-start(f32[1,2,2,64,256]{4,3,2,1,0:T(8,128)S(1)} %choose.3.refs_1_), channel_id=1, source_target_pairs={{16,0},{17,1},{18,2},{19,3},{20,4},{21,5},{22,6},{23,7},{24,8},{25... | collective-permute-start | bytes 786440 | tf_op jit(solution)/shard_map/ppermute | solution.py:68
  17.9 1.6 %collective-permute-done.5.refs_2_ = f32[1,128,256]{2,1,0:T(8,128)S(1)} collective-permute-done((f32[1,128,256]{2,1,0:T(8,128)S(1)}, f32[1,128,256]{2,1,0:T(8,128)S(1)}, u32[]{:S(2)}, u32[]{:S(2)}) %collective-permute-start.5) | collective-permute-done | bytes 131104 | tf_op jit(solution)/shard_map/ppermute | solution.py:75
  20.4 9.4 %collective-permute-done.3.refs_2_ = f32[1,2,2,64,256]{4,3,2,1,0:T(8,128)S(1)} collective-permute-done((f32[1,2,2,64,256]{4,3,2,1,0:T(8,128)S(1)}, f32[1,2,2,64,256]{4,3,2,1,0:T(8,128)S(1)}, u32[]{:S(2)}, u32[]{:S(2)}) %collective-permute-start.3) | collective-permute-done | bytes 262176 | tf_op jit(solution)/shard_map/ppermute | solution.py:68
  29.8 1.5 %collective-permute-done.7.refs_4_ = f32[1,2,2,64,256]{4,3,2,1,0:T(8,128)S(1)} collective-permute-done((f32[1,2,2,64,256]{4,3,2,1,0:T(8,128)S(1)}, f32[1,2,2,64,256]{4,3,2,1,0:T(8,128)S(1)}, u32[]{:S(2)}, u32[]{:S(2)}) %collective-permute-start.7) | collective-permute-done | bytes 262176 | tf_op jit(solution)/shard_map/ppermute | solution.py:75
  31.4 3.4 %first.1 = (f32[1,2,256,256]{3,2,1,0:T(8,128)S(1)}, f32[8,80,256]{2,1,0:T(8,128)S(1)}, f32[2,1,2,32,256]{4,3,2,1,0:T(8,128)S(1)}) custom-call(s32[2,8]{1,0:T(2,128)S(1)} %bitcast.5, f32[1,2,2,64,256]{4,3,2,1,0:T(8,128)S(1)} %choose.3.refs_1_, f32[1,2,2,64,256]{4,3,2,1,0:T(8,128)S(1)} %collective-permute-done.3.refs_2_, ...), custom_call_target="tpu_custom_call" | custom-call | tf_op jit(solution)/shard_map/first/pallas_call | solution.py:594
  34.8 14.2 %all_to_all.10.refs_0_ = f32[8,80,256]{2,1,0:T(8,128)S(1)} all-to-all(f32[8,80,256]{2,1,0:T(8,128)S(1)} %get-tuple-element.29), channel_id=1, replica_groups={{0,4,8,12,2,6,10,14},{1,5,9,13,3,7,11,15},{16,20,24,28,18,22,26,30},{17..., dimensions={0} | all-to-all | bytes 1310720 | tf_op jit(solution)/shard_map/all_to_all | solution.py:97
  49.0 3.2 %collective-permute-start.11 = (f32[80,256]{1,0:T(8,128)S(1)}, f32[80,256]{1,0:T(8,128)S(1)}, u32[]{:S(2)}, u32[]{:S(2)}) collective-permute-start(f32[80,256]{1,0:T(8,128)S(1)} %sum.1.refs_1_), channel_id=1, source_target_pairs={{16,0},{17,1},{18,2},{19,3},{20,4},{21,5},{22,6},{23,7},{24,8},{25... | collective-permute-start | bytes 245768 | tf_op jit(solution)/shard_map/ppermute | solution.py:68
  52.2 3.2 %collective-permute-done.11.refs_2_ = f32[80,256]{1,0:T(8,128)S(1)} collective-permute-done((f32[80,256]{1,0:T(8,128)S(1)}, f32[80,256]{1,0:T(8,128)S(1)}, u32[]{:S(2)}, u32[]{:S(2)}) %collective-permute-start.11) | collective-permute-done | bytes 81952 | tf_op jit(solution)/shard_map/ppermute | solution.py:68
  55.5 16.2 %all_to_all.11.refs_0_.refs_4_ = f32[8,2,1,2,32,256]{5,4,3,2,1,0:T(8,128)S(1)} all-to-all(f32[8,2,1,2,32,256]{5,4,3,2,1,0:T(8,128)S(1)} %step.1), channel_id=1, replica_groups={{0,4,8,12,2,6,10,14},{1,5,9,13,3,7,11,15},{16,20,24,28,18,22,26,30},{17..., dimensions={0} | all-to-all | bytes 2097152 | tf_op jit(solution)/shard_map/all_to_all | solution.py:97
  71.7 1.3 %again.1 = (f32[256,256]{1,0:T(8,128)S(1)}, f32[1,256,256]{2,1,0:T(8,128)S(1)}, f32[1,2,512,256]{3,2,1,0:T(8,128)S(1)}) custom-call(f32[8,2,1,2,32,256]{5,4,3,2,1,0:T(8,128)S(1)} %all_to_all.11.refs_0_.refs_4_, f32[1,2,256,256]{3,2,1,0:T(8,128)S(1)} %get-tuple-element.30.refs_1_, bf16[2,2,256,256]{3,2,1,0:T(8,128)(2,1)S(1)} %copy-done.1, ...), custom_call_target="tpu_custom_call" | custom-call | tf_op jit(solution)/shard_map/again/pallas_call | solution.py:594
  73.0 1.5 %collective-permute-done.13.refs_2_ = f32[1,256,256]{2,1,0:T(8,128)S(1)} collective-permute-done((f32[1,256,256]{2,1,0:T(8,128)S(1)}, f32[1,256,256]{2,1,0:T(8,128)S(1)}, u32[]{:S(2)}, u32[]{:S(2)}) %collective-permute-start.13) | collective-permute-done | bytes 262176 | tf_op jit(solution)/shard_map/ppermute | solution.py:75
  74.5 1.5 %terms.1 = (f32[1,2,2,64,256]{4,3,2,1,0:T(8,128)S(1)}, f32[1,2,2,64,256]{4,3,2,1,0:T(8,128)S(1)}) custom-call(s32[2,8]{1,0:T(2,128)S(1)} %bitcast.6, f32[1,256,256]{2,1,0:T(8,128)S(1)} %get-tuple-element.32.refs_1_, f32[1,256,256]{2,1,0:T(8,128)S(1)} %collective-permute-done.13.refs_2_, f32[1,256,256]{2,1,0:T(8,128)S(1)} %order.1.refs_9_.refs_3_, ...), custom_call_target="tpu_custom_call" | custom-call | tf_op jit(solution)/shard_map/terms/pallas_call | solution.py:594
  76.2 1.4 %collective-permute-done.14.refs_3_ = f32[1,2,2,64,256]{4,3,2,1,0:T(8,128)S(1)} collective-permute-done((f32[1,2,2,64,256]{4,3,2,1,0:T(8,128)S(1)}, f32[1,2,2,64,256]{4,3,2,1,0:T(8,128)S(1)}, u32[]{:S(2)}, u32[]{:S(2)}) %collective-permute-start.14) | collective-permute-done | bytes 262176 | tf_op jit(solution)/shard_map/ppermute | solution.py:75
  78.1 0.9 collective-permute-start.16
  79.0 2.4 %collective-permute-start.17 = (f32[2,64,256]{2,1,0:T(8,128)S(1)}, f32[2,64,256]{2,1,0:T(8,128)S(1)}, u32[]{:S(2)}, u32[]{:S(2)}) collective-permute-start(f32[2,64,256]{2,1,0:T(8,128)S(1)} %get-tuple-element.39), channel_id=1, source_target_pairs={{0,12},{1,13},{2,14},{3,15},{4,8},{5,9},{6,10},{7,11},{8,4},{9,5},... | collective-permute-start | bytes 393224 | tf_op jit(solution)/shard_map/ppermute | solution.py:94
  81.4 2.0 %collective-permute-done.15.refs_3_ = f32[2,64,256]{2,1,0:T(8,128)S(1)} collective-permute-done((f32[2,64,256]{2,1,0:T(8,128)S(1)}, f32[2,64,256]{2,1,0:T(8,128)S(1)}, u32[]{:S(2)}, u32[]{:S(2)}) %collective-permute-start.15) | collective-permute-done | bytes 131104 | tf_op jit(solution)/shard_map/ppermute | solution.py:94
  83.5 1.0 %collective-permute-done.16.refs_4_ = f32[2,64,256]{2,1,0:T(8,128)S(1)} collective-permute-done((f32[2,64,256]{2,1,0:T(8,128)S(1)}, f32[2,64,256]{2,1,0:T(8,128)S(1)}, u32[]{:S(2)}, u32[]{:S(2)}) %collective-permute-start.16) | collective-permute-done | bytes 131104 | tf_op jit(solution)/shard_map/ppermute | solution.py:94
  84.5 3.0 %collective-permute-done.17.refs_5_ = f32[2,64,256]{2,1,0:T(8,128)S(1)} collective-permute-done((f32[2,64,256]{2,1,0:T(8,128)S(1)}, f32[2,64,256]{2,1,0:T(8,128)S(1)}, u32[]{:S(2)}, u32[]{:S(2)}) %collective-permute-start.17) | collective-permute-done | bytes 131104 | tf_op jit(solution)/shard_map/ppermute | solution.py:94
  89.1 6.1 %collective-permute-done.18.refs_3_ = f32[2,64,512]{2,1,0:T(8,128)S(1)} collective-permute-done((f32[2,64,512]{2,1,0:T(8,128)S(1)}, f32[2,64,512]{2,1,0:T(8,128)S(1)}, u32[]{:S(2)}, u32[]{:S(2)}) %collective-permute-start.18) | collective-permute-done | bytes 262176 | tf_op jit(solution)/shard_map/ppermute | solution.py:82
  (47 shorter events, 8.4 us)
Async XLA Ops:
  0.6 16.8 %collective-permute-start.8 = (f32[2,1,256,256]{3,2,1,0:T(8,128)}, f32[2,1,256,256]{3,2,1,0:T(8,128)S(1)}, u32[]{:S(2)}, u32[]{:S(2)}) collective-permute-start(f32[2,1,256,256]{3,2,1,0:T(8,128)} %refs_5_.1), channel_id=1, source_target_pairs={{2,0},{3,1},{0,2},{1,3},{6,4},{7,5},{4,6},{5,7},{10,8},{11,9},{8,1... | collective-permute-start | bytes 1572872 | tf_op jit(solution)/shard_map/ppermute | solution.py:82
  3.7 10.4 %copy-start.4 = (f32[2,1,256,256]{3,2,1,0:T(8,128)S(1)}, f32[2,1,256,256]{3,2,1,0:T(8,128)}, u32[]{:S(2)}) copy-start(f32[2,1,256,256]{3,2,1,0:T(8,128)} %refs_5_.1) | copy-start | bytes 1572868
  5.0 9.0 %collective-permute-start = (f32[2,64,256]{2,1,0:T(8,128)S(1)}, f32[2,64,256]{2,1,0:T(8,128)S(1)}, u32[]{:S(2)}, u32[]{:S(2)}) collective-permute-start(f32[2,64,256]{2,1,0:T(8,128)S(1)} %get-tuple-element.21), channel_id=1, source_target_pairs={{0,4},{1,5},{2,6},{3,7},{4,0},{5,1},{6,2},{7,3},{8,12},{9,13},{10,... | collective-permute-start | bytes 393224 | tf_op jit(solution)/shard_map/ppermute | solution.py:94
  6.5 7.6 %collective-permute-start.1 = (f32[2,64,256]{2,1,0:T(8,128)S(1)}, f32[2,64,256]{2,1,0:T(8,128)S(1)}, u32[]{:S(2)}, u32[]{:S(2)}) collective-permute-start(f32[2,64,256]{2,1,0:T(8,128)S(1)} %get-tuple-element.22), channel_id=1, source_target_pairs={{0,8},{1,9},{2,10},{3,11},{4,12},{5,13},{6,14},{7,15},{8,0},{9,1},... | collective-permute-start | bytes 393224 | tf_op jit(solution)/shard_map/ppermute | solution.py:94
  8.1 6.2 %collective-permute-start.2 = (f32[2,64,256]{2,1,0:T(8,128)S(1)}, f32[2,64,256]{2,1,0:T(8,128)S(1)}, u32[]{:S(2)}, u32[]{:S(2)}) collective-permute-start(f32[2,64,256]{2,1,0:T(8,128)S(1)} %get-tuple-element.23), channel_id=1, source_target_pairs={{0,12},{1,13},{2,14},{3,15},{4,8},{5,9},{6,10},{7,11},{8,4},{9,5},... | collective-permute-start | bytes 393224 | tf_op jit(solution)/shard_map/ppermute | solution.py:94
  8.5 8.9 %collective-permute-start.4 = (f32[1,128,256]{2,1,0:T(8,128)S(1)}, f32[1,128,256]{2,1,0:T(8,128)S(1)}, u32[]{:S(2)}, u32[]{:S(2)}) collective-permute-start(f32[1,128,256]{2,1,0:T(8,128)S(1)} %get-tuple-element.25), channel_id=1, source_target_pairs={{18,2},{19,3},{22,6},{23,7},{26,10},{27,11},{30,14},{31,15},{0,16}... | collective-permute-start | bytes 393224 | tf_op jit(solution)/shard_map/ppermute | solution.py:654
  14.1 15.8 %collective-permute-start.9 = (f32[2,1,256,256]{3,2,1,0:T(8,128)S(1)}, f32[2,1,256,256]{3,2,1,0:T(8,128)S(1)}, u32[]{:S(2)}, u32[]{:S(2)}) collective-permute-start(f32[2,1,256,256]{3,2,1,0:T(8,128)S(1)} %copy-done.4), channel_id=1, source_target_pairs={{1,0},{0,1},{3,2},{2,3},{5,4},{4,5},{7,6},{6,7},{9,8},{8,9},{11,10... | collective-permute-start | bytes 1572872 | tf_op jit(solution)/shard_map/ppermute | solution.py:75
  14.3 17.0 %copy-start.1 = (bf16[2,2,256,256]{3,2,1,0:T(8,128)(2,1)S(1)}, bf16[2,2,256,256]{3,2,1,0:T(8,128)(2,1)}, u32[]{:S(2)}) copy-start(bf16[2,2,256,256]{3,2,1,0:T(8,128)(2,1)} %constant.4.clone.refs_10_.refs_2_.refs_6_) | copy-start | bytes 1572868
  14.7 16.7 %copy-start = (bf16[2,2,256,256]{3,2,1,0:T(8,128)(2,1)S(1)}, bf16[2,2,256,256]{3,2,1,0:T(8,128)(2,1)}, u32[]{:S(2)}) copy-start(bf16[2,2,256,256]{3,2,1,0:T(8,128)(2,1)} %constant.5.clone.refs_11_.refs_3_.refs_7_) | copy-start | bytes 1572868
  14.7 15.1 %collective-permute-start.3 = (f32[1,2,2,64,256]{4,3,2,1,0:T(8,128)S(1)}, f32[1,2,2,64,256]{4,3,2,1,0:T(8,128)S(1)}, u32[]{:S(2)}, u32[]{:S(2)}) collective-permute-start(f32[1,2,2,64,256]{4,3,2,1,0:T(8,128)S(1)} %choose.3.refs_1_), channel_id=1, source_target_pairs={{16,0},{17,1},{18,2},{19,3},{20,4},{21,5},{22,6},{23,7},{24,8},{25... | collective-permute-start | bytes 786440 | tf_op jit(solution)/shard_map/ppermute | solution.py:68
  17.4 14.0 %collective-permute-start.10 = (f32[2,1,256,256]{3,2,1,0:T(8,128)S(1)}, f32[2,1,256,256]{3,2,1,0:T(8,128)S(1)}, u32[]{:S(2)}, u32[]{:S(2)}) collective-permute-start(f32[2,1,256,256]{3,2,1,0:T(8,128)S(1)} %collective-permute-done.8.refs_6_), channel_id=1, source_target_pairs={{1,0},{0,1},{3,2},{2,3},{5,4},{4,5},{7,6},{6,7},{9,8},{8,9},{11,10... | collective-permute-start | bytes 1572872 | tf_op jit(solution)/shard_map/ppermute | solution.py:75
  17.4 2.1 %collective-permute-start.5 = (f32[1,128,256]{2,1,0:T(8,128)S(1)}, f32[1,128,256]{2,1,0:T(8,128)S(1)}, u32[]{:S(2)}, u32[]{:S(2)}) collective-permute-start(f32[1,128,256]{2,1,0:T(8,128)S(1)} %collective-permute-done.4.refs_1_), channel_id=1, source_target_pairs={{1,0},{0,1},{3,2},{2,3},{5,4},{4,5},{7,6},{6,7},{9,8},{8,9},{11,10... | collective-permute-start | bytes 393224 | tf_op jit(solution)/shard_map/ppermute | solution.py:75
  20.2 9.6 %collective-permute-start.6 = (f32[1,2,2,64,256]{4,3,2,1,0:T(8,128)S(1)}, f32[1,2,2,64,256]{4,3,2,1,0:T(8,128)S(1)}, u32[]{:S(2)}, u32[]{:S(2)}) collective-permute-start(f32[1,2,2,64,256]{4,3,2,1,0:T(8,128)S(1)} %choose.3.refs_1_), channel_id=1, source_target_pairs={{1,0},{0,1},{3,2},{2,3},{5,4},{4,5},{7,6},{6,7},{9,8},{8,9},{11,10... | collective-permute-start | bytes 786440 | tf_op jit(solution)/shard_map/ppermute | solution.py:75
  29.8 1.5 %collective-permute-start.7 = (f32[1,2,2,64,256]{4,3,2,1,0:T(8,128)S(1)}, f32[1,2,2,64,256]{4,3,2,1,0:T(8,128)S(1)}, u32[]{:S(2)}, u32[]{:S(2)}) collective-permute-start(f32[1,2,2,64,256]{4,3,2,1,0:T(8,128)S(1)} %collective-permute-done.3.refs_2_), channel_id=1, source_target_pairs={{1,0},{0,1},{3,2},{2,3},{5,4},{4,5},{7,6},{6,7},{9,8},{8,9},{11,10... | collective-permute-start | bytes 786440 | tf_op jit(solution)/shard_map/ppermute | solution.py:75
  49.0 6.4 %collective-permute-start.11 = (f32[80,256]{1,0:T(8,128)S(1)}, f32[80,256]{1,0:T(8,128)S(1)}, u32[]{:S(2)}, u32[]{:S(2)}) collective-permute-start(f32[80,256]{1,0:T(8,128)S(1)} %sum.1.refs_1_), channel_id=1, source_target_pairs={{16,0},{17,1},{18,2},{19,3},{20,4},{21,5},{22,6},{23,7},{24,8},{25... | collective-permute-start | bytes 245768 | tf_op jit(solution)/shard_map/ppermute | solution.py:68
  72.9 1.6 %collective-permute-start.13 = (f32[1,256,256]{2,1,0:T(8,128)S(1)}, f32[1,256,256]{2,1,0:T(8,128)S(1)}, u32[]{:S(2)}, u32[]{:S(2)}) collective-permute-start(f32[1,256,256]{2,1,0:T(8,128)S(1)} %get-tuple-element.32.refs_1_), channel_id=1, source_target_pairs={{1,0},{0,1},{3,2},{2,3},{5,4},{4,5},{7,6},{6,7},{9,8},{8,9},{11,10... | collective-permute-start | bytes 786440 | tf_op jit(solution)/shard_map/ppermute | solution.py:75
  76.0 1.6 %collective-permute-start.14 = (f32[1,2,2,64,256]{4,3,2,1,0:T(8,128)S(1)}, f32[1,2,2,64,256]{4,3,2,1,0:T(8,128)S(1)}, u32[]{:S(2)}, u32[]{:S(2)}) collective-permute-start(f32[1,2,2,64,256]{4,3,2,1,0:T(8,128)S(1)} %get-tuple-element.35), channel_id=1, source_target_pairs={{1,0},{0,1},{3,2},{2,3},{5,4},{4,5},{7,6},{6,7},{9,8},{8,9},{11,10... | collective-permute-start | bytes 786440 | tf_op jit(solution)/shard_map/ppermute | solution.py:75
  77.9 5.6 %collective-permute-start.15 = (f32[2,64,256]{2,1,0:T(8,128)S(1)}, f32[2,64,256]{2,1,0:T(8,128)S(1)}, u32[]{:S(2)}, u32[]{:S(2)}) collective-permute-start(f32[2,64,256]{2,1,0:T(8,128)S(1)} %get-tuple-element.37), channel_id=1, source_target_pairs={{0,4},{1,5},{2,6},{3,7},{4,0},{5,1},{6,2},{7,3},{8,12},{9,13},{10,... | collective-permute-start | bytes 393224 | tf_op jit(solution)/shard_map/ppermute | solution.py:94
  78.1 6.4 %collective-permute-start.16 = (f32[2,64,256]{2,1,0:T(8,128)S(1)}, f32[2,64,256]{2,1,0:T(8,128)S(1)}, u32[]{:S(2)}, u32[]{:S(2)}) collective-permute-start(f32[2,64,256]{2,1,0:T(8,128)S(1)} %get-tuple-element.38), channel_id=1, source_target_pairs={{0,8},{1,9},{2,10},{3,11},{4,12},{5,13},{6,14},{7,15},{8,0},{9,1},... | collective-permute-start | bytes 393224 | tf_op jit(solution)/shard_map/ppermute | solution.py:94
  79.0 8.5 %collective-permute-start.17 = (f32[2,64,256]{2,1,0:T(8,128)S(1)}, f32[2,64,256]{2,1,0:T(8,128)S(1)}, u32[]{:S(2)}, u32[]{:S(2)}) collective-permute-start(f32[2,64,256]{2,1,0:T(8,128)S(1)} %get-tuple-element.39), channel_id=1, source_target_pairs={{0,12},{1,13},{2,14},{3,15},{4,8},{5,9},{6,10},{7,11},{8,4},{9,5},... | collective-permute-start | bytes 393224 | tf_op jit(solution)/shard_map/ppermute | solution.py:94
  81.4 7.1 %collective-permute-start.12 = (f32[256,256]{1,0:T(8,128)S(1)}, f32[256,256]{1,0:T(8,128)S(1)}, u32[]{:S(2)}, u32[]{:S(2)}) collective-permute-start(f32[256,256]{1,0:T(8,128)S(1)} %get-tuple-element.31.refs_2_), channel_id=1, source_target_pairs={{1,0},{0,1},{3,2},{2,3},{5,4},{4,5},{7,6},{6,7},{9,8},{8,9},{11,10... | collective-permute-start | bytes 786440 | tf_op jit(solution)/shard_map/ppermute | solution.py:75
  87.9 7.3 %copy-start.2 = (f32[2,128,512]{2,1,0:T(8,128)S(1)}, f32[2,128,512]{2,1,0:T(8,128)}, u32[]{:S(2)}) copy-start(f32[2,128,512]{2,1,0:T(8,128)} %refs_1_.1) | copy-start | bytes 1572868
  87.9 7.3 %collective-permute-start.18 = (f32[2,64,512]{2,1,0:T(8,128)S(1)}, f32[2,64,512]{2,1,0:T(8,128)S(1)}, u32[]{:S(2)}, u32[]{:S(2)}) collective-permute-start(f32[2,64,512]{2,1,0:T(8,128)S(1)} %place.1.refs_2_), channel_id=1, source_target_pairs={{2,0},{3,1},{0,2},{1,3},{6,4},{7,5},{4,6},{5,7},{10,8},{11,9},{8,1... | collective-permute-start | bytes 786440 | tf_op jit(solution)/shard_map/ppermute | solution.py:82
  95.2 1.6 %collective-permute-start.19 = (f32[2,64,512]{2,1,0:T(8,128)S(1)}, f32[2,64,512]{2,1,0:T(8,128)S(1)}, u32[]{:S(2)}, u32[]{:S(2)}) collective-permute-start(f32[2,64,512]{2,1,0:T(8,128)S(1)} %update.1.refs_0_), channel_id=1, source_target_pairs={{1,0},{0,1},{3,2},{2,3},{5,4},{4,5},{7,6},{6,7},{9,8},{8,9},{11,10... | collective-permute-start | bytes 786440 | tf_op jit(solution)/shard_map/ppermute | solution.py:75
  (3 other events, 6.8 us)

commit v9 on v8

--- a/solution.py
+++ b/solution.py
@@ -535,14 +535,13 @@
     power = powers[0][...]
     for more in powers[1:]:
         power += more[...]
-    doubled[0] = power
-    doubled[1] = power
-    wide = doubled.reshape(2 * length, length)
+    doubled[:length] = power
+    doubled[length:] = power
     total[...] = jnp.zeros_like(total)
     for region in range(layout.regions):
         cover = Cover(layout, offsets, region, band, core)
         start = cover.start()
-        near = wide[pl.ds(pl.multiple_of(start // 8 * 8, 8), strip + 8), :]
+        near = doubled[pl.ds(pl.multiple_of(start // 8 * 8, 8), strip + 8), :]
         near = pltpu.roll(near, (strip + 8 - start % 8) % (strip + 8), 0)[:strip]
         cover.add(total, jnp.where(cover.inside(), near, 0.0))
     out[...] = total[:, : layout.width] + object_damping
@@ -644,7 +643,8 @@
             for array in (corners, band_owner, object_bands, measured)
         )
     )
-    probes = [probe_modes] + [layout.from_twin(probe_modes, step) for step in range(1, halves)]
+    part_measured, held_probes = lax.optimization_barrier((part_measured, probe_modes))
+    probes = [probe_modes] + [layout.from_twin(held_probes, step) for step in range(1, halves)]
     if halves > 1:
         pairs = [
             (layout.device(t, l, t, c), layout.device(u, l, t, c))
@@ -745,7 +745,7 @@
         "density",
         (corners, owners, *from_cores(probe_power)),
         [(strip, layout.width)],
-        scratch=[(2, length, length), (strip, layout.width + lanes)],
+        scratch=[(2 * length, length), (strip, layout.width + lanes)],
         scalar_count=2,
     )
     (placed,) = call(

time: 97.9 us -> 97.8 us (level)
  transfers between devices with their start and end apart: 20 -> 20, of which waited for: 12 -> 12; matrix products, arithmetic and copies ran while one was open for 0% -> 0% of each run, Pallas kernels for 5% -> 3%
where the time goes in v9:
time: 97.8 us; the launch traced here: 97.5 us
  waiting for transfers between devices  31.7 us (32%)
  blocking collectives  30.2 us (31%)
  starting transfers between devices  22.2 us (23%)
  Pallas kernels  11.9 us (12%)
    all_to_all x2, blocking collectives, within_cube(): lax.all_to_all(array, axes, split_axis=0, concat_axis=0, tiled=True, axis...  30.2 us
    ppermute x2, waiting for transfers between devices, from_upper(): return lax.ppermute(array, axes, pairs)  12.7 us
    pallas_call x14, Pallas kernels, call(): pl.pallas_call(inner, name=name, out_shape=shapes, in_specs=[on_chip] * c...  10.6 us
    ppermute x6, starting transfers between devices, to_row(): return lax.ppermute(array, axes, pairs)  7.04 us
    ppermute x9, waiting for transfers between devices, from_core(): return lax.ppermute(array, axes, pairs)  6.71 us
    ppermute x6, waiting for transfers between devices, to_row(): return lax.ppermute(array, axes, pairs)  6.25 us
    ppermute x2, waiting for transfers between devices, from_twin(): return lax.ppermute(array, axes, pairs)  6.08 us
    ppermute x2, starting transfers between devices, from_upper(): return lax.ppermute(array, axes, pairs)  5.86 us
  transfers between devices with their start and end apart: 20, of which 12 were waited for; matrix products, arithmetic and copies ran while one was open for 0% of the time, Pallas kernels for 3%

profile of v9, /device:TPU:0, one launch (start us, length us, event | category | flops | bytes accessed | tf_op | source)
XLA Modules:
  0.0 97.5 jit_solution(17444233886180042116)
XLA Ops:
  0.6 1.3 %cut.1 = (f32[2,64,256]{2,1,0:T(8,128)S(1)}, f32[2,64,256]{2,1,0:T(8,128)S(1)}, f32[2,64,256]{2,1,0:T(8,128)S(1)}, f32[2,64,256]{2,1,0:T(8,128)S(1)}, f32[1,128,256]{2,1,0:T(8,128)S(1)}) custom-call(s32[2,8]{1,0:T(2,128)} %bitcast.2, s32[8]{0:T(128)} %owners.1, f32[2,128,512]{2,1,0:T(8,128)} %refs_1_.1, f32[1,256,256]{2,1,0:T(8,128)} %refs_0_.1), custom_call_target="tpu_custom_call" | custom-call | tf_op jit(solution)/shard_map/cut/pallas_call | solution.py:626
  2.0 3.0 %collective-permute-start.8 = (f32[2,1,256,256]{3,2,1,0:T(8,128)S(1)}, f32[2,1,256,256]{3,2,1,0:T(8,128)S(1)}, u32[]{:S(2)}, u32[]{:S(2)}) collective-permute-start(f32[2,1,256,256]{3,2,1,0:T(8,128)S(1)} %copy-done.4), channel_id=1, source_target_pairs={{2,0},{3,1},{0,2},{1,3},{6,4},{7,5},{4,6},{5,7},{10,8},{11,9},{8,1... | collective-permute-start | bytes 1572872 | tf_op jit(solution)/shard_map/ppermute | solution.py:82
  5.0 1.5 %collective-permute-start = (f32[2,64,256]{2,1,0:T(8,128)S(1)}, f32[2,64,256]{2,1,0:T(8,128)S(1)}, u32[]{:S(2)}, u32[]{:S(2)}) collective-permute-start(f32[2,64,256]{2,1,0:T(8,128)S(1)} %get-tuple-element.23), channel_id=1, source_target_pairs={{0,4},{1,5},{2,6},{3,7},{4,0},{5,1},{6,2},{7,3},{8,12},{9,13},{10,... | collective-permute-start | bytes 393224 | tf_op jit(solution)/shard_map/ppermute | solution.py:94
  6.5 1.6 %collective-permute-start.1 = (f32[2,64,256]{2,1,0:T(8,128)S(1)}, f32[2,64,256]{2,1,0:T(8,128)S(1)}, u32[]{:S(2)}, u32[]{:S(2)}) collective-permute-start(f32[2,64,256]{2,1,0:T(8,128)S(1)} %get-tuple-element.24), channel_id=1, source_target_pairs={{0,8},{1,9},{2,10},{3,11},{4,12},{5,13},{6,14},{7,15},{8,0},{9,1},... | collective-permute-start | bytes 393224 | tf_op jit(solution)/shard_map/ppermute | solution.py:94
  8.5 4.5 %collective-permute-start.4 = (f32[1,128,256]{2,1,0:T(8,128)S(1)}, f32[1,128,256]{2,1,0:T(8,128)S(1)}, u32[]{:S(2)}, u32[]{:S(2)}) collective-permute-start(f32[1,128,256]{2,1,0:T(8,128)S(1)} %get-tuple-element.28), channel_id=1, source_target_pairs={{18,2},{19,3},{22,6},{23,7},{26,10},{27,11},{30,14},{31,15},{0,16}... | collective-permute-start | bytes 393224 | tf_op jit(solution)/shard_map/ppermute | solution.py:654
  14.7 2.7 %collective-permute-start.3 = (f32[1,2,2,64,256]{4,3,2,1,0:T(8,128)S(1)}, f32[1,2,2,64,256]{4,3,2,1,0:T(8,128)S(1)}, u32[]{:S(2)}, u32[]{:S(2)}) collective-permute-start(f32[1,2,2,64,256]{4,3,2,1,0:T(8,128)S(1)} %choose.3.refs_1_), channel_id=1, source_target_pairs={{16,0},{17,1},{18,2},{19,3},{20,4},{21,5},{22,6},{23,7},{24,8},{25... | collective-permute-start | bytes 786440 | tf_op jit(solution)/shard_map/ppermute | solution.py:68
  17.9 1.6 %collective-permute-done.5.refs_2_ = f32[1,128,256]{2,1,0:T(8,128)S(1)} collective-permute-done((f32[1,128,256]{2,1,0:T(8,128)S(1)}, f32[1,128,256]{2,1,0:T(8,128)S(1)}, u32[]{:S(2)}, u32[]{:S(2)}) %collective-permute-start.5) | collective-permute-done | bytes 131104 | tf_op jit(solution)/shard_map/ppermute | solution.py:75
  20.4 9.4 %collective-permute-done.3.refs_2_ = f32[1,2,2,64,256]{4,3,2,1,0:T(8,128)S(1)} collective-permute-done((f32[1,2,2,64,256]{4,3,2,1,0:T(8,128)S(1)}, f32[1,2,2,64,256]{4,3,2,1,0:T(8,128)S(1)}, u32[]{:S(2)}, u32[]{:S(2)}) %collective-permute-start.3) | collective-permute-done | bytes 262176 | tf_op jit(solution)/shard_map/ppermute | solution.py:68
  29.8 1.5 %collective-permute-done.7.refs_4_ = f32[1,2,2,64,256]{4,3,2,1,0:T(8,128)S(1)} collective-permute-done((f32[1,2,2,64,256]{4,3,2,1,0:T(8,128)S(1)}, f32[1,2,2,64,256]{4,3,2,1,0:T(8,128)S(1)}, u32[]{:S(2)}, u32[]{:S(2)}) %collective-permute-start.7) | collective-permute-done | bytes 262176 | tf_op jit(solution)/shard_map/ppermute | solution.py:75
  31.3 3.4 %first.1 = (f32[1,2,256,256]{3,2,1,0:T(8,128)S(1)}, f32[8,80,256]{2,1,0:T(8,128)S(1)}, f32[2,1,2,32,256]{4,3,2,1,0:T(8,128)S(1)}) custom-call(s32[2,8]{1,0:T(2,128)S(1)} %bitcast.5, f32[1,2,2,64,256]{4,3,2,1,0:T(8,128)S(1)} %choose.3.refs_1_, f32[1,2,2,64,256]{4,3,2,1,0:T(8,128)S(1)} %collective-permute-done.3.refs_2_, ...), custom_call_target="tpu_custom_call" | custom-call | tf_op jit(solution)/shard_map/first/pallas_call | solution.py:593
  34.8 14.2 %all_to_all.10.refs_0_ = f32[8,80,256]{2,1,0:T(8,128)S(1)} all-to-all(f32[8,80,256]{2,1,0:T(8,128)S(1)} %get-tuple-element.33), channel_id=1, replica_groups={{0,4,8,12,2,6,10,14},{1,5,9,13,3,7,11,15},{16,20,24,28,18,22,26,30},{17..., dimensions={0} | all-to-all | bytes 1310720 | tf_op jit(solution)/shard_map/all_to_all | solution.py:97
  49.0 3.2 %collective-permute-start.11 = (f32[80,256]{1,0:T(8,128)S(1)}, f32[80,256]{1,0:T(8,128)S(1)}, u32[]{:S(2)}, u32[]{:S(2)}) collective-permute-start(f32[80,256]{1,0:T(8,128)S(1)} %sum.1.refs_1_), channel_id=1, source_target_pairs={{16,0},{17,1},{18,2},{19,3},{20,4},{21,5},{22,6},{23,7},{24,8},{25... | collective-permute-start | bytes 245768 | tf_op jit(solution)/shard_map/ppermute | solution.py:68
  52.1 3.3 %collective-permute-done.11.refs_2_ = f32[80,256]{1,0:T(8,128)S(1)} collective-permute-done((f32[80,256]{1,0:T(8,128)S(1)}, f32[80,256]{1,0:T(8,128)S(1)}, u32[]{:S(2)}, u32[]{:S(2)}) %collective-permute-start.11) | collective-permute-done | bytes 81952 | tf_op jit(solution)/shard_map/ppermute | solution.py:68
  55.6 16.0 %all_to_all.11.refs_0_.refs_4_ = f32[8,2,1,2,32,256]{5,4,3,2,1,0:T(8,128)S(1)} all-to-all(f32[8,2,1,2,32,256]{5,4,3,2,1,0:T(8,128)S(1)} %step.1), channel_id=1, replica_groups={{0,4,8,12,2,6,10,14},{1,5,9,13,3,7,11,15},{16,20,24,28,18,22,26,30},{17..., dimensions={0} | all-to-all | bytes 2097152 | tf_op jit(solution)/shard_map/all_to_all | solution.py:97
  71.6 1.3 %again.1 = (f32[256,256]{1,0:T(8,128)S(1)}, f32[1,256,256]{2,1,0:T(8,128)S(1)}, f32[1,2,512,256]{3,2,1,0:T(8,128)S(1)}) custom-call(f32[8,2,1,2,32,256]{5,4,3,2,1,0:T(8,128)S(1)} %all_to_all.11.refs_0_.refs_4_, f32[1,2,256,256]{3,2,1,0:T(8,128)S(1)} %get-tuple-element.34.refs_1_, bf16[2,2,256,256]{3,2,1,0:T(8,128)(2,1)S(1)} %copy-done.1, ...), custom_call_target="tpu_custom_call" | custom-call | tf_op jit(solution)/shard_map/again/pallas_call | solution.py:593
  72.9 1.5 %collective-permute-done.13.refs_2_ = f32[1,256,256]{2,1,0:T(8,128)S(1)} collective-permute-done((f32[1,256,256]{2,1,0:T(8,128)S(1)}, f32[1,256,256]{2,1,0:T(8,128)S(1)}, u32[]{:S(2)}, u32[]{:S(2)}) %collective-permute-start.13) | collective-permute-done | bytes 262176 | tf_op jit(solution)/shard_map/ppermute | solution.py:75
  74.5 1.5 %terms.1 = (f32[1,2,2,64,256]{4,3,2,1,0:T(8,128)S(1)}, f32[1,2,2,64,256]{4,3,2,1,0:T(8,128)S(1)}) custom-call(s32[2,8]{1,0:T(2,128)S(1)} %bitcast.6, f32[1,256,256]{2,1,0:T(8,128)S(1)} %get-tuple-element.36.refs_1_, f32[1,256,256]{2,1,0:T(8,128)S(1)} %collective-permute-done.13.refs_2_, f32[1,256,256]{2,1,0:T(8,128)S(1)} %order.1.refs_9_.refs_3_, ...), custom_call_target="tpu_custom_call" | custom-call | tf_op jit(solution)/shard_map/terms/pallas_call | solution.py:593
  76.1 1.4 %collective-permute-done.14.refs_3_ = f32[1,2,2,64,256]{4,3,2,1,0:T(8,128)S(1)} collective-permute-done((f32[1,2,2,64,256]{4,3,2,1,0:T(8,128)S(1)}, f32[1,2,2,64,256]{4,3,2,1,0:T(8,128)S(1)}, u32[]{:S(2)}, u32[]{:S(2)}) %collective-permute-start.14) | collective-permute-done | bytes 262176 | tf_op jit(solution)/shard_map/ppermute | solution.py:75
  78.0 0.9 collective-permute-start.16
  78.9 2.4 %collective-permute-start.17 = (f32[2,64,256]{2,1,0:T(8,128)S(1)}, f32[2,64,256]{2,1,0:T(8,128)S(1)}, u32[]{:S(2)}, u32[]{:S(2)}) collective-permute-start(f32[2,64,256]{2,1,0:T(8,128)S(1)} %get-tuple-element.43), channel_id=1, source_target_pairs={{0,12},{1,13},{2,14},{3,15},{4,8},{5,9},{6,10},{7,11},{8,4},{9,5},... | collective-permute-start | bytes 393224 | tf_op jit(solution)/shard_map/ppermute | solution.py:94
  81.3 2.0 %collective-permute-done.15.refs_3_ = f32[2,64,256]{2,1,0:T(8,128)S(1)} collective-permute-done((f32[2,64,256]{2,1,0:T(8,128)S(1)}, f32[2,64,256]{2,1,0:T(8,128)S(1)}, u32[]{:S(2)}, u32[]{:S(2)}) %collective-permute-start.15) | collective-permute-done | bytes 131104 | tf_op jit(solution)/shard_map/ppermute | solution.py:94
  83.4 1.0 %collective-permute-done.16.refs_4_ = f32[2,64,256]{2,1,0:T(8,128)S(1)} collective-permute-done((f32[2,64,256]{2,1,0:T(8,128)S(1)}, f32[2,64,256]{2,1,0:T(8,128)S(1)}, u32[]{:S(2)}, u32[]{:S(2)}) %collective-permute-start.16) | collective-permute-done | bytes 131104 | tf_op jit(solution)/shard_map/ppermute | solution.py:94
  84.4 3.0 %collective-permute-done.17.refs_5_ = f32[2,64,256]{2,1,0:T(8,128)S(1)} collective-permute-done((f32[2,64,256]{2,1,0:T(8,128)S(1)}, f32[2,64,256]{2,1,0:T(8,128)S(1)}, u32[]{:S(2)}, u32[]{:S(2)}) %collective-permute-start.17) | collective-permute-done | bytes 131104 | tf_op jit(solution)/shard_map/ppermute | solution.py:94
  89.0 6.1 %collective-permute-done.18.refs_3_ = f32[2,64,512]{2,1,0:T(8,128)S(1)} collective-permute-done((f32[2,64,512]{2,1,0:T(8,128)S(1)}, f32[2,64,512]{2,1,0:T(8,128)S(1)}, u32[]{:S(2)}, u32[]{:S(2)}) %collective-permute-start.18) | collective-permute-done | bytes 262176 | tf_op jit(solution)/shard_map/ppermute | solution.py:82
  (47 shorter events, 8.5 us)
Async XLA Ops:
  2.0 15.4 %collective-permute-start.8 = (f32[2,1,256,256]{3,2,1,0:T(8,128)S(1)}, f32[2,1,256,256]{3,2,1,0:T(8,128)S(1)}, u32[]{:S(2)}, u32[]{:S(2)}) collective-permute-start(f32[2,1,256,256]{3,2,1,0:T(8,128)S(1)} %copy-done.4), channel_id=1, source_target_pairs={{2,0},{3,1},{0,2},{1,3},{6,4},{7,5},{4,6},{5,7},{10,8},{11,9},{8,1... | collective-permute-start | bytes 1572872 | tf_op jit(solution)/shard_map/ppermute | solution.py:82
  5.0 9.0 %collective-permute-start = (f32[2,64,256]{2,1,0:T(8,128)S(1)}, f32[2,64,256]{2,1,0:T(8,128)S(1)}, u32[]{:S(2)}, u32[]{:S(2)}) collective-permute-start(f32[2,64,256]{2,1,0:T(8,128)S(1)} %get-tuple-element.23), channel_id=1, source_target_pairs={{0,4},{1,5},{2,6},{3,7},{4,0},{5,1},{6,2},{7,3},{8,12},{9,13},{10,... | collective-permute-start | bytes 393224 | tf_op jit(solution)/shard_map/ppermute | solution.py:94
  6.5 7.6 %collective-permute-start.1 = (f32[2,64,256]{2,1,0:T(8,128)S(1)}, f32[2,64,256]{2,1,0:T(8,128)S(1)}, u32[]{:S(2)}, u32[]{:S(2)}) collective-permute-start(f32[2,64,256]{2,1,0:T(8,128)S(1)} %get-tuple-element.24), channel_id=1, source_target_pairs={{0,8},{1,9},{2,10},{3,11},{4,12},{5,13},{6,14},{7,15},{8,0},{9,1},... | collective-permute-start | bytes 393224 | tf_op jit(solution)/shard_map/ppermute | solution.py:94
  8.1 6.2 %collective-permute-start.2 = (f32[2,64,256]{2,1,0:T(8,128)S(1)}, f32[2,64,256]{2,1,0:T(8,128)S(1)}, u32[]{:S(2)}, u32[]{:S(2)}) collective-permute-start(f32[2,64,256]{2,1,0:T(8,128)S(1)} %get-tuple-element.25), channel_id=1, source_target_pairs={{0,12},{1,13},{2,14},{3,15},{4,8},{5,9},{6,10},{7,11},{8,4},{9,5},... | collective-permute-start | bytes 393224 | tf_op jit(solution)/shard_map/ppermute | solution.py:94
  8.5 8.9 %collective-permute-start.4 = (f32[1,128,256]{2,1,0:T(8,128)S(1)}, f32[1,128,256]{2,1,0:T(8,128)S(1)}, u32[]{:S(2)}, u32[]{:S(2)}) collective-permute-start(f32[1,128,256]{2,1,0:T(8,128)S(1)} %get-tuple-element.28), channel_id=1, source_target_pairs={{18,2},{19,3},{22,6},{23,7},{26,10},{27,11},{30,14},{31,15},{0,16}... | collective-permute-start | bytes 393224 | tf_op jit(solution)/shard_map/ppermute | solution.py:654
  14.0 5.5 %copy-start.3 = (f32[1,256,256]{2,1,0:T(8,128)S(1)}, f32[1,256,256]{2,1,0:T(8,128)}, u32[]{:S(2)}) copy-start(f32[1,256,256]{2,1,0:T(8,128)} %refs_0_.1) | copy-start | bytes 786436
  14.0 15.8 %collective-permute-start.9 = (f32[2,1,256,256]{3,2,1,0:T(8,128)S(1)}, f32[2,1,256,256]{3,2,1,0:T(8,128)S(1)}, u32[]{:S(2)}, u32[]{:S(2)}) collective-permute-start(f32[2,1,256,256]{3,2,1,0:T(8,128)S(1)} %copy-done.4), channel_id=1, source_target_pairs={{1,0},{0,1},{3,2},{2,3},{5,4},{4,5},{7,6},{6,7},{9,8},{8,9},{11,10... | collective-permute-start | bytes 1572872 | tf_op jit(solution)/shard_map/ppermute | solution.py:75
  14.3 17.0 %copy-start.1 = (bf16[2,2,256,256]{3,2,1,0:T(8,128)(2,1)S(1)}, bf16[2,2,256,256]{3,2,1,0:T(8,128)(2,1)}, u32[]{:S(2)}) copy-start(bf16[2,2,256,256]{3,2,1,0:T(8,128)(2,1)} %constant.4.clone.refs_10_.refs_2_.refs_6_) | copy-start | bytes 1572868
  14.7 16.7 %copy-start = (bf16[2,2,256,256]{3,2,1,0:T(8,128)(2,1)S(1)}, bf16[2,2,256,256]{3,2,1,0:T(8,128)(2,1)}, u32[]{:S(2)}) copy-start(bf16[2,2,256,256]{3,2,1,0:T(8,128)(2,1)} %constant.5.clone.refs_11_.refs_3_.refs_7_) | copy-start | bytes 1572868
  14.7 15.1 %collective-permute-start.3 = (f32[1,2,2,64,256]{4,3,2,1,0:T(8,128)S(1)}, f32[1,2,2,64,256]{4,3,2,1,0:T(8,128)S(1)}, u32[]{:S(2)}, u32[]{:S(2)}) collective-permute-start(f32[1,2,2,64,256]{4,3,2,1,0:T(8,128)S(1)} %choose.3.refs_1_), channel_id=1, source_target_pairs={{16,0},{17,1},{18,2},{19,3},{20,4},{21,5},{22,6},{23,7},{24,8},{25... | collective-permute-start | bytes 786440 | tf_op jit(solution)/shard_map/ppermute | solution.py:68
  17.4 14.0 %collective-permute-start.10 = (f32[2,1,256,256]{3,2,1,0:T(8,128)S(1)}, f32[2,1,256,256]{3,2,1,0:T(8,128)S(1)}, u32[]{:S(2)}, u32[]{:S(2)}) collective-permute-start(f32[2,1,256,256]{3,2,1,0:T(8,128)S(1)} %collective-permute-done.8.refs_6_), channel_id=1, source_target_pairs={{1,0},{0,1},{3,2},{2,3},{5,4},{4,5},{7,6},{6,7},{9,8},{8,9},{11,10... | collective-permute-start | bytes 1572872 | tf_op jit(solution)/shard_map/ppermute | solution.py:75
  17.4 2.1 %collective-permute-start.5 = (f32[1,128,256]{2,1,0:T(8,128)S(1)}, f32[1,128,256]{2,1,0:T(8,128)S(1)}, u32[]{:S(2)}, u32[]{:S(2)}) collective-permute-start(f32[1,128,256]{2,1,0:T(8,128)S(1)} %collective-permute-done.4.refs_1_), channel_id=1, source_target_pairs={{1,0},{0,1},{3,2},{2,3},{5,4},{4,5},{7,6},{6,7},{9,8},{8,9},{11,10... | collective-permute-start | bytes 393224 | tf_op jit(solution)/shard_map/ppermute | solution.py:75
  20.2 9.6 %collective-permute-start.6 = (f32[1,2,2,64,256]{4,3,2,1,0:T(8,128)S(1)}, f32[1,2,2,64,256]{4,3,2,1,0:T(8,128)S(1)}, u32[]{:S(2)}, u32[]{:S(2)}) collective-permute-start(f32[1,2,2,64,256]{4,3,2,1,0:T(8,128)S(1)} %choose.3.refs_1_), channel_id=1, source_target_pairs={{1,0},{0,1},{3,2},{2,3},{5,4},{4,5},{7,6},{6,7},{9,8},{8,9},{11,10... | collective-permute-start | bytes 786440 | tf_op jit(solution)/shard_map/ppermute | solution.py:75
  29.8 1.5 %collective-permute-start.7 = (f32[1,2,2,64,256]{4,3,2,1,0:T(8,128)S(1)}, f32[1,2,2,64,256]{4,3,2,1,0:T(8,128)S(1)}, u32[]{:S(2)}, u32[]{:S(2)}) collective-permute-start(f32[1,2,2,64,256]{4,3,2,1,0:T(8,128)S(1)} %collective-permute-done.3.refs_2_), channel_id=1, source_target_pairs={{1,0},{0,1},{3,2},{2,3},{5,4},{4,5},{7,6},{6,7},{9,8},{8,9},{11,10... | collective-permute-start | bytes 786440 | tf_op jit(solution)/shard_map/ppermute | solution.py:75
  49.0 6.5 %collective-permute-start.11 = (f32[80,256]{1,0:T(8,128)S(1)}, f32[80,256]{1,0:T(8,128)S(1)}, u32[]{:S(2)}, u32[]{:S(2)}) collective-permute-start(f32[80,256]{1,0:T(8,128)S(1)} %sum.1.refs_1_), channel_id=1, source_target_pairs={{16,0},{17,1},{18,2},{19,3},{20,4},{21,5},{22,6},{23,7},{24,8},{25... | collective-permute-start | bytes 245768 | tf_op jit(solution)/shard_map/ppermute | solution.py:68
  72.8 1.6 %collective-permute-start.13 = (f32[1,256,256]{2,1,0:T(8,128)S(1)}, f32[1,256,256]{2,1,0:T(8,128)S(1)}, u32[]{:S(2)}, u32[]{:S(2)}) collective-permute-start(f32[1,256,256]{2,1,0:T(8,128)S(1)} %get-tuple-element.36.refs_1_), channel_id=1, source_target_pairs={{1,0},{0,1},{3,2},{2,3},{5,4},{4,5},{7,6},{6,7},{9,8},{8,9},{11,10... | collective-permute-start | bytes 786440 | tf_op jit(solution)/shard_map/ppermute | solution.py:75
  75.9 1.6 %collective-permute-start.14 = (f32[1,2,2,64,256]{4,3,2,1,0:T(8,128)S(1)}, f32[1,2,2,64,256]{4,3,2,1,0:T(8,128)S(1)}, u32[]{:S(2)}, u32[]{:S(2)}) collective-permute-start(f32[1,2,2,64,256]{4,3,2,1,0:T(8,128)S(1)} %get-tuple-element.39), channel_id=1, source_target_pairs={{1,0},{0,1},{3,2},{2,3},{5,4},{4,5},{7,6},{6,7},{9,8},{8,9},{11,10... | collective-permute-start | bytes 786440 | tf_op jit(solution)/shard_map/ppermute | solution.py:75
  77.8 5.6 %collective-permute-start.15 = (f32[2,64,256]{2,1,0:T(8,128)S(1)}, f32[2,64,256]{2,1,0:T(8,128)S(1)}, u32[]{:S(2)}, u32[]{:S(2)}) collective-permute-start(f32[2,64,256]{2,1,0:T(8,128)S(1)} %get-tuple-element.41), channel_id=1, source_target_pairs={{0,4},{1,5},{2,6},{3,7},{4,0},{5,1},{6,2},{7,3},{8,12},{9,13},{10,... | collective-permute-start | bytes 393224 | tf_op jit(solution)/shard_map/ppermute | solution.py:94
  78.0 6.4 %collective-permute-start.16 = (f32[2,64,256]{2,1,0:T(8,128)S(1)}, f32[2,64,256]{2,1,0:T(8,128)S(1)}, u32[]{:S(2)}, u32[]{:S(2)}) collective-permute-start(f32[2,64,256]{2,1,0:T(8,128)S(1)} %get-tuple-element.42), channel_id=1, source_target_pairs={{0,8},{1,9},{2,10},{3,11},{4,12},{5,13},{6,14},{7,15},{8,0},{9,1},... | collective-permute-start | bytes 393224 | tf_op jit(solution)/shard_map/ppermute | solution.py:94
  78.9 8.4 %collective-permute-start.17 = (f32[2,64,256]{2,1,0:T(8,128)S(1)}, f32[2,64,256]{2,1,0:T(8,128)S(1)}, u32[]{:S(2)}, u32[]{:S(2)}) collective-permute-start(f32[2,64,256]{2,1,0:T(8,128)S(1)} %get-tuple-element.43), channel_id=1, source_target_pairs={{0,12},{1,13},{2,14},{3,15},{4,8},{5,9},{6,10},{7,11},{8,4},{9,5},... | collective-permute-start | bytes 393224 | tf_op jit(solution)/shard_map/ppermute | solution.py:94
  81.3 7.1 %collective-permute-start.12 = (f32[256,256]{1,0:T(8,128)S(1)}, f32[256,256]{1,0:T(8,128)S(1)}, u32[]{:S(2)}, u32[]{:S(2)}) collective-permute-start(f32[256,256]{1,0:T(8,128)S(1)} %get-tuple-element.35.refs_2_), channel_id=1, source_target_pairs={{1,0},{0,1},{3,2},{2,3},{5,4},{4,5},{7,6},{6,7},{9,8},{8,9},{11,10... | collective-permute-start | bytes 786440 | tf_op jit(solution)/shard_map/ppermute | solution.py:75
  87.8 7.3 %copy-start.2 = (f32[2,128,512]{2,1,0:T(8,128)S(1)}, f32[2,128,512]{2,1,0:T(8,128)}, u32[]{:S(2)}) copy-start(f32[2,128,512]{2,1,0:T(8,128)} %refs_1_.1) | copy-start | bytes 1572868
  87.8 7.3 %collective-permute-start.18 = (f32[2,64,512]{2,1,0:T(8,128)S(1)}, f32[2,64,512]{2,1,0:T(8,128)S(1)}, u32[]{:S(2)}, u32[]{:S(2)}) collective-permute-start(f32[2,64,512]{2,1,0:T(8,128)S(1)} %place.1.refs_2_), channel_id=1, source_target_pairs={{2,0},{3,1},{0,2},{1,3},{6,4},{7,5},{4,6},{5,7},{10,8},{11,9},{8,1... | collective-permute-start | bytes 786440 | tf_op jit(solution)/shard_map/ppermute | solution.py:82
  95.1 1.6 %collective-permute-start.19 = (f32[2,64,512]{2,1,0:T(8,128)S(1)}, f32[2,64,512]{2,1,0:T(8,128)S(1)}, u32[]{:S(2)}, u32[]{:S(2)}) collective-permute-start(f32[2,64,512]{2,1,0:T(8,128)S(1)} %update.1.refs_0_), channel_id=1, source_target_pairs={{1,0},{0,1},{3,2},{2,3},{5,4},{4,5},{7,6},{6,7},{9,8},{8,9},{11,10... | collective-permute-start | bytes 786440 | tf_op jit(solution)/shard_map/ppermute | solution.py:75
  (3 other events, 2.7 us)

commit v10 on v9

--- a/solution.py
+++ b/solution.py
@@ -574,12 +574,18 @@
         out[plane] = block[plane, rows, :] + total / density[...]
 
 
-def join_kernel(layout, *refs):
-    strips, out = refs[:-1], refs[-1]
+def join_kernel(layout, first, *refs):
+    strips, (out, done) = refs[:-2], refs[-2:]
     _, _, _, core = layout.place()
-    for step, strip in enumerate(strips):
-        first = (core + step) % layout.cores * layout.strip
-        out[:, pl.ds(pl.multiple_of(first, layout.strip), layout.strip), :] = strip[...]
+    copies = []
+    for step, strip in enumerate(strips, start=first):
+        row = (core + step) % layout.cores * layout.strip
+        rows = pl.ds(pl.multiple_of(row, layout.strip), layout.strip)
+        copies.append(pltpu.make_async_copy(strip, out.at[:, rows, :], done.at[step]))
+    for copy in copies:
+        copy.start()
+    for copy in copies:
+        copy.wait()
 
 
 def call(kernel, name, operands, outputs, scratch=(), scalar_count=0, after=()):
@@ -747,6 +753,7 @@
         [(strip, layout.width)],
         scratch=[(2 * length, length), (strip, layout.width + lanes)],
         scalar_count=2,
+        after=(probe_out,),
     )
     (placed,) = call(
         functools.partial(place_kernel, layout),
@@ -763,9 +770,25 @@
         (density, object_bands, *placed),
         [(2, strip, layout.width)],
     )
-    (object_out,) = call(
-        functools.partial(join_kernel, layout), "join", from_cores(new_rows), [object_bands.shape]
-    )
+    whole = pl.BlockSpec(memory_space=pl.ANY)
+    settings = {
+        "name": "join",
+        "out_shape": jax.ShapeDtypeStruct(object_bands.shape, single),
+        "out_specs": whole,
+        "scratch_shapes": [pltpu.SemaphoreType.DMA((cores,))],
+        "compiler_params": pltpu.CompilerParams(vmem_limit_bytes=28 * 2**20),
+    }
+    own, *others = from_cores(new_rows)
+    object_out = pl.pallas_call(
+        functools.partial(join_kernel, layout, 0), in_specs=[on_chip], **settings
+    )(own)
+    if others:
+        object_out = pl.pallas_call(
+            lambda before, *refs: join_kernel(layout, 1, *refs),
+            in_specs=[whole] + [on_chip] * len(others),
+            input_output_aliases={0: 0},
+            **settings,
+        )(object_out, *others)
     return probe_out, object_out
 
 

time: 97.8 us -> 97.7 us (level)
  waiting for transfers between devices: 31.7 us -> 30 us
  local copies, waits for them, and re-layouts: 0.7 us -> 1.74 us
    ppermute x2, waiting for transfers between devices: 6.08 us -> 4.2 us  [from_twin(): return lax.ppermute(array, axes, pairs)]
    pallas_call x0 -> x2, Pallas kernels: none -> 1.46 us  [the longest x1 0.74 us: body(): pl.pallas_call(functools.partial(join_kernel, layout, 0), in_specs=[on_ch...]
    unnamed x14 -> x16, local copies, waits for them, and re-layouts: 0.7 us -> 1.74 us
    pallas_call x14 -> x13, Pallas kernels: 10.6 us -> 9.73 us  [call(): pl.pallas_call(inner, name=name, out_shape=shapes, in_specs=[on_chip] * c...]
  transfers between devices with their start and end apart: 20 -> 20, of which waited for: 12 -> 12; matrix products, arithmetic and copies ran while one was open for 0% -> 0% of each run, Pallas kernels for 3% -> 4%
where the time goes in v10:
time: 97.7 us; the launch traced here: 97.4 us
  blocking collectives  30.2 us (31%)
  waiting for transfers between devices  30 us (31%)
  starting transfers between devices  22.2 us (23%)
  Pallas kernels  12.5 us (13%)
  local copies, waits for them, and re-layouts  1.74 us (2%)
    all_to_all x2, blocking collectives, within_cube(): lax.all_to_all(array, axes, split_axis=0, concat_axis=0, tiled=True, axis...  30.2 us
    ppermute x2, waiting for transfers between devices, from_upper(): return lax.ppermute(array, axes, pairs)  12.7 us
    pallas_call x13, Pallas kernels, call(): pl.pallas_call(inner, name=name, out_shape=shapes, in_specs=[on_chip] * c...  9.73 us
    ppermute x6, starting transfers between devices, to_row(): return lax.ppermute(array, axes, pairs)  7.04 us
    ppermute x9, waiting for transfers between devices, from_core(): return lax.ppermute(array, axes, pairs)  6.82 us
    ppermute x6, waiting for transfers between devices, to_row(): return lax.ppermute(array, axes, pairs)  6.25 us
    ppermute x2, starting transfers between devices, from_upper(): return lax.ppermute(array, axes, pairs)  5.86 us
    ppermute x1, starting transfers between devices, body(): part_measured = lax.ppermute(part_measured, axes, pairs)  4.49 us
  transfers between devices with their start and end apart: 20, of which 12 were waited for; matrix products, arithmetic and copies ran while one was open for 0% of the time, Pallas kernels for 4%

profile of v10, /device:TPU:0, one launch (start us, length us, event | category | flops | bytes accessed | tf_op | source)
XLA Modules:
  0.0 97.4 jit_solution(16945194534738776062)
XLA Ops:
  0.6 1.3 %cut.1 = (f32[2,64,256]{2,1,0:T(8,128)S(1)}, f32[2,64,256]{2,1,0:T(8,128)S(1)}, f32[2,64,256]{2,1,0:T(8,128)S(1)}, f32[2,64,256]{2,1,0:T(8,128)S(1)}, f32[1,128,256]{2,1,0:T(8,128)S(1)}) custom-call(s32[2,8]{1,0:T(2,128)} %bitcast.2, s32[8]{0:T(128)} %owners.1, f32[2,128,512]{2,1,0:T(8,128)} %refs_1_.1, f32[1,256,256]{2,1,0:T(8,128)} %refs_0_.1), custom_call_target="tpu_custom_call" | custom-call | tf_op jit(solution)/shard_map/cut/pallas_call | solution.py:632
  2.0 3.0 %collective-permute-start.8 = (f32[2,1,256,256]{3,2,1,0:T(8,128)S(1)}, f32[2,1,256,256]{3,2,1,0:T(8,128)S(1)}, u32[]{:S(2)}, u32[]{:S(2)}) collective-permute-start(f32[2,1,256,256]{3,2,1,0:T(8,128)S(1)} %copy-done.5), channel_id=1, source_target_pairs={{2,0},{3,1},{0,2},{1,3},{6,4},{7,5},{4,6},{5,7},{10,8},{11,9},{8,1... | collective-permute-start | bytes 1572872 | tf_op jit(solution)/shard_map/ppermute | solution.py:82
  5.0 1.5 %collective-permute-start = (f32[2,64,256]{2,1,0:T(8,128)S(1)}, f32[2,64,256]{2,1,0:T(8,128)S(1)}, u32[]{:S(2)}, u32[]{:S(2)}) collective-permute-start(f32[2,64,256]{2,1,0:T(8,128)S(1)} %get-tuple-element.23), channel_id=1, source_target_pairs={{0,4},{1,5},{2,6},{3,7},{4,0},{5,1},{6,2},{7,3},{8,12},{9,13},{10,... | collective-permute-start | bytes 393224 | tf_op jit(solution)/shard_map/ppermute | solution.py:94
  6.5 1.6 %collective-permute-start.1 = (f32[2,64,256]{2,1,0:T(8,128)S(1)}, f32[2,64,256]{2,1,0:T(8,128)S(1)}, u32[]{:S(2)}, u32[]{:S(2)}) collective-permute-start(f32[2,64,256]{2,1,0:T(8,128)S(1)} %get-tuple-element.24), channel_id=1, source_target_pairs={{0,8},{1,9},{2,10},{3,11},{4,12},{5,13},{6,14},{7,15},{8,0},{9,1},... | collective-permute-start | bytes 393224 | tf_op jit(solution)/shard_map/ppermute | solution.py:94
  8.5 4.5 %collective-permute-start.4 = (f32[1,128,256]{2,1,0:T(8,128)S(1)}, f32[1,128,256]{2,1,0:T(8,128)S(1)}, u32[]{:S(2)}, u32[]{:S(2)}) collective-permute-start(f32[1,128,256]{2,1,0:T(8,128)S(1)} %get-tuple-element.28), channel_id=1, source_target_pairs={{18,2},{19,3},{22,6},{23,7},{26,10},{27,11},{30,14},{31,15},{0,16}... | collective-permute-start | bytes 393224 | tf_op jit(solution)/shard_map/ppermute | solution.py:660
  14.7 2.7 %collective-permute-start.3 = (f32[1,2,2,64,256]{4,3,2,1,0:T(8,128)S(1)}, f32[1,2,2,64,256]{4,3,2,1,0:T(8,128)S(1)}, u32[]{:S(2)}, u32[]{:S(2)}) collective-permute-start(f32[1,2,2,64,256]{4,3,2,1,0:T(8,128)S(1)} %choose.3.refs_1_), channel_id=1, source_target_pairs={{16,0},{17,1},{18,2},{19,3},{20,4},{21,5},{22,6},{23,7},{24,8},{25... | collective-permute-start | bytes 786440 | tf_op jit(solution)/shard_map/ppermute | solution.py:68
  17.9 1.6 %collective-permute-done.5.refs_2_ = f32[1,128,256]{2,1,0:T(8,128)S(1)} collective-permute-done((f32[1,128,256]{2,1,0:T(8,128)S(1)}, f32[1,128,256]{2,1,0:T(8,128)S(1)}, u32[]{:S(2)}, u32[]{:S(2)}) %collective-permute-start.5) | collective-permute-done | bytes 131104 | tf_op jit(solution)/shard_map/ppermute | solution.py:75
  20.4 9.4 %collective-permute-done.3.refs_2_ = f32[1,2,2,64,256]{4,3,2,1,0:T(8,128)S(1)} collective-permute-done((f32[1,2,2,64,256]{4,3,2,1,0:T(8,128)S(1)}, f32[1,2,2,64,256]{4,3,2,1,0:T(8,128)S(1)}, u32[]{:S(2)}, u32[]{:S(2)}) %collective-permute-start.3) | collective-permute-done | bytes 262176 | tf_op jit(solution)/shard_map/ppermute | solution.py:68
  29.8 1.5 %collective-permute-done.7.refs_4_ = f32[1,2,2,64,256]{4,3,2,1,0:T(8,128)S(1)} collective-permute-done((f32[1,2,2,64,256]{4,3,2,1,0:T(8,128)S(1)}, f32[1,2,2,64,256]{4,3,2,1,0:T(8,128)S(1)}, u32[]{:S(2)}, u32[]{:S(2)}) %collective-permute-start.7) | collective-permute-done | bytes 262176 | tf_op jit(solution)/shard_map/ppermute | solution.py:75
  31.3 3.4 %first.1 = (f32[1,2,256,256]{3,2,1,0:T(8,128)S(1)}, f32[8,80,256]{2,1,0:T(8,128)S(1)}, f32[2,1,2,32,256]{4,3,2,1,0:T(8,128)S(1)}) custom-call(s32[2,8]{1,0:T(2,128)S(1)} %bitcast.5, f32[1,2,2,64,256]{4,3,2,1,0:T(8,128)S(1)} %choose.3.refs_1_, f32[1,2,2,64,256]{4,3,2,1,0:T(8,128)S(1)} %collective-permute-done.3.refs_2_, ...), custom_call_target="tpu_custom_call" | custom-call | tf_op jit(solution)/shard_map/first/pallas_call | solution.py:599
  34.8 14.2 %all_to_all.10.refs_0_ = f32[8,80,256]{2,1,0:T(8,128)S(1)} all-to-all(f32[8,80,256]{2,1,0:T(8,128)S(1)} %get-tuple-element.33), channel_id=1, replica_groups={{0,4,8,12,2,6,10,14},{1,5,9,13,3,7,11,15},{16,20,24,28,18,22,26,30},{17..., dimensions={0} | all-to-all | bytes 1310720 | tf_op jit(solution)/shard_map/all_to_all | solution.py:97
  49.0 3.2 %collective-permute-start.11 = (f32[80,256]{1,0:T(8,128)S(1)}, f32[80,256]{1,0:T(8,128)S(1)}, u32[]{:S(2)}, u32[]{:S(2)}) collective-permute-start(f32[80,256]{1,0:T(8,128)S(1)} %sum.1.refs_1_), channel_id=1, source_target_pairs={{16,0},{17,1},{18,2},{19,3},{20,4},{21,5},{22,6},{23,7},{24,8},{25... | collective-permute-start | bytes 245768 | tf_op jit(solution)/shard_map/ppermute | solution.py:68
  52.1 3.3 %collective-permute-done.11.refs_2_ = f32[80,256]{1,0:T(8,128)S(1)} collective-permute-done((f32[80,256]{1,0:T(8,128)S(1)}, f32[80,256]{1,0:T(8,128)S(1)}, u32[]{:S(2)}, u32[]{:S(2)}) %collective-permute-start.11) | collective-permute-done | bytes 81952 | tf_op jit(solution)/shard_map/ppermute | solution.py:68
  55.6 16.0 %all_to_all.11.refs_0_.refs_4_ = f32[8,2,1,2,32,256]{5,4,3,2,1,0:T(8,128)S(1)} all-to-all(f32[8,2,1,2,32,256]{5,4,3,2,1,0:T(8,128)S(1)} %step.1), channel_id=1, replica_groups={{0,4,8,12,2,6,10,14},{1,5,9,13,3,7,11,15},{16,20,24,28,18,22,26,30},{17..., dimensions={0} | all-to-all | bytes 2097152 | tf_op jit(solution)/shard_map/all_to_all | solution.py:97
  71.6 1.3 %again.1 = (f32[256,256]{1,0:T(8,128)S(1)}, f32[1,256,256]{2,1,0:T(8,128)S(1)}, f32[1,2,512,256]{3,2,1,0:T(8,128)S(1)}) custom-call(f32[8,2,1,2,32,256]{5,4,3,2,1,0:T(8,128)S(1)} %all_to_all.11.refs_0_.refs_4_, f32[1,2,256,256]{3,2,1,0:T(8,128)S(1)} %get-tuple-element.34.refs_1_, bf16[2,2,256,256]{3,2,1,0:T(8,128)(2,1)S(1)} %copy-done.1, ...), custom_call_target="tpu_custom_call" | custom-call | tf_op jit(solution)/shard_map/again/pallas_call | solution.py:599
  72.9 1.5 %collective-permute-done.13.refs_2_ = f32[1,256,256]{2,1,0:T(8,128)S(1)} collective-permute-done((f32[1,256,256]{2,1,0:T(8,128)S(1)}, f32[1,256,256]{2,1,0:T(8,128)S(1)}, u32[]{:S(2)}, u32[]{:S(2)}) %collective-permute-start.13) | collective-permute-done | bytes 262176 | tf_op jit(solution)/shard_map/ppermute | solution.py:75
  74.5 1.5 %terms.1 = (f32[1,2,2,64,256]{4,3,2,1,0:T(8,128)S(1)}, f32[1,2,2,64,256]{4,3,2,1,0:T(8,128)S(1)}) custom-call(s32[2,8]{1,0:T(2,128)S(1)} %bitcast.6, f32[1,256,256]{2,1,0:T(8,128)S(1)} %get-tuple-element.36.refs_1_, f32[1,256,256]{2,1,0:T(8,128)S(1)} %collective-permute-done.13.refs_2_, f32[1,256,256]{2,1,0:T(8,128)S(1)} %order.1.refs_9_.refs_3_, ...), custom_call_target="tpu_custom_call" | custom-call | tf_op jit(solution)/shard_map/terms/pallas_call | solution.py:599
  76.1 1.4 %collective-permute-done.14.refs_3_ = f32[1,2,2,64,256]{4,3,2,1,0:T(8,128)S(1)} collective-permute-done((f32[1,2,2,64,256]{4,3,2,1,0:T(8,128)S(1)}, f32[1,2,2,64,256]{4,3,2,1,0:T(8,128)S(1)}, u32[]{:S(2)}, u32[]{:S(2)}) %collective-permute-start.14) | collective-permute-done | bytes 262176 | tf_op jit(solution)/shard_map/ppermute | solution.py:75
  78.9 2.4 %collective-permute-start.17 = (f32[2,64,256]{2,1,0:T(8,128)S(1)}, f32[2,64,256]{2,1,0:T(8,128)S(1)}, u32[]{:S(2)}, u32[]{:S(2)}) collective-permute-start(f32[2,64,256]{2,1,0:T(8,128)S(1)} %get-tuple-element.43), channel_id=1, source_target_pairs={{0,12},{1,13},{2,14},{3,15},{4,8},{5,9},{6,10},{7,11},{8,4},{9,5},... | collective-permute-start | bytes 393224 | tf_op jit(solution)/shard_map/ppermute | solution.py:94
  81.3 2.0 %collective-permute-done.15.refs_3_ = f32[2,64,256]{2,1,0:T(8,128)S(1)} collective-permute-done((f32[2,64,256]{2,1,0:T(8,128)S(1)}, f32[2,64,256]{2,1,0:T(8,128)S(1)}, u32[]{:S(2)}, u32[]{:S(2)}) %collective-permute-start.15) | collective-permute-done | bytes 131104 | tf_op jit(solution)/shard_map/ppermute | solution.py:94
  83.4 1.0 %collective-permute-done.16.refs_4_ = f32[2,64,256]{2,1,0:T(8,128)S(1)} collective-permute-done((f32[2,64,256]{2,1,0:T(8,128)S(1)}, f32[2,64,256]{2,1,0:T(8,128)S(1)}, u32[]{:S(2)}, u32[]{:S(2)}) %collective-permute-start.16) | collective-permute-done | bytes 131104 | tf_op jit(solution)/shard_map/ppermute | solution.py:94
  84.4 3.0 %collective-permute-done.17.refs_5_ = f32[2,64,256]{2,1,0:T(8,128)S(1)} collective-permute-done((f32[2,64,256]{2,1,0:T(8,128)S(1)}, f32[2,64,256]{2,1,0:T(8,128)S(1)}, u32[]{:S(2)}, u32[]{:S(2)}) %collective-permute-start.17) | collective-permute-done | bytes 131104 | tf_op jit(solution)/shard_map/ppermute | solution.py:94
  89.2 1.0 %copy-done.2 = f32[2,1,256,256]{3,2,1,0:T(8,128)S(1)} copy-done((f32[2,1,256,256]{3,2,1,0:T(8,128)S(1)}, f32[2,1,256,256]{3,2,1,0:T(8,128)}, u32[]{:S(2)}) %copy-start.2) | copy-done | bytes 524312
  90.8 4.2 %collective-permute-done.18.refs_3_ = f32[2,64,512]{2,1,0:T(8,128)S(1)} collective-permute-done((f32[2,64,512]{2,1,0:T(8,128)S(1)}, f32[2,64,512]{2,1,0:T(8,128)S(1)}, u32[]{:S(2)}, u32[]{:S(2)}) %collective-permute-start.18) | collective-permute-done | bytes 262176 | tf_op jit(solution)/shard_map/ppermute | solution.py:82
  (50 shorter events, 10.1 us)
Async XLA Ops:
  2.0 15.4 %collective-permute-start.8 = (f32[2,1,256,256]{3,2,1,0:T(8,128)S(1)}, f32[2,1,256,256]{3,2,1,0:T(8,128)S(1)}, u32[]{:S(2)}, u32[]{:S(2)}) collective-permute-start(f32[2,1,256,256]{3,2,1,0:T(8,128)S(1)} %copy-done.5), channel_id=1, source_target_pairs={{2,0},{3,1},{0,2},{1,3},{6,4},{7,5},{4,6},{5,7},{10,8},{11,9},{8,1... | collective-permute-start | bytes 1572872 | tf_op jit(solution)/shard_map/ppermute | solution.py:82
  5.0 9.0 %collective-permute-start = (f32[2,64,256]{2,1,0:T(8,128)S(1)}, f32[2,64,256]{2,1,0:T(8,128)S(1)}, u32[]{:S(2)}, u32[]{:S(2)}) collective-permute-start(f32[2,64,256]{2,1,0:T(8,128)S(1)} %get-tuple-element.23), channel_id=1, source_target_pairs={{0,4},{1,5},{2,6},{3,7},{4,0},{5,1},{6,2},{7,3},{8,12},{9,13},{10,... | collective-permute-start | bytes 393224 | tf_op jit(solution)/shard_map/ppermute | solution.py:94
  6.5 7.6 %collective-permute-start.1 = (f32[2,64,256]{2,1,0:T(8,128)S(1)}, f32[2,64,256]{2,1,0:T(8,128)S(1)}, u32[]{:S(2)}, u32[]{:S(2)}) collective-permute-start(f32[2,64,256]{2,1,0:T(8,128)S(1)} %get-tuple-element.24), channel_id=1, source_target_pairs={{0,8},{1,9},{2,10},{3,11},{4,12},{5,13},{6,14},{7,15},{8,0},{9,1},... | collective-permute-start | bytes 393224 | tf_op jit(solution)/shard_map/ppermute | solution.py:94
  8.1 6.2 %collective-permute-start.2 = (f32[2,64,256]{2,1,0:T(8,128)S(1)}, f32[2,64,256]{2,1,0:T(8,128)S(1)}, u32[]{:S(2)}, u32[]{:S(2)}) collective-permute-start(f32[2,64,256]{2,1,0:T(8,128)S(1)} %get-tuple-element.25), channel_id=1, source_target_pairs={{0,12},{1,13},{2,14},{3,15},{4,8},{5,9},{6,10},{7,11},{8,4},{9,5},... | collective-permute-start | bytes 393224 | tf_op jit(solution)/shard_map/ppermute | solution.py:94
  8.5 8.9 %collective-permute-start.4 = (f32[1,128,256]{2,1,0:T(8,128)S(1)}, f32[1,128,256]{2,1,0:T(8,128)S(1)}, u32[]{:S(2)}, u32[]{:S(2)}) collective-permute-start(f32[1,128,256]{2,1,0:T(8,128)S(1)} %get-tuple-element.28), channel_id=1, source_target_pairs={{18,2},{19,3},{22,6},{23,7},{26,10},{27,11},{30,14},{31,15},{0,16}... | collective-permute-start | bytes 393224 | tf_op jit(solution)/shard_map/ppermute | solution.py:660
  14.0 5.5 %copy-start.4 = (f32[1,256,256]{2,1,0:T(8,128)S(1)}, f32[1,256,256]{2,1,0:T(8,128)}, u32[]{:S(2)}) copy-start(f32[1,256,256]{2,1,0:T(8,128)} %refs_0_.1) | copy-start | bytes 786436
  14.0 15.8 %collective-permute-start.9 = (f32[2,1,256,256]{3,2,1,0:T(8,128)S(1)}, f32[2,1,256,256]{3,2,1,0:T(8,128)S(1)}, u32[]{:S(2)}, u32[]{:S(2)}) collective-permute-start(f32[2,1,256,256]{3,2,1,0:T(8,128)S(1)} %copy-done.5), channel_id=1, source_target_pairs={{1,0},{0,1},{3,2},{2,3},{5,4},{4,5},{7,6},{6,7},{9,8},{8,9},{11,10... | collective-permute-start | bytes 1572872 | tf_op jit(solution)/shard_map/ppermute | solution.py:75
  14.3 17.0 %copy-start.1 = (bf16[2,2,256,256]{3,2,1,0:T(8,128)(2,1)S(1)}, bf16[2,2,256,256]{3,2,1,0:T(8,128)(2,1)}, u32[]{:S(2)}) copy-start(bf16[2,2,256,256]{3,2,1,0:T(8,128)(2,1)} %constant.4.clone.refs_10_.refs_2_.refs_6_) | copy-start | bytes 1572868
  14.7 16.7 %copy-start = (bf16[2,2,256,256]{3,2,1,0:T(8,128)(2,1)S(1)}, bf16[2,2,256,256]{3,2,1,0:T(8,128)(2,1)}, u32[]{:S(2)}) copy-start(bf16[2,2,256,256]{3,2,1,0:T(8,128)(2,1)} %constant.5.clone.refs_11_.refs_3_.refs_7_) | copy-start | bytes 1572868
  14.7 15.1 %collective-permute-start.3 = (f32[1,2,2,64,256]{4,3,2,1,0:T(8,128)S(1)}, f32[1,2,2,64,256]{4,3,2,1,0:T(8,128)S(1)}, u32[]{:S(2)}, u32[]{:S(2)}) collective-permute-start(f32[1,2,2,64,256]{4,3,2,1,0:T(8,128)S(1)} %choose.3.refs_1_), channel_id=1, source_target_pairs={{16,0},{17,1},{18,2},{19,3},{20,4},{21,5},{22,6},{23,7},{24,8},{25... | collective-permute-start | bytes 786440 | tf_op jit(solution)/shard_map/ppermute | solution.py:68
  17.4 14.0 %collective-permute-start.10 = (f32[2,1,256,256]{3,2,1,0:T(8,128)S(1)}, f32[2,1,256,256]{3,2,1,0:T(8,128)S(1)}, u32[]{:S(2)}, u32[]{:S(2)}) collective-permute-start(f32[2,1,256,256]{3,2,1,0:T(8,128)S(1)} %collective-permute-done.8.refs_6_), channel_id=1, source_target_pairs={{1,0},{0,1},{3,2},{2,3},{5,4},{4,5},{7,6},{6,7},{9,8},{8,9},{11,10... | collective-permute-start | bytes 1572872 | tf_op jit(solution)/shard_map/ppermute | solution.py:75
  17.4 2.1 %collective-permute-start.5 = (f32[1,128,256]{2,1,0:T(8,128)S(1)}, f32[1,128,256]{2,1,0:T(8,128)S(1)}, u32[]{:S(2)}, u32[]{:S(2)}) collective-permute-start(f32[1,128,256]{2,1,0:T(8,128)S(1)} %collective-permute-done.4.refs_1_), channel_id=1, source_target_pairs={{1,0},{0,1},{3,2},{2,3},{5,4},{4,5},{7,6},{6,7},{9,8},{8,9},{11,10... | collective-permute-start | bytes 393224 | tf_op jit(solution)/shard_map/ppermute | solution.py:75
  20.2 9.6 %collective-permute-start.6 = (f32[1,2,2,64,256]{4,3,2,1,0:T(8,128)S(1)}, f32[1,2,2,64,256]{4,3,2,1,0:T(8,128)S(1)}, u32[]{:S(2)}, u32[]{:S(2)}) collective-permute-start(f32[1,2,2,64,256]{4,3,2,1,0:T(8,128)S(1)} %choose.3.refs_1_), channel_id=1, source_target_pairs={{1,0},{0,1},{3,2},{2,3},{5,4},{4,5},{7,6},{6,7},{9,8},{8,9},{11,10... | collective-permute-start | bytes 786440 | tf_op jit(solution)/shard_map/ppermute | solution.py:75
  29.8 1.5 %collective-permute-start.7 = (f32[1,2,2,64,256]{4,3,2,1,0:T(8,128)S(1)}, f32[1,2,2,64,256]{4,3,2,1,0:T(8,128)S(1)}, u32[]{:S(2)}, u32[]{:S(2)}) collective-permute-start(f32[1,2,2,64,256]{4,3,2,1,0:T(8,128)S(1)} %collective-permute-done.3.refs_2_), channel_id=1, source_target_pairs={{1,0},{0,1},{3,2},{2,3},{5,4},{4,5},{7,6},{6,7},{9,8},{8,9},{11,10... | collective-permute-start | bytes 786440 | tf_op jit(solution)/shard_map/ppermute | solution.py:75
  49.0 6.5 %collective-permute-start.11 = (f32[80,256]{1,0:T(8,128)S(1)}, f32[80,256]{1,0:T(8,128)S(1)}, u32[]{:S(2)}, u32[]{:S(2)}) collective-permute-start(f32[80,256]{1,0:T(8,128)S(1)} %sum.1.refs_1_), channel_id=1, source_target_pairs={{16,0},{17,1},{18,2},{19,3},{20,4},{21,5},{22,6},{23,7},{24,8},{25... | collective-permute-start | bytes 245768 | tf_op jit(solution)/shard_map/ppermute | solution.py:68
  72.8 1.6 %collective-permute-start.13 = (f32[1,256,256]{2,1,0:T(8,128)S(1)}, f32[1,256,256]{2,1,0:T(8,128)S(1)}, u32[]{:S(2)}, u32[]{:S(2)}) collective-permute-start(f32[1,256,256]{2,1,0:T(8,128)S(1)} %get-tuple-element.36.refs_1_), channel_id=1, source_target_pairs={{1,0},{0,1},{3,2},{2,3},{5,4},{4,5},{7,6},{6,7},{9,8},{8,9},{11,10... | collective-permute-start | bytes 786440 | tf_op jit(solution)/shard_map/ppermute | solution.py:75
  75.9 1.6 %collective-permute-start.14 = (f32[1,2,2,64,256]{4,3,2,1,0:T(8,128)S(1)}, f32[1,2,2,64,256]{4,3,2,1,0:T(8,128)S(1)}, u32[]{:S(2)}, u32[]{:S(2)}) collective-permute-start(f32[1,2,2,64,256]{4,3,2,1,0:T(8,128)S(1)} %get-tuple-element.39), channel_id=1, source_target_pairs={{1,0},{0,1},{3,2},{2,3},{5,4},{4,5},{7,6},{6,7},{9,8},{8,9},{11,10... | collective-permute-start | bytes 786440 | tf_op jit(solution)/shard_map/ppermute | solution.py:75
  77.8 5.6 %collective-permute-start.15 = (f32[2,64,256]{2,1,0:T(8,128)S(1)}, f32[2,64,256]{2,1,0:T(8,128)S(1)}, u32[]{:S(2)}, u32[]{:S(2)}) collective-permute-start(f32[2,64,256]{2,1,0:T(8,128)S(1)} %get-tuple-element.41), channel_id=1, source_target_pairs={{0,4},{1,5},{2,6},{3,7},{4,0},{5,1},{6,2},{7,3},{8,12},{9,13},{10,... | collective-permute-start | bytes 393224 | tf_op jit(solution)/shard_map/ppermute | solution.py:94
  78.0 6.4 %collective-permute-start.16 = (f32[2,64,256]{2,1,0:T(8,128)S(1)}, f32[2,64,256]{2,1,0:T(8,128)S(1)}, u32[]{:S(2)}, u32[]{:S(2)}) collective-permute-start(f32[2,64,256]{2,1,0:T(8,128)S(1)} %get-tuple-element.42), channel_id=1, source_target_pairs={{0,8},{1,9},{2,10},{3,11},{4,12},{5,13},{6,14},{7,15},{8,0},{9,1},... | collective-permute-start | bytes 393224 | tf_op jit(solution)/shard_map/ppermute | solution.py:94
  78.9 8.4 %collective-permute-start.17 = (f32[2,64,256]{2,1,0:T(8,128)S(1)}, f32[2,64,256]{2,1,0:T(8,128)S(1)}, u32[]{:S(2)}, u32[]{:S(2)}) collective-permute-start(f32[2,64,256]{2,1,0:T(8,128)S(1)} %get-tuple-element.43), channel_id=1, source_target_pairs={{0,12},{1,13},{2,14},{3,15},{4,8},{5,9},{6,10},{7,11},{8,4},{9,5},... | collective-permute-start | bytes 393224 | tf_op jit(solution)/shard_map/ppermute | solution.py:94
  81.3 7.9 %collective-permute-start.12 = (f32[256,256]{1,0:T(8,128)S(1)}, f32[256,256]{1,0:T(8,128)S(1)}, u32[]{:S(2)}, u32[]{:S(2)}) collective-permute-start(f32[256,256]{1,0:T(8,128)S(1)} %get-tuple-element.35.refs_2_), channel_id=1, source_target_pairs={{1,0},{0,1},{3,2},{2,3},{5,4},{4,5},{7,6},{6,7},{9,8},{8,9},{11,10... | collective-permute-start | bytes 786440 | tf_op jit(solution)/shard_map/ppermute | solution.py:75
  87.8 7.3 %collective-permute-start.18 = (f32[2,64,512]{2,1,0:T(8,128)S(1)}, f32[2,64,512]{2,1,0:T(8,128)S(1)}, u32[]{:S(2)}, u32[]{:S(2)}) collective-permute-start(f32[2,64,512]{2,1,0:T(8,128)S(1)} %place.1.refs_2_), channel_id=1, source_target_pairs={{2,0},{3,1},{0,2},{1,3},{6,4},{7,5},{4,6},{5,7},{10,8},{11,9},{8,1... | collective-permute-start | bytes 786440 | tf_op jit(solution)/shard_map/ppermute | solution.py:82
  90.3 4.8 %copy-start.3 = (f32[2,128,512]{2,1,0:T(8,128)S(1)}, f32[2,128,512]{2,1,0:T(8,128)}, u32[]{:S(2)}) copy-start(f32[2,128,512]{2,1,0:T(8,128)} %refs_1_.1) | copy-start | bytes 1572868
  95.1 1.6 %collective-permute-start.19 = (f32[2,64,512]{2,1,0:T(8,128)S(1)}, f32[2,64,512]{2,1,0:T(8,128)S(1)}, u32[]{:S(2)}, u32[]{:S(2)}) collective-permute-start(f32[2,64,512]{2,1,0:T(8,128)S(1)} %update.1.refs_0_), channel_id=1, source_target_pairs={{1,0},{0,1},{3,2},{2,3},{5,4},{4,5},{7,6},{6,7},{9,8},{8,9},{11,10... | collective-permute-start | bytes 786440 | tf_op jit(solution)/shard_map/ppermute | solution.py:75
  (4 other events, 3.8 us)
